TPU v7x, 32 devices: a whole 2x2x4 slice. The times are simulated.
32 devices in a mesh: dp: 8 (over y, x, core), tensor: 4 (over z).
Axes of the slice: x: 2, y: 2, z: 4, core: 2. Of those that a mesh axis runs over, the one named last changes fastest.
Arguments:
- tokens: bfloat16 [5120, 2048], P('dp'), may hold values from -6 to 6
- w_query: bfloat16 [2048, 2048], P(None, 'tensor'), may hold values from -0.125 to 0.125
- w_key: bfloat16 [2048, 2048], P(None, 'tensor'), may hold values from -0.125 to 0.125
- w_value: bfloat16 [2048, 2048], P(None, 'tensor'), may hold values from -0.125 to 0.125
- w_out: bfloat16 [2048, 2048], P('tensor'), may hold values from -2 to 2
- w_gate: bfloat16 [2048, 8192], P(None, 'tensor'), may hold values from -0.125 to 0.125
- w_up: bfloat16 [2048, 8192], P(None, 'tensor'), may hold values from -0.125 to 0.125
- w_down: bfloat16 [8192, 2048], P('tensor'), may hold values from -0.125 to 0.125
- cotangent: bfloat16 [5120, 2048], P('dp'), may hold values from -6 to 6
- slot_parent: int32 [40], replicated, may hold values from -1 to 39, as said below
Outputs:
- output: bfloat16 [5120, 2048], P('dp')
- grad_tokens: bfloat16 [5120, 2048], P('dp')
- grad_query: float32 [2048, 2048], P('dp', 'tensor')
- grad_key: float32 [2048, 2048], P('dp', 'tensor')
- grad_value: float32 [2048, 2048], P('dp', 'tensor')
- grad_out: float32 [2048, 2048], P('tensor', 'dp')
- grad_gate: float32 [2048, 8192], P('dp', 'tensor')
- grad_up: float32 [2048, 8192], P('dp', 'tensor')
- grad_down: float32 [8192, 2048], P('tensor', 'dp')
Inputs may be any that keep to these rules, and one draw needn't show every extreme that they name: `slot_parent`: the pack holds 2 trees of 8 + 4 * (3) blocks: a trunk of 8 blocks in a chain (its first block's entry is -1, each later one names the one before), 4 branch blocks whose parent is the trunk's last block, and 2 leaf blocks under each branch. Every slot holds one block; slot s lies on index s // 5 of dp.
All inputs are finite; a program needn't handle non-finite values.
Results may differ from a plain program's by a relative error of at most 0.024.
Values may be sent and summed in bfloat16 or wider, within the bound.
No kernel may reach another device: no remote copies, remote signals or barrier semaphores. Data moves between devices by JAX's collectives and lax.ppermute only.
A program may use at most 256 MiB of HBM per device.

v0:
```python
import math

import jax
import jax.numpy as jnp
from jax import lax
from jax.sharding import PartitionSpec as P

HEAD = 128
BLOCK = 128
TRUNK_BLOCKS = 8


EPSILON = 1e-05
NEGATIVE = -1e30
HIGH = lax.Precision.HIGHEST


def layer_norm(values):
    centered = values - jnp.mean(values, axis=-1, keepdims=True)
    variance = jnp.mean(centered * centered, axis=-1, keepdims=True)
    inverse = lax.rsqrt(variance + EPSILON)
    return (centered * inverse, inverse)


def norm_back(gradient, normed, inverse):
    return inverse * (
        gradient
        - jnp.mean(gradient, axis=-1, keepdims=True)
        - normed * jnp.mean(gradient * normed, axis=-1, keepdims=True)
    )


def rope_tables(positions):
    frequency = jnp.exp(
        jnp.arange(HEAD // 2, dtype=jnp.float32) * (-2.0 * math.log(10000.0) / HEAD)
    )
    angle_grid = positions[:, None] * frequency[None, :]
    return (jnp.cos(angle_grid), jnp.sin(angle_grid))


def rotate(values, cosine_table, sine_table, turning):
    shaped = values.reshape(values.shape[0], -1, 2, HEAD // 2)
    first_half = shaped[:, :, 0, :]
    second = shaped[:, :, 1, :]
    cosine_wide = cosine_table[:, None, :]
    sine_wide = turning * sine_table[:, None, :]
    turned = jnp.stack(
        [
            first_half * cosine_wide - second * sine_wide,
            second * cosine_wide + first_half * sine_wide,
        ],
        axis=2,
    )
    return turned.reshape(values.shape)


def head_scores(query_head, key_head, allowed):
    scores = jnp.einsum(
        "qd,kd->qk", query_head, key_head, preferred_element_type=jnp.float32
    ) * HEAD ** (-0.5)
    return jnp.where(allowed, scores, NEGATIVE)


def attend_forward(queries, key_rows, value_rows, allowed):
    head_count = queries.shape[1] // HEAD
    outputs = []
    totals = []
    for head_index in range(head_count):
        column_start = head_index * HEAD
        scores = head_scores(
            queries[:, column_start : column_start + HEAD],
            key_rows[:, column_start : column_start + HEAD],
            allowed,
        )
        peak = jnp.max(scores, axis=1, keepdims=True)
        raised = jnp.exp(scores - peak)
        denominator = jnp.sum(raised, axis=1, keepdims=True)
        prob_low = (raised / denominator).astype(jnp.bfloat16)
        outputs.append(
            jnp.dot(
                prob_low,
                value_rows[:, column_start : column_start + HEAD],
                preferred_element_type=jnp.float32,
            )
        )
        totals.append(peak + jnp.log(denominator))
    return (jnp.concatenate(outputs, axis=1), totals)


def attend_backward(queries, key_rows, value_rows, allowed, totals, grad_attended):
    head_count = queries.shape[1] // HEAD
    grad_query_parts = []
    grad_key_parts = []
    grad_value_parts = []
    for head_index in range(head_count):
        column_start = head_index * HEAD
        query_head = queries[:, column_start : column_start + HEAD]
        key_head = key_rows[:, column_start : column_start + HEAD]
        value_head = value_rows[:, column_start : column_start + HEAD]
        grad_head = grad_attended[:, column_start : column_start + HEAD]
        probability = jnp.exp(head_scores(query_head, key_head, allowed) - totals[head_index])
        prob_low = probability.astype(jnp.bfloat16)
        grad_value_parts.append(
            jnp.einsum("qk,qd->kd", prob_low, grad_head, preferred_element_type=jnp.float32)
        )
        grad_prob = jnp.einsum(
            "qd,kd->qk", grad_head, value_head, preferred_element_type=jnp.float32
        )
        grad_scores = (
            probability * (grad_prob - jnp.sum(grad_prob * probability, axis=1, keepdims=True))
        ).astype(jnp.bfloat16)
        grad_query_parts.append(
            jnp.dot(grad_scores, key_head, preferred_element_type=jnp.float32) * HEAD ** (-0.5)
        )
        grad_key_parts.append(
            jnp.einsum("qk,qd->kd", grad_scores, query_head, preferred_element_type=jnp.float32)
            * HEAD ** (-0.5)
        )
    return (
        jnp.concatenate(grad_query_parts, axis=1),
        jnp.concatenate(grad_key_parts, axis=1),
        jnp.concatenate(grad_value_parts, axis=1),
    )


def body(tokens, w_query, w_key, w_value, w_out, w_gate, w_up, w_down, cotangent, slot_parent):
    rows_here = tokens.shape[0]
    slots_here = rows_here // BLOCK
    block_count = slot_parent.shape[0]
    row_count = block_count * BLOCK
    first_block = lax.axis_index("dp") * slots_here
    block_ids = jnp.arange(block_count, dtype=jnp.int32)
    linked = (slot_parent[:, None] == block_ids[None, :]).astype(jnp.float32)
    walker = lax.dynamic_slice_in_dim(linked, first_block, slots_here, 0)
    reaches = walker
    for rounds in range(TRUNK_BLOCKS + 1):
        walker = jnp.dot(walker, linked, precision=HIGH)
        reaches = reaches + walker
    depths = jnp.sum(reaches, axis=1)
    positions = (depths[:, None] * BLOCK + jnp.arange(BLOCK, dtype=jnp.float32)[None, :]).reshape(
        -1
    )
    cosine_table, sine_table = rope_tables(positions)
    ancestor = jnp.repeat(jnp.repeat(reaches, BLOCK, axis=0), BLOCK, axis=1) > 0.5
    query_index = first_block * BLOCK + jnp.arange(rows_here, dtype=jnp.int32)
    key_index = jnp.arange(row_count, dtype=jnp.int32)
    same_block = (query_index[:, None] // BLOCK == key_index[None, :] // BLOCK) & (
        key_index[None, :] <= query_index[:, None]
    )
    allowed = ancestor | same_block
    token_float = tokens.astype(jnp.float32)
    norm_one, inverse_one = layer_norm(token_float)
    normed_one = norm_one.astype(jnp.bfloat16)
    queries = rotate(
        jnp.dot(normed_one, w_query, preferred_element_type=jnp.float32),
        cosine_table,
        sine_table,
        1.0,
    ).astype(jnp.bfloat16)
    key_local = rotate(
        jnp.dot(normed_one, w_key, preferred_element_type=jnp.float32),
        cosine_table,
        sine_table,
        1.0,
    ).astype(jnp.bfloat16)
    value_local = jnp.dot(normed_one, w_value, preferred_element_type=jnp.float32).astype(
        jnp.bfloat16
    )
    key_rows, value_rows = (
        lax.all_gather(key_local, "dp", axis=0, tiled=True),
        lax.all_gather(value_local, "dp", axis=0, tiled=True),
    )
    attended, totals = attend_forward(queries, key_rows, value_rows, allowed)
    attended_low = attended.astype(jnp.bfloat16)
    middle = token_float + lax.psum(
        jnp.dot(attended_low, w_out, preferred_element_type=jnp.float32), "tensor"
    )
    norm_two, inverse_two = layer_norm(middle)
    normed_two = norm_two.astype(jnp.bfloat16)
    gate_proj = jnp.dot(normed_two, w_gate, preferred_element_type=jnp.float32)
    up_proj = jnp.dot(normed_two, w_up, preferred_element_type=jnp.float32)
    sigmoid_gate = jax.nn.sigmoid(gate_proj)
    activated = gate_proj * sigmoid_gate
    hidden = (activated * up_proj).astype(jnp.bfloat16)
    output = middle + lax.psum(
        jnp.dot(hidden, w_down, preferred_element_type=jnp.float32).astype(jnp.bfloat16), "tensor"
    ).astype(jnp.float32)
    grad_down_full = jnp.einsum("tf,td->fd", hidden, cotangent, preferred_element_type=jnp.float32)
    grad_hidden = jnp.einsum("td,fd->tf", cotangent, w_down, preferred_element_type=jnp.float32)
    grad_up_proj = (grad_hidden * activated).astype(jnp.bfloat16)
    grad_gate_proj = (
        grad_hidden * up_proj * sigmoid_gate * (1.0 + gate_proj * (1.0 - sigmoid_gate))
    ).astype(jnp.bfloat16)
    grad_gate_full = jnp.einsum(
        "td,tf->df", normed_two, grad_gate_proj, preferred_element_type=jnp.float32
    )
    grad_up_full = jnp.einsum(
        "td,tf->df", normed_two, grad_up_proj, preferred_element_type=jnp.float32
    )
    partial_two = jnp.einsum(
        "tf,df->td", grad_gate_proj, w_gate, preferred_element_type=jnp.float32
    ) + jnp.einsum("tf,df->td", grad_up_proj, w_up, preferred_element_type=jnp.float32)
    grad_normed_two = lax.psum(partial_two.astype(jnp.bfloat16), "tensor").astype(jnp.float32)
    grad_middle = cotangent.astype(jnp.float32) + norm_back(grad_normed_two, norm_two, inverse_two)
    grad_branch = grad_middle.astype(jnp.bfloat16)
    grad_out_full = jnp.einsum(
        "tc,td->cd", attended_low, grad_branch, preferred_element_type=jnp.float32
    )
    grad_attended = jnp.einsum(
        "td,cd->tc", grad_branch, w_out, preferred_element_type=jnp.float32
    ).astype(jnp.bfloat16)
    key_back, value_back = (key_rows, value_rows)
    grad_queries_sum, grad_key_rows, grad_value_rows = attend_backward(
        queries, key_back, value_back, allowed, totals, grad_attended
    )
    grad_keys_sum, grad_values_sum = (
        lax.psum_scatter(
            grad_key_rows.astype(jnp.bfloat16), "dp", scatter_dimension=0, tiled=True
        ).astype(jnp.float32),
        lax.psum_scatter(
            grad_value_rows.astype(jnp.bfloat16), "dp", scatter_dimension=0, tiled=True
        ).astype(jnp.float32),
    )
    grad_queries_low = rotate(grad_queries_sum, cosine_table, sine_table, -1.0).astype(jnp.bfloat16)
    grad_keys_low = rotate(grad_keys_sum, cosine_table, sine_table, -1.0).astype(jnp.bfloat16)
    grad_values_low = grad_values_sum.astype(jnp.bfloat16)
    grad_query_full = jnp.einsum(
        "td,tc->dc", normed_one, grad_queries_low, preferred_element_type=jnp.float32
    )
    grad_key_full = jnp.einsum(
        "td,tc->dc", normed_one, grad_keys_low, preferred_element_type=jnp.float32
    )
    grad_value_full = jnp.einsum(
        "td,tc->dc", normed_one, grad_values_low, preferred_element_type=jnp.float32
    )
    partial_one = jnp.einsum(
        "tc,dc->td", grad_queries_low, w_query, preferred_element_type=jnp.float32
    )
    partial_one = partial_one + jnp.einsum(
        "tc,dc->td", grad_keys_low, w_key, preferred_element_type=jnp.float32
    )
    partial_one = partial_one + jnp.einsum(
        "tc,dc->td", grad_values_low, w_value, preferred_element_type=jnp.float32
    )
    grad_normed_one = lax.psum(partial_one.astype(jnp.bfloat16), "tensor").astype(jnp.float32)
    grad_tokens = (grad_middle + norm_back(grad_normed_one, norm_one, inverse_one)).astype(
        jnp.bfloat16
    )
    grad_query, grad_key, grad_value, grad_out, grad_gate, grad_up, grad_down = (
        lax.psum_scatter(
            grad_query_full.astype(jnp.bfloat16), "dp", scatter_dimension=0, tiled=True
        ).astype(jnp.float32),
        lax.psum_scatter(
            grad_key_full.astype(jnp.bfloat16), "dp", scatter_dimension=0, tiled=True
        ).astype(jnp.float32),
        lax.psum_scatter(
            grad_value_full.astype(jnp.bfloat16), "dp", scatter_dimension=0, tiled=True
        ).astype(jnp.float32),
        lax.psum_scatter(
            grad_out_full.astype(jnp.bfloat16), "dp", scatter_dimension=1, tiled=True
        ).astype(jnp.float32),
        lax.psum_scatter(
            grad_gate_full.astype(jnp.bfloat16), "dp", scatter_dimension=0, tiled=True
        ).astype(jnp.float32),
        lax.psum_scatter(
            grad_up_full.astype(jnp.bfloat16), "dp", scatter_dimension=0, tiled=True
        ).astype(jnp.float32),
        lax.psum_scatter(
            grad_down_full.astype(jnp.bfloat16), "dp", scatter_dimension=1, tiled=True
        ).astype(jnp.float32),
    )
    return (
        output.astype(jnp.bfloat16),
        grad_tokens,
        grad_query,
        grad_key,
        grad_value,
        grad_out,
        grad_gate,
        grad_up,
        grad_down,
    )


def solution(mesh):
    in_specs = (
        P("dp", None),
        P(None, "tensor"),
        P(None, "tensor"),
        P(None, "tensor"),
        P("tensor", None),
        P(None, "tensor"),
        P(None, "tensor"),
        P("tensor", None),
        P("dp", None),
        P(),
    )
    out_specs = (
        P("dp", None),
        P("dp", None),
        P("dp", "tensor"),
        P("dp", "tensor"),
        P("dp", "tensor"),
        P("tensor", "dp"),
        P("dp", "tensor"),
        P("dp", "tensor"),
        P("tensor", "dp"),
    )
    return jax.shard_map(body, mesh=mesh, in_specs=in_specs, out_specs=out_specs, check_vma=False)
```

profile of v0, /device:TPU:0, one launch (start us, length us, event | category | flops | bytes accessed | tf_op | source)
XLA Modules:
  0.0 1333.3 jit_solution(3272524688739148105)
XLA Ops:
  24.4 4.7 convolution_convert_fusion.9
  29.5 38.7 %all-gather.3.cloned.1.call-done = bf16[5120,512]{0,1:T(8,128)(2,1)} async-done(((bf16[640,512]{0,1:T(8,128)(2,1)}), bf16[5120,512]{0,1:T(8,128)(2,1)}) %all-gather.3.cloned.1.call-update) | async-done | bytes 5242896 | tf_op jit(solution)/shard_map/all_gather | solution.py:170
  68.3 5.0 broadcast_in_dim.15
  73.3 7.8 fusion.132
  85.8 11.2 fusion.131
  97.1 6.7 fusion.4
  103.7 7.9 fusion.130
  111.6 4.7 copy-done.4
  118.3 8.0 fusion.133
  126.3 4.8 copy-done.3
  133.1 7.7 fusion.62
  140.8 6.4 fusion.61
  147.2 6.4 fusion.60
  156.8 3.9 fusion.100
  160.8 189.0 %all-reduce.5.cloned.1.call-done = f32[640,2048]{1,0:T(8,128)} async-done(((f32[640,2048]{1,0:T(8,128)}), f32[640,2048]{1,0:T(8,128)}) %all-reduce.5.cloned.1.call-update) | async-done | bytes 5242896 | tf_op jit(solution)/shard_map/psum | solution.py:175
  349.9 4.0 fusion.128
  358.1 7.9 fusion.137
  366.0 7.4 fusion.136
  373.4 14.8 %multiply_convert_fusion.4 = (bf16[640,2048]{1,0:T(8,128)(2,1)}, bf16[640,2048]{1,0:T(8,128)(2,1)}, bf16[640,2048]{1,0:T(8,128)(2,1)}) fusion(f32[640,2048]{1,0:T(8,128)} %fusion.136, f32[640,2048]{1,0:T(8,128)} %fusion.137, bf16[640,2048]{1,0:T(8,128)(2,1)S(1)} %copy-done.21, bf16[2048,2048]{1,0:T(8,128)(2,1)} %param.17), kind=kOutput, calls=%fused_computation.89 | convolution fusion | flops 5388369920 | bytes 29360128 | tf_op jit(solution)/shard_map/td,fd->tf/dot_general | solution.py:189
  388.2 8.9 fusion.138
  397.1 11.5 add_convert_fusion.1
  408.7 103.2 %all-reduce.7.cloned.1.call-done = bf16[640,2048]{1,0:T(8,128)(2,1)} async-done(((bf16[640,2048]{1,0:T(8,128)(2,1)}), bf16[640,2048]{1,0:T(8,128)(2,1)}) %all-reduce.7.cloned.1.call-update) | async-done | bytes 2621456 | tf_op jit(solution)/shard_map/psum | solution.py:203
  511.9 5.4 convert_reduce_fusion.1
  517.3 3.8 fusion.53
  525.1 8.0 fusion.34
  538.5 7.0 fusion.43
  545.5 3.4 pad_maximum_fusion.1
  548.9 8.0 copy.21
  557.4 13.7 %multiply_reduce_fusion = (f32[640]{0:T(1024)S(1)}, f32[640,5120]{1,0:T(8,128)}) fusion(f32[640,5120]{1,0:T(8,128)} %copy-done.4, f32[640]{0:T(1024)S(1)} %log_add_fusion, bf16[5120,512]{1,0:T(8,128)(2,1)} %all-gather.5.cloned.1.call-done, bf16[640,512]{1,0:T(8,128)(2,1)S(1)} %convolution_convert_fusion.8), kind=kOutput, calls=%fused_computation.1 | convolution fusion | flops 848690560 | bytes 27695616 | tf_op jit(solution)/shard_map/qd,kd->qk/dot_general | solution.py:106
  571.2 11.6 multiply_convert_fusion
  582.8 9.5 multiply_reduce_fusion.1
  592.3 13.7 %multiply_convert_fusion.1 = bf16[640,5120]{1,0:T(8,128)(2,1)} fusion(f32[640,5120]{1,0:T(8,128)} %get-tuple-element.48, f32[640,5120]{1,0:T(8,128)} %get-tuple-element.40, f32[640]{0:T(1024)S(1)} %get-tuple-element.47, f32[640]{0:T(1024)S(1)} %log_add_fusion.1), kind=kLoop, calls=%fused_computation.3 | loop fusion | flops 13107200 | bytes 32773120 | tf_op jit(solution)/shard_map/convert_element_type | solution.py:111
  610.7 8.6 multiply_reduce_fusion.2
  619.3 11.0 multiply_convert_fusion.2
  630.3 4.2 fusion.31
  634.6 8.5 multiply_reduce_fusion.3
  643.1 6.9 multiply_convert_fusion.3
  652.7 3.5 pad_maximum_fusion
  656.2 7.9 copy.19
  665.3 5.6 convolution_convert_fusion.4
  670.9 11.6 convolution_convert_fusion.1
  682.6 11.4 convolution_convert_fusion.2
  694.1 11.2 convolution_convert_fusion
  705.4 5.1 convolution_convert_fusion.5
  711.0 5.5 convolution_multiply_fusion.4
  716.5 5.6 convolution_multiply_fusion.5
  722.1 3.6 convolution_multiply_fusion.6
  725.7 3.5 convolution_multiply_fusion.7
  732.7 3.2 convolution_convert_fusion.7
  736.1 4.9 convolution_convert_fusion.6
  741.3 11.1 convolution_convert_fusion.3
  755.7 3.2 add_convert_fusion
  758.9 5.5 reduce-scatter.20.cloned.1.call-done
  766.1 73.4 %reduce-scatter.24.cloned.1.call-done = bf16[256,2048]{1,0:T(8,128)(2,1)} async-done(((bf16[2048,2048]{1,0:T(8,128)(2,1)}), bf16[256,2048]{1,0:T(8,128)(2,1)}) %reduce-scatter.24.cloned.1.call-update) | async-done | bytes 1048592 | tf_op jit(solution)/shard_map/reduce_scatter | solution.py:265
  839.5 2.8 convert_element_type.203
  842.3 72.0 %reduce-scatter.22.cloned.1.call-done = bf16[256,2048]{1,0:T(8,128)(2,1)} async-done(((bf16[2048,2048]{1,0:T(8,128)(2,1)}), bf16[256,2048]{1,0:T(8,128)(2,1)}) %reduce-scatter.22.cloned.1.call-update) | async-done | bytes 1048592 | tf_op jit(solution)/shard_map/reduce_scatter | solution.py:262
  917.1 72.2 %reduce-scatter.26.cloned.1.call-done = bf16[2048,256]{1,0:T(8,128)(2,1)} async-done(((bf16[2048,2048]{1,0:T(8,128)(2,1)}), bf16[2048,256]{1,0:T(8,128)(2,1)}) %reduce-scatter.26.cloned.1.call-update) | async-done | bytes 1048592 | tf_op jit(solution)/shard_map/reduce_scatter | solution.py:268
  989.3 2.8 convert_element_type.205
  992.1 41.7 %reduce-scatter.18.cloned.1.call-done = bf16[256,512]{1,0:T(8,128)(2,1)} async-done(((bf16[2048,512]{1,0:T(8,128)(2,1)}), bf16[256,512]{1,0:T(8,128)(2,1)}) %reduce-scatter.18.cloned.1.call-update) | async-done | bytes 262160 | tf_op jit(solution)/shard_map/reduce_scatter | solution.py:256
  1035.6 42.9 %reduce-scatter.14.cloned.1.call-done = bf16[256,512]{1,0:T(8,128)(2,1)} async-done(((bf16[2048,512]{1,0:T(8,128)(2,1)}), bf16[256,512]{1,0:T(8,128)(2,1)}) %reduce-scatter.14.cloned.1.call-update) | async-done | bytes 262160 | tf_op jit(solution)/shard_map/reduce_scatter | solution.py:250
  1080.3 42.7 %reduce-scatter.16.cloned.1.call-done = bf16[256,512]{1,0:T(8,128)(2,1)} async-done(((bf16[2048,512]{1,0:T(8,128)(2,1)}), bf16[256,512]{1,0:T(8,128)(2,1)}) %reduce-scatter.16.cloned.1.call-update) | async-done | bytes 262160 | tf_op jit(solution)/shard_map/reduce_scatter | solution.py:253
  1124.9 190.5 %all-reduce.9.cloned.1.call-done = (bf16[640,2048]{1,0:T(8,128)(2,1)}, bf16[640,2048]{1,0:T(8,128)(2,1)}) async-done(((bf16[640,2048]{1,0:T(8,128)(2,1)}, bf16[640,2048]{1,0:T(8,128)(2,1)}), (bf16[640,2048]{1,0:T(8,128)(2,1)}, bf16[640,2048]{1,0:T(8,128)(2,1)})) %all-reduce.9.cloned.1.call-update) | async-done | bytes 5242896 | tf_op jit(solution)/shard_map/psum | solution.py:185
  1315.3 5.9 add_convert_fusion.2
  1323.6 3.0 fusion.49
  (264 shorter events, 71.8 us)
Async XLA Ops:
  7.2 149.6 %copy-start = (bf16[512,2048]{1,0:T(8,128)(2,1)S(1)}, bf16[512,2048]{1,0:T(8,128)(2,1)}, u32[]{:S(2)}) copy-start(bf16[512,2048]{1,0:T(8,128)(2,1)} %param.14) | copy-start | bytes 6291460
  7.2 5.0 copy-start.44
  7.2 61.1 %all-gather.3.cloned.1.call-start = ((), (), s32[]{:S(2)}) async-start(), calls=%async_computation.9 | async-start | bytes 5898240 | tf_op jit(solution)/shard_map/all_gather | solution.py:170
  9.6 9.0 copy-start.40
  12.2 6.4 copy-start.42
  24.4 108.7 %all-gather.5.cloned.1.call-start = ((), (), s32[]{:S(2)}) async-start(), calls=%async_computation.10 | async-start | bytes 5898240 | tf_op jit(solution)/shard_map/all_gather | solution.py:171
  29.2 320.7 %all-reduce.5.cloned.1.call-start = ((), (), s32[]{:S(2)}) async-start(), calls=%async_computation.11 | async-start | bytes 10485760 | tf_op jit(solution)/shard_map/psum | solution.py:175
  29.5 88.8 %copy-start.14 = (bf16[640,4,2,64]{0,3,2,1:T(8,128)(2,1)}, bf16[640,4,2,64]{0,3,2,1:T(8,128)(2,1)S(1)}, u32[]{:S(2)}) copy-start(bf16[640,4,2,64]{0,3,2,1:T(8,128)(2,1)S(1)} %pad_maximum_fusion.3) | copy-start | bytes 1966084
  73.3 7.8 copy-start.16
  133.1 7.7 copy-start.13
  140.8 15.4 %copy-start.32 = (bf16[640,128]{0,1:T(8,128)(2,1)}, bf16[640,128]{0,1:T(8,128)(2,1)S(1)}, u32[]{:S(2)}) copy-start(bf16[640,128]{0,1:T(8,128)(2,1)S(1)} %fusion.62) | copy-start | bytes 491524
  140.8 12.8 slice-start.8
  140.8 12.8 slice-start.9
  147.2 9.0 copy-start.34
  147.2 6.4 slice-start.10
  147.2 6.4 slice-start.11
  160.8 351.1 %all-reduce.7.cloned.1.call-start = ((), (), s32[]{:S(2)}) async-start(), calls=%async_computation.12 | async-start | bytes 5242880 | tf_op jit(solution)/shard_map/psum | solution.py:203
  349.9 6.7 slice-start.32
  354.6 11.4 slice-start.30
  358.1 7.9 copy-start.20
  358.1 7.9 slice-start.31
  366.0 7.4 copy-start.21
  388.2 8.9 copy-start.45
  408.6 296.8 %reduce-scatter.30.cloned.1.call-start = ((), (), s32[]{:S(2)}) async-start(), calls=%async_computation.21 | async-start | bytes 5898240
  511.9 5.4 copy-start.12
  511.9 5.5 copy-start.22
  523.5 9.6 slice-start
  523.5 9.6 slice-start.1
  525.0 57.7 %copy-start.17 = (bf16[640,512]{1,0:T(8,128)(2,1)}, bf16[640,512]{1,0:T(8,128)(2,1)S(1)}, u32[]{:S(2)}) copy-start(bf16[640,512]{1,0:T(8,128)(2,1)S(1)} %convolution_convert_fusion.8) | copy-start | bytes 1966084
  525.1 8.1 slice-start.2
  525.1 8.1 slice-start.3
  525.1 10.5 slice-start.16
  525.1 10.5 slice-start.17
  556.9 172.4 %reduce-scatter.28.cloned.1.call-start = ((), (), s32[]{:S(2)}) async-start(), calls=%async_computation.20 | async-start | bytes 5898240
  557.4 25.4 %slice-start.20 = ((s8[13107200]{0:T(1024)(128)(4,1)}), s8[4194304]{0:T(1024)(128)(4,1)S(1)}, s32[]{:S(2)}) async-start(s8[13107200]{0:T(1024)(128)(4,1)} %bitcast.89), calls=%async_computation.43 | async-start | bytes 8388608
  557.4 25.4 %slice-start.21 = ((s8[13107200]{0:T(1024)(128)(4,1)}), s8[4194304]{0:T(1024)(128)(4,1)S(1)}, s32[]{:S(2)}) async-start(s8[13107200]{0:T(1024)(128)(4,1)} %bitcast.89), calls=%async_computation.44 | async-start | bytes 8388608
  571.1 11.6 slice-start.22
  571.2 11.6 slice-start.23
  582.8 23.2 %copy-start.7 = (bf16[640,5120]{1,0:T(8,128)(2,1)}, bf16[640,5120]{1,0:T(8,128)(2,1)S(1)}, u32[]{:S(2)}) copy-start(bf16[640,5120]{1,0:T(8,128)(2,1)S(1)} %multiply_convert_fusion) | copy-start | bytes 19660804
  592.3 13.7 %copy-start.15 = (bf16[640,4,2,64]{0,3,2,1:T(8,128)(2,1)S(1)}, bf16[640,4,2,64]{0,3,2,1:T(8,128)(2,1)}, u32[]{:S(2)}) copy-start(bf16[640,4,2,64]{0,3,2,1:T(8,128)(2,1)} %copy-done.14) | copy-start | bytes 1966084
  592.3 18.4 %slice-start.4 = ((s8[13107200]{0:T(1024)(128)(4,1)}), s8[4194304]{0:T(1024)(128)(4,1)S(1)}, s32[]{:S(2)}) async-start(s8[13107200]{0:T(1024)(128)(4,1)} %bitcast.81), calls=%async_computation.27 | async-start | bytes 8388608
  592.3 18.4 %slice-start.5 = ((s8[13107200]{0:T(1024)(128)(4,1)}), s8[4194304]{0:T(1024)(128)(4,1)S(1)}, s32[]{:S(2)}) async-start(s8[13107200]{0:T(1024)(128)(4,1)} %bitcast.81), calls=%async_computation.28 | async-start | bytes 8388608
  592.3 18.4 %slice-start.6 = ((s8[13107200]{0:T(1024)(128)(4,1)}), s8[4194304]{0:T(1024)(128)(4,1)S(1)}, s32[]{:S(2)}) async-start(s8[13107200]{0:T(1024)(128)(4,1)} %bitcast.81), calls=%async_computation.29 | async-start | bytes 8388608
  619.3 15.2 %slice-start.12 = ((s8[13107200]{0:T(1024)(128)(4,1)}), s8[4194304]{0:T(1024)(128)(4,1)S(1)}, s32[]{:S(2)}) async-start(s8[13107200]{0:T(1024)(128)(4,1)} %bitcast.85), calls=%async_computation.35 | async-start | bytes 8388608
  619.3 15.2 %slice-start.13 = ((s8[13107200]{0:T(1024)(128)(4,1)}), s8[4194304]{0:T(1024)(128)(4,1)S(1)}, s32[]{:S(2)}) async-start(s8[13107200]{0:T(1024)(128)(4,1)} %bitcast.85), calls=%async_computation.36 | async-start | bytes 8388608
  619.3 15.3 %slice-start.14 = ((s8[13107200]{0:T(1024)(128)(4,1)}), s8[524288]{0:T(1024)(128)(4,1)S(1)}, s32[]{:S(2)}) async-start(s8[13107200]{0:T(1024)(128)(4,1)} %bitcast.85), calls=%async_computation.37 | async-start | bytes 1048576
  664.1 100.2 %reduce-scatter.20.cloned.1.call-start = ((), (), s32[]{:S(2)}) async-start(), calls=%async_computation.16 | async-start | bytes 2359296 | tf_op jit(solution)/shard_map/reduce_scatter | solution.py:259
  670.9 168.6 %reduce-scatter.24.cloned.1.call-start = ((), (), s32[]{:S(2)}) async-start(), calls=%async_computation.18 | async-start | bytes 9437184 | tf_op jit(solution)/shard_map/reduce_scatter | solution.py:265
  682.6 231.7 %reduce-scatter.22.cloned.1.call-start = ((), (), s32[]{:S(2)}) async-start(), calls=%async_computation.17 | async-start | bytes 9437184 | tf_op jit(solution)/shard_map/reduce_scatter | solution.py:262
  694.1 295.2 %reduce-scatter.26.cloned.1.call-start = ((), (), s32[]{:S(2)}) async-start(), calls=%async_computation.19 | async-start | bytes 9437184 | tf_op jit(solution)/shard_map/reduce_scatter | solution.py:268
  705.3 328.5 %reduce-scatter.18.cloned.1.call-start = ((), (), s32[]{:S(2)}) async-start(), calls=%async_computation.15 | async-start | bytes 2359296 | tf_op jit(solution)/shard_map/reduce_scatter | solution.py:256
  710.5 368.0 %reduce-scatter.14.cloned.1.call-start = ((), (), s32[]{:S(2)}) async-start(), calls=%async_computation.13 | async-start | bytes 2359296 | tf_op jit(solution)/shard_map/reduce_scatter | solution.py:250
  710.9 11.1 slice-start.24
  716.4 5.6 slice-start.25
  716.4 9.3 slice-start.26
  735.9 387.1 %reduce-scatter.16.cloned.1.call-start = ((), (), s32[]{:S(2)}) async-start(), calls=%async_computation.14 | async-start | bytes 2359296 | tf_op jit(solution)/shard_map/reduce_scatter | solution.py:253
  741.0 574.3 %all-reduce.9.cloned.1.call-start = ((), (), s32[]{:S(2)}) async-start(), calls=%async_computation.22 | async-start | bytes 10485760 | tf_op jit(solution)/shard_map/psum | solution.py:185
  741.3 11.1 copy-start.25
  989.3 334.3 %slice-start.28 = ((s8[5242880]{0:T(1024)(128)(4,1)}), s8[1048576]{0:T(1024)(128)(4,1)S(1)}, s32[]{:S(2)}) async-start(s8[5242880]{0:T(1024)(128)(4,1)} %bitcast.95), calls=%async_computation.51 | async-start | bytes 2097152
  1315.3 5.9 copy-start.6
  1315.3 5.9 copy-start.11
  1315.3 5.9 copy-start.41
  1315.3 5.9 copy-start.43
  1315.3 8.2 slice-start.29
  (30 other events, 78.1 us)
Sparse Core Ops, SparseCore 0:
  24.5 43.7 all-gather.2
  70.7 41.1 all-gather.4
  160.9 188.8 all-reduce.4
  408.7 103.0 all-reduce.6
  557.0 55.6 reduce-scatter.29
  664.3 54.9 reduce-scatter.27
  723.1 41.2 reduce-scatter.19
  768.2 71.2 reduce-scatter.23
  843.0 71.2 reduce-scatter.21
  918.0 71.2 reduce-scatter.25
  992.6 41.1 reduce-scatter.17
  1037.3 41.2 reduce-scatter.13
  1081.8 41.1 reduce-scatter.15
  1126.0 189.2 all-reduce.8
where the time goes:
time: 1340 us; the launch traced here: 1330 us
  waiting for transfers between devices  872 us (65%)
  matrix products  281 us (21%)
  other arithmetic  115 us (9%)
  local copies, waits for them, and re-layouts  48.7 us (4%)
  between operations  15.4 us (1%)
    psum x1, waiting for transfers between devices, body(): lax.psum(jnp.dot(hidden, w_down, preferred_element_type=jnp.float32).asty...  190 us
    psum x1, waiting for transfers between devices, body(): lax.psum(jnp.dot(attended_low, w_out, preferred_element_type=jnp.float32)...  189 us
    psum x1, waiting for transfers between devices, body(): lax.psum(partial_two.astype(jnp.bfloat16), 'tensor').astype(jnp.float32)  103 us
    reduce_scatter x1, waiting for transfers between devices, body(): lax.psum_scatter(grad_up_full.astype(jnp.bfloat16), 'dp', scatter_dimensi...  73.4 us
    reduce_scatter x1, waiting for transfers between devices, body(): lax.psum_scatter(grad_down_full.astype(jnp.bfloat16), 'dp', scatter_dimen...  72.2 us
    reduce_scatter x1, waiting for transfers between devices, body(): lax.psum_scatter(grad_gate_full.astype(jnp.bfloat16), 'dp', scatter_dimen...  72 us
    unnamed x163, local copies, waits for them, and re-layouts  43.7 us
    convert_element_type x4, other arithmetic, attend_backward(): grad_scores = (probability * (grad_prob - jnp.sum(grad_prob * probability...  43.2 us
  transfers between devices with their start and end apart: 14, of which 11 were waited for; matrix products, arithmetic and copies ran while one was open for 20% of the time, Pallas kernels for 0%

commit v1 on v0

v1 whole, which is shorter than its diff:
```python
import functools
import math

import jax
import jax.numpy as jnp
import numpy as np
from jax import lax
from jax.experimental import pallas as pl
from jax.experimental.pallas import tpu as pltpu
from jax.sharding import PartitionSpec as P

HEAD = 128
BLOCK = 128
TRUNK_BLOCKS = 8
CHAIN = TRUNK_BLOCKS + 2
EPSILON = 1e-05
NEGATIVE = -1e30
SCALE = HEAD ** (-0.5)
LOW = jnp.bfloat16
F32 = jnp.float32
MIB = 1024 * 1024
NT = (((1,), (1,)), ((), ()))
TN = (((0,), (0,)), ((), ()))


def dot(a, b):
    return jnp.dot(a, b, preferred_element_type=F32)


def dot_nt(a, b):
    return lax.dot_general(a, b, NT, preferred_element_type=F32)


def dot_tn(a, b):
    return lax.dot_general(a, b, TN, preferred_element_type=F32)


def shape(dims, dtype):
    return jax.ShapeDtypeStruct(dims, dtype)


def params(mib):
    return pltpu.CompilerParams(vmem_limit_bytes=mib * MIB)


def layer_norm(values):
    centered = values - jnp.mean(values, axis=-1, keepdims=True)
    variance = jnp.mean(centered * centered, axis=-1, keepdims=True)
    inverse = lax.rsqrt(variance + EPSILON)
    return (centered * inverse, inverse)


def norm_back(gradient, normed, inverse):
    return inverse * (
        gradient
        - jnp.mean(gradient, axis=-1, keepdims=True)
        - normed * jnp.mean(gradient * normed, axis=-1, keepdims=True)
    )


def rope_tables():
    frequency = np.exp(
        np.arange(HEAD // 2, dtype=np.float32) * np.float32(-2.0 * math.log(10000.0) / HEAD)
    ).astype(np.float32)
    angle = np.arange(CHAIN * BLOCK, dtype=np.float32)[:, None] * frequency[None, :]
    cosine, sine = np.cos(angle), np.sin(angle)
    return (
        np.concatenate([cosine, cosine], axis=1).astype(np.float32),
        np.concatenate([-sine, sine], axis=1).astype(np.float32),
    )


def depth_of(parent_ref, slot):
    def up(_, carry):
        at, depth = carry
        parent = jnp.where(at >= 0, parent_ref[jnp.maximum(at, 0)], -1)
        return parent, depth + jnp.where(parent >= 0, 1, 0).astype(jnp.int32)

    return lax.fori_loop(0, CHAIN - 1, up, (slot, jnp.int32(0)))[1]


def xor_pairs(count, mask):
    return [(index, index ^ mask) for index in range(count)]


class Plan:
    def __init__(self, mesh, rows, width, heads, ff):
        self.dp = mesh.shape["dp"]
        self.tensor = mesh.shape["tensor"]
        self.rows, self.width, self.heads, self.ff = rows, width, heads, ff
        self.slots = rows // BLOCK
        self.spread = heads
        self.rest = self.dp // heads
        self.bits = self.dp.bit_length() - 1
        self.piece = width // self.dp
        self.own = rows // self.tensor


def qkv_kernel(plan, parent, place, x, wq, wk, wv, cosine, sine, n_rel, *rest):
    outs, normed, stage = rest[: plan.spread], rest[-2], rest[-1]
    me = place[0]
    part = me // plan.rest
    depth = depth_of(parent, me * plan.slots + pl.program_id(0))
    rows = pl.ds(pl.multiple_of(depth * BLOCK, BLOCK), BLOCK)
    cos, sin = cosine[rows, :], sine[rows, :]
    low = layer_norm(x[...].astype(F32))[0].astype(LOW)
    normed[...] = low
    for kind, w in enumerate((wq, wk, wv)):
        y = dot(low, w[...])
        for head in range(plan.heads):
            yh = y[:, head * HEAD : (head + 1) * HEAD]
            if kind < 2:
                yh = yh * cos + pltpu.roll(yh, HEAD // 2, 1) * sin
            stage[head, kind] = yh.astype(LOW)
    for d in range(plan.spread):
        outs[d][...] = stage[part ^ d]
    store_relative(plan, me, normed, n_rel)


def relative_order(plan):
    return [
        sum(((at >> bit) & 1) << (plan.bits - 1 - bit) for bit in range(plan.bits))
        for at in range(plan.dp)
    ]


def kept_orders(plan):
    up = relative_order(plan)[: plan.dp // 2]
    down = [2 * at for at in range(plan.dp // 2)]
    return up, down


def store_relative(plan, me, source, target):
    up, down = kept_orders(plan)
    order = relative_order(plan) + down
    for at, relative in enumerate(order):
        columns = pl.ds(pl.multiple_of((me ^ relative) * plan.piece, plan.piece), plan.piece)
        target[:, at * plan.piece : (at + 1) * plan.piece] = source[:, columns]


def project_qkv(plan, slot_parent, place, tokens, wq, wk, wv, cosine, sine):
    whole = lambda i, *_: (0, 0)
    once = pl.Buffered(buffer_count=1)
    wide = plan.heads * HEAD
    return pl.pallas_call(
        functools.partial(qkv_kernel, plan),
        grid_spec=pltpu.PrefetchScalarGridSpec(
            num_scalar_prefetch=2,
            grid=(plan.slots,),
            in_specs=[pl.BlockSpec((BLOCK, plan.width), lambda i, *_: (i, 0))]
            + [pl.BlockSpec((plan.width, wide), whole, pipeline_mode=once)] * 3
            + [pl.BlockSpec((CHAIN * BLOCK, HEAD), whole, pipeline_mode=once)] * 2,
            out_specs=[pl.BlockSpec((BLOCK, plan.width * 3 // 2), lambda i, *_: (i, 0))]
            + [pl.BlockSpec((3, BLOCK, HEAD), lambda i, *_: (0, i, 0))] * plan.spread,
            scratch_shapes=[
                pltpu.VMEM((BLOCK, plan.width), LOW),
                pltpu.VMEM((plan.heads, 3, BLOCK, HEAD), LOW),
            ],
        ),
        out_shape=[shape((plan.rows, plan.width * 3 // 2), LOW)]
        + [shape((3, plan.rows, HEAD), LOW)] * plan.spread,
        compiler_params=params(48),
        cost_estimate=pl.CostEstimate(
            flops=6 * plan.rows * plan.width * wide, bytes_accessed=16 * MIB, transcendentals=0
        ),
        name="project_qkv",
    )(slot_parent, place, tokens, wq, wk, wv, cosine, sine)


def relative_kernel(plan, place, source, target):
    store_relative(plan, place[0], source, target)


def relative_columns(plan, place, values):
    return pl.pallas_call(
        functools.partial(relative_kernel, plan),
        grid_spec=pltpu.PrefetchScalarGridSpec(
            num_scalar_prefetch=1,
            grid=(plan.slots,),
            in_specs=[pl.BlockSpec((BLOCK, plan.width), lambda i, *_: (i, 0))],
            out_specs=pl.BlockSpec((BLOCK, plan.width * 3 // 2), lambda i, *_: (i, 0)),
        ),
        out_shape=shape((plan.rows, plan.width * 3 // 2), LOW),
        cost_estimate=pl.CostEstimate(
            flops=0, bytes_accessed=5 * plan.rows * plan.width, transcendentals=0
        ),
        name="relative_columns",
    )(place, values)


def gather_chain(plan, parent, me, slot, kv, keys, values, places=None):
    count = jnp.int32(0)
    at = slot
    for step in range(CHAIN):
        here = jnp.maximum(at, 0)
        relative = (here // plan.slots) ^ me
        block = (
            (relative % plan.rest) * plan.spread + relative // plan.rest
        ) * 2 * plan.slots + here % plan.slots
        keys[step * BLOCK : (step + 1) * BLOCK, :] = kv[block]
        values[step * BLOCK : (step + 1) * BLOCK, :] = kv[block + plan.slots]
        if places is not None:
            places.append(block)
        valid = at >= 0
        count = count + jnp.where(valid, 1, 0).astype(jnp.int32)
        at = jnp.where(valid, parent[here], -1)
    return count


def attend_kernel(plan, parent, place, *refs):
    n = plan.spread
    q_refs, kv, o_refs, keys, values = refs[:n], refs[n], refs[n + 1 : 2 * n + 1], refs[-2], refs[-1]
    me = place[0]
    for d in range(n):

        def one(i, carry, d=d):
            slot = (me ^ (d * plan.rest)) * plan.slots + i
            count = gather_chain(plan, parent, me, slot, kv, keys, values)
            rows = pl.ds(pl.multiple_of(i * BLOCK, BLOCK), BLOCK)
            q = q_refs[d][0, rows, :]
            scores = dot_nt(q, keys[...]) * SCALE
            column = lax.broadcasted_iota(jnp.int32, scores.shape, 1)
            row = lax.broadcasted_iota(jnp.int32, scores.shape, 0)
            allowed = (column < count * BLOCK) & ((column >= BLOCK) | (column <= row))
            scores = jnp.where(allowed, scores, NEGATIVE)
            raised = jnp.exp(scores - jnp.max(scores, axis=1, keepdims=True))
            total = jnp.sum(raised, axis=1, keepdims=True)
            prob = (raised * (1.0 / total)).astype(LOW)
            o_refs[d][rows, :] = dot(prob, values[...]).astype(LOW)
            return carry

        lax.fori_loop(0, plan.slots, one, 0)


def attend(plan, slot_parent, place, parts, kv):
    n = plan.spread
    blocks = plan.dp * 2 * plan.slots
    return pl.pallas_call(
        functools.partial(attend_kernel, plan),
        grid_spec=pltpu.PrefetchScalarGridSpec(
            num_scalar_prefetch=2,
            grid=(1,),
            in_specs=[pl.BlockSpec((1, plan.rows, HEAD), lambda i, *_: (0, 0, 0))] * n
            + [pl.BlockSpec((blocks, BLOCK, HEAD), lambda i, *_: (0, 0, 0))],
            out_specs=[pl.BlockSpec((plan.rows, HEAD), lambda i, *_: (0, 0))] * n,
            scratch_shapes=[pltpu.VMEM((CHAIN * BLOCK, HEAD), LOW)] * 2,
        ),
        out_shape=[shape((plan.rows, HEAD), LOW)] * n,
        compiler_params=params(40),
        cost_estimate=pl.CostEstimate(
            flops=4 * n * plan.rows * CHAIN * BLOCK * HEAD,
            bytes_accessed=8 * MIB,
            transcendentals=n * plan.rows * CHAIN * BLOCK,
        ),
        name="attend",
    )(slot_parent, place, *parts, kv)


def attend_back_kernel(plan, parent, place, *refs):
    n = plan.spread
    q_refs, kv, g_refs = refs[:n], refs[n], refs[n + 1 : 2 * n + 1]
    dq_refs = refs[2 * n + 1 : 3 * n + 1]
    near, far, keys, values, total = refs[3 * n + 1 :]
    me = place[0]
    total[...] = jnp.zeros_like(total)
    for d in range(n):

        def one(i, carry, d=d):
            slot = (me ^ (d * plan.rest)) * plan.slots + i
            places = []
            count = gather_chain(plan, parent, me, slot, kv, keys, values, places)
            rows = pl.ds(pl.multiple_of(i * BLOCK, BLOCK), BLOCK)
            q = q_refs[d][0, rows, :]
            g = g_refs[d][rows, :]
            k = keys[...]
            scores = dot_nt(k, q) * SCALE
            key_at = lax.broadcasted_iota(jnp.int32, scores.shape, 0)
            query_at = lax.broadcasted_iota(jnp.int32, scores.shape, 1)
            allowed = (key_at < count * BLOCK) & ((key_at >= BLOCK) | (key_at <= query_at))
            scores = jnp.where(allowed, scores, NEGATIVE)
            raised = jnp.exp(scores - jnp.max(scores, axis=0, keepdims=True))
            prob = raised * (1.0 / jnp.sum(raised, axis=0, keepdims=True))
            grad_prob = dot_nt(values[...], g)
            inner = jnp.sum(grad_prob * prob, axis=0, keepdims=True)
            grad_scores = (prob * (grad_prob - inner)).astype(LOW)
            dv = dot(prob.astype(LOW), g)
            dk = dot(grad_scores, q) * SCALE
            dq_refs[d][rows, :] = (dot_tn(grad_scores, k) * SCALE).astype(LOW)
            for step, block in enumerate(places):
                span = slice(step * BLOCK, (step + 1) * BLOCK)
                total[block] = total[block] + dk[span]
                total[block + plan.slots] = total[block + plan.slots] + dv[span]
            return carry

        lax.fori_loop(0, plan.slots, one, 0)
    half = near.shape[0]
    near[...] = total[:half]
    far[...] = total[half:].astype(LOW)


def attend_back(plan, slot_parent, place, parts, kv, grads):
    n = plan.spread
    blocks = plan.dp * 2 * plan.slots
    near = n * 2 * plan.slots
    return pl.pallas_call(
        functools.partial(attend_back_kernel, plan),
        grid_spec=pltpu.PrefetchScalarGridSpec(
            num_scalar_prefetch=2,
            grid=(1,),
            in_specs=[pl.BlockSpec((1, plan.rows, HEAD), lambda i, *_: (0, 0, 0))] * n
            + [pl.BlockSpec((blocks, BLOCK, HEAD), lambda i, *_: (0, 0, 0))]
            + [pl.BlockSpec((plan.rows, HEAD), lambda i, *_: (0, 0))] * n,
            out_specs=[pl.BlockSpec((plan.rows, HEAD), lambda i, *_: (0, 0))] * n
            + [
                pl.BlockSpec((near, BLOCK, HEAD), lambda i, *_: (0, 0, 0)),
                pl.BlockSpec((blocks - near, BLOCK, HEAD), lambda i, *_: (0, 0, 0)),
            ],
            scratch_shapes=[pltpu.VMEM((CHAIN * BLOCK, HEAD), LOW)] * 2
            + [pltpu.VMEM((blocks, BLOCK, HEAD), F32)],
        ),
        out_shape=[shape((plan.rows, HEAD), LOW)] * n
        + [shape((near, BLOCK, HEAD), F32), shape((blocks - near, BLOCK, HEAD), LOW)],
        compiler_params=params(56),
        cost_estimate=pl.CostEstimate(
            flops=10 * n * plan.rows * CHAIN * BLOCK * HEAD,
            bytes_accessed=16 * MIB,
            transcendentals=n * plan.rows * CHAIN * BLOCK,
        ),
        name="attend_back",
    )(slot_parent, place, *parts, kv, *grads)


def heads_kernel(plan, place, *refs):
    part = place[0] // plan.rest
    out = refs[-1]
    for d in range(plan.spread):
        head = pl.ds(pl.multiple_of((part ^ d) * HEAD, HEAD), HEAD)
        out[:, head] = refs[d][...]


def gather_heads(plan, place, parts):
    return pl.pallas_call(
        functools.partial(heads_kernel, plan),
        grid_spec=pltpu.PrefetchScalarGridSpec(
            num_scalar_prefetch=1,
            grid=(1,),
            in_specs=[pl.BlockSpec((plan.rows, HEAD), lambda i, *_: (0, 0))] * plan.spread,
            out_specs=pl.BlockSpec((plan.rows, plan.heads * HEAD), lambda i, *_: (0, 0)),
        ),
        out_shape=shape((plan.rows, plan.heads * HEAD), LOW),
        name="gather_heads",
    )(place, *parts)


def scatter_kernel(plan, place, *refs):
    part, z = place[0] // plan.rest, place[1]
    sources, outs = refs[: plan.tensor], refs[plan.tensor :]
    for shift in range(plan.tensor):
        origin = lax.rem(z - shift + plan.tensor, plan.tensor)
        rows = pl.ds(pl.multiple_of(origin * plan.own, 16), plan.own)
        for d in range(plan.spread):
            head = pl.ds(pl.multiple_of((part ^ d) * HEAD, HEAD), HEAD)
            outs[d][rows, :] = sources[shift][:, head]


def scatter_heads(plan, place, sources):
    return pl.pallas_call(
        functools.partial(scatter_kernel, plan),
        grid_spec=pltpu.PrefetchScalarGridSpec(
            num_scalar_prefetch=1,
            grid=(1,),
            in_specs=[pl.BlockSpec((plan.own, plan.heads * HEAD), lambda i, *_: (0, 0))]
            * plan.tensor,
            out_specs=[pl.BlockSpec((plan.rows, HEAD), lambda i, *_: (0, 0))] * plan.spread,
        ),
        out_shape=[shape((plan.rows, HEAD), LOW)] * plan.spread,
        name="scatter_heads",
    )(place, *sources)


def turn_back_kernel(plan, parent, place, cosine, sine, *refs):
    me = place[0]
    part = me // plan.rest
    out = refs[-1]
    depth = depth_of(parent, me * plan.slots + pl.program_id(0))
    rows = pl.ds(pl.multiple_of(depth * BLOCK, BLOCK), BLOCK)
    cos, sin = cosine[rows, :], sine[rows, :]
    for d in range(plan.spread):
        for kind in range(3):
            value = refs[d][kind]
            if kind < 2:
                value = value.astype(F32)
                value = (value * cos - pltpu.roll(value, HEAD // 2, 1) * sin).astype(LOW)
            at = pl.multiple_of((kind * plan.heads + (part ^ d)) * HEAD, HEAD)
            out[:, pl.ds(at, HEAD)] = value


def turn_back(plan, slot_parent, place, cosine, sine, parts):
    whole = lambda i, *_: (0, 0)
    wide = 3 * plan.heads * HEAD
    return pl.pallas_call(
        functools.partial(turn_back_kernel, plan),
        grid_spec=pltpu.PrefetchScalarGridSpec(
            num_scalar_prefetch=2,
            grid=(plan.slots,),
            in_specs=[pl.BlockSpec((CHAIN * BLOCK, HEAD), whole)] * 2
            + [pl.BlockSpec((3, BLOCK, HEAD), lambda i, *_: (0, i, 0))] * plan.spread,
            out_specs=pl.BlockSpec((BLOCK, wide), lambda i, *_: (i, 0)),
        ),
        out_shape=shape((plan.rows, wide), LOW),
        name="turn_back",
    )(slot_parent, place, cosine, sine, *parts)


def out_kernel(plan, place, x, att, near, far, middle, normed):
    half = plan.heads * HEAD // 2
    core = place[0] % 2
    total = x[...].astype(F32)
    for z in range(plan.tensor):
        for side, w in ((core, near), (1 - core, far)):
            columns = pl.ds(pl.multiple_of(side * half, half), half)
            total = total + dot(att[z, :, columns], w[z])
    middle[...] = total
    normed[...] = layer_norm(total)[0].astype(LOW)


def project_out(plan, place, tokens, att, near, far):
    half = plan.heads * HEAD // 2
    once = pl.Buffered(buffer_count=1)
    weights = pl.BlockSpec(
        (plan.tensor, half, plan.width), lambda i, *_: (0, 0, 0), pipeline_mode=once
    )
    rows = pl.BlockSpec((BLOCK, plan.width), lambda i, *_: (i, 0))
    return pl.pallas_call(
        functools.partial(out_kernel, plan),
        grid_spec=pltpu.PrefetchScalarGridSpec(
            num_scalar_prefetch=1,
            grid=(plan.slots,),
            in_specs=[
                rows,
                pl.BlockSpec((plan.tensor, BLOCK, 2 * half), lambda i, *_: (0, i, 0)),
                weights,
                weights,
            ],
            out_specs=[rows, rows],
        ),
        out_shape=[shape((plan.rows, plan.width), F32), shape((plan.rows, plan.width), LOW)],
        compiler_params=params(48),
        cost_estimate=pl.CostEstimate(
            flops=2 * plan.rows * plan.width * plan.width,
            bytes_accessed=20 * MIB,
            transcendentals=0,
        ),
        name="project_out",
    )(place, tokens, att, near, far)


def ff_kernel(rows_each, normed, cot, wg, wu, wd, hidden, grad_gate, grad_up, back, total):
    step = pl.program_id(0)
    for start in range(0, normed.shape[0], rows_each):
        rows = slice(start, start + rows_each)
        n = normed[rows, :]
        gate = dot(n, wg[...])
        up = dot(n, wu[...])
        grad_hidden = dot_nt(cot[rows, :], wd[...])
        s = 1.0 / (1.0 + jnp.exp(-gate))
        active = gate * s
        hidden[rows, :] = (active * up).astype(LOW)
        gu = (grad_hidden * active).astype(LOW)
        gg = (grad_hidden * up * s * (1.0 + gate * (1.0 - s))).astype(LOW)
        grad_up[rows, :] = gu
        grad_gate[rows, :] = gg
        part = dot_nt(gg, wg[...]) + dot_nt(gu, wu[...])

        @pl.when(step == 0)
        def _():
            total[rows, :] = part

        @pl.when(step > 0)
        def _():
            total[rows, :] += part

    @pl.when(step == pl.num_programs(0) - 1)
    def _():
        back[...] = total[...].astype(LOW)


def feed_forward(normed, cot, wg, wu, wd):
    rows, width = normed.shape
    ff = wg.shape[1]
    tile = min(512, ff)
    whole = pl.BlockSpec((rows, width), lambda i: (0, 0), pipeline_mode=pl.Buffered(buffer_count=1))
    across = pl.BlockSpec((width, tile), lambda i: (0, i))
    out = pl.BlockSpec((rows, tile), lambda i: (0, i))
    return pl.pallas_call(
        functools.partial(ff_kernel, rows // 2),
        grid=(ff // tile,),
        in_specs=[whole, whole, across, across, pl.BlockSpec((tile, width), lambda i: (i, 0))],
        out_specs=[out, out, out, pl.BlockSpec((rows, width), lambda i: (0, 0))],
        out_shape=[shape((rows, ff), LOW)] * 3 + [shape((rows, width), LOW)],
        scratch_shapes=[pltpu.VMEM((rows, width), F32)],
        compiler_params=params(60),
        cost_estimate=pl.CostEstimate(
            flops=10 * rows * width * ff, bytes_accessed=40 * MIB, transcendentals=rows * ff
        ),
        name="feed_forward",
    )(normed, cot, wg, wu, wd)


def weight_gradient(plan, lhs, rhs):
    half, piece = plan.dp // 2, plan.piece
    columns = rhs.shape[1]
    kept = half * piece
    pairs = lambda bit: xor_pairs(plan.dp, 1 << bit)
    send = dot_tn(lhs[:, kept : 2 * kept], rhs).astype(LOW)
    recv = lax.ppermute(send, "dp", pairs(0))
    up, down = kept_orders(plan)
    results = []
    for way in range(2):
        cols = slice(way * columns // 2, (way + 1) * columns // 2)
        order = up if way == 0 else down
        base = 0 if way == 0 else 2 * kept
        bits = list(range(1, plan.bits))
        if way == 1:
            bits = bits[::-1]
        size = half // 2
        parts = []
        for side in range(2):
            at = base + side * size * piece
            product = dot_tn(lhs[:, at : at + size * piece], rhs[:, cols])
            arrived = [
                recv[up.index(rel) * piece : (up.index(rel) + 1) * piece, cols]
                for rel in order[side * size : (side + 1) * size]
            ]
            parts.append((product + jnp.concatenate(arrived, 0).astype(F32)).astype(LOW))
        keep, away = parts
        for number, bit in enumerate(bits):
            got = lax.ppermute(away, "dp", pairs(bit))
            total = keep.astype(F32) + got.astype(F32)
            if number == len(bits) - 1:
                results.append(total)
            else:
                size = total.shape[0] // 2
                keep = total[:size].astype(LOW)
                away = total[size:].astype(LOW)
    return jnp.concatenate(results, axis=1)


def body(mesh, tokens, w_query, w_key, w_value, w_out, w_gate, w_up, w_down, cotangent, slot_parent):
    plan = Plan(mesh, tokens.shape[0], tokens.shape[1], w_query.shape[1] // HEAD, w_gate.shape[1])
    me = lax.axis_index("dp")
    z = lax.axis_index("tensor")
    place = jnp.stack([me, z]).astype(jnp.int32)
    cosine, sine = (jnp.asarray(table) for table in rope_tables())
    n = plan.spread

    def swap(array, mask):
        return lax.ppermute(array, "dp", xor_pairs(plan.dp, mask))

    def exchange(parts):
        return [parts[0]] + [swap(parts[d], d * plan.rest) for d in range(1, n)]

    half = w_out.shape[0] // 2
    mine = lax.dynamic_slice_in_dim(w_out, (me % 2) * half, half, 0)
    near = lax.all_gather(mine, "tensor", axis=0, tiled=False)
    far = swap(near, 1)

    normed_one, *sends = project_qkv(
        plan, slot_parent, place, tokens, w_query, w_key, w_value, cosine, sine
    )
    parts = exchange(sends)
    kv = jnp.stack([part[1:] for part in parts])[None]
    mask = 1
    while mask < plan.rest:
        kv = jnp.concatenate([kv, swap(kv, mask)], axis=0)
        mask *= 2
    kv = kv.reshape(plan.dp * 2 * plan.slots, BLOCK, HEAD)
    attended_parts = exchange(attend(plan, slot_parent, place, parts, kv))
    attended = gather_heads(plan, place, attended_parts)
    everyone = lax.all_gather(attended, "tensor", axis=0, tiled=False)
    middle, normed_two = project_out(plan, place, tokens, everyone, near, far)

    hidden, grad_gate_proj, grad_up_proj, partial_two = feed_forward(
        normed_two, cotangent, w_gate, w_up, w_down
    )
    mine_rows = lambda array: lax.dynamic_slice_in_dim(array, z * plan.own, plan.own, 0)
    grad_normed_two = lax.psum_scatter(
        partial_two, "tensor", scatter_dimension=0, tiled=True
    ).astype(F32)
    branch_out = dot(hidden, w_down).astype(LOW)
    middle_own = mine_rows(middle)
    norm_two, inverse_two = layer_norm(middle_own)
    grad_middle = mine_rows(cotangent).astype(F32) + norm_back(grad_normed_two, norm_two, inverse_two)
    grad_branch = grad_middle.astype(LOW)

    ga_near = jnp.einsum("td,zcd->ztc", grad_branch, near, preferred_element_type=F32).astype(LOW)
    ga_far = jnp.einsum("td,zcd->ztc", grad_branch, far, preferred_element_type=F32).astype(LOW)
    even = me % 2 == 0
    ga = jnp.concatenate(
        [jnp.where(even, ga_near, ga_far), jnp.where(even, ga_far, ga_near)], axis=2
    )
    sources = []
    for shift in range(plan.tensor):
        chunk = lax.dynamic_index_in_dim(ga, (z + shift) % plan.tensor, 0, keepdims=False)
        if shift:
            chunk = lax.ppermute(
                chunk, "tensor", [(i, (i + shift) % plan.tensor) for i in range(plan.tensor)]
            )
        sources.append(chunk)
    grads = exchange(scatter_heads(plan, place, sources))
    *grad_queries, grad_near, grad_far = attend_back(plan, slot_parent, place, parts, kv, grads)

    grad_far = grad_far.reshape(plan.rest - 1, n, 2, plan.rows, HEAD)
    grad_near = grad_near.reshape(1, n, 2, plan.rows, HEAD)
    mask = plan.rest // 2
    while mask >= 1:
        got = swap(grad_far[mask - 1 : 2 * mask - 1], mask).astype(F32)
        grad_near = grad_near + got[:1]
        if mask > 1:
            grad_far = (grad_far[: mask - 1].astype(F32) + got[1:]).astype(LOW)
        mask //= 2
    backs = exchange(
        [
            jnp.concatenate([grad_queries[d][None], grad_near[0, d].astype(LOW)], axis=0)
            for d in range(n)
        ]
    )
    turned = turn_back(plan, slot_parent, place, cosine, sine, backs)
    wide = n * HEAD
    partial_one = sum(
        dot_nt(turned[:, kind * wide : (kind + 1) * wide], w)
        for kind, w in enumerate((w_query, w_key, w_value))
    ).astype(LOW)
    grad_normed_one = lax.psum_scatter(
        partial_one, "tensor", scatter_dimension=0, tiled=True
    ).astype(F32)
    norm_one, inverse_one = layer_norm(mine_rows(tokens).astype(F32))
    grad_tokens_own = (grad_middle + norm_back(grad_normed_one, norm_one, inverse_one)).astype(LOW)
    grad_tokens = lax.all_gather(grad_tokens_own, "tensor", axis=0, tiled=True)

    output_own = (
        middle_own
        + lax.psum_scatter(branch_out, "tensor", scatter_dimension=0, tiled=True).astype(F32)
    ).astype(LOW)
    output = lax.all_gather(output_own, "tensor", axis=0, tiled=True)

    cot_relative = relative_columns(plan, place, cotangent)
    two_relative = relative_columns(plan, place, normed_two)
    grad_down = weight_gradient(plan, cot_relative, hidden).T
    grad_gate = weight_gradient(plan, two_relative, grad_gate_proj)
    grad_up = weight_gradient(plan, two_relative, grad_up_proj)
    branch_all = lax.all_gather(grad_branch, "tensor", axis=0, tiled=True)
    grad_out = weight_gradient(plan, relative_columns(plan, place, branch_all), attended).T
    grad_qkv = weight_gradient(plan, normed_one, turned)
    return (
        output,
        grad_tokens,
        grad_qkv[:, :wide],
        grad_qkv[:, wide : 2 * wide],
        grad_qkv[:, 2 * wide :],
        grad_out,
        grad_gate,
        grad_up,
        grad_down,
    )


def solution(mesh):
    in_specs = (
        P("dp", None),
        P(None, "tensor"),
        P(None, "tensor"),
        P(None, "tensor"),
        P("tensor", None),
        P(None, "tensor"),
        P(None, "tensor"),
        P("tensor", None),
        P("dp", None),
        P(),
    )
    out_specs = (
        P("dp", None),
        P("dp", None),
        P("dp", "tensor"),
        P("dp", "tensor"),
        P("dp", "tensor"),
        P("tensor", "dp"),
        P("dp", "tensor"),
        P("dp", "tensor"),
        P("tensor", "dp"),
    )
    return jax.shard_map(
        functools.partial(body, mesh),
        mesh=mesh,
        in_specs=in_specs,
        out_specs=out_specs,
        check_vma=False,
    )
```

time: 1340 us -> 684 us (0.51)
  waiting for transfers between devices: 872 us -> 286 us
  matrix products: 281 us -> 108 us
  Pallas kernels: 0 us -> 138 us
  other arithmetic: 115 us -> 41.7 us
  starting transfers between devices: 1.74 us -> 47.5 us
    psum x3 -> x0, waiting for transfers between devices: 483 us -> none  [the longest x1 190 us: body(): lax.psum(jnp.dot(hidden, w_down, preferred_element_type=jnp.float32).asty...]
    reduce_scatter x7 -> x3, waiting for transfers between devices: 350 us -> 39.3 us  [the longest x1 39.3 us: body(): lax.psum_scatter(branch_out, 'tensor', scatter_dimension=0, tiled=True)]
    dot_general x54 -> x31, matrix products: 281 us -> 108 us  [the longest x25 84.6 us: dot_tn(): return lax.dot_general(a, b, TN, preferred_element_type=F32)]
    pallas_call x0 -> x11, Pallas kernels: none -> 138 us  [the longest x1 39.2 us: feed_forward(): pl.pallas_call(functools.partial(ff_kernel, rows // 2), grid=(ff // tile,...]
    ppermute x0 -> x43, waiting for transfers between devices: none -> 131 us  [the longest x20 67.7 us: weight_gradient(): got = lax.ppermute(away, 'dp', pairs(bit))]
    all_gather x2 -> x5, waiting for transfers between devices: 38.7 us -> 116 us  [the longest x1 52.3 us: body(): everyone = lax.all_gather(attended, 'tensor', axis=0, tiled=False)]
    convert_element_type x14 -> x1, other arithmetic: 67.7 us -> 3.94 us  [body(): grad_branch = grad_middle.astype(LOW)]
    ppermute x0 -> x43, starting transfers between devices: none -> 45.8 us  [the longest x20 24.5 us: weight_gradient(): got = lax.ppermute(away, 'dp', pairs(bit))]
  transfers between devices with their start and end apart: 14 -> 51, of which waited for: 11 -> 25; matrix products, arithmetic and copies ran while one was open for 20% -> 25% of each run, Pallas kernels for 0% -> 13%
where the time goes in v1:
time: 684 us; the launch traced here: 677 us
  waiting for transfers between devices  286 us (42%)
  Pallas kernels  138 us (20%)
  matrix products  108 us (16%)
  starting transfers between devices  47.5 us (7%)
  other arithmetic  41.7 us (6%)
  local copies, waits for them, and re-layouts  40.8 us (6%)
  between operations  15.5 us (2%)
    dot_general x25, matrix products, dot_tn(): return lax.dot_general(a, b, TN, preferred_element_type=F32)  84.6 us
    ppermute x20, waiting for transfers between devices, weight_gradient(): got = lax.ppermute(away, 'dp', pairs(bit))  67.7 us
    all_gather x1, waiting for transfers between devices, body(): everyone = lax.all_gather(attended, 'tensor', axis=0, tiled=False)  52.3 us
    ppermute x15, waiting for transfers between devices, swap(): return lax.ppermute(array, 'dp', xor_pairs(plan.dp, mask))  47.6 us
    reduce_scatter x1, waiting for transfers between devices, body(): lax.psum_scatter(branch_out, 'tensor', scatter_dimension=0, tiled=True)  39.3 us
    pallas_call x1, Pallas kernels, feed_forward(): pl.pallas_call(functools.partial(ff_kernel, rows // 2), grid=(ff // tile,...  39.2 us
    all_gather x1, waiting for transfers between devices, body(): near = lax.all_gather(mine, 'tensor', axis=0, tiled=False)  38.8 us
    pallas_call x1, Pallas kernels, attend_back(): pl.pallas_call(functools.partial(attend_back_kernel, plan), grid_spec=plt...  29.4 us
  transfers between devices with their start and end apart: 51, of which 25 were waited for; matrix products, arithmetic and copies ran while one was open for 25% of the time, Pallas kernels for 13%

profile of v1, /device:TPU:0, one launch (start us, length us, event | category | flops | bytes accessed | tf_op | source)
XLA Modules:
  0.0 677.3 jit_solution(10683086403248912594)
XLA Ops:
  12.7 11.2 %project_qkv.1 = (bf16[640,3072]{1,0:T(8,128)(2,1)}, bf16[3,640,128]{2,1,0:T(8,128)(2,1)S(1)}, bf16[3,640,128]{2,1,0:T(8,128)(2,1)S(1)}, bf16[3,640,128]{2,1,0:T(8,128)(2,1)S(1)}, bf16[3,640,128]{2,1,0:T(8,128)(2,1)S(1)}) custom-call(s32[40]{0:T(128)S(1)} %copy-done.19, s32[2]{0:T(128)S(1)} %pad_add_fusion.place, bf16[640,2048]{1,0:T(8,128)(2,1)} %x.3, ...), custom_call_target="tpu_custom_call" | custom-call | flops 4026531840 | bytes 16777216 | tf_op jit(solution)/shard_map/project_qkv/pallas_call | solution.py:145
  23.9 3.9 collective-permute-start.2
  28.4 11.5 %collective-permute-done.2.refs_3_ = bf16[3,640,128]{2,1,0:T(8,128)(2,1)S(1)} collective-permute-done((bf16[3,640,128]{2,1,0:T(8,128)(2,1)S(1)}, bf16[3,640,128]{2,1,0:T(8,128)(2,1)S(1)}, u32[]{:S(2)}, u32[]{:S(2)}) %collective-permute-start.2) | collective-permute-done | bytes 491552 | tf_op jit(solution)/shard_map/ppermute | solution.py:558
  39.9 9.5 %collective-permute-done.1.refs_2_ = bf16[3,640,128]{2,1,0:T(8,128)(2,1)S(1)} collective-permute-done((bf16[3,640,128]{2,1,0:T(8,128)(2,1)S(1)}, bf16[3,640,128]{2,1,0:T(8,128)(2,1)S(1)}, u32[]{:S(2)}, u32[]{:S(2)}) %collective-permute-start.1) | collective-permute-done | bytes 491552 | tf_op jit(solution)/shard_map/ppermute | solution.py:558
  50.1 3.0 collective-permute-done.3
  54.9 38.8 %all-gather.16.cloned.1.call-done = bf16[1024,2048]{1,0:T(8,128)(2,1)} async-done(((bf16[256,2048]{1,0:T(8,128)(2,1)}), bf16[1024,2048]{1,0:T(8,128)(2,1)}) %all-gather.16.cloned.1.call-update) | async-done | bytes 4194320 | tf_op jit(solution)/shard_map/all_gather | solution.py:565
  98.5 16.1 %attend.1 = (bf16[640,128]{1,0:T(8,128)(2,1)S(1)}, bf16[640,128]{1,0:T(8,128)(2,1)S(1)}, bf16[640,128]{1,0:T(8,128)(2,1)S(1)}, bf16[640,128]{1,0:T(8,128)(2,1)S(1)}) custom-call(s32[40]{0:T(128)S(1)} %copy-done.19, s32[2]{0:T(128)S(1)} %pad_add_fusion.place, bf16[3,640,128]{2,1,0:T(8,128)(2,1)S(1)} %copy-done.9, bf16[3,640,128]{2,1,0:T(8,128)(2,1)S(1)} %copy-done.15, ...), custom_call_target="tpu_custom_call" | custom-call | flops 1677721600 | bytes 8388608 | tf_op jit(solution)/shard_map/attend/pallas_call | solution.py:238
  118.8 3.5 collective-permute-done.4.refs_1_
  122.3 4.4 collective-permute-done.5.refs_2_
  127.4 2.8 gather_heads.1
  130.5 52.3 %all-gather.14.cloned.1.call-done = bf16[2560,512]{1,0:T(8,128)(2,1)} async-done(((bf16[640,512]{1,0:T(8,128)(2,1)}), bf16[2560,512]{1,0:T(8,128)(2,1)}) %all-gather.14.cloned.1.call-update) | async-done | bytes 2621456 | tf_op jit(solution)/shard_map/all_gather | solution.py:580
  183.4 12.9 %project_out.1 = (f32[640,2048]{1,0:T(8,128)}, bf16[640,2048]{1,0:T(8,128)(2,1)S(1)}) custom-call(s32[2]{0:T(128)S(1)} %copy-done.18, bf16[640,2048]{1,0:T(8,128)(2,1)S(1)} %copy-done.2, bf16[4,640,512]{2,1,0:T(8,128)(2,1)} %bitcast.74, bf16[4,256,2048]{2,1,0:T(8,128)(2,1)} %bitcast.72, bf16[4,256,2048]{2,1,0:T(8,128)(2,1)} %collective-permute-done.7.far), custom_call_target="tpu_custom_call" | custom-call | flops 5368709120 | bytes 20971520 | tf_op jit(solution)/shard_map/project_out/pallas_call | solution.py:434
  197.8 39.2 %feed_forward.1 = (bf16[640,2048]{1,0:T(8,128)(2,1)}, bf16[640,2048]{1,0:T(8,128)(2,1)}, bf16[640,2048]{1,0:T(8,128)(2,1)}, bf16[640,2048]{1,0:T(8,128)(2,1)}) custom-call(bf16[640,2048]{1,0:T(8,128)(2,1)} %copy-done.4, bf16[640,2048]{1,0:T(8,128)(2,1)} %source.1, bf16[2048,2048]{1,0:T(8,128)(2,1)} %wg.1, bf16[2048,2048]{1,0:T(8,128)(2,1)} %wu.1, ...), custom_call_target="tpu_custom_call" | custom-call | flops 26843545600 | bytes 41943040 | tf_op jit(solution)/shard_map/feed_forward/pallas_call | solution.py:495
  237.3 5.7 relative_columns.4
  243.1 7.8 %convolution_convert_fusion.3 = bf16[1024,2048]{1,0:T(8,128)(2,1)} fusion(bf16[640,2048]{1,0:T(8,128)(2,1)} %get-tuple-element.57, bf16[640,3072]{1,0:T(8,128)(2,1)} %relative_columns.4), kind=kOutput, calls=%fused_computation.4 | convolution fusion | flops 2686451712 | bytes 8126464 | tf_op jit(solution)/shard_map/dot_general | solution.py:35
  250.8 10.3 %convolution_convert_fusion.4 = bf16[640,2048]{1,0:T(8,128)(2,1)} fusion(bf16[640,2048]{1,0:T(8,128)(2,1)S(1)} %copy-done.67, bf16[2048,2048]{1,0:T(8,128)(2,1)} %wd.1), kind=kOutput, calls=%fused_computation.5 | convolution fusion | flops 5370019840 | bytes 13631488 | tf_op jit(solution)/shard_map/dot_general | solution.py:27
  261.8 7.7 %convolution_convert_fusion.2 = bf16[1024,2048]{1,0:T(8,128)(2,1)} fusion(bf16[640,2048]{1,0:T(8,128)(2,1)} %get-tuple-element.58, bf16[640,3072]{1,0:T(8,128)(2,1)} %relative_columns.4), kind=kOutput, calls=%fused_computation.3 | convolution fusion | flops 2686451712 | bytes 8126464 | tf_op jit(solution)/shard_map/dot_general | solution.py:35
  270.0 5.7 relative_columns.5
  276.0 7.8 %convolution_convert_fusion.1 = bf16[1024,2048]{1,0:T(8,128)(2,1)} fusion(bf16[640,2048]{1,0:T(8,128)(2,1)} %get-tuple-element.44, bf16[640,3072]{1,0:T(8,128)(2,1)} %relative_columns.5), kind=kOutput, calls=%fused_computation.2 | convolution fusion | flops 2686451712 | bytes 8126464 | tf_op jit(solution)/shard_map/dot_general | solution.py:35
  287.2 2.9 fusion.102
  293.5 3.2 add_convert_fusion.18
  298.1 3.2 add_convert_fusion.19
  303.3 39.3 %reduce-scatter.4.cloned.1.call-done = bf16[160,2048]{1,0:T(8,128)(2,1)} async-done(((bf16[640,2048]{1,0:T(8,128)(2,1)}), bf16[160,2048]{1,0:T(8,128)(2,1)}) %reduce-scatter.4.cloned.1.call-update) | async-done | bytes 655376 | tf_op jit(solution)/shard_map/reduce_scatter | solution.py:643
  342.6 3.9 fusion.98
  346.8 3.9 add_convert_fusion.16
  350.7 2.7 fusion.101
  353.8 3.2 add_convert_fusion.12
  357.1 3.4 add_convert_fusion.13
  360.5 3.6 add_convert_fusion.6
  365.6 3.7 select_bitcast_fusion
  372.1 2.7 collective-permute-start.10
  376.8 5.7 collective-permute-done.8.refs_1_
  382.5 10.0 %collective-permute-done.9.refs_2_ = bf16[160,512]{1,0:T(8,128)(2,1)S(1)} collective-permute-done((bf16[160,512]{1,0:T(8,128)(2,1)S(1)}, bf16[160,512]{1,0:T(8,128)(2,1)S(1)}, u32[]{:S(2)}, u32[]{:S(2)}) %collective-permute-start.9) | collective-permute-done | bytes 163872 | tf_op jit(solution)/shard_map/ppermute | solution.py:606
  393.1 2.8 scatter_heads.1
  399.4 2.9 fusion.100
  404.6 2.6 collective-permute-done.12.refs_7_
  407.9 29.4 %attend_back.1 = (bf16[640,128]{1,0:T(8,128)(2,1)}, bf16[640,128]{1,0:T(8,128)(2,1)}, bf16[640,128]{1,0:T(8,128)(2,1)}, bf16[640,128]{1,0:T(8,128)(2,1)}, f32[40...) custom-call(s32[40]{0:T(128)} %parent.7, s32[2]{0:T(128)} %copy-done.17, bf16[3,640,128]{2,1,0:T(8,128)(2,1)} %copy-done.8, ...), custom_call_target="tpu_custom_call" | custom-call | flops 4194304000 | bytes 16777216 | tf_op jit(solution)/shard_map/attend_back/pallas_call | solution.py:305
  437.3 3.6 add_convert_fusion.10
  441.0 3.5 add_convert_fusion.7
  444.8 3.8 add_convert_fusion.3
  448.6 3.2 add_convert_fusion.4
  464.8 3.7 collective-permute-done.15.refs_1_
  468.5 2.4 collective-permute-start.41
  470.9 8.2 %collective-permute-done.16.refs_2_ = bf16[3,640,128]{2,1,0:T(8,128)(2,1)S(1)} collective-permute-done((bf16[3,640,128]{2,1,0:T(8,128)(2,1)S(1)}, bf16[3,640,128]{2,1,0:T(8,128)(2,1)S(1)}, u32[]{:S(2)}, u32[]{:S(2)}) %collective-permute-start.16) | collective-permute-done | bytes 491552 | tf_op jit(solution)/shard_map/ppermute | solution.py:558
  479.1 2.3 collective-permute-start.39
  483.0 5.9 turn_back.1
  488.9 3.5 fusion.70
  494.0 3.0 add_convert_fusion
  497.2 2.3 collective-permute-start.30
  505.7 18.5 %collective-permute-done.39 = bf16[512,1024]{1,0:T(8,128)(2,1)} collective-permute-done((bf16[512,1024]{1,0:T(8,128)(2,1)}, bf16[512,1024]{1,0:T(8,128)(2,1)}, u32[]{:S(2)}, u32[]{:S(2)}) %collective-permute-start.39) | collective-permute-done | bytes 1048608 | tf_op jit(solution)/shard_map/ppermute | solution.py:538
  531.9 25.5 %collective-permute-done.42 = bf16[256,1024]{1,0:T(8,128)(2,1)S(1)} collective-permute-done((bf16[256,1024]{1,0:T(8,128)(2,1)S(1)}, bf16[256,1024]{1,0:T(8,128)(2,1)S(1)}, u32[]{:S(2)}, u32[]{:S(2)}) %collective-permute-start.42) | collective-permute-done | bytes 524320 | tf_op jit(solution)/shard_map/ppermute | solution.py:538
  557.4 2.4 collective-permute-start.35
  561.6 3.1 copy.24
  568.9 5.9 relative_columns.3
  574.8 3.5 convolution_convert_fusion.5
  578.2 5.5 convolution_convert_fusion
  589.4 2.2 fusion.25
  591.6 2.3 fusion.20
  596.4 2.5 fusion.6
  615.0 11.5 %collective-permute-done.21 = bf16[512,768]{1,0:T(8,128)(2,1)S(1)} collective-permute-done((bf16[512,768]{1,0:T(8,128)(2,1)S(1)}, bf16[512,768]{1,0:T(8,128)(2,1)S(1)}, u32[]{:S(2)}, u32[]{:S(2)}) %collective-permute-start.21) | collective-permute-done | bytes 786464 | tf_op jit(solution)/shard_map/ppermute | solution.py:538
  627.8 3.2 collective-permute-done.19
  632.5 5.1 collective-permute-done.22
  640.4 24.4 %all-gather.10.cloned.1.call-done = bf16[640,2048]{1,0:T(8,128)(2,1)} async-done(((bf16[160,2048]{1,0:T(8,128)(2,1)}), bf16[640,2048]{1,0:T(8,128)(2,1)}) %all-gather.10.cloned.1.call-update) | async-done | bytes 2621456 | tf_op jit(solution)/shard_map/all_gather | solution.py:639
  664.8 3.7 copy.30
  (305 shorter events, 113.9 us)
Async XLA Ops:
  7.2 86.5 %all-gather.16.cloned.1.call-start = ((), (), s32[]{:S(2)}) async-start(), calls=%async_computation.10 | async-start | bytes 5242880 | tf_op jit(solution)/shard_map/all_gather | solution.py:565
  9.9 172.9 %all-gather.14.cloned.1.call-start = ((), (), s32[]{:S(2)}) async-start(), calls=%async_computation.9 | async-start | bytes 3276800 | tf_op jit(solution)/shard_map/all_gather | solution.py:580
  12.7 81.0 %copy-start.17 = (s32[2]{0:T(128)}, s32[2]{0:T(128)S(1)}, u32[]{:S(2)}) copy-start(s32[2]{0:T(128)S(1)} %pad_add_fusion.place) | copy-start | bytes 28
  23.9 26.2 %copy-start.8 = (bf16[3,640,128]{2,1,0:T(8,128)(2,1)}, bf16[3,640,128]{2,1,0:T(8,128)(2,1)S(1)}, u32[]{:S(2)}) copy-start(bf16[3,640,128]{2,1,0:T(8,128)(2,1)S(1)} %get-tuple-element.34.refs_0_) | copy-start | bytes 1474564
  23.9 16.0 %collective-permute-start.2 = (bf16[3,640,128]{2,1,0:T(8,128)(2,1)S(1)}, bf16[3,640,128]{2,1,0:T(8,128)(2,1)S(1)}, u32[]{:S(2)}, u32[]{:S(2)}) collective-permute-start(bf16[3,640,128]{2,1,0:T(8,128)(2,1)S(1)} %get-tuple-element.37), channel_id=1, source_target_pairs={{0,24},{4,28},{8,16},{12,20},{16,8},{20,12},{24,0},{28,4},{1,25},{... | collective-permute-start | bytes 1474568 | tf_op jit(solution)/shard_map/ppermute | solution.py:558
  27.7 21.7 %collective-permute-start.1 = (bf16[3,640,128]{2,1,0:T(8,128)(2,1)S(1)}, bf16[3,640,128]{2,1,0:T(8,128)(2,1)S(1)}, u32[]{:S(2)}, u32[]{:S(2)}) collective-permute-start(bf16[3,640,128]{2,1,0:T(8,128)(2,1)S(1)} %get-tuple-element.36), channel_id=1, source_target_pairs={{0,16},{4,20},{8,24},{12,28},{16,0},{20,4},{24,8},{28,12},{1,17},{... | collective-permute-start | bytes 1474568 | tf_op jit(solution)/shard_map/ppermute | solution.py:558
  28.3 21.6 %collective-permute-start = (bf16[3,640,128]{2,1,0:T(8,128)(2,1)S(1)}, bf16[3,640,128]{2,1,0:T(8,128)(2,1)S(1)}, u32[]{:S(2)}, u32[]{:S(2)}) collective-permute-start(bf16[3,640,128]{2,1,0:T(8,128)(2,1)S(1)} %get-tuple-element.35), channel_id=1, source_target_pairs={{0,8},{4,12},{8,0},{12,4},{16,24},{20,28},{24,16},{28,20},{1,9},{5... | collective-permute-start | bytes 1474568 | tf_op jit(solution)/shard_map/ppermute | solution.py:558
  39.8 10.2 %copy-start.10 = (bf16[3,640,128]{2,1,0:T(8,128)(2,1)}, bf16[3,640,128]{2,1,0:T(8,128)(2,1)S(1)}, u32[]{:S(2)}) copy-start(bf16[3,640,128]{2,1,0:T(8,128)(2,1)S(1)} %collective-permute-done.2.refs_3_) | copy-start | bytes 1474564
  50.0 3.1 collective-permute-start.3
  50.1 43.6 %copy-start.9 = (bf16[3,640,128]{2,1,0:T(8,128)(2,1)S(1)}, bf16[3,640,128]{2,1,0:T(8,128)(2,1)}, u32[]{:S(2)}) copy-start(bf16[3,640,128]{2,1,0:T(8,128)(2,1)} %copy-done.8) | copy-start | bytes 1474564
  93.7 89.1 %collective-permute-start.7 = (bf16[4,256,2048]{2,1,0:T(8,128)(2,1)}, bf16[4,256,2048]{2,1,0:T(8,128)(2,1)}, u32[]{:S(2)}, u32[]{:S(2)}) collective-permute-start(bf16[4,256,2048]{2,1,0:T(8,128)(2,1)} %bitcast.71), channel_id=1, source_target_pairs={{0,4},{4,0},{8,12},{12,8},{16,20},{20,16},{24,28},{28,24},{1,5},{5... | collective-permute-start | bytes 12582920 | tf_op jit(solution)/shard_map/ppermute | solution.py:558
  98.5 84.3 %copy-start.2 = (bf16[640,2048]{1,0:T(8,128)(2,1)S(1)}, bf16[640,2048]{1,0:T(8,128)(2,1)}, u32[]{:S(2)}) copy-start(bf16[640,2048]{1,0:T(8,128)(2,1)} %x.3) | copy-start | bytes 7864324
  115.3 7.0 %collective-permute-start.4 = (bf16[640,128]{1,0:T(8,128)(2,1)S(1)}, bf16[640,128]{1,0:T(8,128)(2,1)S(1)}, u32[]{:S(2)}, u32[]{:S(2)}) collective-permute-start(bf16[640,128]{1,0:T(8,128)(2,1)S(1)} %get-tuple-element.39), channel_id=1, source_target_pairs={{0,8},{4,12},{8,0},{12,4},{16,24},{20,28},{24,16},{28,20},{1,9},{5... | collective-permute-start | bytes 491528 | tf_op jit(solution)/shard_map/ppermute | solution.py:558
  116.9 9.8 %collective-permute-start.5 = (bf16[640,128]{1,0:T(8,128)(2,1)S(1)}, bf16[640,128]{1,0:T(8,128)(2,1)S(1)}, u32[]{:S(2)}, u32[]{:S(2)}) collective-permute-start(bf16[640,128]{1,0:T(8,128)(2,1)S(1)} %get-tuple-element.40), channel_id=1, source_target_pairs={{0,16},{4,20},{8,24},{12,28},{16,0},{20,4},{24,8},{28,12},{1,17},{... | collective-permute-start | bytes 491528 | tf_op jit(solution)/shard_map/ppermute | solution.py:558
  118.3 8.4 %collective-permute-start.6 = (bf16[640,128]{1,0:T(8,128)(2,1)S(1)}, bf16[640,128]{1,0:T(8,128)(2,1)S(1)}, u32[]{:S(2)}, u32[]{:S(2)}) collective-permute-start(bf16[640,128]{1,0:T(8,128)(2,1)S(1)} %get-tuple-element.41), channel_id=1, source_target_pairs={{0,24},{4,28},{8,16},{12,20},{16,8},{20,12},{24,0},{28,4},{1,25},{... | collective-permute-start | bytes 491528 | tf_op jit(solution)/shard_map/ppermute | solution.py:558
  130.2 171.1 %reduce-scatter.6.cloned.1.call-start = ((), (), s32[]{:S(2)}) async-start(), calls=%async_computation.5 | async-start | bytes 3276800 | tf_op jit(solution)/shard_map/reduce_scatter | solution.py:587
  237.0 105.6 %reduce-scatter.4.cloned.1.call-start = ((), (), s32[]{:S(2)}) async-start(), calls=%async_computation.3 | async-start | bytes 3276800 | tf_op jit(solution)/shard_map/reduce_scatter | solution.py:643
  243.1 7.8 %copy-start.67 = (bf16[640,2048]{1,0:T(8,128)(2,1)S(1)}, bf16[640,2048]{1,0:T(8,128)(2,1)}, u32[]{:S(2)}) copy-start(bf16[640,2048]{1,0:T(8,128)(2,1)} %get-tuple-element.44) | copy-start | bytes 7864324
  250.8 36.3 %collective-permute-start.28 = (bf16[1024,2048]{1,0:T(8,128)(2,1)}, bf16[1024,2048]{1,0:T(8,128)(2,1)}, u32[]{:S(2)}, u32[]{:S(2)}) collective-permute-start(bf16[1024,2048]{1,0:T(8,128)(2,1)} %convolution_convert_fusion.3), channel_id=1, source_target_pairs={{0,4},{4,0},{8,12},{12,8},{16,20},{20,16},{24,28},{28,24},{1,5},{5... | collective-permute-start | bytes 12582920 | tf_op jit(solution)/shard_map/ppermute | solution.py:516
  261.1 307.8 %all-gather.12.cloned.1.call-start = ((), (), s32[]{:S(2)}) async-start(), calls=%async_computation.8 | async-start | bytes 3276800 | tf_op jit(solution)/shard_map/all_gather | solution.py:652
  269.5 81.2 %collective-permute-start.33 = (bf16[1024,2048]{1,0:T(8,128)(2,1)}, bf16[1024,2048]{1,0:T(8,128)(2,1)}, u32[]{:S(2)}, u32[]{:S(2)}) collective-permute-start(bf16[1024,2048]{1,0:T(8,128)(2,1)} %convolution_convert_fusion.2), channel_id=1, source_target_pairs={{0,4},{4,0},{8,12},{12,8},{16,20},{20,16},{24,28},{28,24},{1,5},{5... | collective-permute-start | bytes 12582920 | tf_op jit(solution)/shard_map/ppermute | solution.py:516
  283.8 76.7 %collective-permute-start.38 = (bf16[1024,2048]{1,0:T(8,128)(2,1)}, bf16[1024,2048]{1,0:T(8,128)(2,1)}, u32[]{:S(2)}, u32[]{:S(2)}) collective-permute-start(bf16[1024,2048]{1,0:T(8,128)(2,1)} %convolution_convert_fusion.1), channel_id=1, source_target_pairs={{0,4},{4,0},{8,12},{12,8},{16,20},{20,16},{24,28},{28,24},{1,5},{5... | collective-permute-start | bytes 12582920 | tf_op jit(solution)/shard_map/ppermute | solution.py:516
  292.0 165.1 %collective-permute-start.31 = (bf16[512,1024]{1,0:T(8,128)(2,1)}, bf16[512,1024]{1,0:T(8,128)(2,1)}, u32[]{:S(2)}, u32[]{:S(2)}) collective-permute-start(bf16[512,1024]{1,0:T(8,128)(2,1)} %add_convert_fusion.15), channel_id=1, source_target_pairs={{0,16},{4,20},{8,24},{12,28},{16,0},{20,4},{24,8},{28,12},{1,17},{... | collective-permute-start | bytes 3145736 | tf_op jit(solution)/shard_map/ppermute | solution.py:538
  296.7 163.6 %collective-permute-start.29 = (bf16[512,1024]{1,0:T(8,128)(2,1)}, bf16[512,1024]{1,0:T(8,128)(2,1)}, u32[]{:S(2)}, u32[]{:S(2)}) collective-permute-start(bf16[512,1024]{1,0:T(8,128)(2,1)} %add_convert_fusion.18), channel_id=1, source_target_pairs={{0,8},{4,12},{8,0},{12,4},{16,24},{20,28},{24,16},{28,20},{1,9},{5... | collective-permute-start | bytes 3145736 | tf_op jit(solution)/shard_map/ppermute | solution.py:538
  301.3 41.3 %copy-start.37 = (bf16[160,2048]{1,0:T(8,128)(2,1)S(1)}, bf16[160,2048]{1,0:T(8,128)(2,1)}, u32[]{:S(2)}) copy-start(bf16[160,2048]{1,0:T(8,128)(2,1)} %reduce-scatter.6.cloned.1.call-done) | copy-start | bytes 1966084
  346.6 241.7 %all-gather.8.cloned.1.call-start = ((), (), s32[]{:S(2)}) async-start(), calls=%async_computation.4 | async-start | bytes 3276800 | tf_op jit(solution)/shard_map/all_gather | solution.py:645
  370.1 12.3 %collective-permute-start.8 = (bf16[160,512]{1,0:T(8,128)(2,1)S(1)}, bf16[160,512]{1,0:T(8,128)(2,1)S(1)}, u32[]{:S(2)}, u32[]{:S(2)}) collective-permute-start(bf16[160,512]{1,0:T(8,128)(2,1)S(1)} %get-tuple-element.104), channel_id=1, source_target_pairs={{0,1},{1,2},{2,3},{3,0},{4,5},{5,6},{6,7},{7,4},{8,9},{9,10},{10,1... | collective-permute-start | bytes 491528 | tf_op jit(solution)/shard_map/ppermute | solution.py:606
  370.4 22.0 %collective-permute-start.9 = (bf16[160,512]{1,0:T(8,128)(2,1)S(1)}, bf16[160,512]{1,0:T(8,128)(2,1)S(1)}, u32[]{:S(2)}, u32[]{:S(2)}) collective-permute-start(bf16[160,512]{1,0:T(8,128)(2,1)S(1)} %get-tuple-element.105), channel_id=1, source_target_pairs={{0,2},{1,3},{2,0},{3,1},{4,6},{5,7},{6,4},{7,5},{8,10},{9,11},{10,... | collective-permute-start | bytes 491528 | tf_op jit(solution)/shard_map/ppermute | solution.py:606
  372.1 20.3 %collective-permute-start.10 = (bf16[160,512]{1,0:T(8,128)(2,1)S(1)}, bf16[160,512]{1,0:T(8,128)(2,1)S(1)}, u32[]{:S(2)}, u32[]{:S(2)}) collective-permute-start(bf16[160,512]{1,0:T(8,128)(2,1)S(1)} %get-tuple-element.102), channel_id=1, source_target_pairs={{0,3},{1,0},{2,1},{3,2},{4,7},{5,4},{6,5},{7,6},{8,11},{9,8},{10,9... | collective-permute-start | bytes 491528 | tf_op jit(solution)/shard_map/ppermute | solution.py:606
  382.5 10.7 %copy-start.55 = (bf16[160,512]{1,0:T(8,128)(2,1)}, bf16[160,512]{1,0:T(8,128)(2,1)S(1)}, u32[]{:S(2)}) copy-start(bf16[160,512]{1,0:T(8,128)(2,1)S(1)} %collective-permute-done.8.refs_1_) | copy-start | bytes 491524
  395.9 7.2 %collective-permute-start.11 = (bf16[640,128]{1,0:T(8,128)(2,1)}, bf16[640,128]{1,0:T(8,128)(2,1)S(1)}, u32[]{:S(2)}, u32[]{:S(2)}) collective-permute-start(bf16[640,128]{1,0:T(8,128)(2,1)} %get-tuple-element.47), channel_id=1, source_target_pairs={{0,8},{4,12},{8,0},{12,4},{16,24},{20,28},{24,16},{28,20},{1,9},{5... | collective-permute-start | bytes 491528 | tf_op jit(solution)/shard_map/ppermute | solution.py:558
  397.4 9.8 %collective-permute-start.12 = (bf16[640,128]{1,0:T(8,128)(2,1)}, bf16[640,128]{1,0:T(8,128)(2,1)S(1)}, u32[]{:S(2)}, u32[]{:S(2)}) collective-permute-start(bf16[640,128]{1,0:T(8,128)(2,1)} %get-tuple-element.48), channel_id=1, source_target_pairs={{0,16},{4,20},{8,24},{12,28},{16,0},{20,4},{24,8},{28,12},{1,17},{... | collective-permute-start | bytes 491528 | tf_op jit(solution)/shard_map/ppermute | solution.py:558
  398.8 8.4 %collective-permute-start.13 = (bf16[640,128]{1,0:T(8,128)(2,1)}, bf16[640,128]{1,0:T(8,128)(2,1)S(1)}, u32[]{:S(2)}, u32[]{:S(2)}) collective-permute-start(bf16[640,128]{1,0:T(8,128)(2,1)} %get-tuple-element.49), channel_id=1, source_target_pairs={{0,24},{4,28},{8,16},{12,20},{16,8},{20,12},{24,0},{28,4},{1,25},{... | collective-permute-start | bytes 491528 | tf_op jit(solution)/shard_map/ppermute | solution.py:558
  403.2 94.0 %collective-permute-start.36 = (bf16[512,1024]{1,0:T(8,128)(2,1)}, bf16[512,1024]{1,0:T(8,128)(2,1)}, u32[]{:S(2)}, u32[]{:S(2)}) collective-permute-start(bf16[512,1024]{1,0:T(8,128)(2,1)} %add_convert_fusion.9), channel_id=1, source_target_pairs={{0,16},{4,20},{8,24},{12,28},{16,0},{20,4},{24,8},{28,12},{1,17},{... | collective-permute-start | bytes 3145736 | tf_op jit(solution)/shard_map/ppermute | solution.py:538
  407.9 29.4 %copy-start.45 = (bf16[256,1024]{1,0:T(8,128)(2,1)S(1)}, bf16[256,1024]{1,0:T(8,128)(2,1)}, u32[]{:S(2)}) copy-start(bf16[256,1024]{1,0:T(8,128)(2,1)} %get-tuple-element.82) | copy-start | bytes 1572868
  437.3 14.5 %collective-permute-start.14 = (bf16[1,4,2,640,128]{4,3,2,1,0:T(8,128)(2,1)}, bf16[1,4,2,640,128]{4,3,2,1,0:T(8,128)(2,1)}, u32[]{:S(2)}, u32[]{:S(2)}) collective-permute-start(bf16[1,4,2,640,128]{4,3,2,1,0:T(8,128)(2,1)} %bitcast.75), channel_id=1, source_target_pairs={{0,4},{4,0},{8,12},{12,8},{16,20},{20,16},{24,28},{28,24},{1,5},{5... | collective-permute-start | bytes 3932168 | tf_op jit(solution)/shard_map/ppermute | solution.py:558
  444.5 150.2 %reduce-scatter.8.cloned.1.call-start = ((), (), s32[]{:S(2)}) async-start(), calls=%async_computation.6 | async-start | bytes 3276800 | tf_op jit(solution)/shard_map/reduce_scatter | solution.py:634
  454.5 14.1 %collective-permute-start.15 = (bf16[3,640,128]{2,1,0:T(8,128)(2,1)S(1)}, bf16[3,640,128]{2,1,0:T(8,128)(2,1)S(1)}, u32[]{:S(2)}, u32[]{:S(2)}) collective-permute-start(bf16[3,640,128]{2,1,0:T(8,128)(2,1)S(1)} %pad_maximum_fusion.5), channel_id=1, source_target_pairs={{0,8},{4,12},{8,0},{12,4},{16,24},{20,28},{24,16},{28,20},{1,9},{5... | collective-permute-start | bytes 1474568 | tf_op jit(solution)/shard_map/ppermute | solution.py:558
  455.7 23.4 %collective-permute-start.16 = (bf16[3,640,128]{2,1,0:T(8,128)(2,1)S(1)}, bf16[3,640,128]{2,1,0:T(8,128)(2,1)S(1)}, u32[]{:S(2)}, u32[]{:S(2)}) collective-permute-start(bf16[3,640,128]{2,1,0:T(8,128)(2,1)S(1)} %pad_maximum_fusion.6), channel_id=1, source_target_pairs={{0,16},{4,20},{8,24},{12,28},{16,0},{20,4},{24,8},{28,12},{1,17},{... | collective-permute-start | bytes 1474568 | tf_op jit(solution)/shard_map/ppermute | solution.py:558
  457.1 24.3 %collective-permute-start.17 = (bf16[3,640,128]{2,1,0:T(8,128)(2,1)S(1)}, bf16[3,640,128]{2,1,0:T(8,128)(2,1)S(1)}, u32[]{:S(2)}, u32[]{:S(2)}) collective-permute-start(bf16[3,640,128]{2,1,0:T(8,128)(2,1)S(1)} %pad_maximum_fusion.7), channel_id=1, source_target_pairs={{0,24},{4,28},{8,16},{12,20},{16,8},{20,12},{24,0},{28,4},{1,25},{... | collective-permute-start | bytes 1474568 | tf_op jit(solution)/shard_map/ppermute | solution.py:558
  460.3 66.6 %collective-permute-start.34 = (bf16[512,1024]{1,0:T(8,128)(2,1)}, bf16[512,1024]{1,0:T(8,128)(2,1)}, u32[]{:S(2)}, u32[]{:S(2)}) collective-permute-start(bf16[512,1024]{1,0:T(8,128)(2,1)} %add_convert_fusion.12), channel_id=1, source_target_pairs={{0,8},{4,12},{8,0},{12,4},{16,24},{20,28},{24,16},{28,20},{1,9},{5... | collective-permute-start | bytes 3145736 | tf_op jit(solution)/shard_map/ppermute | solution.py:538
  468.5 12.9 %copy-start.49 = (bf16[3,640,128]{2,1,0:T(8,128)(2,1)}, bf16[3,640,128]{2,1,0:T(8,128)(2,1)S(1)}, u32[]{:S(2)}) copy-start(bf16[3,640,128]{2,1,0:T(8,128)(2,1)S(1)} %collective-permute-done.15.refs_1_) | copy-start | bytes 1474564
  468.5 34.6 %collective-permute-start.41 = (bf16[512,1024]{1,0:T(8,128)(2,1)}, bf16[512,1024]{1,0:T(8,128)(2,1)}, u32[]{:S(2)}, u32[]{:S(2)}) collective-permute-start(bf16[512,1024]{1,0:T(8,128)(2,1)} %add_convert_fusion.3), channel_id=1, source_target_pairs={{0,16},{4,20},{8,24},{12,28},{16,0},{20,4},{24,8},{28,12},{1,17},{... | collective-permute-start | bytes 3145736 | tf_op jit(solution)/shard_map/ppermute | solution.py:538
  479.1 45.1 %collective-permute-start.39 = (bf16[512,1024]{1,0:T(8,128)(2,1)}, bf16[512,1024]{1,0:T(8,128)(2,1)}, u32[]{:S(2)}, u32[]{:S(2)}) collective-permute-start(bf16[512,1024]{1,0:T(8,128)(2,1)} %add_convert_fusion.6), channel_id=1, source_target_pairs={{0,8},{4,12},{8,0},{12,4},{16,24},{20,28},{24,16},{28,20},{1,9},{5... | collective-permute-start | bytes 3145736 | tf_op jit(solution)/shard_map/ppermute | solution.py:538
  482.2 82.5 %collective-permute-start.32 = (bf16[256,1024]{1,0:T(8,128)(2,1)S(1)}, bf16[256,1024]{1,0:T(8,128)(2,1)}, u32[]{:S(2)}, u32[]{:S(2)}) collective-permute-start(bf16[256,1024]{1,0:T(8,128)(2,1)S(1)} %slice.454), channel_id=1, source_target_pairs={{0,8},{4,12},{8,0},{12,4},{16,24},{20,28},{24,16},{28,20},{1,9},{5... | collective-permute-start | bytes 1572872 | tf_op jit(solution)/shard_map/ppermute | solution.py:538
  497.1 167.7 %all-gather.10.cloned.1.call-start = ((), (), s32[]{:S(2)}) async-start(), calls=%async_computation.7 | async-start | bytes 3276800 | tf_op jit(solution)/shard_map/all_gather | solution.py:639
  497.2 6.8 %copy-start.44 = (bf16[512,1024]{1,0:T(8,128)(2,1)S(1)}, bf16[512,1024]{1,0:T(8,128)(2,1)}, u32[]{:S(2)}) copy-start(bf16[512,1024]{1,0:T(8,128)(2,1)} %add_convert_fusion.4) | copy-start | bytes 3145732
  497.2 69.0 %collective-permute-start.30 = (bf16[256,1024]{1,0:T(8,128)(2,1)}, bf16[256,1024]{1,0:T(8,128)(2,1)}, u32[]{:S(2)}, u32[]{:S(2)}) collective-permute-start(bf16[256,1024]{1,0:T(8,128)(2,1)} %slice.446), channel_id=1, source_target_pairs={{0,16},{4,20},{8,24},{12,28},{16,0},{20,4},{24,8},{28,12},{1,17},{... | collective-permute-start | bytes 1572872 | tf_op jit(solution)/shard_map/ppermute | solution.py:538
  502.3 23.0 %copy-start.43 = (bf16[512,1024]{1,0:T(8,128)(2,1)S(1)}, bf16[512,1024]{1,0:T(8,128)(2,1)}, u32[]{:S(2)}) copy-start(bf16[512,1024]{1,0:T(8,128)(2,1)} %add_convert_fusion.7) | copy-start | bytes 3145732
  503.2 81.1 %collective-permute-start.37 = (bf16[256,1024]{1,0:T(8,128)(2,1)}, bf16[256,1024]{1,0:T(8,128)(2,1)}, u32[]{:S(2)}, u32[]{:S(2)}) collective-permute-start(bf16[256,1024]{1,0:T(8,128)(2,1)} %slice.462), channel_id=1, source_target_pairs={{0,8},{4,12},{8,0},{12,4},{16,24},{20,28},{24,16},{28,20},{1,9},{5... | collective-permute-start | bytes 1572872 | tf_op jit(solution)/shard_map/ppermute | solution.py:538
  505.7 22.7 %copy-start.40 = (bf16[512,1024]{1,0:T(8,128)(2,1)S(1)}, bf16[512,1024]{1,0:T(8,128)(2,1)}, u32[]{:S(2)}) copy-start(bf16[512,1024]{1,0:T(8,128)(2,1)} %add_convert_fusion.13) | copy-start | bytes 3145732
  524.2 33.2 %collective-permute-start.42 = (bf16[256,1024]{1,0:T(8,128)(2,1)S(1)}, bf16[256,1024]{1,0:T(8,128)(2,1)S(1)}, u32[]{:S(2)}, u32[]{:S(2)}) collective-permute-start(bf16[256,1024]{1,0:T(8,128)(2,1)S(1)} %slice.475), channel_id=1, source_target_pairs={{0,8},{4,12},{8,0},{12,4},{16,24},{20,28},{24,16},{28,20},{1,9},{5... | collective-permute-start | bytes 1572872 | tf_op jit(solution)/shard_map/ppermute | solution.py:538
  527.0 32.9 %collective-permute-start.40 = (bf16[256,1024]{1,0:T(8,128)(2,1)S(1)}, bf16[256,1024]{1,0:T(8,128)(2,1)S(1)}, u32[]{:S(2)}, u32[]{:S(2)}) collective-permute-start(bf16[256,1024]{1,0:T(8,128)(2,1)S(1)} %slice.467), channel_id=1, source_target_pairs={{0,16},{4,20},{8,24},{12,28},{16,0},{20,4},{24,8},{28,12},{1,17},{... | collective-permute-start | bytes 1572872 | tf_op jit(solution)/shard_map/ppermute | solution.py:538
  557.4 28.1 %collective-permute-start.35 = (bf16[256,1024]{1,0:T(8,128)(2,1)}, bf16[256,1024]{1,0:T(8,128)(2,1)}, u32[]{:S(2)}, u32[]{:S(2)}) collective-permute-start(bf16[256,1024]{1,0:T(8,128)(2,1)} %slice.456), channel_id=1, source_target_pairs={{0,16},{4,20},{8,24},{12,28},{16,0},{20,4},{24,8},{28,12},{1,17},{... | collective-permute-start | bytes 1572872 | tf_op jit(solution)/shard_map/ppermute | solution.py:538
  578.2 10.0 %collective-permute-start.23 = (bf16[1024,512]{0,1:T(8,128)(2,1)}, bf16[1024,512]{0,1:T(8,128)(2,1)}, u32[]{:S(2)}, u32[]{:S(2)}) collective-permute-start(bf16[1024,512]{0,1:T(8,128)(2,1)} %convolution_convert_fusion.5), channel_id=1, source_target_pairs={{0,4},{4,0},{8,12},{12,8},{16,20},{20,16},{24,28},{28,24},{1,5},{5... | collective-permute-start | bytes 3145736 | tf_op jit(solution)/shard_map/ppermute | solution.py:516
  583.8 22.2 %collective-permute-start.18 = (bf16[1024,1536]{1,0:T(8,128)(2,1)}, bf16[1024,1536]{1,0:T(8,128)(2,1)}, u32[]{:S(2)}, u32[]{:S(2)}) collective-permute-start(bf16[1024,1536]{1,0:T(8,128)(2,1)} %convolution_convert_fusion), channel_id=1, source_target_pairs={{0,4},{4,0},{8,12},{12,8},{16,20},{20,16},{24,28},{28,24},{1,5},{5... | collective-permute-start | bytes 9437192 | tf_op jit(solution)/shard_map/ppermute | solution.py:516
  591.6 8.7 %collective-permute-start.26 = (bf16[512,256]{0,1:T(8,128)(2,1)}, bf16[512,256]{0,1:T(8,128)(2,1)}, u32[]{:S(2)}, u32[]{:S(2)}) collective-permute-start(bf16[512,256]{0,1:T(8,128)(2,1)} %fusion.25), channel_id=1, source_target_pairs={{0,16},{4,20},{8,24},{12,28},{16,0},{20,4},{24,8},{28,12},{1,17},{... | collective-permute-start | bytes 786440 | tf_op jit(solution)/shard_map/ppermute | solution.py:538
  593.9 8.6 %collective-permute-start.24 = (bf16[512,256]{0,1:T(8,128)(2,1)}, bf16[512,256]{0,1:T(8,128)(2,1)}, u32[]{:S(2)}, u32[]{:S(2)}) collective-permute-start(bf16[512,256]{0,1:T(8,128)(2,1)} %fusion.20), channel_id=1, source_target_pairs={{0,8},{4,12},{8,0},{12,4},{16,24},{20,28},{24,16},{28,20},{1,9},{5... | collective-permute-start | bytes 786440 | tf_op jit(solution)/shard_map/ppermute | solution.py:538
  601.9 13.1 %collective-permute-start.27 = (bf16[256,256]{0,1:T(8,128)(2,1)S(1)}, bf16[256,256]{0,1:T(8,128)(2,1)S(1)}, u32[]{:S(2)}, u32[]{:S(2)}) collective-permute-start(bf16[256,256]{0,1:T(8,128)(2,1)S(1)} %slice.441), channel_id=1, source_target_pairs={{0,8},{4,12},{8,0},{12,4},{16,24},{20,28},{24,16},{28,20},{1,9},{5... | collective-permute-start | bytes 393224 | tf_op jit(solution)/shard_map/ppermute | solution.py:538
  604.5 27.1 %collective-permute-start.25 = (bf16[256,256]{0,1:T(8,128)(2,1)S(1)}, bf16[256,256]{0,1:T(8,128)(2,1)S(1)}, u32[]{:S(2)}, u32[]{:S(2)}) collective-permute-start(bf16[256,256]{0,1:T(8,128)(2,1)S(1)} %slice.432), channel_id=1, source_target_pairs={{0,16},{4,20},{8,24},{12,28},{16,0},{20,4},{24,8},{28,12},{1,17},{... | collective-permute-start | bytes 393224 | tf_op jit(solution)/shard_map/ppermute | solution.py:538
  608.4 18.2 %collective-permute-start.21 = (bf16[512,768]{1,0:T(8,128)(2,1)S(1)}, bf16[512,768]{1,0:T(8,128)(2,1)S(1)}, u32[]{:S(2)}, u32[]{:S(2)}) collective-permute-start(bf16[512,768]{1,0:T(8,128)(2,1)S(1)} %add_convert_fusion.21), channel_id=1, source_target_pairs={{0,16},{4,20},{8,24},{12,28},{16,0},{20,4},{24,8},{28,12},{1,17},{... | collective-permute-start | bytes 2359304 | tf_op jit(solution)/shard_map/ppermute | solution.py:538
  611.0 20.0 %collective-permute-start.19 = (bf16[512,768]{1,0:T(8,128)(2,1)S(1)}, bf16[512,768]{1,0:T(8,128)(2,1)S(1)}, u32[]{:S(2)}, u32[]{:S(2)}) collective-permute-start(bf16[512,768]{1,0:T(8,128)(2,1)S(1)} %add_convert_fusion.24), channel_id=1, source_target_pairs={{0,8},{4,12},{8,0},{12,4},{16,24},{20,28},{24,16},{28,20},{1,9},{5... | collective-permute-start | bytes 2359304 | tf_op jit(solution)/shard_map/ppermute | solution.py:538
  626.8 10.8 %collective-permute-start.22 = (bf16[256,768]{1,0:T(8,128)(2,1)S(1)}, bf16[256,768]{1,0:T(8,128)(2,1)S(1)}, u32[]{:S(2)}, u32[]{:S(2)}) collective-permute-start(bf16[256,768]{1,0:T(8,128)(2,1)S(1)} %slice.425), channel_id=1, source_target_pairs={{0,8},{4,12},{8,0},{12,4},{16,24},{20,28},{24,16},{28,20},{1,9},{5... | collective-permute-start | bytes 1179656 | tf_op jit(solution)/shard_map/ppermute | solution.py:538
  631.3 7.8 %collective-permute-start.20 = (bf16[256,768]{1,0:T(8,128)(2,1)S(1)}, bf16[256,768]{1,0:T(8,128)(2,1)S(1)}, u32[]{:S(2)}, u32[]{:S(2)}) collective-permute-start(bf16[256,768]{1,0:T(8,128)(2,1)S(1)} %slice.417), channel_id=1, source_target_pairs={{0,16},{4,20},{8,24},{12,28},{16,0},{20,4},{24,8},{28,12},{1,17},{... | collective-permute-start | bytes 1179656 | tf_op jit(solution)/shard_map/ppermute | solution.py:538
  (60 other events, 170.2 us)
Sparse Core Ops, SparseCore 0:
  10.2 83.4 all-gather.15
  130.3 52.4 all-gather.13
  237.1 50.8 reduce-scatter.5
  290.8 51.7 reduce-scatter.3
  346.7 68.2 all-gather.11
  444.6 65.4 all-gather.7
  513.0 50.8 reduce-scatter.7
  599.0 65.7 all-gather.9

commit v2 on v1

v2 whole, which is shorter than its diff:
```python
import functools
import math

import jax
import jax.numpy as jnp
import numpy as np
from jax import lax
from jax.experimental import pallas as pl
from jax.experimental.pallas import tpu as pltpu
from jax.sharding import PartitionSpec as P

HEAD = 128
BLOCK = 128
TRUNK_BLOCKS = 8
CHAIN = TRUNK_BLOCKS + 2
EPSILON = 1e-05
NEGATIVE = -1e30
SCALE = HEAD ** (-0.5)
LOW = jnp.bfloat16
F32 = jnp.float32
MIB = 1024 * 1024
PER_MICROSECOND = 100e9
NT = (((1,), (1,)), ((), ()))
TN = (((0,), (0,)), ((), ()))


def dot(a, b):
    return jnp.dot(a, b, preferred_element_type=F32)


def dot_nt(a, b):
    return lax.dot_general(a, b, NT, preferred_element_type=F32)


def dot_tn(a, b):
    return lax.dot_general(a, b, TN, preferred_element_type=F32)


def shape(dims, dtype):
    return jax.ShapeDtypeStruct(dims, dtype)


def about(microseconds):
    return pl.CostEstimate(
        flops=int(microseconds * PER_MICROSECOND), bytes_accessed=1, transcendentals=0
    )


def params(mib):
    return pltpu.CompilerParams(vmem_limit_bytes=mib * MIB)


def layer_norm(values):
    centered = values - jnp.mean(values, axis=-1, keepdims=True)
    variance = jnp.mean(centered * centered, axis=-1, keepdims=True)
    inverse = lax.rsqrt(variance + EPSILON)
    return (centered * inverse, inverse)


def norm_back(gradient, normed, inverse):
    return inverse * (
        gradient
        - jnp.mean(gradient, axis=-1, keepdims=True)
        - normed * jnp.mean(gradient * normed, axis=-1, keepdims=True)
    )


def rope_tables():
    frequency = np.exp(
        np.arange(HEAD // 2, dtype=np.float32) * np.float32(-2.0 * math.log(10000.0) / HEAD)
    ).astype(np.float32)
    angle = np.arange(CHAIN * BLOCK, dtype=np.float32)[:, None] * frequency[None, :]
    cosine, sine = np.cos(angle), np.sin(angle)
    return (
        np.concatenate([cosine, cosine], axis=1).astype(np.float32),
        np.concatenate([-sine, sine], axis=1).astype(np.float32),
    )


def depth_of(parent_ref, slot):
    def up(_, carry):
        at, depth = carry
        parent = jnp.where(at >= 0, parent_ref[jnp.maximum(at, 0)], -1)
        return parent, depth + jnp.where(parent >= 0, 1, 0).astype(jnp.int32)

    return lax.fori_loop(0, CHAIN - 1, up, (slot, jnp.int32(0)))[1]


def xor_pairs(count, mask):
    return [(index, index ^ mask) for index in range(count)]


class Plan:
    def __init__(self, mesh, rows, width, heads, ff):
        self.dp = mesh.shape["dp"]
        self.tensor = mesh.shape["tensor"]
        self.rows, self.width, self.heads, self.ff = rows, width, heads, ff
        self.slots = rows // BLOCK
        self.spread = heads
        self.rest = self.dp // heads
        self.bits = self.dp.bit_length() - 1
        self.piece = width // self.dp
        self.own = rows // self.tensor


def fetch(weights, held, sems, kind):
    copies = [
        pltpu.make_async_copy(w, held.at[index], sems.at[index]) for index, w in enumerate(weights)
    ]

    @pl.when(kind == 0)
    def _():
        for copy in copies:
            copy.start()

    def wait():
        for index, copy in enumerate(copies):

            @pl.when(kind == index)
            def _():
                copy.wait()

    return wait


def qkv_kernel(plan, parent, place, x, wq, wk, wv, cosine, sine, normed, *rest):
    outs, stage = rest[: plan.spread], rest[-1]
    me = place[0]
    part = me // plan.rest
    depth = depth_of(parent, me * plan.slots + pl.program_id(0))
    rows = pl.ds(pl.multiple_of(depth * BLOCK, BLOCK), BLOCK)
    cos, sin = cosine[rows, :], sine[rows, :]
    low = layer_norm(x[...].astype(F32))[0].astype(LOW)
    normed[...] = low
    for kind, w in enumerate((wq, wk, wv)):
        y = dot(low, w[...])
        for head in range(plan.heads):
            yh = y[:, head * HEAD : (head + 1) * HEAD]
            if kind < 2:
                yh = yh * cos + pltpu.roll(yh, HEAD // 2, 1) * sin
            stage[head, kind] = yh.astype(LOW)
    for d in range(plan.spread):
        outs[d][...] = stage[part ^ d]


def kept_order(plan):
    return [
        sum(((at >> bit) & 1) << (plan.bits - 1 - bit) for bit in range(plan.bits - 1))
        for at in range(plan.dp // 2)
    ]


def project_qkv(plan, slot_parent, place, tokens, wq, wk, wv, cosine, sine):
    whole = lambda i, *_: (0, 0)
    once = pl.Buffered(buffer_count=1)
    wide = plan.heads * HEAD
    return pl.pallas_call(
        functools.partial(qkv_kernel, plan),
        grid_spec=pltpu.PrefetchScalarGridSpec(
            num_scalar_prefetch=2,
            grid=(plan.slots,),
            in_specs=[pl.BlockSpec((BLOCK, plan.width), lambda i, *_: (i, 0))]
            + [pl.BlockSpec((plan.width, wide), whole, pipeline_mode=once)] * 3
            + [pl.BlockSpec((CHAIN * BLOCK, HEAD), whole, pipeline_mode=once)] * 2,
            out_specs=[pl.BlockSpec((BLOCK, plan.width), lambda i, *_: (i, 0))]
            + [pl.BlockSpec((3, BLOCK, HEAD), lambda i, *_: (0, i, 0))] * plan.spread,
            scratch_shapes=[
                pltpu.VMEM((plan.heads, 3, BLOCK, HEAD), LOW),
            ],
        ),
        out_shape=[shape((plan.rows, plan.width), LOW)]
        + [shape((3, plan.rows, HEAD), LOW)] * plan.spread,
        compiler_params=params(60),
        cost_estimate=about(0),
        name="project_qkv",
    )(slot_parent, place, tokens, wq, wk, wv, cosine, sine)


def gather_chain(plan, parent, me, slot, kv, keys, values):
    count = jnp.int32(0)
    at = slot
    places = []
    for step in range(CHAIN):
        here = jnp.maximum(at, 0)
        relative = (here // plan.slots) ^ me
        block = (
            (relative % plan.rest) * plan.spread + relative // plan.rest
        ) * 2 * plan.slots + here % plan.slots
        keys[step * BLOCK : (step + 1) * BLOCK, :] = kv[block]
        values[step * BLOCK : (step + 1) * BLOCK, :] = kv[block + plan.slots]
        places.append(block)
        valid = at >= 0
        count = count + jnp.where(valid, 1, 0).astype(jnp.int32)
        at = jnp.where(valid, parent[here], -1)
    return count, places


def chain_weights(queries, keys, counts):
    scores = [dot_nt(k, q) * SCALE for q, k in zip(queries, keys)]
    key_at = lax.broadcasted_iota(jnp.int32, scores[0].shape, 0)
    query_at = lax.broadcasted_iota(jnp.int32, scores[0].shape, 1)
    own = (key_at >= BLOCK) | (key_at <= query_at)
    probs = []
    for score, count in zip(scores, counts):
        score = jnp.where(own & (key_at < count * BLOCK), score, NEGATIVE)
        raised = jnp.exp(score - jnp.max(score, axis=0, keepdims=True))
        probs.append(raised * (1.0 / jnp.sum(raised, axis=0, keepdims=True)))
    return probs


def attend_kernel(plan, parent, place, *refs):
    n = plan.spread
    q_refs, kv, o_refs, keys, values = refs[:n], refs[n], refs[n + 1 : 2 * n + 1], refs[-2], refs[-1]
    me = place[0]

    def one(i, carry):
        rows = pl.ds(pl.multiple_of(i * BLOCK, BLOCK), BLOCK)
        slots = [(me ^ (d * plan.rest)) * plan.slots + i for d in range(n)]
        counts = [
            gather_chain(plan, parent, me, slots[d], kv, keys.at[d], values.at[d])[0]
            for d in range(n)
        ]
        queries = [q_refs[d][0, rows, :] for d in range(n)]
        probs = chain_weights(queries, [keys[d] for d in range(n)], counts)
        for d in range(n):
            o_refs[d][rows, :] = dot_tn(probs[d].astype(LOW), values[d]).astype(LOW)
        return carry

    lax.fori_loop(0, plan.slots, one, 0)


def attend(plan, slot_parent, place, parts, kv):
    n = plan.spread
    blocks = plan.dp * 2 * plan.slots
    return pl.pallas_call(
        functools.partial(attend_kernel, plan),
        grid_spec=pltpu.PrefetchScalarGridSpec(
            num_scalar_prefetch=2,
            grid=(1,),
            in_specs=[pl.BlockSpec((1, plan.rows, HEAD), lambda i, *_: (0, 0, 0))] * n
            + [pl.BlockSpec((blocks, BLOCK, HEAD), lambda i, *_: (0, 0, 0))],
            out_specs=[pl.BlockSpec((plan.rows, HEAD), lambda i, *_: (0, 0))] * n,
            scratch_shapes=[pltpu.VMEM((n, CHAIN * BLOCK, HEAD), LOW)] * 2,
        ),
        out_shape=[shape((plan.rows, HEAD), LOW)] * n,
        compiler_params=params(60),
        cost_estimate=about(0),
        name="attend",
    )(slot_parent, place, *parts, kv)


def attend_back_kernel(plan, parent, place, *refs):
    n = plan.spread
    q_refs, kv, g_refs = refs[:n], refs[n], refs[n + 1 : 2 * n + 1]
    dq_refs = refs[2 * n + 1 : 3 * n + 1]
    near, far, keys, values, total = refs[3 * n + 1 :]
    me = place[0]
    total[...] = jnp.zeros_like(total)

    def one(i, carry):
        rows = pl.ds(pl.multiple_of(i * BLOCK, BLOCK), BLOCK)
        slots = [(me ^ (d * plan.rest)) * plan.slots + i for d in range(n)]
        chains = [
            gather_chain(plan, parent, me, slots[d], kv, keys.at[d], values.at[d])
            for d in range(n)
        ]
        queries = [q_refs[d][0, rows, :] for d in range(n)]
        grads = [g_refs[d][rows, :] for d in range(n)]
        probs = chain_weights(queries, [keys[d] for d in range(n)], [chain[0] for chain in chains])
        for d in range(n):
            grad_prob = dot_nt(values[d], grads[d])
            inner = jnp.sum(grad_prob * probs[d], axis=0, keepdims=True)
            grad_scores = (probs[d] * (grad_prob - inner)).astype(LOW)
            dv = dot(probs[d].astype(LOW), grads[d])
            dk = dot(grad_scores, queries[d]) * SCALE
            dq_refs[d][rows, :] = (dot_tn(grad_scores, keys[d]) * SCALE).astype(LOW)
            for step, block in enumerate(chains[d][1]):
                span = slice(step * BLOCK, (step + 1) * BLOCK)
                total[block] = total[block] + dk[span]
                total[block + plan.slots] = total[block + plan.slots] + dv[span]
        return carry

    lax.fori_loop(0, plan.slots, one, 0)
    half = near.shape[0]
    near[...] = total[:half]
    far[...] = total[half:].astype(LOW)


def attend_back(plan, slot_parent, place, parts, kv, grads):
    n = plan.spread
    blocks = plan.dp * 2 * plan.slots
    near = n * 2 * plan.slots
    return pl.pallas_call(
        functools.partial(attend_back_kernel, plan),
        grid_spec=pltpu.PrefetchScalarGridSpec(
            num_scalar_prefetch=2,
            grid=(1,),
            in_specs=[pl.BlockSpec((1, plan.rows, HEAD), lambda i, *_: (0, 0, 0))] * n
            + [pl.BlockSpec((blocks, BLOCK, HEAD), lambda i, *_: (0, 0, 0))]
            + [pl.BlockSpec((plan.rows, HEAD), lambda i, *_: (0, 0))] * n,
            out_specs=[pl.BlockSpec((plan.rows, HEAD), lambda i, *_: (0, 0))] * n
            + [
                pl.BlockSpec((near, BLOCK, HEAD), lambda i, *_: (0, 0, 0)),
                pl.BlockSpec((blocks - near, BLOCK, HEAD), lambda i, *_: (0, 0, 0)),
            ],
            scratch_shapes=[pltpu.VMEM((n, CHAIN * BLOCK, HEAD), LOW)] * 2
            + [pltpu.VMEM((blocks, BLOCK, HEAD), F32)],
        ),
        out_shape=[shape((plan.rows, HEAD), LOW)] * n
        + [shape((near, BLOCK, HEAD), F32), shape((blocks - near, BLOCK, HEAD), LOW)],
        compiler_params=params(60),
        cost_estimate=about(23),
        name="attend_back",
    )(slot_parent, place, *parts, kv, *grads)


def heads_kernel(plan, place, *refs):
    part = place[0] // plan.rest
    out = refs[-1]
    for d in range(plan.spread):
        head = pl.ds(pl.multiple_of((part ^ d) * HEAD, HEAD), HEAD)
        out[:, head] = refs[d][...]


def gather_heads(plan, place, parts):
    return pl.pallas_call(
        functools.partial(heads_kernel, plan),
        grid_spec=pltpu.PrefetchScalarGridSpec(
            num_scalar_prefetch=1,
            grid=(1,),
            in_specs=[pl.BlockSpec((plan.rows, HEAD), lambda i, *_: (0, 0))] * plan.spread,
            out_specs=pl.BlockSpec((plan.rows, plan.heads * HEAD), lambda i, *_: (0, 0)),
        ),
        out_shape=shape((plan.rows, plan.heads * HEAD), LOW),
        name="gather_heads",
    )(place, *parts)


def scatter_kernel(plan, place, *refs):
    part, z = place[0] // plan.rest, place[1]
    sources, outs = refs[: plan.tensor], refs[plan.tensor :]
    for shift in range(plan.tensor):
        origin = lax.rem(z - shift + plan.tensor, plan.tensor)
        rows = pl.ds(pl.multiple_of(origin * plan.own, 16), plan.own)
        for d in range(plan.spread):
            head = pl.ds(pl.multiple_of((part ^ d) * HEAD, HEAD), HEAD)
            outs[d][rows, :] = sources[shift][:, head]


def scatter_heads(plan, place, sources):
    return pl.pallas_call(
        functools.partial(scatter_kernel, plan),
        grid_spec=pltpu.PrefetchScalarGridSpec(
            num_scalar_prefetch=1,
            grid=(1,),
            in_specs=[pl.BlockSpec((plan.own, plan.heads * HEAD), lambda i, *_: (0, 0))]
            * plan.tensor,
            out_specs=[pl.BlockSpec((plan.rows, HEAD), lambda i, *_: (0, 0))] * plan.spread,
        ),
        out_shape=[shape((plan.rows, HEAD), LOW)] * plan.spread,
        name="scatter_heads",
    )(place, *sources)


def turn_back_kernel(plan, parent, place, cosine, sine, wq, wk, wv, *refs):
    parts, refs = refs[: plan.spread], refs[plan.spread :]
    back, out, total, held, sems = refs
    me = place[0]
    part = me // plan.rest
    kind = pl.program_id(0)
    wait = fetch((wq, wk, wv), held, sems, kind)

    @pl.when(kind < 2)
    def _():
        for slot in range(plan.slots):
            depth = depth_of(parent, me * plan.slots + slot)
            table = pl.ds(pl.multiple_of(depth * BLOCK, BLOCK), BLOCK)
            cos, sin = cosine[table, :], sine[table, :]
            rows = slice(slot * BLOCK, (slot + 1) * BLOCK)
            for d in range(plan.spread):
                value = parts[d][0, rows, :].astype(F32)
                value = value * cos - pltpu.roll(value, HEAD // 2, 1) * sin
                columns = pl.ds(pl.multiple_of((part ^ d) * HEAD, HEAD), HEAD)
                out[rows, columns] = value.astype(LOW)

    @pl.when(kind == 2)
    def _():
        for d in range(plan.spread):
            columns = pl.ds(pl.multiple_of((part ^ d) * HEAD, HEAD), HEAD)
            out[:, columns] = parts[d][0]

    wait()
    product = dot_nt(out[...], held[kind])

    @pl.when(kind == 0)
    def _():
        total[...] = product

    @pl.when(kind == 1)
    def _():
        total[...] += product

    @pl.when(kind == 2)
    def _():
        back[...] = (total[...] + product).astype(LOW)


def turn_back(plan, slot_parent, place, cosine, sine, weights, parts):
    whole = lambda i, *_: (0, 0)
    wide = plan.heads * HEAD
    return pl.pallas_call(
        functools.partial(turn_back_kernel, plan),
        grid_spec=pltpu.PrefetchScalarGridSpec(
            num_scalar_prefetch=2,
            grid=(3,),
            in_specs=[pl.BlockSpec((CHAIN * BLOCK, HEAD), whole)] * 2
            + [pl.BlockSpec(memory_space=pl.ANY)] * 3
            + [pl.BlockSpec((1, plan.rows, HEAD), lambda i, *_: (i, 0, 0))] * plan.spread,
            out_specs=[
                pl.BlockSpec((plan.rows, plan.width), whole),
                pl.BlockSpec((plan.rows, wide), lambda i, *_: (0, i)),
            ],
            scratch_shapes=[
                pltpu.VMEM((plan.rows, plan.width), F32),
                pltpu.VMEM((3, plan.width, wide), LOW),
                pltpu.SemaphoreType.DMA((3,)),
            ],
        ),
        out_shape=[shape((plan.rows, plan.width), LOW), shape((plan.rows, 3 * wide), LOW)],
        compiler_params=params(60),
        cost_estimate=about(13),
        name="turn_back",
    )(slot_parent, place, cosine, sine, *weights, *parts)


def out_kernel(plan, place, x, att, near, far, middle, normed):
    half = plan.heads * HEAD // 2
    core = place[0] % 2
    total = x[...].astype(F32)
    for z in range(plan.tensor):
        for side, w in ((core, near), (1 - core, far)):
            columns = pl.ds(pl.multiple_of(side * half, half), half)
            total = total + dot(att[z, :, columns], w[z])
    middle[...] = total
    normed[...] = layer_norm(total)[0].astype(LOW)


def project_out(plan, place, tokens, att, near, far):
    half = plan.heads * HEAD // 2
    weights = pl.BlockSpec(
        (plan.tensor, half, plan.width),
        lambda i, *_: (0, 0, 0),
        pipeline_mode=pl.Buffered(buffer_count=1),
    )
    rows = pl.BlockSpec((BLOCK, plan.width), lambda i, *_: (i, 0))
    return pl.pallas_call(
        functools.partial(out_kernel, plan),
        grid_spec=pltpu.PrefetchScalarGridSpec(
            num_scalar_prefetch=1,
            grid=(plan.slots,),
            in_specs=[
                rows,
                pl.BlockSpec((plan.tensor, BLOCK, 2 * half), lambda i, *_: (0, i, 0)),
                weights,
                weights,
            ],
            out_specs=[rows, rows],
        ),
        out_shape=[shape((plan.rows, plan.width), F32), shape((plan.rows, plan.width), LOW)],
        compiler_params=params(40),
        cost_estimate=about(13),
        name="project_out",
    )(place, tokens, att, near, far)


def grad_hidden_kernel(cot, wd, out):
    out[...] = dot_nt(cot[...], wd[...])


def grad_hidden_of(cot, wd, part):
    rows, width = cot.shape
    ff = wd.shape[0] // 2
    tile = min(512, ff)
    return pl.pallas_call(
        grad_hidden_kernel,
        grid=(ff // tile,),
        in_specs=[
            pl.BlockSpec((rows, width), lambda i: (0, 0)),
            pl.BlockSpec((tile, width), lambda i: (part * (ff // tile) + i, 0)),
        ],
        out_specs=pl.BlockSpec((rows, tile), lambda i: (0, i)),
        out_shape=shape((rows, ff), F32),
        compiler_params=params(60),
        cost_estimate=about(0),
        name="grad_hidden",
    )(cot, wd)


def ff_kernel(plan, place, normed, seed, late_seed, wg, wu, *refs):
    back, hidden, grad_gate, grad_up, total = refs
    step = pl.program_id(0)
    gate = dot(normed[...], wg[...])
    up = dot(normed[...], wu[...])
    grad_hidden = jnp.where(step < pl.num_programs(0) // 2, seed[...], late_seed[...])
    s = 1.0 / (1.0 + jnp.exp(-gate))
    active = gate * s
    hidden[...] = (active * up).astype(LOW)
    gu = (grad_hidden * active).astype(LOW)
    gg = (grad_hidden * up * s * (1.0 + gate * (1.0 - s))).astype(LOW)
    grad_up[...] = gu
    grad_gate[...] = gg
    part = dot_nt(gg, wg[...]) + dot_nt(gu, wu[...])

    @pl.when(step == 0)
    def _():
        total[...] = part

    @pl.when(step > 0)
    def _():
        total[...] += part

    @pl.when(step == pl.num_programs(0) - 1)
    def _():
        back[...] = total[...].astype(LOW)


def feed_forward(plan, place, normed, seeds, wg, wu):
    rows, width = normed.shape
    ff = wg.shape[1]
    tile = min(512, ff)
    whole = pl.BlockSpec(
        (rows, width), lambda i, *_: (0, 0), pipeline_mode=pl.Buffered(buffer_count=1)
    )
    count = ff // tile
    across = pl.BlockSpec((width, tile), lambda i, *_: (0, i))
    out = pl.BlockSpec((rows, tile), lambda i, *_: (0, i))
    back = pl.BlockSpec((rows, width), lambda i, *_: (0, 0))
    return pl.pallas_call(
        functools.partial(ff_kernel, plan),
        grid_spec=pltpu.PrefetchScalarGridSpec(
            num_scalar_prefetch=1,
            grid=(ff // tile,),
            in_specs=[
                whole,
                pl.BlockSpec((rows, tile), lambda i, *_: (0, jnp.minimum(i, count // 2 - 1))),
                pl.BlockSpec((rows, tile), lambda i, *_: (0, jnp.maximum(i - count // 2, 0))),
                across,
                across,
            ],
            out_specs=[back, out, out, out],
            scratch_shapes=[pltpu.VMEM((rows, width), F32)],
        ),
        out_shape=[shape((rows, width), LOW)] + [shape((rows, ff), LOW)] * 3,
        compiler_params=params(62),
        cost_estimate=about(32),
        name="feed_forward",
    )(place, normed, *seeds, wg, wu)


def down_kernel(hidden, w, out):
    out[...] = dot(hidden[...], w[...]).astype(LOW)


def project_down(hidden, w):
    rows, ff = hidden.shape
    width = w.shape[1]
    tile = min(512, width)
    return pl.pallas_call(
        down_kernel,
        grid=(width // tile,),
        in_specs=[
            pl.BlockSpec((rows, ff), lambda i: (0, 0)),
            pl.BlockSpec((ff, tile), lambda i: (0, i)),
        ],
        out_specs=pl.BlockSpec((rows, tile), lambda i: (0, i)),
        out_shape=shape((rows, width), LOW),
        compiler_params=params(60),
        cost_estimate=about(11),
        name="project_down",
    )(hidden, w)


def branch_back_kernel(plan, place, part, middle, cot, near, far, grad_middle, low, *refs):
    outs, held = refs[:-1], refs[-1]
    step = pl.program_id(0)

    @pl.when(step == 0)
    def _():
        normed, inverse = layer_norm(middle[...])
        grad = cot[...].astype(F32) + norm_back(part[...].astype(F32), normed, inverse)
        grad_middle[...] = grad
        held[...] = grad.astype(LOW)
        low[...] = held[...]

    core = place[0] % 2
    half = near.shape[1]
    for side, w in ((core, near), (1 - core, far)):
        columns = pl.ds(pl.multiple_of(side * half, half), half)
        product = dot_nt(held[...], w[0]).astype(LOW)
        for shift in range(plan.tensor):

            @pl.when(step == shift)
            def _():
                outs[shift][:, columns] = product


def branch_back(plan, place, part, middle, cot, near, far):
    half = plan.heads * HEAD // 2
    own = pl.BlockSpec((plan.own, plan.width), lambda i, place: (place[1], 0))
    mine = pl.BlockSpec((plan.own, plan.width), lambda i, *_: (0, 0))
    weights = pl.BlockSpec(
        (1, half, plan.width), lambda i, place: (lax.rem(place[1] + i, plan.tensor), 0, 0)
    )
    return pl.pallas_call(
        functools.partial(branch_back_kernel, plan),
        grid_spec=pltpu.PrefetchScalarGridSpec(
            num_scalar_prefetch=1,
            grid=(plan.tensor,),
            in_specs=[mine, own, own, weights, weights],
            out_specs=[mine, mine]
            + [pl.BlockSpec((plan.own, 2 * half), lambda i, *_: (0, 0))] * plan.tensor,
            scratch_shapes=[pltpu.VMEM((plan.own, plan.width), LOW)],
        ),
        out_shape=[shape((plan.own, plan.width), F32), shape((plan.own, plan.width), LOW)]
        + [shape((plan.own, 2 * half), LOW)] * plan.tensor,
        compiler_params=params(60),
        cost_estimate=about(9),
        name="branch_back",
    )(place, part, middle, cot, near, far)


def tokens_back_kernel(place, part, tokens, grad_middle, out):
    normed, inverse = layer_norm(tokens[...].astype(F32))
    back = norm_back(part[...].astype(F32), normed, inverse)
    out[...] = (grad_middle[...] + back).astype(LOW)


def tokens_back(plan, place, part, tokens, grad_middle):
    mine = pl.BlockSpec((plan.own, plan.width), lambda i, *_: (0, 0))
    return pl.pallas_call(
        tokens_back_kernel,
        grid_spec=pltpu.PrefetchScalarGridSpec(
            num_scalar_prefetch=1,
            grid=(1,),
            in_specs=[
                mine,
                pl.BlockSpec((plan.own, plan.width), lambda i, place: (place[1], 0)),
                mine,
            ],
            out_specs=mine,
        ),
        out_shape=shape((plan.own, plan.width), LOW),
        compiler_params=params(60),
        cost_estimate=about(4),
        name="tokens_back",
    )(place, part, tokens, grad_middle)


def joined_rows(plan, place, parts, held):
    if len(parts) == 1:
        return parts[0][...]
    for shift, part in enumerate(parts):
        origin = lax.rem(place[1] - shift + plan.tensor, plan.tensor)
        held[pl.ds(pl.multiple_of(origin * plan.own, 16), plan.own), :] = part[...]
    return held[...]


def away_kernel(plan, count, place, *refs):
    lhs, (rhs, out, held) = refs[:count], refs[count:]
    out[...] = dot_tn(joined_rows(plan, place, lhs, held), rhs[...]).astype(LOW)


def wgrad_away(plan, place, lhs, rhs):
    rows, columns = rhs.shape
    piece, count = plan.piece, plan.dp // 2
    return pl.pallas_call(
        functools.partial(away_kernel, plan, len(lhs)),
        grid_spec=pltpu.PrefetchScalarGridSpec(
            num_scalar_prefetch=1,
            grid=(count,),
            in_specs=[
                pl.BlockSpec((part.shape[0], piece), lambda i, place: (0, place[2 + i] ^ 1))
                for part in lhs
            ]
            + [pl.BlockSpec((rows, columns), lambda i, *_: (0, 0))],
            out_specs=pl.BlockSpec((piece, columns), lambda i, *_: (i, 0)),
            scratch_shapes=[pltpu.VMEM((rows, piece), LOW)],
        ),
        out_shape=shape((count * piece, columns), LOW),
        compiler_params=params(60),
        cost_estimate=about(8),
        name="wgrad_away",
    )(place, *lhs, rhs)


def keep_kernel(plan, arrays, count, place, *refs):
    lhs, (rhs, recv, a_keep, a_send, b_keep, b_send, held) = refs[:arrays], refs[arrays:]
    step = pl.program_id(0)
    product = dot_tn(joined_rows(plan, place, lhs, held), rhs[...])
    total = (product + recv[...].astype(F32)).astype(LOW)
    half = total.shape[1] // 2

    @pl.when(step < count // 2)
    def _():
        a_keep[...] = total[:, :half]

    @pl.when(step >= count // 2)
    def _():
        a_send[...] = total[:, :half]

    @pl.when(step % 2 == 0)
    def _():
        b_keep[...] = total[:, half:]

    @pl.when(step % 2 == 1)
    def _():
        b_send[...] = total[:, half:]


def wgrad_keep(plan, place, lhs, rhs, recv):
    rows, columns = rhs.shape
    piece, count = plan.piece, plan.dp // 2
    half = count // 2
    block = lambda index: pl.BlockSpec((piece, columns // 2), index)
    return pl.pallas_call(
        functools.partial(keep_kernel, plan, len(lhs), count),
        grid_spec=pltpu.PrefetchScalarGridSpec(
            num_scalar_prefetch=1,
            grid=(count,),
            in_specs=[
                pl.BlockSpec((part.shape[0], piece), lambda i, place: (0, place[2 + i]))
                for part in lhs
            ]
            + [
                pl.BlockSpec((rows, columns), lambda i, *_: (0, 0)),
                pl.BlockSpec((piece, columns), lambda i, *_: (i, 0)),
            ],
            out_specs=[
                block(lambda i, *_: (jnp.minimum(i, half - 1), 0)),
                block(lambda i, *_: (jnp.maximum(i - half, 0), 0)),
                block(lambda i, *_: (i // 2, 0)),
                block(lambda i, *_: (i // 2, 0)),
            ],
            scratch_shapes=[pltpu.VMEM((rows, piece), LOW)],
        ),
        out_shape=[shape((half * piece, columns // 2), LOW)] * 4,
        compiler_params=params(60),
        cost_estimate=about(9),
        name="wgrad_keep",
    )(place, *lhs, rhs, recv)


def stage_kernel(piece, a, a_got, b, b_got, a_keep, a_send, b_keep, b_send):
    total = a[...].astype(F32) + a_got[...].astype(F32)
    half = total.shape[0] // 2
    a_keep[...] = total[:half].astype(LOW)
    a_send[...] = total[half:].astype(LOW)
    for at in range(0, 2 * half, 2 * piece):
        for start, out in ((at, b_keep), (at + piece, b_send)):
            rows = slice(start, start + piece)
            total = b[rows, :].astype(F32) + b_got[rows, :].astype(F32)
            out[at // 2 : at // 2 + piece, :] = total.astype(LOW)


def wgrad_stage(piece, *arrays):
    rows, columns = arrays[0].shape
    tile = min(256, columns)
    block = lambda size: pl.BlockSpec((size, tile), lambda i: (0, i))
    return pl.pallas_call(
        functools.partial(stage_kernel, piece),
        grid=(columns // tile,),
        in_specs=[block(rows)] * 4,
        out_specs=[block(rows // 2)] * 4,
        out_shape=[shape((rows // 2, columns), LOW)] * 4,
        compiler_params=params(60),
        cost_estimate=about(3),
        name="wgrad_stage",
    )(*arrays)


def finish_kernel(turned, a, a_got, b, b_got, out):
    half = a.shape[1]
    for way, (keep, got) in enumerate(((a, a_got), (b, b_got))):
        total = keep[...].astype(F32) + got[...].astype(F32)
        span = slice(way * half, (way + 1) * half)
        if turned:
            out[span, :] = total.T
        else:
            out[:, span] = total


def wgrad_finish(turned, *arrays):
    piece, half = arrays[0].shape
    return pl.pallas_call(
        functools.partial(finish_kernel, turned),
        out_shape=shape((2 * half, piece) if turned else (piece, 2 * half), F32),
        compiler_params=params(60),
        cost_estimate=about(3),
        name="wgrad_finish",
    )(*arrays)


def tie(values, *others):
    many = isinstance(values, (list, tuple))
    held = lax.optimization_barrier((tuple(values) if many else (values,)) + others)
    return list(held[: len(values)]) if many else held[0]


class WeightGradient:
    def __init__(self, plan, place, chain, lhs, rhs, turned=False):
        self.plan, self.place, self.chain = plan, place, chain
        self.lhs, self.rhs, self.turned = lhs, rhs, turned
        self.stage = 0

    def swap(self, array, bit):
        return lax.ppermute(array, "dp", xor_pairs(self.plan.dp, 1 << bit))

    def away(self):
        sent = self.chain.run(lambda r: wgrad_away(self.plan, self.place, self.lhs, r), self.rhs)
        self.recv = self.swap(sent, 0)

    def keep(self):
        self.a_keep, self.a_send, self.b_keep, self.b_send = self.chain.run(
            lambda r: wgrad_keep(self.plan, self.place, self.lhs, self.rhs, r), self.recv
        )

    def send(self):
        upwards = list(range(1, self.plan.bits))
        a, b = self.chain.after(self.a_send, self.b_send)
        self.a_got = self.swap(a, upwards[self.stage])
        self.b_got = self.swap(b, upwards[-1 - self.stage])
        self.stage += 1

    def wait(self):
        self.a_got, self.b_got = self.chain.wait(self.a_got, self.b_got)

    def add(self):
        self.a_keep, self.a_send, self.b_keep, self.b_send = self.chain.run(
            lambda *p: wgrad_stage(self.plan.piece, *p),
            self.a_keep,
            self.a_got,
            self.b_keep,
            self.b_got,
        )

    def finish(self):
        while self.stage < self.plan.bits - 1:
            self.add()
            self.send()
        return self.chain.run(
            lambda *p: wgrad_finish(self.turned, *p),
            self.a_keep,
            self.a_got,
            self.b_keep,
            self.b_got,
        )


class Chain:
    def __init__(self, last):
        self.last = last

    def after(self, *values):
        held = lax.optimization_barrier(values + (self.last,))
        return held[0] if len(values) == 1 else list(held[:-1])

    def wait(self, *values):
        held = lax.optimization_barrier(values + (self.last,))
        self.last = held[0]
        return held[0] if len(values) == 1 else list(held[:-1])

    def run(self, step, *values):
        held = self.after(*values)
        out = step(*held) if len(values) > 1 else step(held)
        self.last = out[0] if isinstance(out, (list, tuple)) else out
        return out


def add_kernel(middle, part, out):
    out[...] = (middle[...] + part[...].astype(F32)).astype(LOW)


def add_residual(middle, part):
    rows, width = middle.shape
    block = pl.BlockSpec((rows // 4, width), lambda i: (i, 0))
    return pl.pallas_call(
        add_kernel,
        grid=(4,),
        in_specs=[block, block],
        out_specs=block,
        out_shape=shape((rows, width), LOW),
        compiler_params=params(60),
        cost_estimate=about(6),
        name="add_residual",
    )(middle, part)


def body(mesh, tokens, w_query, w_key, w_value, w_out, w_gate, w_up, w_down, cotangent, slot_parent):
    plan = Plan(mesh, tokens.shape[0], tokens.shape[1], w_query.shape[1] // HEAD, w_gate.shape[1])
    me = lax.axis_index("dp")
    z = lax.axis_index("tensor")
    place = jnp.stack([me, z] + [me ^ relative for relative in kept_order(plan)]).astype(jnp.int32)
    cosine, sine = (jnp.asarray(table) for table in rope_tables())
    n = plan.spread
    wide = n * HEAD

    def swap(array, mask):
        return lax.ppermute(array, "dp", xor_pairs(plan.dp, mask))

    def exchange(parts):
        return [parts[0]] + [swap(parts[d], d * plan.rest) for d in range(1, n)]

    def shifted(array, shift):
        return lax.ppermute(
            array, "tensor", [(i, (i + shift) % plan.tensor) for i in range(plan.tensor)]
        )

    half = w_out.shape[0] // 2
    mine = lax.dynamic_slice_in_dim(w_out, (me % 2) * half, half, 0)
    near = lax.all_gather(mine, "tensor", axis=0, tiled=False)

    normed_one, *sends = project_qkv(
        plan, slot_parent, place, tokens, w_query, w_key, w_value, cosine, sine
    )
    chain = Chain(normed_one)
    parts = exchange(sends)
    seeds = [chain.run(lambda cot: grad_hidden_of(cot, w_down, 0), cotangent)]
    parts = chain.wait(*parts)
    kv = jnp.stack([part[1:] for part in parts])[None]
    mask = 1
    while mask < plan.rest:
        kv = jnp.concatenate([kv, swap(kv, mask)], axis=0)
        mask *= 2
    seeds.append(chain.run(lambda cot: grad_hidden_of(cot, w_down, 1), cotangent))
    kv = chain.wait(kv.reshape(plan.dp * 2 * plan.slots, BLOCK, HEAD))
    attended_parts = exchange(chain.run(lambda *p: attend(plan, slot_parent, place, p, kv), *parts))
    attended = chain.run(lambda *p: gather_heads(plan, place, p), *attended_parts)
    everyone = lax.all_gather(tie(attended, near), "tensor", axis=0, tiled=False)
    near = chain.after(near)
    far = swap(near, 1)
    middle, normed_two = chain.run(
        lambda e, f: project_out(plan, place, tokens, e, near, f), everyone, far
    )

    partial_two, hidden, grad_gate_proj, grad_up_proj = chain.run(
        lambda v: feed_forward(plan, place, v, seeds, w_gate, w_up), normed_two
    )
    grad_normed_two = lax.psum_scatter(partial_two, "tensor", scatter_dimension=0, tiled=True)
    down = WeightGradient(plan, place, chain, [cotangent], hidden, turned=True)
    gate = WeightGradient(plan, place, chain, [normed_two], grad_gate_proj)
    up = WeightGradient(plan, place, chain, [normed_two], grad_up_proj)
    down.away()
    gate.away()
    down.keep()
    down.send()
    gate.keep()
    gate.send()
    up.away()
    mine_all = lax.dynamic_slice_in_dim(chain.after(everyone), z * plan.own, plan.own, 1)
    mine_all = mine_all.transpose(1, 0, 2).reshape(plan.own, plan.width)
    down.wait()

    grad_middle, grad_branch, *chunks = chain.run(
        lambda g: branch_back(plan, place, g, middle, cotangent, near, far), grad_normed_two
    )
    sources = [chunks[0]] + [shifted(chunks[shift], shift) for shift in range(1, plan.tensor)]
    branch_out = chain.run(lambda h: project_down(h, w_down), hidden)
    gate.wait()
    scattered = chain.run(lambda *p: scatter_heads(plan, place, p), *sources)
    grads = exchange(scattered)
    output_part = lax.psum(chain.after(branch_out), "tensor")
    out = WeightGradient(plan, place, chain, [grad_branch], mine_all, turned=True)
    out.away()
    down.add()
    out.keep()
    grads = chain.wait(*grads)
    out.send()
    *grad_queries, grad_near, grad_far = chain.run(
        lambda *g: attend_back(plan, slot_parent, place, parts, kv, g), *grads
    )
    out.wait()

    grad_far = chain.after(grad_far).reshape(plan.rest - 1, n, 2, plan.rows, HEAD)
    grad_near = grad_near.reshape(1, n, 2, plan.rows, HEAD)
    mask = plan.rest // 2
    while mask >= 1:
        got = swap(grad_far[mask - 1 : 2 * mask - 1], mask)
        if mask == 1:
            out.add()
            got = chain.wait(got)
        got = got.astype(F32)
        grad_near = grad_near + got[:1]
        if mask > 1:
            grad_far = (grad_far[: mask - 1].astype(F32) + got[1:]).astype(LOW)
        mask //= 2
    backs = chain.wait(
        *(
            jnp.concatenate([grad_queries[d][None], grad_near[0, d].astype(LOW)], axis=0)
            for d in range(n)
        )
    )
    backs = exchange(backs)
    up.keep()
    gate.add()
    partial_one, turned = chain.run(
        lambda *p: turn_back(
            plan, slot_parent, place, cosine, sine, (w_query, w_key, w_value), p
        ),
        *backs,
    )
    grad_normed_one = lax.psum_scatter(partial_one, "tensor", scatter_dimension=0, tiled=True)
    out.send()
    qkv = WeightGradient(plan, place, chain, [normed_one], turned)
    qkv.away()
    output = chain.run(lambda p: add_residual(middle, p), output_part)
    out.wait()
    out_partial = out.finish().astype(LOW)
    down.send()
    up.send()
    qkv.keep()
    grad_tokens_own = chain.run(
        lambda g: tokens_back(plan, place, g, tokens, grad_middle), grad_normed_one
    )
    grad_tokens = lax.all_gather(grad_tokens_own, "tensor", axis=0, tiled=True)
    down.wait()
    gate.send()
    up.wait()
    up.add()
    up.send()
    grad_down = down.finish()
    gate.wait()
    qkv.send()
    grad_gate = gate.finish()
    up.wait()
    grad_up = up.finish()
    qkv.wait()
    qkv.add()
    qkv.send()
    grad_qkv = qkv.finish()
    grad_out = lax.psum_scatter(
        tie(out_partial, grad_tokens), "tensor", scatter_dimension=0, tiled=True
    ).astype(F32)
    return (
        output,
        grad_tokens,
        grad_qkv[:, :wide],
        grad_qkv[:, wide : 2 * wide],
        grad_qkv[:, 2 * wide :],
        grad_out,
        grad_gate,
        grad_up,
        grad_down,
    )


def solution(mesh):
    in_specs = (
        P("dp", None),
        P(None, "tensor"),
        P(None, "tensor"),
        P(None, "tensor"),
        P("tensor", None),
        P(None, "tensor"),
        P(None, "tensor"),
        P("tensor", None),
        P("dp", None),
        P(),
    )
    out_specs = (
        P("dp", None),
        P("dp", None),
        P("dp", "tensor"),
        P("dp", "tensor"),
        P("dp", "tensor"),
        P("tensor", "dp"),
        P("dp", "tensor"),
        P("dp", "tensor"),
        P("tensor", "dp"),
    )
    return jax.shard_map(
        functools.partial(body, mesh),
        mesh=mesh,
        in_specs=in_specs,
        out_specs=out_specs,
        check_vma=False,
    )
```

time: 684 us -> 545 us (0.80)
  Pallas kernels: 138 us -> 270 us
  matrix products: 108 us -> 0 us
  waiting for transfers between devices: 286 us -> 184 us
  other arithmetic: 41.7 us -> 9.63 us
  local copies, waits for them, and re-layouts: 40.8 us -> 17.8 us
    pallas_call x4 -> x27, Pallas kernels: 56.5 us -> 193 us  [the longest x5 43.8 us: wgrad_keep(): pl.pallas_call(functools.partial(keep_kernel, plan, len(lhs), count), gri...]
    dot_general x31 -> x0, matrix products: 108 us -> none  [the longest x25 84.6 us: dot_tn(): return lax.dot_general(a, b, TN, preferred_element_type=F32)]
    ppermute x28, waiting for transfers between devices: 83.4 us -> 47 us  [the longest x25 47 us: swap(): return lax.ppermute(array, 'dp', xor_pairs(self.plan.dp, 1 << bit))]
    all_gather x1, waiting for transfers between devices: 38.8 us -> 8.55 us  [body(): near = lax.all_gather(mine, 'tensor', axis=0, tiled=False)]
    all_gather x1, waiting for transfers between devices: 24.4 us -> 0.01 us  [body(): grad_tokens = lax.all_gather(grad_tokens_own, 'tensor', axis=0, tiled=True)]
    reduce_scatter x1, waiting for transfers between devices: 0.01 us -> 21.1 us  [body(): lax.psum_scatter(partial_one, 'tensor', scatter_dimension=0, tiled=True)]
    reduce_scatter x1, waiting for transfers between devices: 39.3 us -> 21.4 us  [body(): lax.psum_scatter(tie(out_partial, grad_tokens), 'tensor', scatter_dimensi...]
    ppermute x15, waiting for transfers between devices: 47.6 us -> 31.3 us  [swap(): return lax.ppermute(array, 'dp', xor_pairs(plan.dp, mask))]
  transfers between devices with their start and end apart: 51 -> 50, of which waited for: 25 -> 24; matrix products, arithmetic and copies ran while one was open for 25% -> 2% of each run, Pallas kernels for 13% -> 42%
where the time goes in v2:
time: 545 us; the launch traced here: 538 us
  Pallas kernels  270 us (50%)
  waiting for transfers between devices  184 us (34%)
  starting transfers between devices  41.6 us (8%)
  local copies, waits for them, and re-layouts  17.8 us (3%)
  between operations  14.7 us (3%)
  other arithmetic  9.63 us (2%)
    all_gather x1, waiting for transfers between devices, body(): lax.all_gather(tie(attended, near), 'tensor', axis=0, tiled=False)  54.9 us
    ppermute x25, waiting for transfers between devices, swap(): return lax.ppermute(array, 'dp', xor_pairs(self.plan.dp, 1 << bit))  47 us
    pallas_call x5, Pallas kernels, wgrad_keep(): pl.pallas_call(functools.partial(keep_kernel, plan, len(lhs), count), gri...  43.8 us
    pallas_call x5, Pallas kernels, wgrad_away(): pl.pallas_call(functools.partial(away_kernel, plan, len(lhs)), grid_spec=...  36.2 us
    pallas_call x1, Pallas kernels, feed_forward(): pl.pallas_call(functools.partial(ff_kernel, plan), grid_spec=pltpu.Prefet...  32.1 us
    ppermute x15, waiting for transfers between devices, swap(): return lax.ppermute(array, 'dp', xor_pairs(plan.dp, mask))  31.3 us
    pallas_call x1, Pallas kernels, attend_back(): pl.pallas_call(functools.partial(attend_back_kernel, plan), grid_spec=plt...  23.1 us
    reduce_scatter x1, waiting for transfers between devices, body(): lax.psum_scatter(tie(out_partial, grad_tokens), 'tensor', scatter_dimensi...  21.4 us
  transfers between devices with their start and end apart: 50, of which 24 were waited for; matrix products, arithmetic and copies ran while one was open for 2% of the time, Pallas kernels for 42%

profile of v2, /device:TPU:0, one launch (start us, length us, event | category | flops | bytes accessed | tf_op | source)
XLA Modules:
  0.0 537.6 jit_solution(9460629745433203538)
XLA Ops:
  7.2 2.3 constant_dynamic-slice_fusion
  10.3 11.8 %project_qkv.1 = (bf16[640,2048]{1,0:T(8,128)(2,1)}, bf16[3,640,128]{2,1,0:T(8,128)(2,1)}, bf16[3,640,128]{2,1,0:T(8,128)(2,1)}, bf16[3,640,128]{2,1,0:T(8,128)(2,1)}, bf16[3,640,128]{2,1,0:T(8,128)(2,1)}) custom-call(s32[40]{0:T(128)} %parent.7, s32[6]{0:T(128)} %stack.39.place, bf16[640,2048]{1,0:T(8,128)(2,1)} %tokens.1, bf16[2048,512]{1,0:T(8,128)(2,1)} %wq.3, ...), custom_call_target="tpu_custom_call" | custom-call | bytes 1 | tf_op jit(solution)/shard_map/project_qkv/pallas_call | solution.py:157
  22.1 2.9 collective-permute-start
  25.0 1.5 collective-permute-start.1
  26.5 6.7 %grad_hidden.2.seed = f32[640,1024]{1,0:T(8,128)} custom-call(bf16[640,2048]{1,0:T(8,128)(2,1)} %cot.3, bf16[2048,2048]{1,0:T(8,128)(2,1)} %w.1), custom_call_target="tpu_custom_call" | custom-call | bytes 1 | tf_op jit(solution)/shard_map/grad_hidden/pallas_call | solution.py:484
  33.2 4.0 collective-permute-done.refs_1_
  37.3 11.2 %collective-permute-done.1.refs_2_ = bf16[3,640,128]{2,1,0:T(8,128)(2,1)S(1)} collective-permute-done((bf16[3,640,128]{2,1,0:T(8,128)(2,1)}, bf16[3,640,128]{2,1,0:T(8,128)(2,1)S(1)}, u32[]{:S(2)}, u32[]{:S(2)}) %collective-permute-start.1) | collective-permute-done | bytes 491552 | tf_op jit(solution)/shard_map/ppermute | solution.py:908
  49.6 6.7 %grad_hidden.3.late_seed = f32[640,1024]{1,0:T(8,128)} custom-call(bf16[640,2048]{1,0:T(8,128)(2,1)} %cot.3, bf16[2048,2048]{1,0:T(8,128)(2,1)} %w.1), custom_call_target="tpu_custom_call" | custom-call | bytes 1 | tf_op jit(solution)/shard_map/grad_hidden/pallas_call | solution.py:484
  56.3 1.7 pad_maximum_fusion
  58.0 12.4 %attend.1 = (bf16[640,128]{1,0:T(8,128)(2,1)}, bf16[640,128]{1,0:T(8,128)(2,1)}, bf16[640,128]{1,0:T(8,128)(2,1)}, bf16[640,128]{1,0:T(8,128)(2,1)}) custom-call(s32[40]{0:T(128)} %parent.7, s32[6]{0:T(128)} %stack.39.place, bf16[3,640,128]{2,1,0:T(8,128)(2,1)} %get-tuple-element.231.refs_0_, bf16[3,640,128]{2,1,0:T(8,128)(2,1)} %copy-done.9, ...), custom_call_target="tpu_custom_call" | custom-call | bytes 1 | tf_op jit(solution)/shard_map/attend/pallas_call | solution.py:235
  73.9 3.7 collective-permute-done.4.refs_1_
  77.7 2.6 collective-permute-done.5.refs_2_
  82.4 2.8 gather_heads.1
  85.1 8.5 %all-gather.8.cloned.1.call-done = bf16[1024,2048]{1,0:T(8,128)(2,1)} async-done(((bf16[256,2048]{1,0:T(8,128)(2,1)}), bf16[1024,2048]{1,0:T(8,128)(2,1)}) %all-gather.8.cloned.1.call-update) | async-done | bytes 4194320 | tf_op jit(solution)/shard_map/all_gather | solution.py:920
  94.3 54.9 %all-gather.10.cloned.1.call-done = bf16[2560,512]{1,0:T(8,128)(2,1)} async-done(((bf16[640,512]{1,0:T(8,128)(2,1)}), bf16[2560,512]{1,0:T(8,128)(2,1)}) %all-gather.10.cloned.1.call-update) | async-done | bytes 2621456 | tf_op jit(solution)/shard_map/all_gather | solution.py:938
  149.2 1.7 copy-done.1
  150.9 2.2 copy-done.3
  153.1 11.5 %project_out.1 = (f32[640,2048]{1,0:T(8,128)}, bf16[640,2048]{1,0:T(8,128)(2,1)S(1)}) custom-call(s32[6]{0:T(128)S(1)} %copy-done.2, bf16[640,2048]{1,0:T(8,128)(2,1)S(1)} %copy-done, bf16[4,640,512]{2,1,0:T(8,128)(2,1)S(1)} %bitcast.37, bf16[4,256,2048]{2,1,0:T(8,128)(2,1)S(1)} %bitcast.40, bf16[4,256,2048]{2,1,0:T(8,128)(2,1)} %collective-permute-done.7.far), custom_call_target="tpu_custom_call" | custom-call | flops 1300000014336 | bytes 1 | tf_op jit(solution)/shard_map/project_out/pallas_call | solution.py:456
  166.1 32.1 %feed_forward.1 = (bf16[640,2048]{1,0:T(8,128)(2,1)}, bf16[640,2048]{1,0:T(8,128)(2,1)}, bf16[640,2048]{1,0:T(8,128)(2,1)}, bf16[640,2048]{1,0:T(8,128)(2,1)}) custom-call(s32[6]{0:T(128)} %stack.39.place, bf16[640,2048]{1,0:T(8,128)(2,1)} %copy-done.4, f32[640,1024]{1,0:T(8,128)} %grad_hidden.2.seed, f32[640,1024]{1,0:T(8,128)} %grad_hidden.3.late_seed, ...), custom_call_target="tpu_custom_call" | custom-call | flops 3199999934464 | bytes 1 | tf_op jit(solution)/shard_map/feed_forward/pallas_call | solution.py:538
  198.5 7.8 %wgrad_away.5 = bf16[1024,2048]{1,0:T(8,128)(2,1)} custom-call(s32[6]{0:T(128)} %stack.39.place, bf16[640,2048]{1,0:T(8,128)(2,1)} %cot.3, bf16[640,2048]{1,0:T(8,128)(2,1)} %get-tuple-element.268.refs_1_.hidden), custom_call_target="tpu_custom_call" | custom-call | flops 799999983616 | bytes 1 | tf_op jit(solution)/shard_map/wgrad_away/pallas_call | solution.py:676
  206.3 7.9 %wgrad_away.6 = bf16[1024,2048]{1,0:T(8,128)(2,1)} custom-call(s32[6]{0:T(128)} %stack.39.place, bf16[640,2048]{1,0:T(8,128)(2,1)} %copy-done.4, bf16[640,2048]{1,0:T(8,128)(2,1)} %get-tuple-element.254.refs_1_), custom_call_target="tpu_custom_call" | custom-call | flops 799999983616 | bytes 1 | tf_op jit(solution)/shard_map/wgrad_away/pallas_call | solution.py:676
  214.6 9.4 %wgrad_keep.5 = (bf16[512,1024]{1,0:T(8,128)(2,1)}, bf16[512,1024]{1,0:T(8,128)(2,1)}, bf16[512,1024]{1,0:T(8,128)(2,1)}, bf16[512,1024]{1,0:T(8,128)(2,1)}) custom-call(s32[6]{0:T(128)} %stack.39.place, bf16[640,2048]{1,0:T(8,128)(2,1)} %cot.3, bf16[640,2048]{1,0:T(8,128)(2,1)} %get-tuple-element.268.refs_1_.hidden, ...), custom_call_target="tpu_custom_call" | custom-call | flops 899999989760 | bytes 1 | tf_op jit(solution)/shard_map/wgrad_keep/pallas_call | solution.py:725
  227.0 9.5 %wgrad_keep.6 = (bf16[512,1024]{1,0:T(8,128)(2,1)}, bf16[512,1024]{1,0:T(8,128)(2,1)}, bf16[512,1024]{1,0:T(8,128)(2,1)}, bf16[512,1024]{1,0:T(8,128)(2,1)}) custom-call(s32[6]{0:T(128)} %stack.39.place, bf16[640,2048]{1,0:T(8,128)(2,1)} %copy-done.4, bf16[640,2048]{1,0:T(8,128)(2,1)} %get-tuple-element.254.refs_1_, ...), custom_call_target="tpu_custom_call" | custom-call | flops 899999989760 | bytes 1 | tf_op jit(solution)/shard_map/wgrad_keep/pallas_call | solution.py:725
  236.5 7.9 %wgrad_away.7 = bf16[1024,2048]{1,0:T(8,128)(2,1)} custom-call(s32[6]{0:T(128)} %stack.39.place, bf16[640,2048]{1,0:T(8,128)(2,1)} %copy-done.4, bf16[640,2048]{1,0:T(8,128)(2,1)} %get-tuple-element.264.refs_1_), custom_call_target="tpu_custom_call" | custom-call | flops 799999983616 | bytes 1 | tf_op jit(solution)/shard_map/wgrad_away/pallas_call | solution.py:676
  247.5 2.9 collective-permute-done.9.a_got
  250.4 1.5 collective-permute-done.10.b_got
  251.9 11.3 %branch_back.1 = (f32[160,2048]{1,0:T(8,128)}, bf16[160,2048]{1,0:T(8,128)(2,1)}, bf16[160,512]{1,0:T(8,128)(2,1)}, bf16[160,512]{1,0:T(8,128)(2,1)}, bf16[160,5...) custom-call(s32[6]{0:T(128)} %stack.39.place, bf16[160,2048]{1,0:T(8,128)(2,1)} %reduce-scatter.4.cloned.1.call-done.part, ...), custom_call_target="tpu_custom_call" | custom-call | flops 899999989760 | bytes 1 | tf_op jit(solution)/shard_map/branch_back/pallas_call | solution.py:614
  263.3 1.6 collective-permute-start.13
  264.9 2.5 collective-permute-start.14
  267.4 9.8 %project_down.1 = bf16[640,2048]{1,0:T(8,128)(2,1)} custom-call(bf16[640,2048]{1,0:T(8,128)(2,1)} %get-tuple-element.268.refs_1_.hidden, bf16[2048,2048]{1,0:T(8,128)(2,1)} %w.1), custom_call_target="tpu_custom_call" | custom-call | flops 1100000002048 | bytes 1 | tf_op jit(solution)/shard_map/project_down/pallas_call | solution.py:568
  277.2 2.8 scatter_heads.1
  283.8 5.6 %wgrad_away.8 = bf16[1024,2048]{1,0:T(8,128)(2,1)} custom-call(s32[6]{0:T(128)} %stack.39.place, bf16[160,2048]{1,0:T(8,128)(2,1)} %get-tuple-element.287.refs_0_, bf16[160,2048]{1,0:T(8,128)(2,1)} %bitcast.44), custom_call_target="tpu_custom_call" | custom-call | flops 799999983616 | bytes 1 | tf_op jit(solution)/shard_map/wgrad_away/pallas_call | solution.py:676
  289.4 4.3 wgrad_stage.5
  293.7 3.2 collective-permute-done.20.refs_2_
  296.9 7.1 %wgrad_keep.7 = (bf16[512,1024]{1,0:T(8,128)(2,1)}, bf16[512,1024]{1,0:T(8,128)(2,1)}, bf16[512,1024]{1,0:T(8,128)(2,1)}, bf16[512,1024]{1,0:T(8,128)(2,1)}) custom-call(s32[6]{0:T(128)} %stack.39.place, bf16[160,2048]{1,0:T(8,128)(2,1)} %get-tuple-element.287.refs_0_, bf16[160,2048]{1,0:T(8,128)(2,1)} %bitcast.45, ...), custom_call_target="tpu_custom_call" | custom-call | flops 899999989760 | bytes 1 | tf_op jit(solution)/shard_map/wgrad_keep/pallas_call | solution.py:725
  306.1 23.1 %attend_back.1 = (bf16[640,128]{1,0:T(8,128)(2,1)}, bf16[640,128]{1,0:T(8,128)(2,1)}, bf16[640,128]{1,0:T(8,128)(2,1)}, bf16[640,128]{1,0:T(8,128)(2,1)}, f32[40...) custom-call(s32[40]{0:T(128)} %parent.7, s32[6]{0:T(128)} %stack.39.place, ...), custom_call_target="tpu_custom_call" | custom-call | flops 2300000075776 | bytes 1 | tf_op jit(solution)/shard_map/attend_back/pallas_call | solution.py:293
  329.9 4.3 wgrad_stage.6
  334.3 1.6 add_convert_fusion
  343.6 9.5 %wgrad_keep.8 = (bf16[512,1024]{1,0:T(8,128)(2,1)}, bf16[512,1024]{1,0:T(8,128)(2,1)}, bf16[512,1024]{1,0:T(8,128)(2,1)}, bf16[512,1024]{1,0:T(8,128)(2,1)}) custom-call(s32[6]{0:T(128)} %stack.39.place, bf16[640,2048]{1,0:T(8,128)(2,1)} %copy-done.4, bf16[640,2048]{1,0:T(8,128)(2,1)} %get-tuple-element.264.refs_1_, ...), custom_call_target="tpu_custom_call" | custom-call | flops 899999989760 | bytes 1 | tf_op jit(solution)/shard_map/wgrad_keep/pallas_call | solution.py:725
  353.1 4.3 wgrad_stage.7
  357.4 8.3 %collective-permute-done.25.refs_2_ = bf16[3,640,128]{2,1,0:T(8,128)(2,1)} collective-permute-done((bf16[3,640,128]{2,1,0:T(8,128)(2,1)}, bf16[3,640,128]{2,1,0:T(8,128)(2,1)}, u32[]{:S(2)}, u32[]{:S(2)}) %collective-permute-start.25) | collective-permute-done | bytes 491552 | tf_op jit(solution)/shard_map/ppermute | solution.py:908
  365.7 12.8 %turn_back.1 = (bf16[640,2048]{1,0:T(8,128)(2,1)}, bf16[640,1536]{1,0:T(8,128)(2,1)}) custom-call(s32[40]{0:T(128)} %parent.7, s32[6]{0:T(128)} %stack.39.place, f32[1280,128]{1,0:T(8,128)} %constant.39.clone.cosine, f32[1280,128]{1,0:T(8,128)} %constant.40.clone.sine, bf16[2048,512]{1,0:T(8,128)(2,1)} %wq.3, bf16[2048,512]{1,0:T(8,128)(2,1)} %wk.3, ...), custom_call_target="tpu_custom_call" | custom-call | flops 1300000014336 | bytes 1 | tf_op jit(solution)/shard_map/turn_back/pallas_call | solution.py:411
  378.5 7.0 %wgrad_away.9 = bf16[1024,1536]{1,0:T(8,128)(2,1)} custom-call(s32[6]{0:T(128)} %stack.39.place, bf16[640,2048]{1,0:T(8,128)(2,1)} %get-tuple-element.223.refs_0_, bf16[640,1536]{1,0:T(8,128)(2,1)} %get-tuple-element.346.refs_1_), custom_call_target="tpu_custom_call" | custom-call | flops 799999983616 | bytes 1 | tf_op jit(solution)/shard_map/wgrad_away/pallas_call | solution.py:676
  385.9 1.5 collective-permute-start.29
  388.1 5.2 add_residual.1
  393.2 7.3 %collective-permute-done.29.a_got = bf16[256,1024]{1,0:T(8,128)(2,1)} collective-permute-done((bf16[256,1024]{1,0:T(8,128)(2,1)}, bf16[256,1024]{1,0:T(8,128)(2,1)}, u32[]{:S(2)}, u32[]{:S(2)}) %collective-permute-start.29) | collective-permute-done | bytes 524320 | tf_op jit(solution)/shard_map/ppermute | solution.py:816
  401.7 3.5 wgrad_finish.5
  409.2 8.3 %wgrad_keep.9 = (bf16[512,768]{1,0:T(8,128)(2,1)}, bf16[512,768]{1,0:T(8,128)(2,1)}, bf16[512,768]{1,0:T(8,128)(2,1)}, bf16[512,768]{1,0:T(8,128)(2,1)}) custom-call(s32[6]{0:T(128)} %stack.39.place, bf16[640,2048]{1,0:T(8,128)(2,1)} %get-tuple-element.223.refs_0_, bf16[640,1536]{1,0:T(8,128)(2,1)} %get-tuple-element.346.refs_1_, ...), custom_call_target="tpu_custom_call" | custom-call | flops 899999989760 | bytes 1 | tf_op jit(solution)/shard_map/wgrad_keep/pallas_call | solution.py:725
  417.5 21.1 %reduce-scatter.6.cloned.1.call-done.part = bf16[160,2048]{1,0:T(8,128)(2,1)} async-done(((bf16[640,2048]{1,0:T(8,128)(2,1)}), bf16[160,2048]{1,0:T(8,128)(2,1)}) %reduce-scatter.6.cloned.1.call-update) | async-done | bytes 655376 | tf_op jit(solution)/shard_map/reduce_scatter | solution.py:1011
  438.6 4.1 tokens_back.1
  442.7 1.5 collective-permute-start.33
  445.8 4.2 wgrad_stage.8
  451.0 3.5 wgrad_finish.6
  454.6 3.4 collective-permute-done.33.a_got
  461.5 3.0 wgrad_finish.7
  464.5 4.7 collective-permute-done.39.a_got
  470.7 3.0 wgrad_finish.8
  473.7 12.1 %collective-permute-done.37.a_got = bf16[512,768]{1,0:T(8,128)(2,1)} collective-permute-done((bf16[512,768]{1,0:T(8,128)(2,1)}, bf16[512,768]{1,0:T(8,128)(2,1)}, u32[]{:S(2)}, u32[]{:S(2)}) %collective-permute-start.37) | collective-permute-done | bytes 786464 | tf_op jit(solution)/shard_map/ppermute | solution.py:816
  485.9 3.9 wgrad_stage.9
  492.9 6.6 %collective-permute-done.41.a_got = bf16[256,768]{1,0:T(8,128)(2,1)S(1)} collective-permute-done((bf16[256,768]{1,0:T(8,128)(2,1)}, bf16[256,768]{1,0:T(8,128)(2,1)S(1)}, u32[]{:S(2)}, u32[]{:S(2)}) %collective-permute-start.41) | collective-permute-done | bytes 393248 | tf_op jit(solution)/shard_map/ppermute | solution.py:816
  500.5 2.6 wgrad_finish.9
  503.2 2.7 fusion
  505.8 21.4 %reduce-scatter.8.cloned.1.call-done = bf16[512,256]{1,0:T(8,128)(2,1)} async-done(((bf16[2048,256]{1,0:T(8,128)(2,1)}), bf16[512,256]{1,0:T(8,128)(2,1)}) %reduce-scatter.8.cloned.1.call-update) | async-done | bytes 262160 | tf_op jit(solution)/shard_map/reduce_scatter | solution.py:1040
  527.2 1.8 convert_element_type.31
  (137 shorter events, 50.3 us)
Async XLA Ops:
  7.2 86.5 %all-gather.8.cloned.1.call-start = ((), (), s32[]{:S(2)}) async-start(), calls=%async_computation.8 | async-start | bytes 5242880 | tf_op jit(solution)/shard_map/all_gather | solution.py:920
  9.6 139.6 %all-gather.10.cloned.1.call-start = ((), (), s32[]{:S(2)}) async-start(), calls=%async_computation.9 | async-start | bytes 3276800 | tf_op jit(solution)/shard_map/all_gather | solution.py:938
  22.1 15.2 %collective-permute-start = (bf16[3,640,128]{2,1,0:T(8,128)(2,1)}, bf16[3,640,128]{2,1,0:T(8,128)(2,1)S(1)}, u32[]{:S(2)}, u32[]{:S(2)}) collective-permute-start(bf16[3,640,128]{2,1,0:T(8,128)(2,1)} %get-tuple-element.220), channel_id=1, source_target_pairs={{0,8},{4,12},{8,0},{12,4},{16,24},{20,28},{24,16},{28,20},{1,9},{5... | collective-permute-start | bytes 1474568 | tf_op jit(solution)/shard_map/ppermute | solution.py:908
  25.0 23.4 %collective-permute-start.1 = (bf16[3,640,128]{2,1,0:T(8,128)(2,1)}, bf16[3,640,128]{2,1,0:T(8,128)(2,1)S(1)}, u32[]{:S(2)}, u32[]{:S(2)}) collective-permute-start(bf16[3,640,128]{2,1,0:T(8,128)(2,1)} %get-tuple-element.221), channel_id=1, source_target_pairs={{0,16},{4,20},{8,24},{12,28},{16,0},{20,4},{24,8},{28,12},{1,17},{... | collective-permute-start | bytes 1474568 | tf_op jit(solution)/shard_map/ppermute | solution.py:908
  26.5 21.9 %collective-permute-start.2 = (bf16[3,640,128]{2,1,0:T(8,128)(2,1)}, bf16[3,640,128]{2,1,0:T(8,128)(2,1)S(1)}, u32[]{:S(2)}, u32[]{:S(2)}) collective-permute-start(bf16[3,640,128]{2,1,0:T(8,128)(2,1)} %get-tuple-element.222), channel_id=1, source_target_pairs={{0,24},{4,28},{8,16},{12,20},{16,8},{20,12},{24,0},{28,4},{1,25},{... | collective-permute-start | bytes 1474568 | tf_op jit(solution)/shard_map/ppermute | solution.py:908
  26.5 22.0 %copy-start.8 = (bf16[3,640,128]{2,1,0:T(8,128)(2,1)S(1)}, bf16[3,640,128]{2,1,0:T(8,128)(2,1)}, u32[]{:S(2)}) copy-start(bf16[3,640,128]{2,1,0:T(8,128)(2,1)} %get-tuple-element.231.refs_0_) | copy-start | bytes 1474564
  37.3 11.3 %copy-start.9 = (bf16[3,640,128]{2,1,0:T(8,128)(2,1)}, bf16[3,640,128]{2,1,0:T(8,128)(2,1)S(1)}, u32[]{:S(2)}) copy-start(bf16[3,640,128]{2,1,0:T(8,128)(2,1)S(1)} %collective-permute-done.refs_1_) | copy-start | bytes 1474564
  49.5 6.8 %collective-permute-start.3 = (bf16[1,4,2,640,128]{4,3,2,1,0:T(8,128)(2,1)S(1)}, bf16[1,4,2,640,128]{4,3,2,1,0:T(8,128)(2,1)S(1)}, u32[]{:S(2)}, u32[]{:S(2)}) collective-permute-start(bf16[1,4,2,640,128]{4,3,2,1,0:T(8,128)(2,1)S(1)} %maximum_bitcast_fusion), channel_id=1, source_target_pairs={{0,4},{4,0},{8,12},{12,8},{16,20},{20,16},{24,28},{28,24},{1,5},{5... | collective-permute-start | bytes 3932168 | tf_op jit(solution)/shard_map/ppermute | solution.py:908
  58.0 91.2 %copy-start = (bf16[640,2048]{1,0:T(8,128)(2,1)S(1)}, bf16[640,2048]{1,0:T(8,128)(2,1)}, u32[]{:S(2)}) copy-start(bf16[640,2048]{1,0:T(8,128)(2,1)} %tokens.1) | copy-start | bytes 7864324
  58.0 91.2 %copy-start.2 = (s32[6]{0:T(128)S(1)}, s32[6]{0:T(128)}, u32[]{:S(2)}) copy-start(s32[6]{0:T(128)} %stack.39.place) | copy-start | bytes 76
  70.4 7.2 %collective-permute-start.4 = (bf16[640,128]{1,0:T(8,128)(2,1)}, bf16[640,128]{1,0:T(8,128)(2,1)S(1)}, u32[]{:S(2)}, u32[]{:S(2)}) collective-permute-start(bf16[640,128]{1,0:T(8,128)(2,1)} %get-tuple-element.236), channel_id=1, source_target_pairs={{0,8},{4,12},{8,0},{12,4},{16,24},{20,28},{24,16},{28,20},{1,9},{5... | collective-permute-start | bytes 491528 | tf_op jit(solution)/shard_map/ppermute | solution.py:908
  71.5 8.7 %collective-permute-start.5 = (bf16[640,128]{1,0:T(8,128)(2,1)}, bf16[640,128]{1,0:T(8,128)(2,1)S(1)}, u32[]{:S(2)}, u32[]{:S(2)}) collective-permute-start(bf16[640,128]{1,0:T(8,128)(2,1)} %get-tuple-element.237), channel_id=1, source_target_pairs={{0,16},{4,20},{8,24},{12,28},{16,0},{20,4},{24,8},{28,12},{1,17},{... | collective-permute-start | bytes 491528 | tf_op jit(solution)/shard_map/ppermute | solution.py:908
  72.5 9.2 %collective-permute-start.6 = (bf16[640,128]{1,0:T(8,128)(2,1)}, bf16[640,128]{1,0:T(8,128)(2,1)S(1)}, u32[]{:S(2)}, u32[]{:S(2)}) collective-permute-start(bf16[640,128]{1,0:T(8,128)(2,1)} %get-tuple-element.238), channel_id=1, source_target_pairs={{0,24},{4,28},{8,16},{12,20},{16,8},{20,12},{24,0},{28,4},{1,25},{... | collective-permute-start | bytes 491528 | tf_op jit(solution)/shard_map/ppermute | solution.py:908
  77.7 4.1 copy-start.12
  80.2 1.5 copy-start.13
  93.7 55.5 %collective-permute-start.7 = (bf16[4,256,2048]{2,1,0:T(8,128)(2,1)}, bf16[4,256,2048]{2,1,0:T(8,128)(2,1)}, u32[]{:S(2)}, u32[]{:S(2)}) collective-permute-start(bf16[4,256,2048]{2,1,0:T(8,128)(2,1)} %bitcast.38), channel_id=1, source_target_pairs={{0,4},{4,0},{8,12},{12,8},{16,20},{20,16},{24,28},{28,24},{1,5},{5... | collective-permute-start | bytes 12582920 | tf_op jit(solution)/shard_map/ppermute | solution.py:908
  93.7 158.2 %reduce-scatter.4.cloned.1.call-start = ((), (), s32[]{:S(2)}) async-start(), calls=%async_computation.3 | async-start | bytes 3276800 | tf_op jit(solution)/shard_map/reduce_scatter | solution.py:948
  149.2 1.7 copy-start.1
  150.9 2.2 copy-start.3
  198.2 187.6 %all-reduce.2.cloned.1.call-start = ((), (), s32[]{:S(2)}) async-start(), calls=%async_computation.4 | async-start | bytes 5242880 | tf_op jit(solution)/shard_map/psum | solution.py:971
  206.3 8.3 %collective-permute-start.8 = (bf16[1024,2048]{1,0:T(8,128)(2,1)}, bf16[1024,2048]{1,0:T(8,128)(2,1)}, u32[]{:S(2)}, u32[]{:S(2)}) collective-permute-start(bf16[1024,2048]{1,0:T(8,128)(2,1)} %wgrad_away.5), channel_id=1, source_target_pairs={{0,4},{4,0},{8,12},{12,8},{16,20},{20,16},{24,28},{28,24},{1,5},{5... | collective-permute-start | bytes 12582920 | tf_op jit(solution)/shard_map/ppermute | solution.py:816
  214.2 12.9 %collective-permute-start.11 = (bf16[1024,2048]{1,0:T(8,128)(2,1)}, bf16[1024,2048]{1,0:T(8,128)(2,1)}, u32[]{:S(2)}, u32[]{:S(2)}) collective-permute-start(bf16[1024,2048]{1,0:T(8,128)(2,1)} %wgrad_away.6), channel_id=1, source_target_pairs={{0,4},{4,0},{8,12},{12,8},{16,20},{20,16},{24,28},{28,24},{1,5},{5... | collective-permute-start | bytes 12582920 | tf_op jit(solution)/shard_map/ppermute | solution.py:816
  224.1 26.3 %collective-permute-start.9 = (bf16[512,1024]{1,0:T(8,128)(2,1)}, bf16[512,1024]{1,0:T(8,128)(2,1)}, u32[]{:S(2)}, u32[]{:S(2)}) collective-permute-start(bf16[512,1024]{1,0:T(8,128)(2,1)} %get-tuple-element.259), channel_id=1, source_target_pairs={{0,8},{4,12},{8,0},{12,4},{16,24},{20,28},{24,16},{28,20},{1,9},{5... | collective-permute-start | bytes 3145736 | tf_op jit(solution)/shard_map/ppermute | solution.py:816
  225.6 26.4 %collective-permute-start.10 = (bf16[512,1024]{1,0:T(8,128)(2,1)}, bf16[512,1024]{1,0:T(8,128)(2,1)}, u32[]{:S(2)}, u32[]{:S(2)}) collective-permute-start(bf16[512,1024]{1,0:T(8,128)(2,1)} %get-tuple-element.260), channel_id=1, source_target_pairs={{0,16},{4,20},{8,24},{12,28},{16,0},{20,4},{24,8},{28,12},{1,17},{... | collective-permute-start | bytes 3145736 | tf_op jit(solution)/shard_map/ppermute | solution.py:816
  244.4 32.7 %collective-permute-start.15 = (bf16[512,1024]{1,0:T(8,128)(2,1)}, bf16[512,1024]{1,0:T(8,128)(2,1)}, u32[]{:S(2)}, u32[]{:S(2)}) collective-permute-start(bf16[512,1024]{1,0:T(8,128)(2,1)} %get-tuple-element.275), channel_id=1, source_target_pairs={{0,8},{4,12},{8,0},{12,4},{16,24},{20,28},{24,16},{28,20},{1,9},{5... | collective-permute-start | bytes 3145736 | tf_op jit(solution)/shard_map/ppermute | solution.py:816
  244.9 32.3 %collective-permute-start.16 = (bf16[512,1024]{1,0:T(8,128)(2,1)}, bf16[512,1024]{1,0:T(8,128)(2,1)}, u32[]{:S(2)}, u32[]{:S(2)}) collective-permute-start(bf16[512,1024]{1,0:T(8,128)(2,1)} %get-tuple-element.276), channel_id=1, source_target_pairs={{0,16},{4,20},{8,24},{12,28},{16,0},{20,4},{24,8},{28,12},{1,17},{... | collective-permute-start | bytes 3145736 | tf_op jit(solution)/shard_map/ppermute | solution.py:816
  263.3 13.9 %collective-permute-start.12 = (bf16[160,512]{1,0:T(8,128)(2,1)}, bf16[160,512]{1,0:T(8,128)(2,1)}, u32[]{:S(2)}, u32[]{:S(2)}) collective-permute-start(bf16[160,512]{1,0:T(8,128)(2,1)} %get-tuple-element.270), channel_id=1, source_target_pairs={{0,1},{1,2},{2,3},{3,0},{4,5},{5,6},{6,7},{7,4},{8,9},{9,10},{10,1... | collective-permute-start | bytes 491528 | tf_op jit(solution)/shard_map/ppermute | solution.py:914
  263.3 13.9 %collective-permute-start.13 = (bf16[160,512]{1,0:T(8,128)(2,1)}, bf16[160,512]{1,0:T(8,128)(2,1)}, u32[]{:S(2)}, u32[]{:S(2)}) collective-permute-start(bf16[160,512]{1,0:T(8,128)(2,1)} %get-tuple-element.271), channel_id=1, source_target_pairs={{0,2},{1,3},{2,0},{3,1},{4,6},{5,7},{6,4},{7,5},{8,10},{9,11},{10,... | collective-permute-start | bytes 491528 | tf_op jit(solution)/shard_map/ppermute | solution.py:914
  264.9 12.3 %collective-permute-start.14 = (bf16[160,512]{1,0:T(8,128)(2,1)}, bf16[160,512]{1,0:T(8,128)(2,1)}, u32[]{:S(2)}, u32[]{:S(2)}) collective-permute-start(bf16[160,512]{1,0:T(8,128)(2,1)} %get-tuple-element.272), channel_id=1, source_target_pairs={{0,3},{1,0},{2,1},{3,2},{4,7},{5,4},{6,5},{7,6},{8,11},{9,8},{10,9... | collective-permute-start | bytes 491528 | tf_op jit(solution)/shard_map/ppermute | solution.py:914
  277.1 66.4 %collective-permute-start.27 = (bf16[1024,2048]{1,0:T(8,128)(2,1)}, bf16[1024,2048]{1,0:T(8,128)(2,1)}, u32[]{:S(2)}, u32[]{:S(2)}) collective-permute-start(bf16[1024,2048]{1,0:T(8,128)(2,1)} %wgrad_away.7), channel_id=1, source_target_pairs={{0,4},{4,0},{8,12},{12,8},{16,20},{20,16},{24,28},{28,24},{1,5},{5... | collective-permute-start | bytes 12582920 | tf_op jit(solution)/shard_map/ppermute | solution.py:816
  280.0 158.6 %reduce-scatter.6.cloned.1.call-start = ((), (), s32[]{:S(2)}) async-start(), calls=%async_computation.5 | async-start | bytes 3276800 | tf_op jit(solution)/shard_map/reduce_scatter | solution.py:1011
  280.2 23.7 %collective-permute-start.17 = (bf16[640,128]{1,0:T(8,128)(2,1)}, bf16[640,128]{1,0:T(8,128)(2,1)}, u32[]{:S(2)}, u32[]{:S(2)}) collective-permute-start(bf16[640,128]{1,0:T(8,128)(2,1)} %get-tuple-element.284), channel_id=1, source_target_pairs={{0,8},{4,12},{8,0},{12,4},{16,24},{20,28},{24,16},{28,20},{1,9},{5... | collective-permute-start | bytes 491528 | tf_op jit(solution)/shard_map/ppermute | solution.py:908
  280.9 23.1 %collective-permute-start.18 = (bf16[640,128]{1,0:T(8,128)(2,1)}, bf16[640,128]{1,0:T(8,128)(2,1)}, u32[]{:S(2)}, u32[]{:S(2)}) collective-permute-start(bf16[640,128]{1,0:T(8,128)(2,1)} %get-tuple-element.285), channel_id=1, source_target_pairs={{0,16},{4,20},{8,24},{12,28},{16,0},{20,4},{24,8},{28,12},{1,17},{... | collective-permute-start | bytes 491528 | tf_op jit(solution)/shard_map/ppermute | solution.py:908
  282.3 21.7 %collective-permute-start.19 = (bf16[640,128]{1,0:T(8,128)(2,1)}, bf16[640,128]{1,0:T(8,128)(2,1)}, u32[]{:S(2)}, u32[]{:S(2)}) collective-permute-start(bf16[640,128]{1,0:T(8,128)(2,1)} %get-tuple-element.286), channel_id=1, source_target_pairs={{0,24},{4,28},{8,16},{12,20},{16,8},{20,12},{24,0},{28,4},{1,25},{... | collective-permute-start | bytes 491528 | tf_op jit(solution)/shard_map/ppermute | solution.py:908
  289.4 7.5 %collective-permute-start.20 = (bf16[1024,2048]{1,0:T(8,128)(2,1)}, bf16[1024,2048]{1,0:T(8,128)(2,1)}, u32[]{:S(2)}, u32[]{:S(2)}) collective-permute-start(bf16[1024,2048]{1,0:T(8,128)(2,1)} %wgrad_away.8), channel_id=1, source_target_pairs={{0,4},{4,0},{8,12},{12,8},{16,20},{20,16},{24,28},{28,24},{1,5},{5... | collective-permute-start | bytes 12582920 | tf_op jit(solution)/shard_map/ppermute | solution.py:816
  304.0 25.6 %collective-permute-start.21 = (bf16[512,1024]{1,0:T(8,128)(2,1)}, bf16[512,1024]{1,0:T(8,128)(2,1)}, u32[]{:S(2)}, u32[]{:S(2)}) collective-permute-start(bf16[512,1024]{1,0:T(8,128)(2,1)} %get-tuple-element.312), channel_id=1, source_target_pairs={{0,8},{4,12},{8,0},{12,4},{16,24},{20,28},{24,16},{28,20},{1,9},{5... | collective-permute-start | bytes 3145736 | tf_op jit(solution)/shard_map/ppermute | solution.py:816
  304.7 25.3 %collective-permute-start.22 = (bf16[512,1024]{1,0:T(8,128)(2,1)}, bf16[512,1024]{1,0:T(8,128)(2,1)}, u32[]{:S(2)}, u32[]{:S(2)}) collective-permute-start(bf16[512,1024]{1,0:T(8,128)(2,1)} %get-tuple-element.313), channel_id=1, source_target_pairs={{0,16},{4,20},{8,24},{12,28},{16,0},{20,4},{24,8},{28,12},{1,17},{... | collective-permute-start | bytes 3145736 | tf_op jit(solution)/shard_map/ppermute | solution.py:816
  329.9 4.3 collective-permute-start.23
  329.9 4.3 copy-start.6
  335.9 1.7 copy-start.17
  335.9 2.5 copy-start.16
  335.9 3.4 copy-start.15
  340.1 17.3 %collective-permute-start.24 = (bf16[3,640,128]{2,1,0:T(8,128)(2,1)}, bf16[3,640,128]{2,1,0:T(8,128)(2,1)}, u32[]{:S(2)}, u32[]{:S(2)}) collective-permute-start(bf16[3,640,128]{2,1,0:T(8,128)(2,1)} %pad_maximum_fusion.2), channel_id=1, source_target_pairs={{0,8},{4,12},{8,0},{12,4},{16,24},{20,28},{24,16},{28,20},{1,9},{5... | collective-permute-start | bytes 1474568 | tf_op jit(solution)/shard_map/ppermute | solution.py:908
  341.5 24.2 %collective-permute-start.25 = (bf16[3,640,128]{2,1,0:T(8,128)(2,1)}, bf16[3,640,128]{2,1,0:T(8,128)(2,1)}, u32[]{:S(2)}, u32[]{:S(2)}) collective-permute-start(bf16[3,640,128]{2,1,0:T(8,128)(2,1)} %pad_maximum_fusion.3), channel_id=1, source_target_pairs={{0,16},{4,20},{8,24},{12,28},{16,0},{20,4},{24,8},{28,12},{1,17},{... | collective-permute-start | bytes 1474568 | tf_op jit(solution)/shard_map/ppermute | solution.py:908
  342.9 22.7 %collective-permute-start.26 = (bf16[3,640,128]{2,1,0:T(8,128)(2,1)}, bf16[3,640,128]{2,1,0:T(8,128)(2,1)}, u32[]{:S(2)}, u32[]{:S(2)}) collective-permute-start(bf16[3,640,128]{2,1,0:T(8,128)(2,1)} %pad_maximum_fusion.4), channel_id=1, source_target_pairs={{0,24},{4,28},{8,16},{12,20},{16,8},{20,12},{24,0},{28,4},{1,25},{... | collective-permute-start | bytes 1474568 | tf_op jit(solution)/shard_map/ppermute | solution.py:908
  385.5 114.3 %all-gather.6.cloned.1.call-start = ((), (), s32[]{:S(2)}) async-start(), calls=%async_computation.6 | async-start | bytes 3276800 | tf_op jit(solution)/shard_map/all_gather | solution.py:1024
  385.8 23.5 %collective-permute-start.28 = (bf16[1024,1536]{1,0:T(8,128)(2,1)}, bf16[1024,1536]{1,0:T(8,128)(2,1)}, u32[]{:S(2)}, u32[]{:S(2)}) collective-permute-start(bf16[1024,1536]{1,0:T(8,128)(2,1)} %wgrad_away.9), channel_id=1, source_target_pairs={{0,4},{4,0},{8,12},{12,8},{16,20},{20,16},{24,28},{28,24},{1,5},{5... | collective-permute-start | bytes 9437192 | tf_op jit(solution)/shard_map/ppermute | solution.py:816
  385.9 14.6 %collective-permute-start.29 = (bf16[256,1024]{1,0:T(8,128)(2,1)}, bf16[256,1024]{1,0:T(8,128)(2,1)}, u32[]{:S(2)}, u32[]{:S(2)}) collective-permute-start(bf16[256,1024]{1,0:T(8,128)(2,1)} %get-tuple-element.350), channel_id=1, source_target_pairs={{0,16},{4,20},{8,24},{12,28},{16,0},{20,4},{24,8},{28,12},{1,17},{... | collective-permute-start | bytes 1572872 | tf_op jit(solution)/shard_map/ppermute | solution.py:816
  387.4 14.3 %collective-permute-start.30 = (bf16[256,1024]{1,0:T(8,128)(2,1)}, bf16[256,1024]{1,0:T(8,128)(2,1)}, u32[]{:S(2)}, u32[]{:S(2)}) collective-permute-start(bf16[256,1024]{1,0:T(8,128)(2,1)} %get-tuple-element.351), channel_id=1, source_target_pairs={{0,8},{4,12},{8,0},{12,4},{16,24},{20,28},{24,16},{28,20},{1,9},{5... | collective-permute-start | bytes 1572872 | tf_op jit(solution)/shard_map/ppermute | solution.py:816
  405.2 37.6 %collective-permute-start.31 = (bf16[256,1024]{1,0:T(8,128)(2,1)}, bf16[256,1024]{1,0:T(8,128)(2,1)}, u32[]{:S(2)}, u32[]{:S(2)}) collective-permute-start(bf16[256,1024]{1,0:T(8,128)(2,1)} %get-tuple-element.368), channel_id=1, source_target_pairs={{0,16},{4,20},{8,24},{12,28},{16,0},{20,4},{24,8},{28,12},{1,17},{... | collective-permute-start | bytes 1572872 | tf_op jit(solution)/shard_map/ppermute | solution.py:816
  405.7 37.0 %collective-permute-start.32 = (bf16[256,1024]{1,0:T(8,128)(2,1)}, bf16[256,1024]{1,0:T(8,128)(2,1)}, u32[]{:S(2)}, u32[]{:S(2)}) collective-permute-start(bf16[256,1024]{1,0:T(8,128)(2,1)} %get-tuple-element.369), channel_id=1, source_target_pairs={{0,8},{4,12},{8,0},{12,4},{16,24},{20,28},{24,16},{28,20},{1,9},{5... | collective-permute-start | bytes 1572872 | tf_op jit(solution)/shard_map/ppermute | solution.py:816
  406.9 38.8 %collective-permute-start.35 = (bf16[512,1024]{1,0:T(8,128)(2,1)}, bf16[512,1024]{1,0:T(8,128)(2,1)}, u32[]{:S(2)}, u32[]{:S(2)}) collective-permute-start(bf16[512,1024]{1,0:T(8,128)(2,1)} %get-tuple-element.377), channel_id=1, source_target_pairs={{0,8},{4,12},{8,0},{12,4},{16,24},{20,28},{24,16},{28,20},{1,9},{5... | collective-permute-start | bytes 3145736 | tf_op jit(solution)/shard_map/ppermute | solution.py:816
  407.7 38.0 %collective-permute-start.36 = (bf16[512,1024]{1,0:T(8,128)(2,1)}, bf16[512,1024]{1,0:T(8,128)(2,1)}, u32[]{:S(2)}, u32[]{:S(2)}) collective-permute-start(bf16[512,1024]{1,0:T(8,128)(2,1)} %get-tuple-element.378), channel_id=1, source_target_pairs={{0,16},{4,20},{8,24},{12,28},{16,0},{20,4},{24,8},{28,12},{1,17},{... | collective-permute-start | bytes 3145736 | tf_op jit(solution)/shard_map/ppermute | solution.py:816
  442.7 84.5 %reduce-scatter.8.cloned.1.call-start = ((), (), s32[]{:S(2)}) async-start(), calls=%async_computation.7 | async-start | bytes 1310720 | tf_op jit(solution)/shard_map/reduce_scatter | solution.py:1040
  442.7 15.2 %collective-permute-start.33 = (bf16[256,1024]{1,0:T(8,128)(2,1)}, bf16[256,1024]{1,0:T(8,128)(2,1)}, u32[]{:S(2)}, u32[]{:S(2)}) collective-permute-start(bf16[256,1024]{1,0:T(8,128)(2,1)} %get-tuple-element.371), channel_id=1, source_target_pairs={{0,16},{4,20},{8,24},{12,28},{16,0},{20,4},{24,8},{28,12},{1,17},{... | collective-permute-start | bytes 1572872 | tf_op jit(solution)/shard_map/ppermute | solution.py:816
  444.3 15.2 %collective-permute-start.34 = (bf16[256,1024]{1,0:T(8,128)(2,1)}, bf16[256,1024]{1,0:T(8,128)(2,1)}, u32[]{:S(2)}, u32[]{:S(2)}) collective-permute-start(bf16[256,1024]{1,0:T(8,128)(2,1)} %get-tuple-element.372), channel_id=1, source_target_pairs={{0,8},{4,12},{8,0},{12,4},{16,24},{20,28},{24,16},{28,20},{1,9},{5... | collective-permute-start | bytes 1572872 | tf_op jit(solution)/shard_map/ppermute | solution.py:816
  450.0 19.2 %collective-permute-start.39 = (bf16[256,1024]{1,0:T(8,128)(2,1)}, bf16[256,1024]{1,0:T(8,128)(2,1)}, u32[]{:S(2)}, u32[]{:S(2)}) collective-permute-start(bf16[256,1024]{1,0:T(8,128)(2,1)} %get-tuple-element.396), channel_id=1, source_target_pairs={{0,16},{4,20},{8,24},{12,28},{16,0},{20,4},{24,8},{28,12},{1,17},{... | collective-permute-start | bytes 1572872 | tf_op jit(solution)/shard_map/ppermute | solution.py:816
  450.5 20.2 %collective-permute-start.40 = (bf16[256,1024]{1,0:T(8,128)(2,1)}, bf16[256,1024]{1,0:T(8,128)(2,1)}, u32[]{:S(2)}, u32[]{:S(2)}) collective-permute-start(bf16[256,1024]{1,0:T(8,128)(2,1)} %get-tuple-element.397), channel_id=1, source_target_pairs={{0,8},{4,12},{8,0},{12,4},{16,24},{20,28},{24,16},{28,20},{1,9},{5... | collective-permute-start | bytes 1572872 | tf_op jit(solution)/shard_map/ppermute | solution.py:816
  459.5 26.4 %collective-permute-start.37 = (bf16[512,768]{1,0:T(8,128)(2,1)}, bf16[512,768]{1,0:T(8,128)(2,1)}, u32[]{:S(2)}, u32[]{:S(2)}) collective-permute-start(bf16[512,768]{1,0:T(8,128)(2,1)} %get-tuple-element.392), channel_id=1, source_target_pairs={{0,8},{4,12},{8,0},{12,4},{16,24},{20,28},{24,16},{28,20},{1,9},{5... | collective-permute-start | bytes 2359304 | tf_op jit(solution)/shard_map/ppermute | solution.py:816
  460.9 25.0 %collective-permute-start.38 = (bf16[512,768]{1,0:T(8,128)(2,1)}, bf16[512,768]{1,0:T(8,128)(2,1)}, u32[]{:S(2)}, u32[]{:S(2)}) collective-permute-start(bf16[512,768]{1,0:T(8,128)(2,1)} %get-tuple-element.393), channel_id=1, source_target_pairs={{0,16},{4,20},{8,24},{12,28},{16,0},{20,4},{24,8},{28,12},{1,17},{... | collective-permute-start | bytes 2359304 | tf_op jit(solution)/shard_map/ppermute | solution.py:816
  485.9 5.9 %copy-start.7 = (f32[2048,256]{1,0:T(8,128)S(1)}, f32[2048,256]{1,0:T(8,128)}, u32[]{:S(2)}) copy-start(f32[2048,256]{1,0:T(8,128)} %wgrad_finish.5) | copy-start | bytes 6291460
  489.8 9.7 %collective-permute-start.41 = (bf16[256,768]{1,0:T(8,128)(2,1)}, bf16[256,768]{1,0:T(8,128)(2,1)S(1)}, u32[]{:S(2)}, u32[]{:S(2)}) collective-permute-start(bf16[256,768]{1,0:T(8,128)(2,1)} %get-tuple-element.421), channel_id=1, source_target_pairs={{0,16},{4,20},{8,24},{12,28},{16,0},{20,4},{24,8},{28,12},{1,17},{... | collective-permute-start | bytes 1179656 | tf_op jit(solution)/shard_map/ppermute | solution.py:816
  490.3 9.4 %collective-permute-start.42 = (bf16[256,768]{1,0:T(8,128)(2,1)}, bf16[256,768]{1,0:T(8,128)(2,1)S(1)}, u32[]{:S(2)}, u32[]{:S(2)}) collective-permute-start(bf16[256,768]{1,0:T(8,128)(2,1)} %get-tuple-element.423), channel_id=1, source_target_pairs={{0,8},{4,12},{8,0},{12,4},{16,24},{20,28},{24,16},{28,20},{1,9},{5... | collective-permute-start | bytes 1179656 | tf_op jit(solution)/shard_map/ppermute | solution.py:816
  503.2 25.8 %copy-start.5 = (bf16[640,2048]{1,0:T(8,128)(2,1)S(1)}, bf16[640,2048]{1,0:T(8,128)(2,1)}, u32[]{:S(2)}) copy-start(bf16[640,2048]{1,0:T(8,128)(2,1)} %all-gather.6.cloned.1.call-done) | copy-start | bytes 7864324
  (7 other events, 6.2 us)
Sparse Core Ops, SparseCore 0:
  10.2 83.4 all-gather.7
  95.8 53.2 all-gather.9
  198.4 50.8 reduce-scatter.3
  280.1 104.9 all-reduce.1
  387.2 51.3 reduce-scatter.5
  442.8 54.4 all-gather.5
  499.9 27.2 reduce-scatter.7

commit v3 on v2

--- a/solution.py
+++ b/solution.py
@@ -19,7 +19,8 @@
 LOW = jnp.bfloat16
 F32 = jnp.float32
 MIB = 1024 * 1024
-PER_MICROSECOND = 100e9
+PER_MICROSECOND = 8.0e+09
+
 NT = (((1,), (1,)), ((), ()))
 TN = (((0,), (0,)), ((), ()))
 
@@ -42,7 +43,7 @@
 
 def about(microseconds):
     return pl.CostEstimate(
-        flops=int(microseconds * PER_MICROSECOND), bytes_accessed=1, transcendentals=0
+        flops=int(microseconds * PER_MICROSECOND * Chain.weight), bytes_accessed=1, transcendentals=0
     )
 
 
@@ -101,6 +102,17 @@
         self.bits = self.dp.bit_length() - 1
         self.piece = width // self.dp
         self.own = rows // self.tensor
+        self.groups = 2 if self.own % 32 == 0 else 1
+        self.part = rows // self.groups
+        self.share = self.own // self.groups
+
+    def own_rows(self, group):
+        return pl.BlockSpec(
+            (self.share, self.width), lambda i, place: (group * self.tensor + place[1], 0)
+        )
+
+    def own_part(self):
+        return pl.BlockSpec((self.share, self.width), lambda i, place: (place[1], 0))
 
 
 def fetch(weights, held, sems, kind):
@@ -314,24 +326,52 @@
     )(slot_parent, place, *parts, kv, *grads)
 
 
+def combine_kernel(plan, *refs):
+    n = plan.spread
+    queries, (near, got), outs = refs[:n], refs[n : n + 2], refs[n + 2 :]
+    for d in range(n):
+        outs[d][0] = queries[d][...]
+        for kind in range(2):
+            for slot in range(plan.slots):
+                block = (d * 2 + kind) * plan.slots + slot
+                rows = slice(slot * BLOCK, (slot + 1) * BLOCK)
+                total = near[block] + got[block].astype(F32)
+                outs[d][kind + 1, rows, :] = total.astype(LOW)
+
+
+def combine_back(plan, queries, near, got):
+    n = plan.spread
+    return pl.pallas_call(
+        functools.partial(combine_kernel, plan),
+        out_shape=[shape((3, plan.rows, HEAD), LOW)] * n,
+        compiler_params=params(60),
+        cost_estimate=about(3),
+        name="combine_back",
+    )(*queries, near, got)
+
+
 def heads_kernel(plan, place, *refs):
     part = place[0] // plan.rest
-    out = refs[-1]
+    outs = refs[plan.spread :]
     for d in range(plan.spread):
         head = pl.ds(pl.multiple_of((part ^ d) * HEAD, HEAD), HEAD)
-        out[:, head] = refs[d][...]
+        for group, out in enumerate(outs):
+            out[:, head] = refs[d][group * plan.part : (group + 1) * plan.part, :]
 
 
 def gather_heads(plan, place, parts):
+    wide = plan.heads * HEAD
     return pl.pallas_call(
         functools.partial(heads_kernel, plan),
         grid_spec=pltpu.PrefetchScalarGridSpec(
             num_scalar_prefetch=1,
             grid=(1,),
             in_specs=[pl.BlockSpec((plan.rows, HEAD), lambda i, *_: (0, 0))] * plan.spread,
-            out_specs=pl.BlockSpec((plan.rows, plan.heads * HEAD), lambda i, *_: (0, 0)),
+            out_specs=[pl.BlockSpec((plan.part, wide), lambda i, *_: (0, 0))] * plan.groups,
         ),
-        out_shape=shape((plan.rows, plan.heads * HEAD), LOW),
+        out_shape=[shape((plan.part, wide), LOW)] * plan.groups,
+        compiler_params=params(60),
+        cost_estimate=about(0),
         name="gather_heads",
     )(place, *parts)
 
@@ -341,10 +381,13 @@
     sources, outs = refs[: plan.tensor], refs[plan.tensor :]
     for shift in range(plan.tensor):
         origin = lax.rem(z - shift + plan.tensor, plan.tensor)
-        rows = pl.ds(pl.multiple_of(origin * plan.own, 16), plan.own)
-        for d in range(plan.spread):
-            head = pl.ds(pl.multiple_of((part ^ d) * HEAD, HEAD), HEAD)
-            outs[d][rows, :] = sources[shift][:, head]
+        for group in range(plan.groups):
+            start = group * plan.part + origin * plan.share
+            rows = pl.ds(pl.multiple_of(start, 16), plan.share)
+            share = slice(group * plan.share, (group + 1) * plan.share)
+            for d in range(plan.spread):
+                head = pl.ds(pl.multiple_of((part ^ d) * HEAD, HEAD), HEAD)
+                outs[d][rows, :] = sources[shift][share, head]
 
 
 def scatter_heads(plan, place, sources):
@@ -363,14 +406,12 @@
 
 
 def turn_back_kernel(plan, parent, place, cosine, sine, wq, wk, wv, *refs):
-    parts, refs = refs[: plan.spread], refs[plan.spread :]
-    back, out, total, held, sems = refs
+    parts, (back, out, product) = refs[: plan.spread], refs[plan.spread :]
     me = place[0]
     part = me // plan.rest
-    kind = pl.program_id(0)
-    wait = fetch((wq, wk, wv), held, sems, kind)
-
-    @pl.when(kind < 2)
+    wide = plan.heads * HEAD
+
+    @pl.when(pl.program_id(0) == 0)
     def _():
         for slot in range(plan.slots):
             depth = depth_of(parent, me * plan.slots + slot)
@@ -378,53 +419,44 @@
             cos, sin = cosine[table, :], sine[table, :]
             rows = slice(slot * BLOCK, (slot + 1) * BLOCK)
             for d in range(plan.spread):
-                value = parts[d][0, rows, :].astype(F32)
-                value = value * cos - pltpu.roll(value, HEAD // 2, 1) * sin
-                columns = pl.ds(pl.multiple_of((part ^ d) * HEAD, HEAD), HEAD)
-                out[rows, columns] = value.astype(LOW)
-
-    @pl.when(kind == 2)
-    def _():
-        for d in range(plan.spread):
-            columns = pl.ds(pl.multiple_of((part ^ d) * HEAD, HEAD), HEAD)
-            out[:, columns] = parts[d][0]
-
-    wait()
-    product = dot_nt(out[...], held[kind])
-
-    @pl.when(kind == 0)
-    def _():
-        total[...] = product
-
-    @pl.when(kind == 1)
-    def _():
-        total[...] += product
-
-    @pl.when(kind == 2)
-    def _():
-        back[...] = (total[...] + product).astype(LOW)
+                for kind in range(3):
+                    value = parts[d][kind, rows, :]
+                    if kind < 2:
+                        value = value.astype(F32)
+                        value = value * cos - pltpu.roll(value, HEAD // 2, 1) * sin
+                    at = pl.multiple_of((kind * plan.heads + (part ^ d)) * HEAD, HEAD)
+                    out[rows, pl.ds(at, HEAD)] = value.astype(LOW)
+
+    total = 0.0
+    for kind, w in enumerate((wq, wk, wv)):
+        total = total + dot_nt(out[:, kind * wide : (kind + 1) * wide], w[...])
+    product[...] = total
+    for device in range(plan.tensor):
+        for group in range(plan.groups):
+            source = (group * plan.tensor + device) * plan.share
+            target = (device * plan.groups + group) * plan.share
+            back[target : target + plan.share, :] = product[
+                source : source + plan.share, :
+            ].astype(LOW)
 
 
 def turn_back(plan, slot_parent, place, cosine, sine, weights, parts):
     whole = lambda i, *_: (0, 0)
     wide = plan.heads * HEAD
+    tile = min(512, plan.width)
     return pl.pallas_call(
         functools.partial(turn_back_kernel, plan),
         grid_spec=pltpu.PrefetchScalarGridSpec(
             num_scalar_prefetch=2,
-            grid=(3,),
+            grid=(plan.width // tile,),
             in_specs=[pl.BlockSpec((CHAIN * BLOCK, HEAD), whole)] * 2
-            + [pl.BlockSpec(memory_space=pl.ANY)] * 3
-            + [pl.BlockSpec((1, plan.rows, HEAD), lambda i, *_: (i, 0, 0))] * plan.spread,
+            + [pl.BlockSpec((tile, wide), lambda i, *_: (i, 0))] * 3
+            + [pl.BlockSpec((3, plan.rows, HEAD), lambda i, *_: (0, 0, 0))] * plan.spread,
             out_specs=[
-                pl.BlockSpec((plan.rows, plan.width), whole),
-                pl.BlockSpec((plan.rows, wide), lambda i, *_: (0, i)),
+                pl.BlockSpec((plan.rows, tile), lambda i, *_: (0, i)),
+                pl.BlockSpec((plan.rows, 3 * wide), whole),
             ],
-            scratch_shapes=[
-                pltpu.VMEM((plan.rows, plan.width), F32),
-                pltpu.VMEM((3, plan.width, wide), LOW),
-                pltpu.SemaphoreType.DMA((3,)),
-            ],
+            scratch_shapes=[pltpu.VMEM((plan.rows, tile), F32)],
         ),
         out_shape=[shape((plan.rows, plan.width), LOW), shape((plan.rows, 3 * wide), LOW)],
         compiler_params=params(60),
@@ -445,30 +477,32 @@
     normed[...] = layer_norm(total)[0].astype(LOW)
 
 
-def project_out(plan, place, tokens, att, near, far):
+def project_out(plan, place, group, tokens, att, near, far):
     half = plan.heads * HEAD // 2
+    count = 2
+    rows = plan.part // count
     weights = pl.BlockSpec(
         (plan.tensor, half, plan.width),
         lambda i, *_: (0, 0, 0),
         pipeline_mode=pl.Buffered(buffer_count=1),
     )
-    rows = pl.BlockSpec((BLOCK, plan.width), lambda i, *_: (i, 0))
+    out = pl.BlockSpec((rows, plan.width), lambda i, *_: (i, 0))
     return pl.pallas_call(
         functools.partial(out_kernel, plan),
         grid_spec=pltpu.PrefetchScalarGridSpec(
             num_scalar_prefetch=1,
-            grid=(plan.slots,),
+            grid=(count,),
             in_specs=[
-                rows,
-                pl.BlockSpec((plan.tensor, BLOCK, 2 * half), lambda i, *_: (0, i, 0)),
+                pl.BlockSpec((rows, plan.width), lambda i, *_: (group * count + i, 0)),
+                pl.BlockSpec((plan.tensor, rows, 2 * half), lambda i, *_: (0, i, 0)),
                 weights,
                 weights,
             ],
-            out_specs=[rows, rows],
+            out_specs=[out, out],
         ),
-        out_shape=[shape((plan.rows, plan.width), F32), shape((plan.rows, plan.width), LOW)],
-        compiler_params=params(40),
-        cost_estimate=about(13),
+        out_shape=[shape((plan.part, plan.width), F32), shape((plan.part, plan.width), LOW)],
+        compiler_params=params(60),
+        cost_estimate=about(7),
         name="project_out",
     )(place, tokens, att, near, far)
 
@@ -477,16 +511,16 @@
     out[...] = dot_nt(cot[...], wd[...])
 
 
-def grad_hidden_of(cot, wd, part):
+def grad_hidden_of(cot, wd):
     rows, width = cot.shape
-    ff = wd.shape[0] // 2
+    ff = wd.shape[0]
     tile = min(512, ff)
     return pl.pallas_call(
         grad_hidden_kernel,
         grid=(ff // tile,),
         in_specs=[
             pl.BlockSpec((rows, width), lambda i: (0, 0)),
-            pl.BlockSpec((tile, width), lambda i: (part * (ff // tile) + i, 0)),
+            pl.BlockSpec((tile, width), lambda i: (i, 0)),
         ],
         out_specs=pl.BlockSpec((rows, tile), lambda i: (0, i)),
         out_shape=shape((rows, ff), F32),
@@ -496,185 +530,212 @@
     )(cot, wd)
 
 
-def ff_kernel(plan, place, normed, seed, late_seed, wg, wu, *refs):
-    back, hidden, grad_gate, grad_up, total = refs
-    step = pl.program_id(0)
-    gate = dot(normed[...], wg[...])
-    up = dot(normed[...], wu[...])
-    grad_hidden = jnp.where(step < pl.num_programs(0) // 2, seed[...], late_seed[...])
-    s = 1.0 / (1.0 + jnp.exp(-gate))
-    active = gate * s
-    hidden[...] = (active * up).astype(LOW)
-    gu = (grad_hidden * active).astype(LOW)
-    gg = (grad_hidden * up * s * (1.0 + gate * (1.0 - s))).astype(LOW)
-    grad_up[...] = gu
-    grad_gate[...] = gg
-    part = dot_nt(gg, wg[...]) + dot_nt(gu, wu[...])
-
-    @pl.when(step == 0)
-    def _():
-        total[...] = part
-
-    @pl.when(step > 0)
-    def _():
-        total[...] += part
-
-    @pl.when(step == pl.num_programs(0) - 1)
-    def _():
-        back[...] = total[...].astype(LOW)
-
-
-def feed_forward(plan, place, normed, seeds, wg, wu):
+def ff_kernel(tile, normed, seed, wg, wu, back, hidden, grad_gate, grad_up, *scratch):
+    gate_held, up_held, results, total, in_sems, out_sems = scratch
+    count = wg.shape[1] // tile
+    spans = [slice(index * tile, (index + 1) * tile) for index in range(count)]
+    arrivals = [
+        [
+            pltpu.make_async_copy(w.at[:, span], held.at[:, span], in_sems.at[which, index])
+            for which, (w, held) in enumerate(((wg, gate_held), (wu, up_held)))
+        ]
+        for index, span in enumerate(spans)
+    ]
+    departures = [
+        [
+            pltpu.make_async_copy(
+                results.at[which, :, span], out.at[:, span], out_sems.at[which, index]
+            )
+            for which, out in enumerate((hidden, grad_gate, grad_up))
+        ]
+        for index, span in enumerate(spans)
+    ]
+    for pair in arrivals:
+        for copy in pair:
+            copy.start()
+    for index, span in enumerate(spans):
+        for copy in arrivals[index]:
+            copy.wait()
+        gate = dot(normed[...], gate_held[:, span])
+        up = dot(normed[...], up_held[:, span])
+        grad_hidden = seed[:, span]
+        s = 1.0 / (1.0 + jnp.exp(-gate))
+        active = gate * s
+        gu = (grad_hidden * active).astype(LOW)
+        gg = (grad_hidden * up * s * (1.0 + gate * (1.0 - s))).astype(LOW)
+        results[0, :, span] = (active * up).astype(LOW)
+        results[1, :, span] = gg
+        results[2, :, span] = gu
+        for copy in departures[index]:
+            copy.start()
+        part = dot_nt(gg, gate_held[:, span]) + dot_nt(gu, up_held[:, span])
+        if index == 0:
+            total[...] = part
+        elif index < count - 1:
+            total[...] += part
+        else:
+            back[...] = (total[...] + part).astype(LOW)
+    for triple in departures:
+        for copy in triple:
+            copy.wait()
+
+
+def feed_forward(plan, place, group, normed, seed, wg, wu):
     rows, width = normed.shape
     ff = wg.shape[1]
-    tile = min(512, ff)
-    whole = pl.BlockSpec(
-        (rows, width), lambda i, *_: (0, 0), pipeline_mode=pl.Buffered(buffer_count=1)
-    )
-    count = ff // tile
-    across = pl.BlockSpec((width, tile), lambda i, *_: (0, i))
-    out = pl.BlockSpec((rows, tile), lambda i, *_: (0, i))
-    back = pl.BlockSpec((rows, width), lambda i, *_: (0, 0))
-    return pl.pallas_call(
-        functools.partial(ff_kernel, plan),
-        grid_spec=pltpu.PrefetchScalarGridSpec(
-            num_scalar_prefetch=1,
-            grid=(ff // tile,),
-            in_specs=[
-                whole,
-                pl.BlockSpec((rows, tile), lambda i, *_: (0, jnp.minimum(i, count // 2 - 1))),
-                pl.BlockSpec((rows, tile), lambda i, *_: (0, jnp.maximum(i - count // 2, 0))),
-                across,
-                across,
-            ],
-            out_specs=[back, out, out, out],
-            scratch_shapes=[pltpu.VMEM((rows, width), F32)],
-        ),
+    tile = min(512, ff // 2)
+    whole = pl.BlockSpec((rows, width), lambda i: (0, 0))
+    anywhere = pl.BlockSpec(memory_space=pl.ANY)
+    return pl.pallas_call(
+        functools.partial(ff_kernel, tile),
+        grid=(1,),
+        in_specs=[whole, pl.BlockSpec((rows, ff), lambda i: (group, 0)), anywhere, anywhere],
+        out_specs=[whole, anywhere, anywhere, anywhere],
         out_shape=[shape((rows, width), LOW)] + [shape((rows, ff), LOW)] * 3,
+        scratch_shapes=[
+            pltpu.VMEM((width, ff), LOW),
+            pltpu.VMEM((width, ff), LOW),
+            pltpu.VMEM((3, rows, ff), LOW),
+            pltpu.VMEM((rows, width), F32),
+            pltpu.SemaphoreType.DMA((2, ff // tile)),
+            pltpu.SemaphoreType.DMA((3, ff // tile)),
+        ],
         compiler_params=params(62),
-        cost_estimate=about(32),
+        cost_estimate=about(17),
         name="feed_forward",
-    )(place, normed, *seeds, wg, wu)
-
-
-def down_kernel(hidden, w, out):
-    out[...] = dot(hidden[...], w[...]).astype(LOW)
-
-
-def project_down(hidden, w):
-    rows, ff = hidden.shape
-    width = w.shape[1]
+    )(normed, seed, wg, wu)
+
+
+def down_kernel(plan, *refs):
+    hiddens, (w, out) = refs[: plan.groups], refs[plan.groups :]
+    for group, hidden in enumerate(hiddens):
+        rows = slice(group * plan.part, (group + 1) * plan.part)
+        out[rows, :] = dot(hidden[...], w[...]).astype(LOW)
+
+
+def project_down(plan, hiddens, w):
+    ff, width = w.shape
     tile = min(512, width)
     return pl.pallas_call(
-        down_kernel,
+        functools.partial(down_kernel, plan),
         grid=(width // tile,),
-        in_specs=[
-            pl.BlockSpec((rows, ff), lambda i: (0, 0)),
-            pl.BlockSpec((ff, tile), lambda i: (0, i)),
-        ],
-        out_specs=pl.BlockSpec((rows, tile), lambda i: (0, i)),
-        out_shape=shape((rows, width), LOW),
+        in_specs=[pl.BlockSpec((plan.part, ff), lambda i: (0, 0))] * plan.groups
+        + [pl.BlockSpec((ff, tile), lambda i: (0, i))],
+        out_specs=pl.BlockSpec((plan.rows, tile), lambda i: (0, i)),
+        out_shape=shape((plan.rows, width), LOW),
         compiler_params=params(60),
         cost_estimate=about(11),
         name="project_down",
-    )(hidden, w)
-
-
-def branch_back_kernel(plan, place, part, middle, cot, near, far, grad_middle, low, *refs):
-    outs, held = refs[:-1], refs[-1]
-    step = pl.program_id(0)
-
-    @pl.when(step == 0)
-    def _():
-        normed, inverse = layer_norm(middle[...])
-        grad = cot[...].astype(F32) + norm_back(part[...].astype(F32), normed, inverse)
-        grad_middle[...] = grad
-        held[...] = grad.astype(LOW)
-        low[...] = held[...]
-
-    core = place[0] % 2
-    half = near.shape[1]
-    for side, w in ((core, near), (1 - core, far)):
-        columns = pl.ds(pl.multiple_of(side * half, half), half)
-        product = dot_nt(held[...], w[0]).astype(LOW)
-        for shift in range(plan.tensor):
-
-            @pl.when(step == shift)
-            def _():
-                outs[shift][:, columns] = product
-
-
-def branch_back(plan, place, part, middle, cot, near, far):
+    )(*hiddens, w)
+
+
+def branch_back_kernel(plan, place, *refs):
+    count = plan.groups
+    parts, middles, cots = refs[:count], refs[count : 2 * count], refs[2 * count : 3 * count]
+    near, far, grad_middle, low = refs[3 * count : 3 * count + 4]
+    outs, (near_held, far_held, sems) = refs[3 * count + 4 : -3], refs[-3:]
+    core, z = place[0] % 2, place[1]
     half = plan.heads * HEAD // 2
-    own = pl.BlockSpec((plan.own, plan.width), lambda i, place: (place[1], 0))
-    mine = pl.BlockSpec((plan.own, plan.width), lambda i, *_: (0, 0))
-    weights = pl.BlockSpec(
-        (1, half, plan.width), lambda i, place: (lax.rem(place[1] + i, plan.tensor), 0, 0)
-    )
+    sides = ((core, near, near_held), (1 - core, far, far_held))
+    copies = [
+        [
+            pltpu.make_async_copy(
+                w.at[lax.rem(z + shift, plan.tensor)], held.at[shift], sems.at[index, shift]
+            )
+            for index, (_, w, held) in enumerate(sides)
+        ]
+        for shift in range(plan.tensor)
+    ]
+    for pair in copies:
+        for copy in pair:
+            copy.start()
+    for group in range(count):
+        rows = slice(group * plan.share, (group + 1) * plan.share)
+        normed, inverse = layer_norm(middles[group][...])
+        back = norm_back(parts[group][...].astype(F32), normed, inverse)
+        grad = cots[group][...].astype(F32) + back
+        grad_middle[rows, :] = grad
+        low[rows, :] = grad.astype(LOW)
+    for shift in range(plan.tensor):
+        for copy, (side, _, held) in zip(copies[shift], sides):
+            copy.wait()
+            columns = pl.ds(pl.multiple_of(side * half, half), half)
+            outs[shift][:, columns] = dot_nt(low[...], held[shift]).astype(LOW)
+
+
+def branch_back(plan, place, parts, middles, cot, near, far):
+    half = plan.heads * HEAD // 2
+    own = pl.BlockSpec((plan.own, plan.width), lambda i, *_: (0, 0))
+    share = pl.BlockSpec((plan.share, plan.width), lambda i, *_: (0, 0))
+    anywhere = pl.BlockSpec(memory_space=pl.ANY)
     return pl.pallas_call(
         functools.partial(branch_back_kernel, plan),
         grid_spec=pltpu.PrefetchScalarGridSpec(
             num_scalar_prefetch=1,
-            grid=(plan.tensor,),
-            in_specs=[mine, own, own, weights, weights],
-            out_specs=[mine, mine]
+            grid=(1,),
+            in_specs=[share] * plan.groups
+            + [plan.own_part()] * plan.groups
+            + [plan.own_rows(group) for group in range(plan.groups)]
+            + [anywhere, anywhere],
+            out_specs=[own, own]
             + [pl.BlockSpec((plan.own, 2 * half), lambda i, *_: (0, 0))] * plan.tensor,
-            scratch_shapes=[pltpu.VMEM((plan.own, plan.width), LOW)],
+            scratch_shapes=[pltpu.VMEM((plan.tensor, half, plan.width), LOW)] * 2
+            + [pltpu.SemaphoreType.DMA((2, plan.tensor))],
         ),
         out_shape=[shape((plan.own, plan.width), F32), shape((plan.own, plan.width), LOW)]
         + [shape((plan.own, 2 * half), LOW)] * plan.tensor,
         compiler_params=params(60),
         cost_estimate=about(9),
         name="branch_back",
-    )(place, part, middle, cot, near, far)
-
-
-def tokens_back_kernel(place, part, tokens, grad_middle, out):
-    normed, inverse = layer_norm(tokens[...].astype(F32))
-    back = norm_back(part[...].astype(F32), normed, inverse)
-    out[...] = (grad_middle[...] + back).astype(LOW)
+    )(place, *parts, *middles, *([cot] * plan.groups), near, far)
+
+
+def tokens_back_kernel(plan, place, part, *refs):
+    tokens, (grad_middle, out) = refs[: plan.groups], refs[plan.groups :]
+    for group in range(plan.groups):
+        rows = slice(group * plan.share, (group + 1) * plan.share)
+        normed, inverse = layer_norm(tokens[group][...].astype(F32))
+        back = norm_back(part[rows, :].astype(F32), normed, inverse)
+        out[rows, :] = (grad_middle[rows, :] + back).astype(LOW)
 
 
 def tokens_back(plan, place, part, tokens, grad_middle):
-    mine = pl.BlockSpec((plan.own, plan.width), lambda i, *_: (0, 0))
-    return pl.pallas_call(
-        tokens_back_kernel,
+    own = pl.BlockSpec((plan.own, plan.width), lambda i, *_: (0, 0))
+    return pl.pallas_call(
+        functools.partial(tokens_back_kernel, plan),
         grid_spec=pltpu.PrefetchScalarGridSpec(
             num_scalar_prefetch=1,
             grid=(1,),
-            in_specs=[
-                mine,
-                pl.BlockSpec((plan.own, plan.width), lambda i, place: (place[1], 0)),
-                mine,
-            ],
-            out_specs=mine,
+            in_specs=[own] + [plan.own_rows(group) for group in range(plan.groups)] + [own],
+            out_specs=own,
         ),
         out_shape=shape((plan.own, plan.width), LOW),
         compiler_params=params(60),
         cost_estimate=about(4),
         name="tokens_back",
-    )(place, part, tokens, grad_middle)
-
-
-def joined_rows(plan, place, parts, held):
-    if len(parts) == 1:
-        return parts[0][...]
-    for shift, part in enumerate(parts):
-        origin = lax.rem(place[1] - shift + plan.tensor, plan.tensor)
-        held[pl.ds(pl.multiple_of(origin * plan.own, 16), plan.own), :] = part[...]
-    return held[...]
-
-
-def away_kernel(plan, count, place, *refs):
-    lhs, (rhs, out, held) = refs[:count], refs[count:]
-    out[...] = dot_tn(joined_rows(plan, place, lhs, held), rhs[...]).astype(LOW)
+    )(place, part, *([tokens] * plan.groups), grad_middle)
+
+
+def products(lhs, rhs):
+    total, start = 0.0, 0
+    for index, right in enumerate(rhs):
+        rows = right.shape[0]
+        left = lhs[index][...] if len(lhs) > 1 else lhs[0][start : start + rows, :]
+        total = total + dot_tn(left, right[...])
+        start += rows
+    return total
+
+
+def away_kernel(count, place, *refs):
+    lhs, rhs, out = refs[:count], refs[count:-1], refs[-1]
+    out[...] = products(lhs, rhs).astype(LOW)
 
 
 def wgrad_away(plan, place, lhs, rhs):
-    rows, columns = rhs.shape
+    columns = rhs[0].shape[1]
     piece, count = plan.piece, plan.dp // 2
     return pl.pallas_call(
-        functools.partial(away_kernel, plan, len(lhs)),
+        functools.partial(away_kernel, len(lhs)),
         grid_spec=pltpu.PrefetchScalarGridSpec(
             num_scalar_prefetch=1,
             grid=(count,),
@@ -682,22 +743,21 @@
                 pl.BlockSpec((part.shape[0], piece), lambda i, place: (0, place[2 + i] ^ 1))
                 for part in lhs
             ]
-            + [pl.BlockSpec((rows, columns), lambda i, *_: (0, 0))],
+            + [pl.BlockSpec(part.shape, lambda i, *_: (0, 0)) for part in rhs],
             out_specs=pl.BlockSpec((piece, columns), lambda i, *_: (i, 0)),
-            scratch_shapes=[pltpu.VMEM((rows, piece), LOW)],
         ),
         out_shape=shape((count * piece, columns), LOW),
         compiler_params=params(60),
         cost_estimate=about(8),
         name="wgrad_away",
-    )(place, *lhs, rhs)
-
-
-def keep_kernel(plan, arrays, count, place, *refs):
-    lhs, (rhs, recv, a_keep, a_send, b_keep, b_send, held) = refs[:arrays], refs[arrays:]
+    )(place, *lhs, *rhs)
+
+
+def keep_kernel(arrays, count, place, *refs):
+    lhs, rhs = refs[:arrays], refs[arrays:-5]
+    recv, a_keep, a_send, b_keep, b_send = refs[-5:]
     step = pl.program_id(0)
-    product = dot_tn(joined_rows(plan, place, lhs, held), rhs[...])
-    total = (product + recv[...].astype(F32)).astype(LOW)
+    total = (products(lhs, rhs) + recv[...].astype(F32)).astype(LOW)
     half = total.shape[1] // 2
 
     @pl.when(step < count // 2)
@@ -718,12 +778,12 @@
 
 
 def wgrad_keep(plan, place, lhs, rhs, recv):
-    rows, columns = rhs.shape
+    columns = rhs[0].shape[1]
     piece, count = plan.piece, plan.dp // 2
     half = count // 2
     block = lambda index: pl.BlockSpec((piece, columns // 2), index)
     return pl.pallas_call(
-        functools.partial(keep_kernel, plan, len(lhs), count),
+        functools.partial(keep_kernel, len(lhs), count),
         grid_spec=pltpu.PrefetchScalarGridSpec(
             num_scalar_prefetch=1,
             grid=(count,),
@@ -731,23 +791,20 @@
                 pl.BlockSpec((part.shape[0], piece), lambda i, place: (0, place[2 + i]))
                 for part in lhs
             ]
-            + [
-                pl.BlockSpec((rows, columns), lambda i, *_: (0, 0)),
-                pl.BlockSpec((piece, columns), lambda i, *_: (i, 0)),
-            ],
+            + [pl.BlockSpec(part.shape, lambda i, *_: (0, 0)) for part in rhs]
+            + [pl.BlockSpec((piece, columns), lambda i, *_: (i, 0))],
             out_specs=[
                 block(lambda i, *_: (jnp.minimum(i, half - 1), 0)),
                 block(lambda i, *_: (jnp.maximum(i - half, 0), 0)),
                 block(lambda i, *_: (i // 2, 0)),
                 block(lambda i, *_: (i // 2, 0)),
             ],
-            scratch_shapes=[pltpu.VMEM((rows, piece), LOW)],
         ),
         out_shape=[shape((half * piece, columns // 2), LOW)] * 4,
         compiler_params=params(60),
         cost_estimate=about(9),
         name="wgrad_keep",
-    )(place, *lhs, rhs, recv)
+    )(place, *lhs, *rhs, recv)
 
 
 def stage_kernel(piece, a, a_got, b, b_got, a_keep, a_send, b_keep, b_send):
@@ -800,6 +857,53 @@
     )(*arrays)
 
 
+def split_kernel(*refs):
+    arrays, outs, held = refs[:4], refs[4:-1], refs[-1]
+    finish_kernel(False, *arrays, held)
+    width = outs[0].shape[1]
+    for index, out in enumerate(outs):
+        out[...] = held[:, index * width : (index + 1) * width]
+
+
+def wgrad_finish_split(*arrays):
+    piece, half = arrays[0].shape
+    return pl.pallas_call(
+        split_kernel,
+        out_shape=[shape((piece, 2 * half // 3), F32)] * 3,
+        scratch_shapes=[pltpu.VMEM((piece, 2 * half), F32)],
+        compiler_params=params(60),
+        cost_estimate=about(3),
+        name="wgrad_finish_split",
+    )(*arrays)
+
+
+def chunks_kernel(plan, place, *refs):
+    arrays, chunks, held = refs[:4], refs[4:-1], refs[-1]
+    finish_kernel(True, *arrays, held)
+    rows = plan.heads * HEAD
+    for index, chunk in enumerate(chunks):
+        chunk[...] = held[ring_rows(plan, place, index, rows), :].astype(LOW)
+
+
+def wgrad_finish_chunks(plan, place, *arrays):
+    piece, half = arrays[0].shape
+    rows = plan.heads * HEAD
+    return pl.pallas_call(
+        functools.partial(chunks_kernel, plan),
+        grid_spec=pltpu.PrefetchScalarGridSpec(
+            num_scalar_prefetch=1,
+            grid=(1,),
+            in_specs=[pl.BlockSpec((piece, half), lambda i, *_: (0, 0))] * 4,
+            out_specs=[pl.BlockSpec((rows, piece), lambda i, *_: (0, 0))] * plan.tensor,
+            scratch_shapes=[pltpu.VMEM((2 * half, piece), F32)],
+        ),
+        out_shape=[shape((rows, piece), LOW)] * plan.tensor,
+        compiler_params=params(60),
+        cost_estimate=about(4),
+        name="wgrad_finish_chunks",
+    )(place, *arrays)
+
+
 def tie(values, *others):
     many = isinstance(values, (list, tuple))
     held = lax.optimization_barrier((tuple(values) if many else (values,)) + others)
@@ -807,7 +911,8 @@
 
 
 class WeightGradient:
-    def __init__(self, plan, place, chain, lhs, rhs, turned=False):
+    def __init__(self, plan, place, chain, lhs, rhs, turned=False, chunks=False, split=False):
+        self.chunks, self.split = chunks, split
         self.plan, self.place, self.chain = plan, place, chain
         self.lhs, self.rhs, self.turned = lhs, rhs, turned
         self.stage = 0
@@ -816,7 +921,9 @@
         return lax.ppermute(array, "dp", xor_pairs(self.plan.dp, 1 << bit))
 
     def away(self):
-        sent = self.chain.run(lambda r: wgrad_away(self.plan, self.place, self.lhs, r), self.rhs)
+        sent = self.chain.run(
+            lambda *r: wgrad_away(self.plan, self.place, self.lhs, r), *self.rhs
+        )
         self.recv = self.swap(sent, 0)
 
     def keep(self):
@@ -833,6 +940,9 @@
 
     def wait(self):
         self.a_got, self.b_got = self.chain.wait(self.a_got, self.b_got)
+
+    def took(self):
+        self.recv = self.chain.wait(self.recv)
 
     def add(self):
         self.a_keep, self.a_send, self.b_keep, self.b_send = self.chain.run(
@@ -848,7 +958,13 @@
             self.add()
             self.send()
         return self.chain.run(
-            lambda *p: wgrad_finish(self.turned, *p),
+            lambda *p: (
+                wgrad_finish_chunks(self.plan, self.place, *p)
+                if self.chunks
+                else wgrad_finish_split(*p)
+                if self.split
+                else wgrad_finish(self.turned, *p)
+            ),
             self.a_keep,
             self.a_got,
             self.b_keep,
@@ -857,6 +973,8 @@
 
 
 class Chain:
+    weight = 1.0
+
     def __init__(self, last):
         self.last = last
 
@@ -876,23 +994,83 @@
         return out
 
 
-def add_kernel(middle, part, out):
-    out[...] = (middle[...] + part[...].astype(F32)).astype(LOW)
-
-
-def add_residual(middle, part):
-    rows, width = middle.shape
-    block = pl.BlockSpec((rows // 4, width), lambda i: (i, 0))
-    return pl.pallas_call(
-        add_kernel,
-        grid=(4,),
-        in_specs=[block, block],
+def shifted(plan, array, shift):
+    pairs = [(i, (i + shift) % plan.tensor) for i in range(plan.tensor)]
+    return lax.ppermute(array, "tensor", pairs)
+
+
+class RingSum:
+    def __init__(self, plan, chain, chunks):
+        self.plan, self.chain, self.chunks, self.at = plan, chain, chunks, 1
+        self.moving = shifted(plan, chunks[0], 1)
+
+    def step(self):
+        if self.at < self.plan.tensor - 1:
+            got, mine = self.chain.wait(self.moving, self.chunks[self.at])
+            total = (got.astype(F32) + mine.astype(F32)).astype(LOW)
+            self.chain.last = total
+            self.moving = shifted(self.plan, total, 1)
+            self.at += 1
+
+    def finish(self):
+        while self.at < self.plan.tensor - 1:
+            self.step()
+        return self.moving, self.chunks[-1]
+
+
+def ring_rows(plan, place, step, rows):
+    chunk = lax.rem(place[1] + (2 * plan.tensor - 1 - step), plan.tensor)
+    return pl.ds(pl.multiple_of(chunk * rows, 16), rows)
+
+
+def add_last_kernel(a, b, out):
+    out[...] = a[...].astype(F32) + b[...].astype(F32)
+
+
+def add_last(a, b):
+    return pl.pallas_call(
+        add_last_kernel,
+        out_shape=shape(a.shape, F32),
+        compiler_params=params(60),
+        cost_estimate=about(2),
+        name="add_last",
+    )(a, b)
+
+
+def add_kernel(plan, *refs):
+    middles, (part, out) = refs[: plan.groups], refs[plan.groups :]
+    step = pl.program_id(0)
+    for group, middle in enumerate(middles):
+
+        @pl.when(step // 2 == group)
+        def _():
+            out[...] = (middle[...] + part[...].astype(F32)).astype(LOW)
+
+
+def add_residual(plan, middles, part):
+    rows = plan.part // 2
+    block = pl.BlockSpec((rows, plan.width), lambda i: (i, 0))
+    return pl.pallas_call(
+        functools.partial(add_kernel, plan),
+        grid=(2 * plan.groups,),
+        in_specs=[
+            pl.BlockSpec(
+                (rows, plan.width),
+                lambda i, group=group: (jnp.clip(i - 2 * group, 0, 1), 0),
+            )
+            for group in range(plan.groups)
+        ]
+        + [block],
         out_specs=block,
-        out_shape=shape((rows, width), LOW),
+        out_shape=shape((plan.rows, plan.width), LOW),
         compiler_params=params(60),
         cost_estimate=about(6),
         name="add_residual",
-    )(middle, part)
+    )(*middles, part)
+
+
+class State:
+    pass
 
 
 def body(mesh, tokens, w_query, w_key, w_value, w_out, w_gate, w_up, w_down, cotangent, slot_parent):
@@ -910,11 +1088,6 @@
     def exchange(parts):
         return [parts[0]] + [swap(parts[d], d * plan.rest) for d in range(1, n)]
 
-    def shifted(array, shift):
-        return lax.ppermute(
-            array, "tensor", [(i, (i + shift) % plan.tensor) for i in range(plan.tensor)]
-        )
-
     half = w_out.shape[0] // 2
     mine = lax.dynamic_slice_in_dim(w_out, (me % 2) * half, half, 0)
     near = lax.all_gather(mine, "tensor", axis=0, tiled=False)
@@ -924,132 +1097,207 @@
     )
     chain = Chain(normed_one)
     parts = exchange(sends)
-    seeds = [chain.run(lambda cot: grad_hidden_of(cot, w_down, 0), cotangent)]
+    seed = chain.run(lambda cot: grad_hidden_of(cot, w_down), cotangent)
     parts = chain.wait(*parts)
     kv = jnp.stack([part[1:] for part in parts])[None]
     mask = 1
     while mask < plan.rest:
         kv = jnp.concatenate([kv, swap(kv, mask)], axis=0)
         mask *= 2
-    seeds.append(chain.run(lambda cot: grad_hidden_of(cot, w_down, 1), cotangent))
     kv = chain.wait(kv.reshape(plan.dp * 2 * plan.slots, BLOCK, HEAD))
     attended_parts = exchange(chain.run(lambda *p: attend(plan, slot_parent, place, p, kv), *parts))
     attended = chain.run(lambda *p: gather_heads(plan, place, p), *attended_parts)
-    everyone = lax.all_gather(tie(attended, near), "tensor", axis=0, tiled=False)
+    everyone = [
+        lax.all_gather(tie(part, near), "tensor", axis=0, tiled=False) for part in attended
+    ]
     near = chain.after(near)
     far = swap(near, 1)
-    middle, normed_two = chain.run(
-        lambda e, f: project_out(plan, place, tokens, e, near, f), everyone, far
-    )
-
-    partial_two, hidden, grad_gate_proj, grad_up_proj = chain.run(
-        lambda v: feed_forward(plan, place, v, seeds, w_gate, w_up), normed_two
-    )
-    grad_normed_two = lax.psum_scatter(partial_two, "tensor", scatter_dimension=0, tiled=True)
+
+    middles, normed_two, hidden, grad_gate_proj, grad_up_proj, grad_normed_two = ([] for _ in range(6))
+    for group in range(plan.groups):
+        middle, normed = chain.run(
+            lambda e, f: project_out(plan, place, group, tokens, e, near, f), everyone[group], far
+        )
+        partial_two, *rest = chain.run(
+            lambda v: feed_forward(plan, place, group, v, seed, w_gate, w_up), normed
+        )
+        grad_normed_two.append(
+            lax.psum_scatter(partial_two, "tensor", scatter_dimension=0, tiled=True)
+        )
+        middles.append(middle)
+        normed_two.append(normed)
+        for held, value in zip((hidden, grad_gate_proj, grad_up_proj), rest):
+            held.append(value)
+    state = State()
     down = WeightGradient(plan, place, chain, [cotangent], hidden, turned=True)
-    gate = WeightGradient(plan, place, chain, [normed_two], grad_gate_proj)
-    up = WeightGradient(plan, place, chain, [normed_two], grad_up_proj)
+    gate = WeightGradient(plan, place, chain, normed_two, grad_gate_proj)
+    up = WeightGradient(plan, place, chain, normed_two, grad_up_proj)
+    out = WeightGradient(plan, place, chain, None, None, chunks=True)
+    qkv = WeightGradient(plan, place, chain, None, None, split=True)
+
+    def own():
+        state.own = jnp.concatenate(
+            [
+                lax.dynamic_slice_in_dim(part, z * plan.share, plan.share, 1)
+                .transpose(1, 0, 2)
+                .reshape(plan.share, plan.width)
+                for part in map(chain.after, everyone)
+            ]
+        )
+
+    def branch():
+        grad_middle, grad_branch, *chunks = chain.run(
+            lambda *g: branch_back(plan, place, g, middles, cotangent, near, far),
+            *grad_normed_two,
+        )
+        state.sources = [chunks[0]] + [
+            shifted(plan, chunks[shift], shift) for shift in range(1, plan.tensor)
+        ]
+        state.grad_middle = grad_middle
+        out.lhs, out.rhs = [grad_branch], [state.own]
+
+    def output():
+        branch_out = chain.run(lambda *h: project_down(plan, h, w_down), *hidden)
+        state.part = lax.psum(branch_out, "tensor")
+
+    def scatter():
+        scattered = chain.run(lambda *p: scatter_heads(plan, place, p), *state.sources)
+        state.grads = exchange(scattered)
+
+    def heads():
+        state.grads = chain.wait(*state.grads)
+
+    def attend_step():
+        *state.queries, state.near, state.far = chain.run(
+            lambda *g: attend_back(plan, slot_parent, place, parts, kv, g), *state.grads
+        )
+
+    def sum_far():
+        far_part = chain.after(state.far).reshape(plan.rest - 1, -1, BLOCK, HEAD)
+        mask = plan.rest // 2
+        while mask > 1:
+            got = swap(far_part[mask - 1 : 2 * mask - 1], mask).astype(F32)
+            state.near = state.near + got[0]
+            far_part = (far_part[: mask - 1].astype(F32) + got[1:]).astype(LOW)
+            mask //= 2
+        state.got = swap(far_part.reshape(state.near.shape), 1)
+
+    def sum_near():
+        backs = chain.run(
+            lambda g: combine_back(plan, state.queries, state.near, g), state.got
+        )
+        state.backs = exchange(backs)
+
+    def arrive():
+        state.backs = chain.wait(*state.backs)
+
+    def turn():
+        partial_one, turned = chain.run(
+            lambda *p: turn_back(
+                plan, slot_parent, place, cosine, sine, (w_query, w_key, w_value), p
+            ),
+            *state.backs,
+        )
+        state.one = lax.psum_scatter(partial_one, "tensor", scatter_dimension=0, tiled=True)
+        qkv.lhs, qkv.rhs = [normed_one], [turned]
+
+    def residual():
+        state.output = chain.run(lambda p: add_residual(plan, middles, p), state.part)
+
+    def tokens_step():
+        grad_own = chain.run(
+            lambda g: tokens_back(plan, place, g, tokens, state.grad_middle), state.one
+        )
+        state.tokens = lax.all_gather(grad_own, "tensor", axis=0, tiled=True)
+
+    def gathered():
+        state.tokens = chain.wait(state.tokens)
+
+    def ring_start():
+        state.ring = RingSum(plan, chain, chain.after(*state.out))
+
+    def ring_end():
+        got, mine = chain.wait(*state.ring.finish())
+        state.out = chain.run(add_last, got, mine)
+
+    def ring_step():
+        state.ring.step()
+
     down.away()
     gate.away()
     down.keep()
     down.send()
+    own()
     gate.keep()
+    branch()
+    output()
+    down.wait()
+    scatter()
+    out.away()
+    out.keep()
+    heads()
+    out.send()
+    attend_step()
+    out.wait()
+    sum_far()
+    out.add()
+    sum_near()
+    down.add()
+    up.away()
+    arrive()
     gate.send()
-    up.away()
-    mine_all = lax.dynamic_slice_in_dim(chain.after(everyone), z * plan.own, plan.own, 1)
-    mine_all = mine_all.transpose(1, 0, 2).reshape(plan.own, plan.width)
-    down.wait()
-
-    grad_middle, grad_branch, *chunks = chain.run(
-        lambda g: branch_back(plan, place, g, middle, cotangent, near, far), grad_normed_two
-    )
-    sources = [chunks[0]] + [shifted(chunks[shift], shift) for shift in range(1, plan.tensor)]
-    branch_out = chain.run(lambda h: project_down(h, w_down), hidden)
+    turn()
+    up.took()
+    out.send()
+    qkv.away()
+    up.keep()
     gate.wait()
-    scattered = chain.run(lambda *p: scatter_heads(plan, place, p), *sources)
-    grads = exchange(scattered)
-    output_part = lax.psum(chain.after(branch_out), "tensor")
-    out = WeightGradient(plan, place, chain, [grad_branch], mine_all, turned=True)
-    out.away()
-    down.add()
-    out.keep()
-    grads = chain.wait(*grads)
-    out.send()
-    *grad_queries, grad_near, grad_far = chain.run(
-        lambda *g: attend_back(plan, slot_parent, place, parts, kv, g), *grads
-    )
     out.wait()
-
-    grad_far = chain.after(grad_far).reshape(plan.rest - 1, n, 2, plan.rows, HEAD)
-    grad_near = grad_near.reshape(1, n, 2, plan.rows, HEAD)
-    mask = plan.rest // 2
-    while mask >= 1:
-        got = swap(grad_far[mask - 1 : 2 * mask - 1], mask)
-        if mask == 1:
-            out.add()
-            got = chain.wait(got)
-        got = got.astype(F32)
-        grad_near = grad_near + got[:1]
-        if mask > 1:
-            grad_far = (grad_far[: mask - 1].astype(F32) + got[1:]).astype(LOW)
-        mask //= 2
-    backs = chain.wait(
-        *(
-            jnp.concatenate([grad_queries[d][None], grad_near[0, d].astype(LOW)], axis=0)
-            for d in range(n)
-        )
-    )
-    backs = exchange(backs)
-    up.keep()
+    up.send()
+    state.out = out.finish()
     gate.add()
-    partial_one, turned = chain.run(
-        lambda *p: turn_back(
-            plan, slot_parent, place, cosine, sine, (w_query, w_key, w_value), p
-        ),
-        *backs,
-    )
-    grad_normed_one = lax.psum_scatter(partial_one, "tensor", scatter_dimension=0, tiled=True)
-    out.send()
-    qkv = WeightGradient(plan, place, chain, [normed_one], turned)
-    qkv.away()
-    output = chain.run(lambda p: add_residual(middle, p), output_part)
-    out.wait()
-    out_partial = out.finish().astype(LOW)
+    qkv.keep()
+    residual()
+    ring_start()
     down.send()
-    up.send()
-    qkv.keep()
-    grad_tokens_own = chain.run(
-        lambda g: tokens_back(plan, place, g, tokens, grad_middle), grad_normed_one
-    )
-    grad_tokens = lax.all_gather(grad_tokens_own, "tensor", axis=0, tiled=True)
-    down.wait()
     gate.send()
     up.wait()
+    Chain.weight = 0.03
+    tokens_step()
+    Chain.weight = 1.0
+    state.ring.step()
+    qkv.send()
+    down.wait()
     up.add()
     up.send()
-    grad_down = down.finish()
+    state.down = down.finish()
     gate.wait()
-    qkv.send()
-    grad_gate = gate.finish()
-    up.wait()
-    grad_up = up.finish()
+    Chain.weight = 0.03
+    state.gate = gate.finish()
+    Chain.weight = 1.0
+    state.ring.step()
     qkv.wait()
     qkv.add()
     qkv.send()
-    grad_qkv = qkv.finish()
-    grad_out = lax.psum_scatter(
-        tie(out_partial, grad_tokens), "tensor", scatter_dimension=0, tiled=True
-    ).astype(F32)
+    ring_end()
+    Chain.weight = 100.0
+    state.qkv = qkv.finish()
+    Chain.weight = 1.0
+    state.up = up.finish()
+    grad_tokens = (
+        state.tokens
+        .reshape(plan.tensor, plan.groups, plan.share, plan.width)
+        .transpose(1, 0, 2, 3)
+        .reshape(plan.rows, plan.width)
+    )
     return (
-        output,
+        state.output,
         grad_tokens,
-        grad_qkv[:, :wide],
-        grad_qkv[:, wide : 2 * wide],
-        grad_qkv[:, 2 * wide :],
-        grad_out,
-        grad_gate,
-        grad_up,
-        grad_down,
+        *state.qkv,
+        state.out,
+        state.gate,
+        state.up,
+        state.down,
     )
 
 

time: 545 us -> 510 us (0.936)
  waiting for transfers between devices: 184 us -> 138 us
  Pallas kernels: 270 us -> 286 us
  other arithmetic: 9.63 us -> 2.01 us
    reduce_scatter x2 -> x1, waiting for transfers between devices: 42.4 us -> 18.2 us  [turn(): lax.psum_scatter(partial_one, 'tensor', scatter_dimension=0, tiled=True)]
    pallas_call x14 -> x19, Pallas kernels: 131 us -> 153 us  [the longest x5 46.4 us: wgrad_keep(): pl.pallas_call(functools.partial(keep_kernel, len(lhs), count), grid_spec...]
    all_gather x2 -> x3, waiting for transfers between devices: 54.9 us -> 41.6 us  [the longest x2 38.6 us: body(): lax.all_gather(tie(part, near), 'tensor', axis=0, tiled=False)]
    ppermute x25, waiting for transfers between devices: 47 us -> 34.1 us  [swap(): return lax.ppermute(array, 'dp', xor_pairs(self.plan.dp, 1 << bit))]
    pallas_call x1 -> x2, Pallas kernels: 11.5 us -> 18.5 us  [project_out(): pl.pallas_call(functools.partial(out_kernel, plan), grid_spec=pltpu.Prefe...]
    pallas_call x5 -> x3, Pallas kernels: 15.7 us -> 9.56 us  [wgrad_finish(): pl.pallas_call(functools.partial(finish_kernel, turned), out_shape=shape(...]
    pallas_call x2 -> x1, Pallas kernels: 13.4 us -> 10.4 us  [grad_hidden_of(): pl.pallas_call(grad_hidden_kernel, grid=(ff // tile,), in_specs=[pl.Block...]
    unnamed x44 -> x71, local copies, waits for them, and re-layouts: 11 us -> 9.96 us
  transfers between devices with their start and end apart: 50 -> 54, of which waited for: 24 -> 22; matrix products, arithmetic and copies ran while one was open for 2% -> 1% of each run, Pallas kernels for 42% -> 55%
where the time goes in v3:
time: 510 us; the launch traced here: 503 us
  Pallas kernels  286 us (56%)
  waiting for transfers between devices  138 us (27%)
  starting transfers between devices  44.9 us (9%)
  local copies, waits for them, and re-layouts  16.6 us (3%)
  between operations  14.8 us (3%)
    pallas_call x5, Pallas kernels, wgrad_keep(): pl.pallas_call(functools.partial(keep_kernel, len(lhs), count), grid_spec...  46.4 us
    pallas_call x5, Pallas kernels, wgrad_away(): pl.pallas_call(functools.partial(away_kernel, len(lhs)), grid_spec=pltpu....  39.4 us
    all_gather x2, waiting for transfers between devices, body(): lax.all_gather(tie(part, near), 'tensor', axis=0, tiled=False)  38.6 us
    pallas_call x2, Pallas kernels, feed_forward(): pl.pallas_call(functools.partial(ff_kernel, tile), grid=(1,), in_specs=[w...  35.6 us
    ppermute x25, waiting for transfers between devices, swap(): return lax.ppermute(array, 'dp', xor_pairs(self.plan.dp, 1 << bit))  34.1 us
    ppermute x15, waiting for transfers between devices, swap(): return lax.ppermute(array, 'dp', xor_pairs(plan.dp, mask))  30.7 us
    pallas_call x1, Pallas kernels, attend_back(): pl.pallas_call(functools.partial(attend_back_kernel, plan), grid_spec=plt...  23 us
    ppermute x25, starting transfers between devices, swap(): return lax.ppermute(array, 'dp', xor_pairs(self.plan.dp, 1 << bit))  21.1 us
  transfers between devices with their start and end apart: 54, of which 22 were waited for; matrix products, arithmetic and copies ran while one was open for 1% of the time, Pallas kernels for 55%

profile of v3, /device:TPU:0, one launch (start us, length us, event | category | flops | bytes accessed | tf_op | source)
XLA Modules:
  0.0 502.6 jit_solution(15677660017791700861)
XLA Ops:
  7.2 2.3 constant_dynamic-slice_fusion
  10.2 11.8 %project_qkv.1 = (bf16[640,2048]{1,0:T(8,128)(2,1)}, bf16[3,640,128]{2,1,0:T(8,128)(2,1)}, bf16[3,640,128]{2,1,0:T(8,128)(2,1)}, bf16[3,640,128]{2,1,0:T(8,128)(2,1)}, bf16[3,640,128]{2,1,0:T(8,128)(2,1)}) custom-call(s32[40]{0:T(128)} %parent.7, s32[6]{0:T(128)} %stack.39.place, bf16[640,2048]{1,0:T(8,128)(2,1)} %refs_1_.1, bf16[2048,512]{1,0:T(8,128)(2,1)} %wq.3, ...), custom_call_target="tpu_custom_call" | custom-call | bytes 1 | tf_op jit(solution)/shard_map/project_qkv/pallas_call | solution.py:169
  22.0 2.9 collective-permute-start
  25.0 1.5 collective-permute-start.1
  26.5 10.4 %grad_hidden.1.seed = f32[640,2048]{1,0:T(8,128)} custom-call(bf16[640,2048]{1,0:T(8,128)(2,1)} %refs_5_.1, bf16[2048,2048]{1,0:T(8,128)(2,1)} %refs_2_.1), custom_call_target="tpu_custom_call" | custom-call | bytes 1 | tf_op jit(solution)/shard_map/grad_hidden/pallas_call | solution.py:518
  37.2 11.2 %collective-permute-done.1.refs_2_ = bf16[3,640,128]{2,1,0:T(8,128)(2,1)S(1)} collective-permute-done((bf16[3,640,128]{2,1,0:T(8,128)(2,1)}, bf16[3,640,128]{2,1,0:T(8,128)(2,1)S(1)}, u32[]{:S(2)}, u32[]{:S(2)}) %collective-permute-start.1) | collective-permute-done | bytes 491552 | tf_op jit(solution)/shard_map/ppermute | solution.py:1086
  49.4 3.0 collective-permute-done.3
  52.4 1.7 pad_maximum_fusion
  54.1 12.3 %attend.1 = (bf16[640,128]{1,0:T(8,128)(2,1)}, bf16[640,128]{1,0:T(8,128)(2,1)}, bf16[640,128]{1,0:T(8,128)(2,1)}, bf16[640,128]{1,0:T(8,128)(2,1)}) custom-call(s32[40]{0:T(128)} %parent.7, s32[6]{0:T(128)} %stack.39.place, bf16[3,640,128]{2,1,0:T(8,128)(2,1)} %get-tuple-element.267.refs_0_, bf16[3,640,128]{2,1,0:T(8,128)(2,1)} %copy-done.1, ...), custom_call_target="tpu_custom_call" | custom-call | bytes 1 | tf_op jit(solution)/shard_map/attend/pallas_call | solution.py:247
  70.0 3.8 collective-permute-done.4.refs_1_
  73.7 2.2 collective-permute-done.5.refs_2_
  78.0 2.8 gather_heads.1
  80.8 12.9 %all-gather.10.cloned.1.call-done = bf16[1024,2048]{1,0:T(8,128)(2,1)} async-done(((bf16[256,2048]{1,0:T(8,128)(2,1)}), bf16[1024,2048]{1,0:T(8,128)(2,1)}) %all-gather.10.cloned.1.call-update) | async-done | bytes 4194320 | tf_op jit(solution)/shard_map/all_gather | solution.py:1093
  95.0 32.0 %all-gather.12.cloned.1.call-done = bf16[1280,512]{1,0:T(8,128)(2,1)} async-done(((bf16[320,512]{1,0:T(8,128)(2,1)}), bf16[1280,512]{1,0:T(8,128)(2,1)}) %all-gather.12.cloned.1.call-update) | async-done | bytes 1310736 | tf_op jit(solution)/shard_map/all_gather | solution.py:1111
  127.0 9.2 %project_out.2 = (f32[320,2048]{1,0:T(8,128)}, bf16[320,2048]{1,0:T(8,128)(2,1)}) custom-call(s32[6]{0:T(128)} %stack.39.place, bf16[640,2048]{1,0:T(8,128)(2,1)} %refs_1_.1, bf16[4,320,512]{2,1,0:T(8,128)(2,1)} %bitcast.37, bf16[4,256,2048]{2,1,0:T(8,128)(2,1)} %bitcast.42, bf16[4,256,2048]{2,1,0:T(8,128)(2,1)} %collective-permute-done.7.far.refs_7_), custom_call_target="tpu_custom_call" | custom-call | flops 56000000000 | bytes 1 | tf_op jit(solution)/shard_map/project_out/pallas_call | solution.py:490
  136.3 17.8 %feed_forward.2 = (bf16[320,2048]{1,0:T(8,128)(2,1)}, bf16[320,2048]{1,0:T(8,128)(2,1)}, bf16[320,2048]{1,0:T(8,128)(2,1)}, bf16[320,2048]{1,0:T(8,128)(2,1)}) custom-call(bf16[320,2048]{1,0:T(8,128)(2,1)} %get-tuple-element.288.normed.refs_0_, f32[640,2048]{1,0:T(8,128)} %grad_hidden.1.seed, bf16[2048,2048]{1,0:T(8,128)(2,1)} %wg.3, bf16[2048,2048]{1,0:T(8,128)(2,1)} %wu.3), custom_call_target="tpu_custom_call" | custom-call | flops 135999995904 | bytes 1 | tf_op jit(solution)/shard_map/feed_forward/pallas_call | solution.py:589
  154.3 6.6 %all-gather.14.cloned.1.call-done = bf16[1280,512]{1,0:T(8,128)(2,1)} async-done(((bf16[320,512]{1,0:T(8,128)(2,1)}), bf16[1280,512]{1,0:T(8,128)(2,1)}) %all-gather.14.cloned.1.call-update) | async-done | bytes 1310736 | tf_op jit(solution)/shard_map/all_gather | solution.py:1111
  160.9 9.2 %project_out.3 = (f32[320,2048]{1,0:T(8,128)}, bf16[320,2048]{1,0:T(8,128)(2,1)}) custom-call(s32[6]{0:T(128)} %stack.39.place, bf16[640,2048]{1,0:T(8,128)(2,1)} %refs_1_.1, bf16[4,320,512]{2,1,0:T(8,128)(2,1)} %bitcast.39, bf16[4,256,2048]{2,1,0:T(8,128)(2,1)} %bitcast.43, bf16[4,256,2048]{2,1,0:T(8,128)(2,1)} %collective-permute-done.7.far.refs_7_), custom_call_target="tpu_custom_call" | custom-call | flops 56000000000 | bytes 1 | tf_op jit(solution)/shard_map/project_out/pallas_call | solution.py:490
  170.2 17.8 %feed_forward.3 = (bf16[320,2048]{1,0:T(8,128)(2,1)}, bf16[320,2048]{1,0:T(8,128)(2,1)}, bf16[320,2048]{1,0:T(8,128)(2,1)}, bf16[320,2048]{1,0:T(8,128)(2,1)}) custom-call(bf16[320,2048]{1,0:T(8,128)(2,1)} %get-tuple-element.295.normed.refs_1_, f32[640,2048]{1,0:T(8,128)} %grad_hidden.1.seed, bf16[2048,2048]{1,0:T(8,128)(2,1)} %wg.3, bf16[2048,2048]{1,0:T(8,128)(2,1)} %wu.3), custom_call_target="tpu_custom_call" | custom-call | flops 135999995904 | bytes 1 | tf_op jit(solution)/shard_map/feed_forward/pallas_call | solution.py:589
  188.0 8.8 %wgrad_away.5 = bf16[1024,2048]{1,0:T(8,128)(2,1)} custom-call(s32[6]{0:T(128)} %stack.39.place, bf16[640,2048]{1,0:T(8,128)(2,1)} %refs_5_.1, bf16[320,2048]{1,0:T(8,128)(2,1)} %get-tuple-element.311.refs_1_.refs_0_, bf16[320,2048]{1,0:T(8,128)(2,1)} %get-tuple-element.312.refs_2_.refs_1_), custom_call_target="tpu_custom_call" | custom-call | flops 64000000000 | bytes 1 | tf_op jit(solution)/shard_map/wgrad_away/pallas_call | solution.py:737
  197.0 8.8 %wgrad_away.6 = bf16[1024,2048]{1,0:T(8,128)(2,1)} custom-call(s32[6]{0:T(128)} %stack.39.place, bf16[320,2048]{1,0:T(8,128)(2,1)} %get-tuple-element.288.normed.refs_0_, bf16[320,2048]{1,0:T(8,128)(2,1)} %get-tuple-element.295.normed.refs_1_, bf16[320,2048]{1,0:T(8,128)(2,1)} %get-tuple-element.302.refs_2_, bf16[320,2048]{1,0:T(8,128)(2,1)} %get-tuple-element.303.refs_3_), custom_call_target="tpu_custom_call" | custom-call | flops 64000000000 | bytes 1 | tf_op jit(solution)/shard_map/wgrad_away/pallas_call | solution.py:737
  206.3 10.2 %wgrad_keep.5 = (bf16[512,1024]{1,0:T(8,128)(2,1)}, bf16[512,1024]{1,0:T(8,128)(2,1)}, bf16[512,1024]{1,0:T(8,128)(2,1)}, bf16[512,1024]{1,0:T(8,128)(2,1)}) custom-call(s32[6]{0:T(128)} %stack.39.place, bf16[640,2048]{1,0:T(8,128)(2,1)} %refs_5_.1, bf16[320,2048]{1,0:T(8,128)(2,1)} %get-tuple-element.311.refs_1_.refs_0_, ...), custom_call_target="tpu_custom_call" | custom-call | flops 71999995904 | bytes 1 | tf_op jit(solution)/shard_map/wgrad_keep/pallas_call | solution.py:785
  219.5 10.3 %wgrad_keep.6 = (bf16[512,1024]{1,0:T(8,128)(2,1)}, bf16[512,1024]{1,0:T(8,128)(2,1)}, bf16[512,1024]{1,0:T(8,128)(2,1)}, bf16[512,1024]{1,0:T(8,128)(2,1)}) custom-call(s32[6]{0:T(128)} %stack.39.place, bf16[320,2048]{1,0:T(8,128)(2,1)} %get-tuple-element.288.normed.refs_0_, bf16[320,2048]{1,0:T(8,128)(2,1)} %get-tuple-element.295.normed.refs_1_, ...), custom_call_target="tpu_custom_call" | custom-call | flops 71999995904 | bytes 1 | tf_op jit(solution)/shard_map/wgrad_keep/pallas_call | solution.py:785
  229.8 10.1 %branch_back.1 = (f32[160,2048]{1,0:T(8,128)}, bf16[160,2048]{1,0:T(8,128)(2,1)}, bf16[160,512]{1,0:T(8,128)(2,1)}, bf16[160,512]{1,0:T(8,128)(2,1)}, bf16[160,5...) custom-call(s32[6]{0:T(128)} %stack.39.place, bf16[80,2048]{1,0:T(8,128)(2,1)} %reduce-scatter.4.cloned.1.call-done.refs_0_, ...), custom_call_target="tpu_custom_call" | custom-call | flops 71999995904 | bytes 1 | tf_op jit(solution)/shard_map/branch_back/pallas_call | solution.py:671
  242.2 2.2 collective-permute-start.12
  244.3 9.7 %project_down.1 = bf16[640,2048]{1,0:T(8,128)(2,1)} custom-call(bf16[320,2048]{1,0:T(8,128)(2,1)} %get-tuple-element.311.refs_1_.refs_0_, bf16[320,2048]{1,0:T(8,128)(2,1)} %get-tuple-element.312.refs_2_.refs_1_, bf16[2048,2048]{1,0:T(8,128)(2,1)} %refs_2_.1), custom_call_target="tpu_custom_call" | custom-call | flops 88000004096 | bytes 1 | tf_op jit(solution)/shard_map/project_down/pallas_call | solution.py:619
  257.1 2.8 scatter_heads.1
  259.9 5.6 %wgrad_away.7 = bf16[1024,2048]{1,0:T(8,128)(2,1)} custom-call(s32[6]{0:T(128)} %stack.39.place, bf16[160,2048]{1,0:T(8,128)(2,1)} %get-tuple-element.330.refs_0_, bf16[160,2048]{1,0:T(8,128)(2,1)} %copy-done.8), custom_call_target="tpu_custom_call" | custom-call | flops 64000000000 | bytes 1 | tf_op jit(solution)/shard_map/wgrad_away/pallas_call | solution.py:737
  267.6 2.3 collective-permute-start.17
  269.9 3.2 collective-permute-done.18.refs_2_
  273.1 7.4 %wgrad_keep.7 = (bf16[512,1024]{1,0:T(8,128)(2,1)}, bf16[512,1024]{1,0:T(8,128)(2,1)}, bf16[512,1024]{1,0:T(8,128)(2,1)}, bf16[512,1024]{1,0:T(8,128)(2,1)}) custom-call(s32[6]{0:T(128)} %stack.39.place, bf16[160,2048]{1,0:T(8,128)(2,1)} %get-tuple-element.330.refs_0_, bf16[160,2048]{1,0:T(8,128)(2,1)} %copy-done.8, ...), custom_call_target="tpu_custom_call" | custom-call | flops 71999995904 | bytes 1 | tf_op jit(solution)/shard_map/wgrad_keep/pallas_call | solution.py:785
  281.8 23.0 %attend_back.1 = (bf16[640,128]{1,0:T(8,128)(2,1)}, bf16[640,128]{1,0:T(8,128)(2,1)}, bf16[640,128]{1,0:T(8,128)(2,1)}, bf16[640,128]{1,0:T(8,128)(2,1)}, f32[40...) custom-call(s32[40]{0:T(128)} %parent.7, s32[6]{0:T(128)} %stack.39.place, ...), custom_call_target="tpu_custom_call" | custom-call | flops 184000004096 | bytes 1 | tf_op jit(solution)/shard_map/attend_back/pallas_call | solution.py:305
  306.5 4.2 wgrad_stage.5
  311.7 3.9 combine_back.1
  317.5 1.5 collective-permute-start.24
  319.0 4.4 wgrad_stage.6
  323.4 8.9 %wgrad_away.8 = bf16[1024,2048]{1,0:T(8,128)(2,1)} custom-call(s32[6]{0:T(128)} %stack.39.place, bf16[320,2048]{1,0:T(8,128)(2,1)} %get-tuple-element.288.normed.refs_0_, bf16[320,2048]{1,0:T(8,128)(2,1)} %get-tuple-element.295.normed.refs_1_, bf16[320,2048]{1,0:T(8,128)(2,1)} %get-tuple-element.377.refs_2_, bf16[320,2048]{1,0:T(8,128)(2,1)} %get-tuple-element.378.refs_3_), custom_call_target="tpu_custom_call" | custom-call | flops 64000000000 | bytes 1 | tf_op jit(solution)/shard_map/wgrad_away/pallas_call | solution.py:737
  332.3 8.7 %collective-permute-done.23.refs_2_ = bf16[3,640,128]{2,1,0:T(8,128)(2,1)S(1)} collective-permute-done((bf16[3,640,128]{2,1,0:T(8,128)(2,1)}, bf16[3,640,128]{2,1,0:T(8,128)(2,1)S(1)}, u32[]{:S(2)}, u32[]{:S(2)}) %collective-permute-start.23) | collective-permute-done | bytes 491552 | tf_op jit(solution)/shard_map/ppermute | solution.py:1086
  342.8 11.0 %turn_back.1 = (bf16[640,2048]{1,0:T(8,128)(2,1)}, bf16[640,1536]{1,0:T(8,128)(2,1)}) custom-call(s32[40]{0:T(128)} %parent.7, s32[6]{0:T(128)} %stack.39.place, f32[1280,128]{1,0:T(8,128)} %constant.39.clone.cosine, f32[1280,128]{1,0:T(8,128)} %constant.40.clone.sine, bf16[2048,512]{1,0:T(8,128)(2,1)} %wq.3, bf16[2048,512]{1,0:T(8,128)(2,1)} %wk.3, ...), custom_call_target="tpu_custom_call" | custom-call | flops 103999995904 | bytes 1 | tf_op jit(solution)/shard_map/turn_back/pallas_call | solution.py:447
  353.8 7.3 %wgrad_away.9 = bf16[1024,1536]{1,0:T(8,128)(2,1)} custom-call(s32[6]{0:T(128)} %stack.39.place, bf16[640,2048]{1,0:T(8,128)(2,1)} %get-tuple-element.260.refs_0_, bf16[640,1536]{1,0:T(8,128)(2,1)} %get-tuple-element.390.refs_1_), custom_call_target="tpu_custom_call" | custom-call | flops 64000000000 | bytes 1 | tf_op jit(solution)/shard_map/wgrad_away/pallas_call | solution.py:737
  363.5 10.3 %wgrad_keep.8 = (bf16[512,1024]{1,0:T(8,128)(2,1)}, bf16[512,1024]{1,0:T(8,128)(2,1)}, bf16[512,1024]{1,0:T(8,128)(2,1)}, bf16[512,1024]{1,0:T(8,128)(2,1)}) custom-call(s32[6]{0:T(128)} %stack.39.place, bf16[320,2048]{1,0:T(8,128)(2,1)} %get-tuple-element.288.normed.refs_0_, bf16[320,2048]{1,0:T(8,128)(2,1)} %get-tuple-element.295.normed.refs_1_, ...), custom_call_target="tpu_custom_call" | custom-call | flops 71999995904 | bytes 1 | tf_op jit(solution)/shard_map/wgrad_keep/pallas_call | solution.py:785
  373.9 3.8 collective-permute-done.29.refs_1_
  377.7 3.9 wgrad_finish_chunks.1
  383.4 4.2 wgrad_stage.7
  387.6 1.7 copy-done.15
  389.3 8.2 %wgrad_keep.9 = (bf16[512,768]{1,0:T(8,128)(2,1)}, bf16[512,768]{1,0:T(8,128)(2,1)}, bf16[512,768]{1,0:T(8,128)(2,1)}, bf16[512,768]{1,0:T(8,128)(2,1)}) custom-call(s32[6]{0:T(128)} %stack.39.place, bf16[640,2048]{1,0:T(8,128)(2,1)} %get-tuple-element.260.refs_0_, bf16[640,1536]{1,0:T(8,128)(2,1)} %get-tuple-element.390.refs_1_, bf16[1024,1536]{1,0:T(8,128)(2,1)} %copy-done.15), custom_call_target="tpu_custom_call" | custom-call | flops 71999995904 | bytes 1 | tf_op jit(solution)/shard_map/wgrad_keep/pallas_call | solution.py:785
  397.5 5.4 %add_residual.1 = bf16[640,2048]{1,0:T(8,128)(2,1)} custom-call(f32[320,2048]{1,0:T(8,128)} %get-tuple-element.284.refs_2_.refs_0_, f32[320,2048]{1,0:T(8,128)} %get-tuple-element.292.refs_3_.refs_1_, bf16[640,2048]{1,0:T(8,128)(2,1)} %all-reduce.2.cloned.1.call-done.refs_2_), custom_call_target="tpu_custom_call" | custom-call | flops 48000000000 | bytes 1 | tf_op jit(solution)/shard_map/add_residual/pallas_call | solution.py:1053
  405.2 1.7 collective-permute-start.33
  406.9 1.9 collective-permute-done.32.b_got
  408.8 18.2 %reduce-scatter.8.cloned.1.call-done.part = bf16[160,2048]{1,0:T(8,128)(2,1)} async-done(((bf16[640,2048]{1,0:T(8,128)(2,1)}), bf16[160,2048]{1,0:T(8,128)(2,1)}) %reduce-scatter.8.cloned.1.call-update) | async-done | bytes 655376 | tf_op jit(solution)/shard_map/reduce_scatter | solution.py:1201
  427.1 4.1 tokens_back.1
  431.1 1.5 collective-permute-start.37
  436.2 4.4 wgrad_stage.8
  440.5 3.4 wgrad_finish.3
  444.0 2.3 collective-permute-done.37.a_got
  448.5 3.1 wgrad_finish.4
  454.6 10.2 %collective-permute-done.34.a_got = bf16[512,768]{1,0:T(8,128)(2,1)} collective-permute-done((bf16[512,768]{1,0:T(8,128)(2,1)S(1)}, bf16[512,768]{1,0:T(8,128)(2,1)}, u32[]{:S(2)}, u32[]{:S(2)}) %collective-permute-start.34) | collective-permute-done | bytes 786464 | tf_op jit(solution)/shard_map/ppermute | solution.py:921
  464.7 3.7 wgrad_stage.9
  471.2 1.9 add_last.1
  473.1 8.4 %collective-permute-done.41.refs_1_ = bf16[256,768]{1,0:T(8,128)(2,1)S(1)} collective-permute-done((bf16[256,768]{1,0:T(8,128)(2,1)}, bf16[256,768]{1,0:T(8,128)(2,1)S(1)}, u32[]{:S(2)}, u32[]{:S(2)}) %collective-permute-start.41) | collective-permute-done | bytes 393248 | tf_op jit(solution)/shard_map/ppermute | solution.py:921
  483.4 2.5 wgrad_finish_split.1
  486.0 3.0 wgrad_finish.5
  489.0 3.0 all-gather.8.cloned.1.call-done
  492.0 3.6 copy.23
  (172 shorter events, 47.5 us)
Async XLA Ops:
  7.2 86.5 %all-gather.10.cloned.1.call-start = ((), (), s32[]{:S(2)}) async-start(), calls=%async_computation.8 | async-start | bytes 5242880 | tf_op jit(solution)/shard_map/all_gather | solution.py:1093
  9.6 117.5 %all-gather.12.cloned.1.call-start = ((), (), s32[]{:S(2)}) async-start(), calls=%async_computation.9 | async-start | bytes 1638400 | tf_op jit(solution)/shard_map/all_gather | solution.py:1111
  22.0 15.2 %collective-permute-start = (bf16[3,640,128]{2,1,0:T(8,128)(2,1)}, bf16[3,640,128]{2,1,0:T(8,128)(2,1)S(1)}, u32[]{:S(2)}, u32[]{:S(2)}) collective-permute-start(bf16[3,640,128]{2,1,0:T(8,128)(2,1)} %get-tuple-element.257), channel_id=1, source_target_pairs={{0,8},{4,12},{8,0},{12,4},{16,24},{20,28},{24,16},{28,20},{1,9},{5... | collective-permute-start | bytes 1474568 | tf_op jit(solution)/shard_map/ppermute | solution.py:1086
  25.0 23.4 %collective-permute-start.1 = (bf16[3,640,128]{2,1,0:T(8,128)(2,1)}, bf16[3,640,128]{2,1,0:T(8,128)(2,1)S(1)}, u32[]{:S(2)}, u32[]{:S(2)}) collective-permute-start(bf16[3,640,128]{2,1,0:T(8,128)(2,1)} %get-tuple-element.258), channel_id=1, source_target_pairs={{0,16},{4,20},{8,24},{12,28},{16,0},{20,4},{24,8},{28,12},{1,17},{... | collective-permute-start | bytes 1474568 | tf_op jit(solution)/shard_map/ppermute | solution.py:1086
  26.5 21.9 %collective-permute-start.2 = (bf16[3,640,128]{2,1,0:T(8,128)(2,1)}, bf16[3,640,128]{2,1,0:T(8,128)(2,1)S(1)}, u32[]{:S(2)}, u32[]{:S(2)}) collective-permute-start(bf16[3,640,128]{2,1,0:T(8,128)(2,1)} %get-tuple-element.259), channel_id=1, source_target_pairs={{0,24},{4,28},{8,16},{12,20},{16,8},{20,12},{24,0},{28,4},{1,25},{... | collective-permute-start | bytes 1474568 | tf_op jit(solution)/shard_map/ppermute | solution.py:1086
  26.5 22.0 %copy-start = (bf16[3,640,128]{2,1,0:T(8,128)(2,1)S(1)}, bf16[3,640,128]{2,1,0:T(8,128)(2,1)}, u32[]{:S(2)}) copy-start(bf16[3,640,128]{2,1,0:T(8,128)(2,1)} %get-tuple-element.267.refs_0_) | copy-start | bytes 1474564
  37.2 11.5 %copy-start.1 = (bf16[3,640,128]{2,1,0:T(8,128)(2,1)}, bf16[3,640,128]{2,1,0:T(8,128)(2,1)S(1)}, u32[]{:S(2)}) copy-start(bf16[3,640,128]{2,1,0:T(8,128)(2,1)S(1)} %collective-permute-done.refs_1_) | copy-start | bytes 1474564
  49.4 3.0 collective-permute-start.3
  66.5 7.2 %collective-permute-start.4 = (bf16[640,128]{1,0:T(8,128)(2,1)}, bf16[640,128]{1,0:T(8,128)(2,1)S(1)}, u32[]{:S(2)}, u32[]{:S(2)}) collective-permute-start(bf16[640,128]{1,0:T(8,128)(2,1)} %get-tuple-element.272), channel_id=1, source_target_pairs={{0,8},{4,12},{8,0},{12,4},{16,24},{20,28},{24,16},{28,20},{1,9},{5... | collective-permute-start | bytes 491528 | tf_op jit(solution)/shard_map/ppermute | solution.py:1086
  67.5 8.3 %collective-permute-start.5 = (bf16[640,128]{1,0:T(8,128)(2,1)}, bf16[640,128]{1,0:T(8,128)(2,1)S(1)}, u32[]{:S(2)}, u32[]{:S(2)}) collective-permute-start(bf16[640,128]{1,0:T(8,128)(2,1)} %get-tuple-element.273), channel_id=1, source_target_pairs={{0,16},{4,20},{8,24},{12,28},{16,0},{20,4},{24,8},{28,12},{1,17},{... | collective-permute-start | bytes 491528 | tf_op jit(solution)/shard_map/ppermute | solution.py:1086
  68.5 8.9 %collective-permute-start.6 = (bf16[640,128]{1,0:T(8,128)(2,1)}, bf16[640,128]{1,0:T(8,128)(2,1)S(1)}, u32[]{:S(2)}, u32[]{:S(2)}) collective-permute-start(bf16[640,128]{1,0:T(8,128)(2,1)} %get-tuple-element.274), channel_id=1, source_target_pairs={{0,24},{4,28},{8,16},{12,20},{16,8},{20,12},{24,0},{28,4},{1,25},{... | collective-permute-start | bytes 491528 | tf_op jit(solution)/shard_map/ppermute | solution.py:1086
  93.7 33.4 %collective-permute-start.7 = (bf16[4,256,2048]{2,1,0:T(8,128)(2,1)}, bf16[4,256,2048]{2,1,0:T(8,128)(2,1)}, u32[]{:S(2)}, u32[]{:S(2)}) collective-permute-start(bf16[4,256,2048]{2,1,0:T(8,128)(2,1)} %bitcast.41), channel_id=1, source_target_pairs={{0,4},{4,0},{8,12},{12,8},{16,20},{20,16},{24,28},{28,24},{1,5},{5... | collective-permute-start | bytes 12582920 | tf_op jit(solution)/shard_map/ppermute | solution.py:1086
  93.7 67.2 %all-gather.14.cloned.1.call-start = ((), (), s32[]{:S(2)}) async-start(), calls=%async_computation.10 | async-start | bytes 1638400 | tf_op jit(solution)/shard_map/all_gather | solution.py:1111
  94.4 135.4 %reduce-scatter.4.cloned.1.call-start = ((), (), s32[]{:S(2)}) async-start(), calls=%async_computation.3 | async-start | bytes 1638400 | tf_op jit(solution)/shard_map/reduce_scatter | solution.py:1125
  154.1 75.7 %reduce-scatter.6.cloned.1.call-start = ((), (), s32[]{:S(2)}) async-start(), calls=%async_computation.4 | async-start | bytes 1638400 | tf_op jit(solution)/shard_map/reduce_scatter | solution.py:1125
  196.8 9.5 %collective-permute-start.9 = (bf16[1024,2048]{1,0:T(8,128)(2,1)}, bf16[1024,2048]{1,0:T(8,128)(2,1)}, u32[]{:S(2)}, u32[]{:S(2)}) collective-permute-start(bf16[1024,2048]{1,0:T(8,128)(2,1)} %wgrad_away.5), channel_id=1, source_target_pairs={{0,4},{4,0},{8,12},{12,8},{16,20},{20,16},{24,28},{28,24},{1,5},{5... | collective-permute-start | bytes 12582920 | tf_op jit(solution)/shard_map/ppermute | solution.py:921
  196.9 200.5 %all-reduce.2.cloned.1.call-start = ((), (), s32[]{:S(2)}) async-start(), calls=%async_computation.5 | async-start | bytes 5242880 | tf_op jit(solution)/shard_map/psum | solution.py:1161
  205.8 13.7 %collective-permute-start.8 = (bf16[1024,2048]{1,0:T(8,128)(2,1)}, bf16[1024,2048]{1,0:T(8,128)(2,1)}, u32[]{:S(2)}, u32[]{:S(2)}) collective-permute-start(bf16[1024,2048]{1,0:T(8,128)(2,1)} %wgrad_away.6), channel_id=1, source_target_pairs={{0,4},{4,0},{8,12},{12,8},{16,20},{20,16},{24,28},{28,24},{1,5},{5... | collective-permute-start | bytes 12582920 | tf_op jit(solution)/shard_map/ppermute | solution.py:921
  216.6 39.7 %collective-permute-start.13 = (bf16[512,1024]{1,0:T(8,128)(2,1)}, bf16[512,1024]{1,0:T(8,128)(2,1)}, u32[]{:S(2)}, u32[]{:S(2)}) collective-permute-start(bf16[512,1024]{1,0:T(8,128)(2,1)} %get-tuple-element.319), channel_id=1, source_target_pairs={{0,8},{4,12},{8,0},{12,4},{16,24},{20,28},{24,16},{28,20},{1,9},{5... | collective-permute-start | bytes 3145736 | tf_op jit(solution)/shard_map/ppermute | solution.py:921
  218.0 38.2 %collective-permute-start.14 = (bf16[512,1024]{1,0:T(8,128)(2,1)}, bf16[512,1024]{1,0:T(8,128)(2,1)}, u32[]{:S(2)}, u32[]{:S(2)}) collective-permute-start(bf16[512,1024]{1,0:T(8,128)(2,1)} %get-tuple-element.320), channel_id=1, source_target_pairs={{0,16},{4,20},{8,24},{12,28},{16,0},{20,4},{24,8},{28,12},{1,17},{... | collective-permute-start | bytes 3145736 | tf_op jit(solution)/shard_map/ppermute | solution.py:921
  239.9 16.3 %collective-permute-start.10 = (bf16[160,512]{1,0:T(8,128)(2,1)}, bf16[160,512]{1,0:T(8,128)(2,1)S(1)}, u32[]{:S(2)}, u32[]{:S(2)}) collective-permute-start(bf16[160,512]{1,0:T(8,128)(2,1)} %get-tuple-element.314), channel_id=1, source_target_pairs={{0,1},{1,2},{2,3},{3,0},{4,5},{5,6},{6,7},{7,4},{8,9},{9,10},{10,1... | collective-permute-start | bytes 491528 | tf_op jit(solution)/shard_map/ppermute | solution.py:999
  240.8 15.4 %collective-permute-start.11 = (bf16[160,512]{1,0:T(8,128)(2,1)}, bf16[160,512]{1,0:T(8,128)(2,1)S(1)}, u32[]{:S(2)}, u32[]{:S(2)}) collective-permute-start(bf16[160,512]{1,0:T(8,128)(2,1)} %get-tuple-element.315), channel_id=1, source_target_pairs={{0,2},{1,3},{2,0},{3,1},{4,6},{5,7},{6,4},{7,5},{8,10},{9,11},{10,... | collective-permute-start | bytes 491528 | tf_op jit(solution)/shard_map/ppermute | solution.py:999
  242.2 14.1 %collective-permute-start.12 = (bf16[160,512]{1,0:T(8,128)(2,1)}, bf16[160,512]{1,0:T(8,128)(2,1)S(1)}, u32[]{:S(2)}, u32[]{:S(2)}) collective-permute-start(bf16[160,512]{1,0:T(8,128)(2,1)} %get-tuple-element.316), channel_id=1, source_target_pairs={{0,3},{1,0},{2,1},{3,2},{4,7},{5,4},{6,5},{7,6},{8,11},{9,8},{10,9... | collective-permute-start | bytes 491528 | tf_op jit(solution)/shard_map/ppermute | solution.py:999
  256.2 3.7 copy-start.8
  265.5 7.6 %collective-permute-start.18 = (bf16[1024,2048]{1,0:T(8,128)(2,1)}, bf16[1024,2048]{1,0:T(8,128)(2,1)}, u32[]{:S(2)}, u32[]{:S(2)}) collective-permute-start(bf16[1024,2048]{1,0:T(8,128)(2,1)} %wgrad_away.7), channel_id=1, source_target_pairs={{0,4},{4,0},{8,12},{12,8},{16,20},{20,16},{24,28},{28,24},{1,5},{5... | collective-permute-start | bytes 12582920 | tf_op jit(solution)/shard_map/ppermute | solution.py:921
  265.6 161.4 %reduce-scatter.8.cloned.1.call-start = ((), (), s32[]{:S(2)}) async-start(), calls=%async_computation.6 | async-start | bytes 3276800 | tf_op jit(solution)/shard_map/reduce_scatter | solution.py:1201
  266.4 14.1 %collective-permute-start.15 = (bf16[640,128]{1,0:T(8,128)(2,1)S(1)}, bf16[640,128]{1,0:T(8,128)(2,1)S(1)}, u32[]{:S(2)}, u32[]{:S(2)}) collective-permute-start(bf16[640,128]{1,0:T(8,128)(2,1)S(1)} %copy-done.33), channel_id=1, source_target_pairs={{0,8},{4,12},{8,0},{12,4},{16,24},{20,28},{24,16},{28,20},{1,9},{5... | collective-permute-start | bytes 491528 | tf_op jit(solution)/shard_map/ppermute | solution.py:1086
  267.0 13.6 %collective-permute-start.16 = (bf16[640,128]{1,0:T(8,128)(2,1)S(1)}, bf16[640,128]{1,0:T(8,128)(2,1)S(1)}, u32[]{:S(2)}, u32[]{:S(2)}) collective-permute-start(bf16[640,128]{1,0:T(8,128)(2,1)S(1)} %copy-done.31), channel_id=1, source_target_pairs={{0,16},{4,20},{8,24},{12,28},{16,0},{20,4},{24,8},{28,12},{1,17},{... | collective-permute-start | bytes 491528 | tf_op jit(solution)/shard_map/ppermute | solution.py:1086
  267.6 13.0 %collective-permute-start.17 = (bf16[640,128]{1,0:T(8,128)(2,1)S(1)}, bf16[640,128]{1,0:T(8,128)(2,1)S(1)}, u32[]{:S(2)}, u32[]{:S(2)}) collective-permute-start(bf16[640,128]{1,0:T(8,128)(2,1)S(1)} %copy-done.29), channel_id=1, source_target_pairs={{0,24},{4,28},{8,16},{12,20},{16,8},{20,12},{24,0},{28,4},{1,25},{... | collective-permute-start | bytes 491528 | tf_op jit(solution)/shard_map/ppermute | solution.py:1086
  280.6 25.6 %collective-permute-start.19 = (bf16[512,1024]{1,0:T(8,128)(2,1)}, bf16[512,1024]{1,0:T(8,128)(2,1)}, u32[]{:S(2)}, u32[]{:S(2)}) collective-permute-start(bf16[512,1024]{1,0:T(8,128)(2,1)} %get-tuple-element.352), channel_id=1, source_target_pairs={{0,8},{4,12},{8,0},{12,4},{16,24},{20,28},{24,16},{28,20},{1,9},{5... | collective-permute-start | bytes 3145736 | tf_op jit(solution)/shard_map/ppermute | solution.py:921
  281.2 25.3 %collective-permute-start.20 = (bf16[512,1024]{1,0:T(8,128)(2,1)}, bf16[512,1024]{1,0:T(8,128)(2,1)}, u32[]{:S(2)}, u32[]{:S(2)}) collective-permute-start(bf16[512,1024]{1,0:T(8,128)(2,1)} %get-tuple-element.353), channel_id=1, source_target_pairs={{0,16},{4,20},{8,24},{12,28},{16,0},{20,4},{24,8},{28,12},{1,17},{... | collective-permute-start | bytes 3145736 | tf_op jit(solution)/shard_map/ppermute | solution.py:921
  306.5 4.2 collective-permute-start.21
  315.6 16.7 %collective-permute-start.22 = (bf16[3,640,128]{2,1,0:T(8,128)(2,1)}, bf16[3,640,128]{2,1,0:T(8,128)(2,1)S(1)}, u32[]{:S(2)}, u32[]{:S(2)}) collective-permute-start(bf16[3,640,128]{2,1,0:T(8,128)(2,1)} %get-tuple-element.365), channel_id=1, source_target_pairs={{0,8},{4,12},{8,0},{12,4},{16,24},{20,28},{24,16},{28,20},{1,9},{5... | collective-permute-start | bytes 1474568 | tf_op jit(solution)/shard_map/ppermute | solution.py:1086
  317.0 24.0 %collective-permute-start.23 = (bf16[3,640,128]{2,1,0:T(8,128)(2,1)}, bf16[3,640,128]{2,1,0:T(8,128)(2,1)S(1)}, u32[]{:S(2)}, u32[]{:S(2)}) collective-permute-start(bf16[3,640,128]{2,1,0:T(8,128)(2,1)} %get-tuple-element.366), channel_id=1, source_target_pairs={{0,16},{4,20},{8,24},{12,28},{16,0},{20,4},{24,8},{28,12},{1,17},{... | collective-permute-start | bytes 1474568 | tf_op jit(solution)/shard_map/ppermute | solution.py:1086
  317.5 23.5 %collective-permute-start.24 = (bf16[3,640,128]{2,1,0:T(8,128)(2,1)}, bf16[3,640,128]{2,1,0:T(8,128)(2,1)S(1)}, u32[]{:S(2)}, u32[]{:S(2)}) collective-permute-start(bf16[3,640,128]{2,1,0:T(8,128)(2,1)} %get-tuple-element.367), channel_id=1, source_target_pairs={{0,24},{4,28},{8,16},{12,20},{16,8},{20,12},{24,0},{28,4},{1,25},{... | collective-permute-start | bytes 1474568 | tf_op jit(solution)/shard_map/ppermute | solution.py:1086
  332.3 21.5 %collective-permute-start.25 = (bf16[1024,2048]{1,0:T(8,128)(2,1)}, bf16[1024,2048]{1,0:T(8,128)(2,1)}, u32[]{:S(2)}, u32[]{:S(2)}) collective-permute-start(bf16[1024,2048]{1,0:T(8,128)(2,1)} %wgrad_away.8), channel_id=1, source_target_pairs={{0,4},{4,0},{8,12},{12,8},{16,20},{20,16},{24,28},{28,24},{1,5},{5... | collective-permute-start | bytes 12582920 | tf_op jit(solution)/shard_map/ppermute | solution.py:921
  332.3 10.5 %copy-start.21 = (bf16[3,640,128]{2,1,0:T(8,128)(2,1)}, bf16[3,640,128]{2,1,0:T(8,128)(2,1)S(1)}, u32[]{:S(2)}) copy-start(bf16[3,640,128]{2,1,0:T(8,128)(2,1)S(1)} %collective-permute-done.22.refs_1_) | copy-start | bytes 1474564
  341.0 32.8 %collective-permute-start.27 = (bf16[512,1024]{1,0:T(8,128)(2,1)}, bf16[512,1024]{1,0:T(8,128)(2,1)}, u32[]{:S(2)}, u32[]{:S(2)}) collective-permute-start(bf16[512,1024]{1,0:T(8,128)(2,1)} %get-tuple-element.393), channel_id=1, source_target_pairs={{0,8},{4,12},{8,0},{12,4},{16,24},{20,28},{24,16},{28,20},{1,9},{5... | collective-permute-start | bytes 3145736 | tf_op jit(solution)/shard_map/ppermute | solution.py:921
  341.7 32.2 %collective-permute-start.28 = (bf16[512,1024]{1,0:T(8,128)(2,1)}, bf16[512,1024]{1,0:T(8,128)(2,1)}, u32[]{:S(2)}, u32[]{:S(2)}) collective-permute-start(bf16[512,1024]{1,0:T(8,128)(2,1)} %get-tuple-element.394), channel_id=1, source_target_pairs={{0,16},{4,20},{8,24},{12,28},{16,0},{20,4},{24,8},{28,12},{1,17},{... | collective-permute-start | bytes 3145736 | tf_op jit(solution)/shard_map/ppermute | solution.py:921
  353.8 138.2 %all-gather.8.cloned.1.call-start = ((), (), s32[]{:S(2)}) async-start(), calls=%async_computation.7 | async-start | bytes 3276800 | tf_op jit(solution)/shard_map/all_gather | solution.py:1211
  353.8 8.3 %copy-start.20 = (bf16[256,1024]{1,0:T(8,128)(2,1)S(1)}, bf16[256,1024]{1,0:T(8,128)(2,1)}, u32[]{:S(2)}) copy-start(bf16[256,1024]{1,0:T(8,128)(2,1)} %get-tuple-element.403) | copy-start | bytes 1572868
  361.2 26.4 %collective-permute-start.26 = (bf16[1024,1536]{1,0:T(8,128)(2,1)}, bf16[1024,1536]{1,0:T(8,128)(2,1)S(1)}, u32[]{:S(2)}, u32[]{:S(2)}) collective-permute-start(bf16[1024,1536]{1,0:T(8,128)(2,1)} %wgrad_away.9), channel_id=1, source_target_pairs={{0,4},{4,0},{8,12},{12,8},{16,20},{20,16},{24,28},{28,24},{1,5},{5... | collective-permute-start | bytes 9437192 | tf_op jit(solution)/shard_map/ppermute | solution.py:921
  361.2 16.5 %collective-permute-start.29 = (bf16[256,1024]{1,0:T(8,128)(2,1)}, bf16[256,1024]{1,0:T(8,128)(2,1)}, u32[]{:S(2)}, u32[]{:S(2)}) collective-permute-start(bf16[256,1024]{1,0:T(8,128)(2,1)} %get-tuple-element.402), channel_id=1, source_target_pairs={{0,16},{4,20},{8,24},{12,28},{16,0},{20,4},{24,8},{28,12},{1,17},{... | collective-permute-start | bytes 1572872 | tf_op jit(solution)/shard_map/ppermute | solution.py:921
  362.1 15.6 %collective-permute-start.30 = (bf16[256,1024]{1,0:T(8,128)(2,1)S(1)}, bf16[256,1024]{1,0:T(8,128)(2,1)}, u32[]{:S(2)}, u32[]{:S(2)}) collective-permute-start(bf16[256,1024]{1,0:T(8,128)(2,1)S(1)} %copy-done.20), channel_id=1, source_target_pairs={{0,8},{4,12},{8,0},{12,4},{16,24},{20,28},{24,16},{28,20},{1,9},{5... | collective-permute-start | bytes 1572872 | tf_op jit(solution)/shard_map/ppermute | solution.py:921
  381.6 25.3 %collective-permute-start.31 = (bf16[512,1024]{1,0:T(8,128)(2,1)}, bf16[512,1024]{1,0:T(8,128)(2,1)}, u32[]{:S(2)}, u32[]{:S(2)}) collective-permute-start(bf16[512,1024]{1,0:T(8,128)(2,1)} %get-tuple-element.422), channel_id=1, source_target_pairs={{0,8},{4,12},{8,0},{12,4},{16,24},{20,28},{24,16},{28,20},{1,9},{5... | collective-permute-start | bytes 3145736 | tf_op jit(solution)/shard_map/ppermute | solution.py:921
  382.8 26.0 %collective-permute-start.32 = (bf16[512,1024]{1,0:T(8,128)(2,1)}, bf16[512,1024]{1,0:T(8,128)(2,1)}, u32[]{:S(2)}, u32[]{:S(2)}) collective-permute-start(bf16[512,1024]{1,0:T(8,128)(2,1)} %get-tuple-element.423), channel_id=1, source_target_pairs={{0,16},{4,20},{8,24},{12,28},{16,0},{20,4},{24,8},{28,12},{1,17},{... | collective-permute-start | bytes 3145736 | tf_op jit(solution)/shard_map/ppermute | solution.py:921
  397.5 6.9 %copy-start.19 = (bf16[256,1024]{1,0:T(8,128)(2,1)S(1)}, bf16[256,1024]{1,0:T(8,128)(2,1)}, u32[]{:S(2)}) copy-start(bf16[256,1024]{1,0:T(8,128)(2,1)} %get-tuple-element.445) | copy-start | bytes 1572868
  397.5 7.7 %copy-start.26 = (bf16[512,256]{1,0:T(8,128)(2,1)S(1)}, bf16[512,256]{1,0:T(8,128)(2,1)}, u32[]{:S(2)}) copy-start(bf16[512,256]{1,0:T(8,128)(2,1)} %get-tuple-element.431) | copy-start | bytes 786436
  402.9 32.1 %collective-permute-start.39 = (bf16[256,1024]{1,0:T(8,128)(2,1)}, bf16[256,1024]{1,0:T(8,128)(2,1)}, u32[]{:S(2)}, u32[]{:S(2)}) collective-permute-start(bf16[256,1024]{1,0:T(8,128)(2,1)} %get-tuple-element.444), channel_id=1, source_target_pairs={{0,16},{4,20},{8,24},{12,28},{16,0},{20,4},{24,8},{28,12},{1,17},{... | collective-permute-start | bytes 1572872 | tf_op jit(solution)/shard_map/ppermute | solution.py:921
  404.3 31.3 %collective-permute-start.40 = (bf16[256,1024]{1,0:T(8,128)(2,1)S(1)}, bf16[256,1024]{1,0:T(8,128)(2,1)}, u32[]{:S(2)}, u32[]{:S(2)}) collective-permute-start(bf16[256,1024]{1,0:T(8,128)(2,1)S(1)} %copy-done.19), channel_id=1, source_target_pairs={{0,8},{4,12},{8,0},{12,4},{16,24},{20,28},{24,16},{28,20},{1,9},{5... | collective-permute-start | bytes 1572872 | tf_op jit(solution)/shard_map/ppermute | solution.py:921
  405.2 29.0 %copy-start.7 = (bf16[512,256]{1,0:T(8,128)(2,1)S(1)}, bf16[512,256]{1,0:T(8,128)(2,1)}, u32[]{:S(2)}) copy-start(bf16[512,256]{1,0:T(8,128)(2,1)} %get-tuple-element.434) | copy-start | bytes 786436
  405.2 29.9 %copy-start.18 = (bf16[512,768]{1,0:T(8,128)(2,1)S(1)}, bf16[512,768]{1,0:T(8,128)(2,1)}, u32[]{:S(2)}) copy-start(bf16[512,768]{1,0:T(8,128)(2,1)} %get-tuple-element.435) | copy-start | bytes 2359300
  405.2 30.4 %copy-start.17 = (bf16[512,768]{1,0:T(8,128)(2,1)S(1)}, bf16[512,768]{1,0:T(8,128)(2,1)}, u32[]{:S(2)}) copy-start(bf16[512,768]{1,0:T(8,128)(2,1)} %get-tuple-element.436) | copy-start | bytes 2359300
  405.2 29.0 %collective-permute-start.33 = (bf16[512,256]{1,0:T(8,128)(2,1)S(1)}, bf16[512,256]{1,0:T(8,128)(2,1)S(1)}, u32[]{:S(2)}, u32[]{:S(2)}) collective-permute-start(bf16[512,256]{1,0:T(8,128)(2,1)S(1)} %copy-done.26), channel_id=1, source_target_pairs={{0,1},{1,2},{2,3},{3,0},{4,5},{5,6},{6,7},{7,4},{8,9},{9,10},{10,1... | collective-permute-start | bytes 786440 | tf_op jit(solution)/shard_map/ppermute | solution.py:999
  431.1 15.1 %collective-permute-start.37 = (bf16[256,1024]{1,0:T(8,128)(2,1)}, bf16[256,1024]{1,0:T(8,128)(2,1)S(1)}, u32[]{:S(2)}, u32[]{:S(2)}) collective-permute-start(bf16[256,1024]{1,0:T(8,128)(2,1)} %get-tuple-element.440), channel_id=1, source_target_pairs={{0,16},{4,20},{8,24},{12,28},{16,0},{20,4},{24,8},{28,12},{1,17},{... | collective-permute-start | bytes 1572872 | tf_op jit(solution)/shard_map/ppermute | solution.py:921
  432.7 15.1 %collective-permute-start.38 = (bf16[256,1024]{1,0:T(8,128)(2,1)}, bf16[256,1024]{1,0:T(8,128)(2,1)S(1)}, u32[]{:S(2)}, u32[]{:S(2)}) collective-permute-start(bf16[256,1024]{1,0:T(8,128)(2,1)} %get-tuple-element.441), channel_id=1, source_target_pairs={{0,8},{4,12},{8,0},{12,4},{16,24},{20,28},{24,16},{28,20},{1,9},{5... | collective-permute-start | bytes 1572872 | tf_op jit(solution)/shard_map/ppermute | solution.py:921
  434.2 17.4 %collective-permute-start.36 = (bf16[512,256]{1,0:T(8,128)(2,1)S(1)}, bf16[512,256]{1,0:T(8,128)(2,1)S(1)}, u32[]{:S(2)}, u32[]{:S(2)}) collective-permute-start(bf16[512,256]{1,0:T(8,128)(2,1)S(1)} %add_convert_fusion.1), channel_id=1, source_target_pairs={{0,1},{1,2},{2,3},{3,0},{4,5},{5,6},{6,7},{7,4},{8,9},{9,10},{10,1... | collective-permute-start | bytes 786440 | tf_op jit(solution)/shard_map/ppermute | solution.py:999
  435.1 29.6 %collective-permute-start.34 = (bf16[512,768]{1,0:T(8,128)(2,1)S(1)}, bf16[512,768]{1,0:T(8,128)(2,1)}, u32[]{:S(2)}, u32[]{:S(2)}) collective-permute-start(bf16[512,768]{1,0:T(8,128)(2,1)S(1)} %copy-done.18), channel_id=1, source_target_pairs={{0,8},{4,12},{8,0},{12,4},{16,24},{20,28},{24,16},{28,20},{1,9},{5... | collective-permute-start | bytes 2359304 | tf_op jit(solution)/shard_map/ppermute | solution.py:921
  435.6 29.1 %collective-permute-start.35 = (bf16[512,768]{1,0:T(8,128)(2,1)S(1)}, bf16[512,768]{1,0:T(8,128)(2,1)}, u32[]{:S(2)}, u32[]{:S(2)}) collective-permute-start(bf16[512,768]{1,0:T(8,128)(2,1)S(1)} %copy-done.17), channel_id=1, source_target_pairs={{0,16},{4,20},{8,24},{12,28},{16,0},{20,4},{24,8},{28,12},{1,17},{... | collective-permute-start | bytes 2359304 | tf_op jit(solution)/shard_map/ppermute | solution.py:921
  451.7 18.8 %collective-permute-start.43 = (bf16[512,256]{1,0:T(8,128)(2,1)S(1)}, bf16[512,256]{1,0:T(8,128)(2,1)S(1)}, u32[]{:S(2)}, u32[]{:S(2)}) collective-permute-start(bf16[512,256]{1,0:T(8,128)(2,1)S(1)} %add_convert_fusion), channel_id=1, source_target_pairs={{0,1},{1,2},{2,3},{3,0},{4,5},{5,6},{6,7},{7,4},{8,9},{9,10},{10,1... | collective-permute-start | bytes 786440 | tf_op jit(solution)/shard_map/ppermute | solution.py:999
  452.5 33.4 %collective-permute-start.44 = (bf16[256,1024]{1,0:T(8,128)(2,1)}, bf16[256,1024]{1,0:T(8,128)(2,1)}, u32[]{:S(2)}, u32[]{:S(2)}) collective-permute-start(bf16[256,1024]{1,0:T(8,128)(2,1)} %get-tuple-element.496), channel_id=1, source_target_pairs={{0,16},{4,20},{8,24},{12,28},{16,0},{20,4},{24,8},{28,12},{1,17},{... | collective-permute-start | bytes 1572872 | tf_op jit(solution)/shard_map/ppermute | solution.py:921
  453.1 32.9 %collective-permute-start.45 = (bf16[256,1024]{1,0:T(8,128)(2,1)}, bf16[256,1024]{1,0:T(8,128)(2,1)}, u32[]{:S(2)}, u32[]{:S(2)}) collective-permute-start(bf16[256,1024]{1,0:T(8,128)(2,1)} %get-tuple-element.498), channel_id=1, source_target_pairs={{0,8},{4,12},{8,0},{12,4},{16,24},{20,28},{24,16},{28,20},{1,9},{5... | collective-permute-start | bytes 1572872 | tf_op jit(solution)/shard_map/ppermute | solution.py:921
  468.5 13.0 %collective-permute-start.41 = (bf16[256,768]{1,0:T(8,128)(2,1)}, bf16[256,768]{1,0:T(8,128)(2,1)S(1)}, u32[]{:S(2)}, u32[]{:S(2)}) collective-permute-start(bf16[256,768]{1,0:T(8,128)(2,1)} %get-tuple-element.479), channel_id=1, source_target_pairs={{0,16},{4,20},{8,24},{12,28},{16,0},{20,4},{24,8},{28,12},{1,17},{... | collective-permute-start | bytes 1179656 | tf_op jit(solution)/shard_map/ppermute | solution.py:921
  469.0 13.6 %collective-permute-start.42 = (bf16[256,768]{1,0:T(8,128)(2,1)}, bf16[256,768]{1,0:T(8,128)(2,1)S(1)}, u32[]{:S(2)}, u32[]{:S(2)}) collective-permute-start(bf16[256,768]{1,0:T(8,128)(2,1)} %get-tuple-element.481), channel_id=1, source_target_pairs={{0,8},{4,12},{8,0},{12,4},{16,24},{20,28},{24,16},{28,20},{1,9},{5... | collective-permute-start | bytes 1179656 | tf_op jit(solution)/shard_map/ppermute | solution.py:921
  (24 other events, 32.4 us)
Sparse Core Ops, SparseCore 0:
  10.2 83.4 all-gather.9
  95.8 31.1 all-gather.11
  129.2 31.6 all-gather.13
  163.6 30.1 reduce-scatter.3
  197.1 30.5 reduce-scatter.5
  265.7 102.3 all-reduce.1
  370.4 56.6 reduce-scatter.7
  431.3 60.6 all-gather.7

commit v4 on v3

--- a/solution.py
+++ b/solution.py
@@ -19,7 +19,7 @@
 LOW = jnp.bfloat16
 F32 = jnp.float32
 MIB = 1024 * 1024
-PER_MICROSECOND = 8.0e+09
+PER_MICROSECOND = 1.6e+10
 
 NT = (((1,), (1,)), ((), ()))
 TN = (((0,), (0,)), ((), ()))
@@ -821,7 +821,7 @@
 
 def wgrad_stage(piece, *arrays):
     rows, columns = arrays[0].shape
-    tile = min(256, columns)
+    tile = columns // 2 if columns % 256 == 0 else columns
     block = lambda size: pl.BlockSpec((size, tile), lambda i: (0, i))
     return pl.pallas_call(
         functools.partial(stage_kernel, piece),
@@ -1225,41 +1225,59 @@
 
     down.away()
     gate.away()
+    down.took()
     down.keep()
+    Chain.weight = 100.0
     down.send()
+    Chain.weight = 1.0
     own()
-    gate.keep()
     branch()
+    down.wait()
     output()
-    down.wait()
     scatter()
+    Chain.weight = 10.0
     out.away()
+    Chain.weight = 1.0
+    out.took()
     out.keep()
     heads()
     out.send()
     attend_step()
+    Chain.weight = 0.001
     out.wait()
+    Chain.weight = 1.0
     sum_far()
+    Chain.weight = 0.3
     out.add()
+    Chain.weight = 1.0
     sum_near()
     down.add()
     up.away()
+    gate.keep()
+    gate.send()
     arrive()
-    gate.send()
     turn()
     up.took()
+    Chain.weight = 0.3
     out.send()
+    Chain.weight = 1.0
     qkv.away()
+    Chain.weight = 0.03
     up.keep()
+    Chain.weight = 1.0
+    up.send()
+    Chain.weight = 100.0
     gate.wait()
-    out.wait()
-    up.send()
+    Chain.weight = 1.0
     state.out = out.finish()
     gate.add()
+    qkv.took()
     qkv.keep()
     residual()
     ring_start()
+    Chain.weight = 100.0
     down.send()
+    Chain.weight = 1.0
     gate.send()
     up.wait()
     Chain.weight = 0.03
@@ -1269,21 +1287,21 @@
     qkv.send()
     down.wait()
     up.add()
+    state.ring.step()
+    gate.wait()
+    state.down = down.finish()
     up.send()
-    state.down = down.finish()
-    gate.wait()
-    Chain.weight = 0.03
     state.gate = gate.finish()
+    qkv.wait()
+    Chain.weight = 0.3
+    qkv.add()
     Chain.weight = 1.0
-    state.ring.step()
-    qkv.wait()
-    qkv.add()
     qkv.send()
+    state.up = up.finish()
     ring_end()
     Chain.weight = 100.0
     state.qkv = qkv.finish()
     Chain.weight = 1.0
-    state.up = up.finish()
     grad_tokens = (
         state.tokens
         .reshape(plan.tensor, plan.groups, plan.share, plan.width)

time: 510 us -> 515 us (level)
  waiting for transfers between devices: 138 us -> 148 us
    reduce_scatter x2, waiting for transfers between devices: 0.01 us -> 9.86 us  [body(): lax.psum_scatter(partial_two, 'tensor', scatter_dimension=0, tiled=True)]
    ppermute x15, waiting for transfers between devices: 30.7 us -> 21.9 us  [swap(): return lax.ppermute(array, 'dp', xor_pairs(plan.dp, mask))]
    reduce_scatter x1, waiting for transfers between devices: 18.2 us -> 23.6 us  [turn(): lax.psum_scatter(partial_one, 'tensor', scatter_dimension=0, tiled=True)]
  transfers between devices with their start and end apart: 54 -> 54, of which waited for: 22 -> 26; matrix products, arithmetic and copies ran while one was open for 1% -> 1% of each run, Pallas kernels for 55% -> 54%
where the time goes in v4:
time: 515 us; the launch traced here: 508 us
  Pallas kernels  281 us (55%)
  waiting for transfers between devices  148 us (29%)
  starting transfers between devices  46.1 us (9%)
  local copies, waits for them, and re-layouts  15.5 us (3%)
  between operations  14.8 us (3%)
    pallas_call x5, Pallas kernels, wgrad_keep(): pl.pallas_call(functools.partial(keep_kernel, len(lhs), count), grid_spec...  46.1 us
    pallas_call x5, Pallas kernels, wgrad_away(): pl.pallas_call(functools.partial(away_kernel, len(lhs)), grid_spec=pltpu....  39.2 us
    all_gather x2, waiting for transfers between devices, body(): lax.all_gather(tie(part, near), 'tensor', axis=0, tiled=False)  38.9 us
    pallas_call x2, Pallas kernels, feed_forward(): pl.pallas_call(functools.partial(ff_kernel, tile), grid=(1,), in_specs=[w...  35.6 us
    ppermute x25, waiting for transfers between devices, swap(): return lax.ppermute(array, 'dp', xor_pairs(self.plan.dp, 1 << bit))  30.3 us
    reduce_scatter x1, waiting for transfers between devices, turn(): lax.psum_scatter(partial_one, 'tensor', scatter_dimension=0, tiled=True)  23.6 us
    pallas_call x1, Pallas kernels, attend_back(): pl.pallas_call(functools.partial(attend_back_kernel, plan), grid_spec=plt...  23.1 us
    ppermute x25, starting transfers between devices, swap(): return lax.ppermute(array, 'dp', xor_pairs(self.plan.dp, 1 << bit))  22.6 us
  transfers between devices with their start and end apart: 54, of which 26 were waited for; matrix products, arithmetic and copies ran while one was open for 1% of the time, Pallas kernels for 54%

profile of v4, /device:TPU:0, one launch (start us, length us, event | category | flops | bytes accessed | tf_op | source)
XLA Modules:
  0.0 508.1 jit_solution(16721805559672640501)
XLA Ops:
  7.2 2.3 constant_dynamic-slice_fusion
  10.3 11.8 %project_qkv.1 = (bf16[640,2048]{1,0:T(8,128)(2,1)}, bf16[3,640,128]{2,1,0:T(8,128)(2,1)}, bf16[3,640,128]{2,1,0:T(8,128)(2,1)}, bf16[3,640,128]{2,1,0:T(8,128)(2,1)}, bf16[3,640,128]{2,1,0:T(8,128)(2,1)}) custom-call(s32[40]{0:T(128)} %parent.7, s32[6]{0:T(128)} %stack.39.place, bf16[640,2048]{1,0:T(8,128)(2,1)} %refs_1_.1, bf16[2048,512]{1,0:T(8,128)(2,1)} %wq.3, ...), custom_call_target="tpu_custom_call" | custom-call | bytes 1 | tf_op jit(solution)/shard_map/project_qkv/pallas_call | solution.py:169
  22.1 2.9 collective-permute-start
  26.6 10.4 %grad_hidden.1.seed = f32[640,2048]{1,0:T(8,128)} custom-call(bf16[640,2048]{1,0:T(8,128)(2,1)} %refs_5_.1, bf16[2048,2048]{1,0:T(8,128)(2,1)} %refs_2_.1), custom_call_target="tpu_custom_call" | custom-call | bytes 1 | tf_op jit(solution)/shard_map/grad_hidden/pallas_call | solution.py:518
  37.3 11.2 %collective-permute-done.1.refs_2_ = bf16[3,640,128]{2,1,0:T(8,128)(2,1)S(1)} collective-permute-done((bf16[3,640,128]{2,1,0:T(8,128)(2,1)}, bf16[3,640,128]{2,1,0:T(8,128)(2,1)S(1)}, u32[]{:S(2)}, u32[]{:S(2)}) %collective-permute-start.1) | collective-permute-done | bytes 491552 | tf_op jit(solution)/shard_map/ppermute | solution.py:1086
  49.4 3.0 collective-permute-done.3
  52.4 1.7 pad_maximum_fusion
  54.1 12.3 %attend.1 = (bf16[640,128]{1,0:T(8,128)(2,1)}, bf16[640,128]{1,0:T(8,128)(2,1)}, bf16[640,128]{1,0:T(8,128)(2,1)}, bf16[640,128]{1,0:T(8,128)(2,1)}) custom-call(s32[40]{0:T(128)} %parent.7, s32[6]{0:T(128)} %stack.39.place, bf16[3,640,128]{2,1,0:T(8,128)(2,1)} %get-tuple-element.265.refs_0_, bf16[3,640,128]{2,1,0:T(8,128)(2,1)} %copy-done.1, ...), custom_call_target="tpu_custom_call" | custom-call | bytes 1 | tf_op jit(solution)/shard_map/attend/pallas_call | solution.py:247
  70.0 3.8 collective-permute-done.4.refs_1_
  73.7 2.1 collective-permute-done.5.refs_2_
  78.1 2.8 gather_heads.1
  80.8 12.9 %all-gather.10.cloned.1.call-done = bf16[1024,2048]{1,0:T(8,128)(2,1)} async-done(((bf16[256,2048]{1,0:T(8,128)(2,1)}), bf16[1024,2048]{1,0:T(8,128)(2,1)}) %all-gather.10.cloned.1.call-update) | async-done | bytes 4194320 | tf_op jit(solution)/shard_map/all_gather | solution.py:1093
  94.7 32.4 %all-gather.12.cloned.1.call-done = bf16[1280,512]{1,0:T(8,128)(2,1)} async-done(((bf16[320,512]{1,0:T(8,128)(2,1)}), bf16[1280,512]{1,0:T(8,128)(2,1)}) %all-gather.12.cloned.1.call-update) | async-done | bytes 1310736 | tf_op jit(solution)/shard_map/all_gather | solution.py:1111
  127.1 9.2 %project_out.2 = (f32[320,2048]{1,0:T(8,128)}, bf16[320,2048]{1,0:T(8,128)(2,1)}) custom-call(s32[6]{0:T(128)} %stack.39.place, bf16[640,2048]{1,0:T(8,128)(2,1)} %refs_1_.1, bf16[4,320,512]{2,1,0:T(8,128)(2,1)} %bitcast.37, bf16[4,256,2048]{2,1,0:T(8,128)(2,1)} %bitcast.42, bf16[4,256,2048]{2,1,0:T(8,128)(2,1)} %collective-permute-done.7.far.refs_7_), custom_call_target="tpu_custom_call" | custom-call | flops 112000000000 | bytes 1 | tf_op jit(solution)/shard_map/project_out/pallas_call | solution.py:490
  136.3 17.8 %feed_forward.2 = (bf16[320,2048]{1,0:T(8,128)(2,1)}, bf16[320,2048]{1,0:T(8,128)(2,1)}, bf16[320,2048]{1,0:T(8,128)(2,1)}, bf16[320,2048]{1,0:T(8,128)(2,1)}) custom-call(bf16[320,2048]{1,0:T(8,128)(2,1)} %get-tuple-element.286.normed.refs_0_, f32[640,2048]{1,0:T(8,128)} %grad_hidden.1.seed, bf16[2048,2048]{1,0:T(8,128)(2,1)} %wg.3, bf16[2048,2048]{1,0:T(8,128)(2,1)} %wu.3), custom_call_target="tpu_custom_call" | custom-call | flops 271999991808 | bytes 1 | tf_op jit(solution)/shard_map/feed_forward/pallas_call | solution.py:589
  154.4 6.5 %all-gather.14.cloned.1.call-done = bf16[1280,512]{1,0:T(8,128)(2,1)} async-done(((bf16[320,512]{1,0:T(8,128)(2,1)}), bf16[1280,512]{1,0:T(8,128)(2,1)}) %all-gather.14.cloned.1.call-update) | async-done | bytes 1310736 | tf_op jit(solution)/shard_map/all_gather | solution.py:1111
  160.9 9.2 %project_out.3 = (f32[320,2048]{1,0:T(8,128)}, bf16[320,2048]{1,0:T(8,128)(2,1)}) custom-call(s32[6]{0:T(128)} %stack.39.place, bf16[640,2048]{1,0:T(8,128)(2,1)} %refs_1_.1, bf16[4,320,512]{2,1,0:T(8,128)(2,1)} %bitcast.39, bf16[4,256,2048]{2,1,0:T(8,128)(2,1)} %bitcast.43, bf16[4,256,2048]{2,1,0:T(8,128)(2,1)} %collective-permute-done.7.far.refs_7_), custom_call_target="tpu_custom_call" | custom-call | flops 112000000000 | bytes 1 | tf_op jit(solution)/shard_map/project_out/pallas_call | solution.py:490
  170.2 17.8 %feed_forward.3 = (bf16[320,2048]{1,0:T(8,128)(2,1)}, bf16[320,2048]{1,0:T(8,128)(2,1)}, bf16[320,2048]{1,0:T(8,128)(2,1)}, bf16[320,2048]{1,0:T(8,128)(2,1)}) custom-call(bf16[320,2048]{1,0:T(8,128)(2,1)} %get-tuple-element.293.normed.refs_1_, f32[640,2048]{1,0:T(8,128)} %grad_hidden.1.seed, bf16[2048,2048]{1,0:T(8,128)(2,1)} %wg.3, bf16[2048,2048]{1,0:T(8,128)(2,1)} %wu.3), custom_call_target="tpu_custom_call" | custom-call | flops 271999991808 | bytes 1 | tf_op jit(solution)/shard_map/feed_forward/pallas_call | solution.py:589
  188.5 8.7 %wgrad_away.5 = bf16[1024,2048]{1,0:T(8,128)(2,1)} custom-call(s32[6]{0:T(128)} %stack.39.place, bf16[640,2048]{1,0:T(8,128)(2,1)} %refs_5_.1, bf16[320,2048]{1,0:T(8,128)(2,1)} %get-tuple-element.312.refs_1_.refs_0_, bf16[320,2048]{1,0:T(8,128)(2,1)} %get-tuple-element.313.refs_2_.refs_1_), custom_call_target="tpu_custom_call" | custom-call | flops 128000000000 | bytes 1 | tf_op jit(solution)/shard_map/wgrad_away/pallas_call | solution.py:737
  197.2 8.8 %wgrad_away.6 = bf16[1024,2048]{1,0:T(8,128)(2,1)} custom-call(s32[6]{0:T(128)} %stack.39.place, bf16[320,2048]{1,0:T(8,128)(2,1)} %get-tuple-element.286.normed.refs_0_, bf16[320,2048]{1,0:T(8,128)(2,1)} %get-tuple-element.293.normed.refs_1_, bf16[320,2048]{1,0:T(8,128)(2,1)} %get-tuple-element.300.refs_2_, bf16[320,2048]{1,0:T(8,128)(2,1)} %get-tuple-element.301.refs_3_), custom_call_target="tpu_custom_call" | custom-call | flops 128000000000 | bytes 1 | tf_op jit(solution)/shard_map/wgrad_away/pallas_call | solution.py:737
  206.1 10.2 %wgrad_keep.5 = (bf16[512,1024]{1,0:T(8,128)(2,1)}, bf16[512,1024]{1,0:T(8,128)(2,1)}, bf16[512,1024]{1,0:T(8,128)(2,1)}, bf16[512,1024]{1,0:T(8,128)(2,1)}) custom-call(s32[6]{0:T(128)} %stack.39.place, bf16[640,2048]{1,0:T(8,128)(2,1)} %refs_5_.1, bf16[320,2048]{1,0:T(8,128)(2,1)} %get-tuple-element.312.refs_1_.refs_0_, ...), custom_call_target="tpu_custom_call" | custom-call | flops 143999991808 | bytes 1 | tf_op jit(solution)/shard_map/wgrad_keep/pallas_call | solution.py:785
  216.3 9.9 %reduce-scatter.6.cloned.1.call-done.refs_1_ = bf16[80,2048]{1,0:T(8,128)(2,1)} async-done(((bf16[320,2048]{1,0:T(8,128)(2,1)}), bf16[80,2048]{1,0:T(8,128)(2,1)}) %reduce-scatter.6.cloned.1.call-update) | async-done | bytes 327696 | tf_op jit(solution)/shard_map/reduce_scatter | solution.py:1125
  229.1 10.1 %branch_back.1 = (f32[160,2048]{1,0:T(8,128)}, bf16[160,2048]{1,0:T(8,128)(2,1)}, bf16[160,512]{1,0:T(8,128)(2,1)}, bf16[160,512]{1,0:T(8,128)(2,1)}, bf16[160,5...) custom-call(s32[6]{0:T(128)} %stack.39.place, bf16[80,2048]{1,0:T(8,128)(2,1)} %reduce-scatter.4.cloned.1.call-done.refs_0_, ...), custom_call_target="tpu_custom_call" | custom-call | flops 143999991808 | bytes 1 | tf_op jit(solution)/shard_map/branch_back/pallas_call | solution.py:671
  239.2 1.7 collective-permute-start.12
  241.0 2.4 collective-permute-start.13
  246.4 4.8 collective-permute-done.9.a_got
  252.4 9.7 %project_down.1 = bf16[640,2048]{1,0:T(8,128)(2,1)} custom-call(bf16[320,2048]{1,0:T(8,128)(2,1)} %get-tuple-element.312.refs_1_.refs_0_, bf16[320,2048]{1,0:T(8,128)(2,1)} %get-tuple-element.313.refs_2_.refs_1_, bf16[2048,2048]{1,0:T(8,128)(2,1)} %refs_2_.1), custom_call_target="tpu_custom_call" | custom-call | flops 176000008192 | bytes 1 | tf_op jit(solution)/shard_map/project_down/pallas_call | solution.py:619
  262.1 2.8 scatter_heads.1
  264.9 5.6 %wgrad_away.7 = bf16[1024,2048]{1,0:T(8,128)(2,1)} custom-call(s32[6]{0:T(128)} %stack.39.place, bf16[160,2048]{1,0:T(8,128)(2,1)} %get-tuple-element.326.refs_0_, bf16[160,2048]{1,0:T(8,128)(2,1)} %copy-done.6), custom_call_target="tpu_custom_call" | custom-call | flops 1280000000000 | bytes 1 | tf_op jit(solution)/shard_map/wgrad_away/pallas_call | solution.py:737
  274.9 3.2 collective-permute-done.17.refs_2_
  278.1 7.0 %wgrad_keep.6 = (bf16[512,1024]{1,0:T(8,128)(2,1)}, bf16[512,1024]{1,0:T(8,128)(2,1)}, bf16[512,1024]{1,0:T(8,128)(2,1)}, bf16[512,1024]{1,0:T(8,128)(2,1)}) custom-call(s32[6]{0:T(128)} %stack.39.place, bf16[160,2048]{1,0:T(8,128)(2,1)} %get-tuple-element.326.refs_0_, bf16[160,2048]{1,0:T(8,128)(2,1)} %copy-done.6, ...), custom_call_target="tpu_custom_call" | custom-call | flops 143999991808 | bytes 1 | tf_op jit(solution)/shard_map/wgrad_keep/pallas_call | solution.py:785
  287.3 23.1 %attend_back.1 = (bf16[640,128]{1,0:T(8,128)(2,1)}, bf16[640,128]{1,0:T(8,128)(2,1)}, bf16[640,128]{1,0:T(8,128)(2,1)}, bf16[640,128]{1,0:T(8,128)(2,1)}, f32[40...) custom-call(s32[40]{0:T(128)} %parent.7, s32[6]{0:T(128)} %stack.39.place, ...), custom_call_target="tpu_custom_call" | custom-call | flops 368000008192 | bytes 1 | tf_op jit(solution)/shard_map/attend_back/pallas_call | solution.py:305
  311.0 3.3 wgrad_stage.5
  315.4 3.8 combine_back.1
  322.7 3.3 wgrad_stage.6
  326.0 9.1 %wgrad_away.8 = bf16[1024,2048]{1,0:T(8,128)(2,1)} custom-call(s32[6]{0:T(128)} %stack.39.place, bf16[320,2048]{1,0:T(8,128)(2,1)} %get-tuple-element.286.normed.refs_0_, bf16[320,2048]{1,0:T(8,128)(2,1)} %get-tuple-element.293.normed.refs_1_, bf16[320,2048]{1,0:T(8,128)(2,1)} %get-tuple-element.373.refs_2_, bf16[320,2048]{1,0:T(8,128)(2,1)} %get-tuple-element.374.refs_3_), custom_call_target="tpu_custom_call" | custom-call | flops 128000000000 | bytes 1 | tf_op jit(solution)/shard_map/wgrad_away/pallas_call | solution.py:737
  335.1 10.3 %wgrad_keep.7 = (bf16[512,1024]{1,0:T(8,128)(2,1)}, bf16[512,1024]{1,0:T(8,128)(2,1)}, bf16[512,1024]{1,0:T(8,128)(2,1)}, bf16[512,1024]{1,0:T(8,128)(2,1)}) custom-call(s32[6]{0:T(128)} %stack.39.place, bf16[320,2048]{1,0:T(8,128)(2,1)} %get-tuple-element.286.normed.refs_0_, bf16[320,2048]{1,0:T(8,128)(2,1)} %get-tuple-element.293.normed.refs_1_, ...), custom_call_target="tpu_custom_call" | custom-call | flops 143999991808 | bytes 1 | tf_op jit(solution)/shard_map/wgrad_keep/pallas_call | solution.py:785
  348.4 10.9 %turn_back.1 = (bf16[640,2048]{1,0:T(8,128)(2,1)}, bf16[640,1536]{1,0:T(8,128)(2,1)}) custom-call(s32[40]{0:T(128)} %parent.7, s32[6]{0:T(128)} %stack.39.place, f32[1280,128]{1,0:T(8,128)} %constant.39.clone.cosine, f32[1280,128]{1,0:T(8,128)} %constant.40.clone.sine, bf16[2048,512]{1,0:T(8,128)(2,1)} %wq.3, bf16[2048,512]{1,0:T(8,128)(2,1)} %wk.3, ...), custom_call_target="tpu_custom_call" | custom-call | flops 207999991808 | bytes 1 | tf_op jit(solution)/shard_map/turn_back/pallas_call | solution.py:447
  360.8 7.0 %wgrad_away.9 = bf16[1024,1536]{1,0:T(8,128)(2,1)} custom-call(s32[6]{0:T(128)} %stack.39.place, bf16[640,2048]{1,0:T(8,128)(2,1)} %get-tuple-element.258.refs_0_, bf16[640,1536]{1,0:T(8,128)(2,1)} %get-tuple-element.388.refs_1_), custom_call_target="tpu_custom_call" | custom-call | flops 128000000000 | bytes 1 | tf_op jit(solution)/shard_map/wgrad_away/pallas_call | solution.py:737
  367.8 10.4 %wgrad_keep.8 = (bf16[512,1024]{1,0:T(8,128)(2,1)}, bf16[512,1024]{1,0:T(8,128)(2,1)}, bf16[512,1024]{1,0:T(8,128)(2,1)}, bf16[512,1024]{1,0:T(8,128)(2,1)}) custom-call(s32[6]{0:T(128)} %stack.39.place, bf16[320,2048]{1,0:T(8,128)(2,1)} %get-tuple-element.286.normed.refs_0_, bf16[320,2048]{1,0:T(8,128)(2,1)} %get-tuple-element.293.normed.refs_1_, ...), custom_call_target="tpu_custom_call" | custom-call | flops 4320000000 | bytes 1 | tf_op jit(solution)/shard_map/wgrad_keep/pallas_call | solution.py:785
  378.2 1.5 collective-permute-start.31
  381.1 3.3 collective-permute-done.29.refs_1_
  384.4 3.9 wgrad_finish_chunks.1
  388.3 3.3 wgrad_stage.7
  391.6 1.6 copy-done.10
  393.2 8.2 %wgrad_keep.9 = (bf16[512,768]{1,0:T(8,128)(2,1)}, bf16[512,768]{1,0:T(8,128)(2,1)}, bf16[512,768]{1,0:T(8,128)(2,1)}, bf16[512,768]{1,0:T(8,128)(2,1)}) custom-call(s32[6]{0:T(128)} %stack.39.place, bf16[640,2048]{1,0:T(8,128)(2,1)} %get-tuple-element.258.refs_0_, bf16[640,1536]{1,0:T(8,128)(2,1)} %get-tuple-element.388.refs_1_, bf16[1024,1536]{1,0:T(8,128)(2,1)} %copy-done.10), custom_call_target="tpu_custom_call" | custom-call | flops 143999991808 | bytes 1 | tf_op jit(solution)/shard_map/wgrad_keep/pallas_call | solution.py:785
  401.5 5.5 %add_residual.1 = bf16[640,2048]{1,0:T(8,128)(2,1)} custom-call(f32[320,2048]{1,0:T(8,128)} %get-tuple-element.282.refs_2_.refs_0_, f32[320,2048]{1,0:T(8,128)} %get-tuple-element.290.refs_3_.refs_1_, bf16[640,2048]{1,0:T(8,128)(2,1)} %all-reduce.2.cloned.1.call-done.refs_2_), custom_call_target="tpu_custom_call" | custom-call | flops 96000000000 | bytes 1 | tf_op jit(solution)/shard_map/add_residual/pallas_call | solution.py:1053
  409.0 23.6 %reduce-scatter.8.cloned.1.call-done.part = bf16[160,2048]{1,0:T(8,128)(2,1)} async-done(((bf16[640,2048]{1,0:T(8,128)(2,1)}), bf16[160,2048]{1,0:T(8,128)(2,1)}) %reduce-scatter.8.cloned.1.call-update) | async-done | bytes 655376 | tf_op jit(solution)/shard_map/reduce_scatter | solution.py:1201
  432.5 4.1 tokens_back.1
  436.6 1.5 collective-permute-start.36
  441.6 3.6 wgrad_stage.8
  445.2 3.8 collective-permute-done.38
  449.8 2.0 collective-permute-start.43
  453.4 3.6 wgrad_finish.3
  458.9 3.0 wgrad_finish.4
  462.0 8.1 %collective-permute-done.34.a_got = bf16[512,768]{1,0:T(8,128)(2,1)S(1)} collective-permute-done((bf16[512,768]{1,0:T(8,128)(2,1)S(1)}, bf16[512,768]{1,0:T(8,128)(2,1)S(1)}, u32[]{:S(2)}, u32[]{:S(2)}) %collective-permute-start.34) | collective-permute-done | bytes 786464 | tf_op jit(solution)/shard_map/ppermute | solution.py:921
  471.0 2.8 wgrad_stage.9
  475.8 4.1 collective-permute-done.44.a_got
  479.9 1.6 collective-permute-done.45.b_got
  481.5 3.1 wgrad_finish.5
  484.5 1.9 add_last.1
  488.8 2.5 wgrad_finish_split.1
  491.4 6.1 %all-gather.8.cloned.1.call-done = bf16[640,2048]{1,0:T(8,128)(2,1)} async-done(((bf16[160,2048]{1,0:T(8,128)(2,1)}), bf16[640,2048]{1,0:T(8,128)(2,1)}) %all-gather.8.cloned.1.call-update) | async-done | bytes 2621456 | tf_op jit(solution)/shard_map/all_gather | solution.py:1211
  497.5 3.6 copy.23
  (164 shorter events, 50.8 us)
Async XLA Ops:
  7.2 86.5 %all-gather.10.cloned.1.call-start = ((), (), s32[]{:S(2)}) async-start(), calls=%async_computation.8 | async-start | bytes 5242880 | tf_op jit(solution)/shard_map/all_gather | solution.py:1093
  9.6 117.5 %all-gather.12.cloned.1.call-start = ((), (), s32[]{:S(2)}) async-start(), calls=%async_computation.9 | async-start | bytes 1638400 | tf_op jit(solution)/shard_map/all_gather | solution.py:1111
  22.1 15.2 %collective-permute-start = (bf16[3,640,128]{2,1,0:T(8,128)(2,1)}, bf16[3,640,128]{2,1,0:T(8,128)(2,1)S(1)}, u32[]{:S(2)}, u32[]{:S(2)}) collective-permute-start(bf16[3,640,128]{2,1,0:T(8,128)(2,1)} %get-tuple-element.255), channel_id=1, source_target_pairs={{0,8},{4,12},{8,0},{12,4},{16,24},{20,28},{24,16},{28,20},{1,9},{5... | collective-permute-start | bytes 1474568 | tf_op jit(solution)/shard_map/ppermute | solution.py:1086
  25.0 23.4 %collective-permute-start.1 = (bf16[3,640,128]{2,1,0:T(8,128)(2,1)}, bf16[3,640,128]{2,1,0:T(8,128)(2,1)S(1)}, u32[]{:S(2)}, u32[]{:S(2)}) collective-permute-start(bf16[3,640,128]{2,1,0:T(8,128)(2,1)} %get-tuple-element.256), channel_id=1, source_target_pairs={{0,16},{4,20},{8,24},{12,28},{16,0},{20,4},{24,8},{28,12},{1,17},{... | collective-permute-start | bytes 1474568 | tf_op jit(solution)/shard_map/ppermute | solution.py:1086
  26.6 21.9 %collective-permute-start.2 = (bf16[3,640,128]{2,1,0:T(8,128)(2,1)}, bf16[3,640,128]{2,1,0:T(8,128)(2,1)S(1)}, u32[]{:S(2)}, u32[]{:S(2)}) collective-permute-start(bf16[3,640,128]{2,1,0:T(8,128)(2,1)} %get-tuple-element.257), channel_id=1, source_target_pairs={{0,24},{4,28},{8,16},{12,20},{16,8},{20,12},{24,0},{28,4},{1,25},{... | collective-permute-start | bytes 1474568 | tf_op jit(solution)/shard_map/ppermute | solution.py:1086
  26.6 21.9 %copy-start = (bf16[3,640,128]{2,1,0:T(8,128)(2,1)S(1)}, bf16[3,640,128]{2,1,0:T(8,128)(2,1)}, u32[]{:S(2)}) copy-start(bf16[3,640,128]{2,1,0:T(8,128)(2,1)} %get-tuple-element.265.refs_0_) | copy-start | bytes 1474564
  37.3 11.5 %copy-start.1 = (bf16[3,640,128]{2,1,0:T(8,128)(2,1)}, bf16[3,640,128]{2,1,0:T(8,128)(2,1)S(1)}, u32[]{:S(2)}) copy-start(bf16[3,640,128]{2,1,0:T(8,128)(2,1)S(1)} %collective-permute-done.refs_1_) | copy-start | bytes 1474564
  49.4 3.0 collective-permute-start.3
  66.5 7.3 %collective-permute-start.4 = (bf16[640,128]{1,0:T(8,128)(2,1)}, bf16[640,128]{1,0:T(8,128)(2,1)S(1)}, u32[]{:S(2)}, u32[]{:S(2)}) collective-permute-start(bf16[640,128]{1,0:T(8,128)(2,1)} %get-tuple-element.270), channel_id=1, source_target_pairs={{0,8},{4,12},{8,0},{12,4},{16,24},{20,28},{24,16},{28,20},{1,9},{5... | collective-permute-start | bytes 491528 | tf_op jit(solution)/shard_map/ppermute | solution.py:1086
  67.6 8.3 %collective-permute-start.5 = (bf16[640,128]{1,0:T(8,128)(2,1)}, bf16[640,128]{1,0:T(8,128)(2,1)S(1)}, u32[]{:S(2)}, u32[]{:S(2)}) collective-permute-start(bf16[640,128]{1,0:T(8,128)(2,1)} %get-tuple-element.271), channel_id=1, source_target_pairs={{0,16},{4,20},{8,24},{12,28},{16,0},{20,4},{24,8},{28,12},{1,17},{... | collective-permute-start | bytes 491528 | tf_op jit(solution)/shard_map/ppermute | solution.py:1086
  68.5 8.9 %collective-permute-start.6 = (bf16[640,128]{1,0:T(8,128)(2,1)}, bf16[640,128]{1,0:T(8,128)(2,1)S(1)}, u32[]{:S(2)}, u32[]{:S(2)}) collective-permute-start(bf16[640,128]{1,0:T(8,128)(2,1)} %get-tuple-element.272), channel_id=1, source_target_pairs={{0,24},{4,28},{8,16},{12,20},{16,8},{20,12},{24,0},{28,4},{1,25},{... | collective-permute-start | bytes 491528 | tf_op jit(solution)/shard_map/ppermute | solution.py:1086
  93.7 33.4 %collective-permute-start.7 = (bf16[4,256,2048]{2,1,0:T(8,128)(2,1)}, bf16[4,256,2048]{2,1,0:T(8,128)(2,1)}, u32[]{:S(2)}, u32[]{:S(2)}) collective-permute-start(bf16[4,256,2048]{2,1,0:T(8,128)(2,1)} %bitcast.41), channel_id=1, source_target_pairs={{0,4},{4,0},{8,12},{12,8},{16,20},{20,16},{24,28},{28,24},{1,5},{5... | collective-permute-start | bytes 12582920 | tf_op jit(solution)/shard_map/ppermute | solution.py:1086
  93.7 67.2 %all-gather.14.cloned.1.call-start = ((), (), s32[]{:S(2)}) async-start(), calls=%async_computation.10 | async-start | bytes 1638400 | tf_op jit(solution)/shard_map/all_gather | solution.py:1111
  94.5 121.8 %reduce-scatter.4.cloned.1.call-start = ((), (), s32[]{:S(2)}) async-start(), calls=%async_computation.3 | async-start | bytes 1638400 | tf_op jit(solution)/shard_map/reduce_scatter | solution.py:1125
  154.1 72.0 %reduce-scatter.6.cloned.1.call-start = ((), (), s32[]{:S(2)}) async-start(), calls=%async_computation.4 | async-start | bytes 1638400 | tf_op jit(solution)/shard_map/reduce_scatter | solution.py:1125
  188.1 213.4 %all-reduce.2.cloned.1.call-start = ((), (), s32[]{:S(2)}) async-start(), calls=%async_computation.5 | async-start | bytes 5242880 | tf_op jit(solution)/shard_map/psum | solution.py:1161
  197.2 8.9 %collective-permute-start.8 = (bf16[1024,2048]{1,0:T(8,128)(2,1)}, bf16[1024,2048]{1,0:T(8,128)(2,1)}, u32[]{:S(2)}, u32[]{:S(2)}) collective-permute-start(bf16[1024,2048]{1,0:T(8,128)(2,1)} %wgrad_away.5), channel_id=1, source_target_pairs={{0,4},{4,0},{8,12},{12,8},{16,20},{20,16},{24,28},{28,24},{1,5},{5... | collective-permute-start | bytes 12582920 | tf_op jit(solution)/shard_map/ppermute | solution.py:921
  226.1 25.1 %collective-permute-start.9 = (bf16[512,1024]{1,0:T(8,128)(2,1)}, bf16[512,1024]{1,0:T(8,128)(2,1)}, u32[]{:S(2)}, u32[]{:S(2)}) collective-permute-start(bf16[512,1024]{1,0:T(8,128)(2,1)} %get-tuple-element.306), channel_id=1, source_target_pairs={{0,8},{4,12},{8,0},{12,4},{16,24},{20,28},{24,16},{28,20},{1,9},{5... | collective-permute-start | bytes 3145736 | tf_op jit(solution)/shard_map/ppermute | solution.py:921
  227.6 24.8 %collective-permute-start.10 = (bf16[512,1024]{1,0:T(8,128)(2,1)}, bf16[512,1024]{1,0:T(8,128)(2,1)}, u32[]{:S(2)}, u32[]{:S(2)}) collective-permute-start(bf16[512,1024]{1,0:T(8,128)(2,1)} %get-tuple-element.307), channel_id=1, source_target_pairs={{0,16},{4,20},{8,24},{12,28},{16,0},{20,4},{24,8},{28,12},{1,17},{... | collective-permute-start | bytes 3145736 | tf_op jit(solution)/shard_map/ppermute | solution.py:921
  239.2 22.9 %collective-permute-start.11 = (bf16[160,512]{1,0:T(8,128)(2,1)}, bf16[160,512]{1,0:T(8,128)(2,1)}, u32[]{:S(2)}, u32[]{:S(2)}) collective-permute-start(bf16[160,512]{1,0:T(8,128)(2,1)} %get-tuple-element.315), channel_id=1, source_target_pairs={{0,1},{1,2},{2,3},{3,0},{4,5},{5,6},{6,7},{7,4},{8,9},{9,10},{10,1... | collective-permute-start | bytes 491528 | tf_op jit(solution)/shard_map/ppermute | solution.py:999
  239.2 22.9 %collective-permute-start.12 = (bf16[160,512]{1,0:T(8,128)(2,1)}, bf16[160,512]{1,0:T(8,128)(2,1)}, u32[]{:S(2)}, u32[]{:S(2)}) collective-permute-start(bf16[160,512]{1,0:T(8,128)(2,1)} %get-tuple-element.316), channel_id=1, source_target_pairs={{0,2},{1,3},{2,0},{3,1},{4,6},{5,7},{6,4},{7,5},{8,10},{9,11},{10,... | collective-permute-start | bytes 491528 | tf_op jit(solution)/shard_map/ppermute | solution.py:999
  241.0 21.1 %collective-permute-start.13 = (bf16[160,512]{1,0:T(8,128)(2,1)}, bf16[160,512]{1,0:T(8,128)(2,1)}, u32[]{:S(2)}, u32[]{:S(2)}) collective-permute-start(bf16[160,512]{1,0:T(8,128)(2,1)} %get-tuple-element.317), channel_id=1, source_target_pairs={{0,3},{1,0},{2,1},{3,2},{4,7},{5,4},{6,5},{7,6},{8,11},{9,8},{10,9... | collective-permute-start | bytes 491528 | tf_op jit(solution)/shard_map/ppermute | solution.py:999
  270.5 7.6 %collective-permute-start.17 = (bf16[1024,2048]{1,0:T(8,128)(2,1)}, bf16[1024,2048]{1,0:T(8,128)(2,1)}, u32[]{:S(2)}, u32[]{:S(2)}) collective-permute-start(bf16[1024,2048]{1,0:T(8,128)(2,1)} %wgrad_away.7), channel_id=1, source_target_pairs={{0,4},{4,0},{8,12},{12,8},{16,20},{20,16},{24,28},{28,24},{1,5},{5... | collective-permute-start | bytes 12582920 | tf_op jit(solution)/shard_map/ppermute | solution.py:921
  270.6 64.5 %collective-permute-start.24 = (bf16[1024,2048]{1,0:T(8,128)(2,1)}, bf16[1024,2048]{1,0:T(8,128)(2,1)}, u32[]{:S(2)}, u32[]{:S(2)}) collective-permute-start(bf16[1024,2048]{1,0:T(8,128)(2,1)} %wgrad_away.6), channel_id=1, source_target_pairs={{0,4},{4,0},{8,12},{12,8},{16,20},{20,16},{24,28},{28,24},{1,5},{5... | collective-permute-start | bytes 12582920 | tf_op jit(solution)/shard_map/ppermute | solution.py:921
  271.1 161.4 %reduce-scatter.8.cloned.1.call-start = ((), (), s32[]{:S(2)}) async-start(), calls=%async_computation.6 | async-start | bytes 3276800 | tf_op jit(solution)/shard_map/reduce_scatter | solution.py:1201
  271.4 13.7 %collective-permute-start.14 = (bf16[640,128]{1,0:T(8,128)(2,1)S(1)}, bf16[640,128]{1,0:T(8,128)(2,1)S(1)}, u32[]{:S(2)}, u32[]{:S(2)}) collective-permute-start(bf16[640,128]{1,0:T(8,128)(2,1)S(1)} %copy-done.28), channel_id=1, source_target_pairs={{0,8},{4,12},{8,0},{12,4},{16,24},{20,28},{24,16},{28,20},{1,9},{5... | collective-permute-start | bytes 491528 | tf_op jit(solution)/shard_map/ppermute | solution.py:1086
  272.0 13.1 %collective-permute-start.15 = (bf16[640,128]{1,0:T(8,128)(2,1)S(1)}, bf16[640,128]{1,0:T(8,128)(2,1)S(1)}, u32[]{:S(2)}, u32[]{:S(2)}) collective-permute-start(bf16[640,128]{1,0:T(8,128)(2,1)S(1)} %copy-done.26), channel_id=1, source_target_pairs={{0,16},{4,20},{8,24},{12,28},{16,0},{20,4},{24,8},{28,12},{1,17},{... | collective-permute-start | bytes 491528 | tf_op jit(solution)/shard_map/ppermute | solution.py:1086
  273.5 11.7 %collective-permute-start.16 = (bf16[640,128]{1,0:T(8,128)(2,1)S(1)}, bf16[640,128]{1,0:T(8,128)(2,1)S(1)}, u32[]{:S(2)}, u32[]{:S(2)}) collective-permute-start(bf16[640,128]{1,0:T(8,128)(2,1)S(1)} %copy-done.24), channel_id=1, source_target_pairs={{0,24},{4,28},{8,16},{12,20},{16,8},{20,12},{24,0},{28,4},{1,25},{... | collective-permute-start | bytes 491528 | tf_op jit(solution)/shard_map/ppermute | solution.py:1086
  285.2 25.6 %collective-permute-start.18 = (bf16[512,1024]{1,0:T(8,128)(2,1)}, bf16[512,1024]{1,0:T(8,128)(2,1)}, u32[]{:S(2)}, u32[]{:S(2)}) collective-permute-start(bf16[512,1024]{1,0:T(8,128)(2,1)} %get-tuple-element.348), channel_id=1, source_target_pairs={{0,8},{4,12},{8,0},{12,4},{16,24},{20,28},{24,16},{28,20},{1,9},{5... | collective-permute-start | bytes 3145736 | tf_op jit(solution)/shard_map/ppermute | solution.py:921
  285.8 25.2 %collective-permute-start.19 = (bf16[512,1024]{1,0:T(8,128)(2,1)}, bf16[512,1024]{1,0:T(8,128)(2,1)}, u32[]{:S(2)}, u32[]{:S(2)}) collective-permute-start(bf16[512,1024]{1,0:T(8,128)(2,1)} %get-tuple-element.349), channel_id=1, source_target_pairs={{0,16},{4,20},{8,24},{12,28},{16,0},{20,4},{24,8},{28,12},{1,17},{... | collective-permute-start | bytes 3145736 | tf_op jit(solution)/shard_map/ppermute | solution.py:921
  311.0 3.3 collective-permute-start.20
  319.2 27.7 %collective-permute-start.21 = (bf16[3,640,128]{2,1,0:T(8,128)(2,1)}, bf16[3,640,128]{2,1,0:T(8,128)(2,1)}, u32[]{:S(2)}, u32[]{:S(2)}) collective-permute-start(bf16[3,640,128]{2,1,0:T(8,128)(2,1)} %get-tuple-element.361), channel_id=1, source_target_pairs={{0,8},{4,12},{8,0},{12,4},{16,24},{20,28},{24,16},{28,20},{1,9},{5... | collective-permute-start | bytes 1474568 | tf_op jit(solution)/shard_map/ppermute | solution.py:1086
  320.7 27.7 %collective-permute-start.22 = (bf16[3,640,128]{2,1,0:T(8,128)(2,1)}, bf16[3,640,128]{2,1,0:T(8,128)(2,1)}, u32[]{:S(2)}, u32[]{:S(2)}) collective-permute-start(bf16[3,640,128]{2,1,0:T(8,128)(2,1)} %get-tuple-element.362), channel_id=1, source_target_pairs={{0,16},{4,20},{8,24},{12,28},{16,0},{20,4},{24,8},{28,12},{1,17},{... | collective-permute-start | bytes 1474568 | tf_op jit(solution)/shard_map/ppermute | solution.py:1086
  322.2 26.2 %collective-permute-start.23 = (bf16[3,640,128]{2,1,0:T(8,128)(2,1)}, bf16[3,640,128]{2,1,0:T(8,128)(2,1)}, u32[]{:S(2)}, u32[]{:S(2)}) collective-permute-start(bf16[3,640,128]{2,1,0:T(8,128)(2,1)} %get-tuple-element.363), channel_id=1, source_target_pairs={{0,24},{4,28},{8,16},{12,20},{16,8},{20,12},{24,0},{28,4},{1,25},{... | collective-permute-start | bytes 1474568 | tf_op jit(solution)/shard_map/ppermute | solution.py:1086
  335.1 24.5 %collective-permute-start.25 = (bf16[1024,2048]{1,0:T(8,128)(2,1)}, bf16[1024,2048]{1,0:T(8,128)(2,1)}, u32[]{:S(2)}, u32[]{:S(2)}) collective-permute-start(bf16[1024,2048]{1,0:T(8,128)(2,1)} %wgrad_away.8), channel_id=1, source_target_pairs={{0,4},{4,0},{8,12},{12,8},{16,20},{20,16},{24,28},{28,24},{1,5},{5... | collective-permute-start | bytes 12582920 | tf_op jit(solution)/shard_map/ppermute | solution.py:921
  345.4 32.7 %collective-permute-start.27 = (bf16[512,1024]{1,0:T(8,128)(2,1)}, bf16[512,1024]{1,0:T(8,128)(2,1)}, u32[]{:S(2)}, u32[]{:S(2)}) collective-permute-start(bf16[512,1024]{1,0:T(8,128)(2,1)} %get-tuple-element.391), channel_id=1, source_target_pairs={{0,8},{4,12},{8,0},{12,4},{16,24},{20,28},{24,16},{28,20},{1,9},{5... | collective-permute-start | bytes 3145736 | tf_op jit(solution)/shard_map/ppermute | solution.py:921
  346.9 31.3 %collective-permute-start.28 = (bf16[512,1024]{1,0:T(8,128)(2,1)}, bf16[512,1024]{1,0:T(8,128)(2,1)}, u32[]{:S(2)}, u32[]{:S(2)}) collective-permute-start(bf16[512,1024]{1,0:T(8,128)(2,1)} %get-tuple-element.392), channel_id=1, source_target_pairs={{0,16},{4,20},{8,24},{12,28},{16,0},{20,4},{24,8},{28,12},{1,17},{... | collective-permute-start | bytes 3145736 | tf_op jit(solution)/shard_map/ppermute | solution.py:921
  359.3 138.1 %all-gather.8.cloned.1.call-start = ((), (), s32[]{:S(2)}) async-start(), calls=%async_computation.7 | async-start | bytes 3276800 | tf_op jit(solution)/shard_map/all_gather | solution.py:1211
  359.6 24.8 %collective-permute-start.29 = (bf16[256,1024]{1,0:T(8,128)(2,1)}, bf16[256,1024]{1,0:T(8,128)(2,1)}, u32[]{:S(2)}, u32[]{:S(2)}) collective-permute-start(bf16[256,1024]{1,0:T(8,128)(2,1)} %get-tuple-element.400), channel_id=1, source_target_pairs={{0,16},{4,20},{8,24},{12,28},{16,0},{20,4},{24,8},{28,12},{1,17},{... | collective-permute-start | bytes 1572872 | tf_op jit(solution)/shard_map/ppermute | solution.py:921
  360.3 24.1 %collective-permute-start.30 = (bf16[256,1024]{1,0:T(8,128)(2,1)S(1)}, bf16[256,1024]{1,0:T(8,128)(2,1)}, u32[]{:S(2)}, u32[]{:S(2)}) collective-permute-start(bf16[256,1024]{1,0:T(8,128)(2,1)S(1)} %copy-done.17), channel_id=1, source_target_pairs={{0,8},{4,12},{8,0},{12,4},{16,24},{20,28},{24,16},{28,20},{1,9},{5... | collective-permute-start | bytes 1572872 | tf_op jit(solution)/shard_map/ppermute | solution.py:921
  367.8 23.8 %collective-permute-start.26 = (bf16[1024,1536]{1,0:T(8,128)(2,1)}, bf16[1024,1536]{1,0:T(8,128)(2,1)S(1)}, u32[]{:S(2)}, u32[]{:S(2)}) collective-permute-start(bf16[1024,1536]{1,0:T(8,128)(2,1)} %wgrad_away.9), channel_id=1, source_target_pairs={{0,4},{4,0},{8,12},{12,8},{16,20},{20,16},{24,28},{28,24},{1,5},{5... | collective-permute-start | bytes 9437192 | tf_op jit(solution)/shard_map/ppermute | solution.py:921
  378.2 30.8 %collective-permute-start.31 = (bf16[512,1024]{1,0:T(8,128)(2,1)}, bf16[512,1024]{1,0:T(8,128)(2,1)}, u32[]{:S(2)}, u32[]{:S(2)}) collective-permute-start(bf16[512,1024]{1,0:T(8,128)(2,1)} %get-tuple-element.418), channel_id=1, source_target_pairs={{0,8},{4,12},{8,0},{12,4},{16,24},{20,28},{24,16},{28,20},{1,9},{5... | collective-permute-start | bytes 3145736 | tf_op jit(solution)/shard_map/ppermute | solution.py:921
  379.7 29.2 %collective-permute-start.32 = (bf16[512,1024]{1,0:T(8,128)(2,1)}, bf16[512,1024]{1,0:T(8,128)(2,1)}, u32[]{:S(2)}, u32[]{:S(2)}) collective-permute-start(bf16[512,1024]{1,0:T(8,128)(2,1)} %get-tuple-element.419), channel_id=1, source_target_pairs={{0,16},{4,20},{8,24},{12,28},{16,0},{20,4},{24,8},{28,12},{1,17},{... | collective-permute-start | bytes 3145736 | tf_op jit(solution)/shard_map/ppermute | solution.py:921
  401.4 5.5 %copy-start.16 = (bf16[256,1024]{1,0:T(8,128)(2,1)S(1)}, bf16[256,1024]{1,0:T(8,128)(2,1)}, u32[]{:S(2)}) copy-start(bf16[256,1024]{1,0:T(8,128)(2,1)} %get-tuple-element.442) | copy-start | bytes 1572868
  401.4 7.0 %copy-start.15 = (bf16[256,1024]{1,0:T(8,128)(2,1)S(1)}, bf16[256,1024]{1,0:T(8,128)(2,1)}, u32[]{:S(2)}) copy-start(bf16[256,1024]{1,0:T(8,128)(2,1)} %get-tuple-element.443) | copy-start | bytes 1572868
  401.5 7.4 %copy-start.23 = (bf16[512,256]{1,0:T(8,128)(2,1)S(1)}, bf16[512,256]{1,0:T(8,128)(2,1)}, u32[]{:S(2)}) copy-start(bf16[512,256]{1,0:T(8,128)(2,1)} %get-tuple-element.427) | copy-start | bytes 786436
  406.9 33.6 %collective-permute-start.39 = (bf16[256,1024]{1,0:T(8,128)(2,1)S(1)}, bf16[256,1024]{1,0:T(8,128)(2,1)}, u32[]{:S(2)}, u32[]{:S(2)}) collective-permute-start(bf16[256,1024]{1,0:T(8,128)(2,1)S(1)} %copy-done.16), channel_id=1, source_target_pairs={{0,16},{4,20},{8,24},{12,28},{16,0},{20,4},{24,8},{28,12},{1,17},{... | collective-permute-start | bytes 1572872 | tf_op jit(solution)/shard_map/ppermute | solution.py:921
  408.4 32.7 %collective-permute-start.40 = (bf16[256,1024]{1,0:T(8,128)(2,1)S(1)}, bf16[256,1024]{1,0:T(8,128)(2,1)}, u32[]{:S(2)}, u32[]{:S(2)}) collective-permute-start(bf16[256,1024]{1,0:T(8,128)(2,1)S(1)} %copy-done.15), channel_id=1, source_target_pairs={{0,8},{4,12},{8,0},{12,4},{16,24},{20,28},{24,16},{28,20},{1,9},{5... | collective-permute-start | bytes 1572872 | tf_op jit(solution)/shard_map/ppermute | solution.py:921
  408.9 30.8 %copy-start.5 = (bf16[512,256]{1,0:T(8,128)(2,1)S(1)}, bf16[512,256]{1,0:T(8,128)(2,1)}, u32[]{:S(2)}) copy-start(bf16[512,256]{1,0:T(8,128)(2,1)} %get-tuple-element.430) | copy-start | bytes 786436
  408.9 31.6 %copy-start.13 = (bf16[512,768]{1,0:T(8,128)(2,1)S(1)}, bf16[512,768]{1,0:T(8,128)(2,1)}, u32[]{:S(2)}) copy-start(bf16[512,768]{1,0:T(8,128)(2,1)} %get-tuple-element.431) | copy-start | bytes 2359300
  408.9 32.2 %copy-start.12 = (bf16[512,768]{1,0:T(8,128)(2,1)S(1)}, bf16[512,768]{1,0:T(8,128)(2,1)}, u32[]{:S(2)}) copy-start(bf16[512,768]{1,0:T(8,128)(2,1)} %get-tuple-element.432) | copy-start | bytes 2359300
  408.9 30.8 %collective-permute-start.33 = (bf16[512,256]{1,0:T(8,128)(2,1)S(1)}, bf16[512,256]{1,0:T(8,128)(2,1)S(1)}, u32[]{:S(2)}, u32[]{:S(2)}) collective-permute-start(bf16[512,256]{1,0:T(8,128)(2,1)S(1)} %copy-done.23), channel_id=1, source_target_pairs={{0,1},{1,2},{2,3},{3,0},{4,5},{5,6},{6,7},{7,4},{8,9},{9,10},{10,1... | collective-permute-start | bytes 786440 | tf_op jit(solution)/shard_map/ppermute | solution.py:999
  436.6 15.2 %collective-permute-start.36 = (bf16[256,1024]{1,0:T(8,128)(2,1)}, bf16[256,1024]{1,0:T(8,128)(2,1)}, u32[]{:S(2)}, u32[]{:S(2)}) collective-permute-start(bf16[256,1024]{1,0:T(8,128)(2,1)} %get-tuple-element.435), channel_id=1, source_target_pairs={{0,16},{4,20},{8,24},{12,28},{16,0},{20,4},{24,8},{28,12},{1,17},{... | collective-permute-start | bytes 1572872 | tf_op jit(solution)/shard_map/ppermute | solution.py:921
  438.2 15.2 %collective-permute-start.37 = (bf16[256,1024]{1,0:T(8,128)(2,1)}, bf16[256,1024]{1,0:T(8,128)(2,1)}, u32[]{:S(2)}, u32[]{:S(2)}) collective-permute-start(bf16[256,1024]{1,0:T(8,128)(2,1)} %get-tuple-element.436), channel_id=1, source_target_pairs={{0,8},{4,12},{8,0},{12,4},{16,24},{20,28},{24,16},{28,20},{1,9},{5... | collective-permute-start | bytes 1572872 | tf_op jit(solution)/shard_map/ppermute | solution.py:921
  439.7 9.3 %collective-permute-start.38 = (bf16[512,256]{1,0:T(8,128)(2,1)S(1)}, bf16[512,256]{1,0:T(8,128)(2,1)S(1)}, u32[]{:S(2)}, u32[]{:S(2)}) collective-permute-start(bf16[512,256]{1,0:T(8,128)(2,1)S(1)} %add_convert_fusion.1), channel_id=1, source_target_pairs={{0,1},{1,2},{2,3},{3,0},{4,5},{5,6},{6,7},{7,4},{8,9},{9,10},{10,1... | collective-permute-start | bytes 786440 | tf_op jit(solution)/shard_map/ppermute | solution.py:999
  440.5 29.6 %collective-permute-start.34 = (bf16[512,768]{1,0:T(8,128)(2,1)S(1)}, bf16[512,768]{1,0:T(8,128)(2,1)S(1)}, u32[]{:S(2)}, u32[]{:S(2)}) collective-permute-start(bf16[512,768]{1,0:T(8,128)(2,1)S(1)} %copy-done.13), channel_id=1, source_target_pairs={{0,8},{4,12},{8,0},{12,4},{16,24},{20,28},{24,16},{28,20},{1,9},{5... | collective-permute-start | bytes 2359304 | tf_op jit(solution)/shard_map/ppermute | solution.py:921
  441.1 29.0 %collective-permute-start.35 = (bf16[512,768]{1,0:T(8,128)(2,1)S(1)}, bf16[512,768]{1,0:T(8,128)(2,1)}, u32[]{:S(2)}, u32[]{:S(2)}) collective-permute-start(bf16[512,768]{1,0:T(8,128)(2,1)S(1)} %copy-done.12), channel_id=1, source_target_pairs={{0,16},{4,20},{8,24},{12,28},{16,0},{20,4},{24,8},{28,12},{1,17},{... | collective-permute-start | bytes 2359304 | tf_op jit(solution)/shard_map/ppermute | solution.py:921
  441.6 7.4 %copy-start.4 = (bf16[512,256]{1,0:T(8,128)(2,1)S(1)}, bf16[512,256]{1,0:T(8,128)(2,1)}, u32[]{:S(2)}) copy-start(bf16[512,256]{1,0:T(8,128)(2,1)} %get-tuple-element.451) | copy-start | bytes 786436
  449.8 34.7 %collective-permute-start.43 = (bf16[512,256]{1,0:T(8,128)(2,1)}, bf16[512,256]{1,0:T(8,128)(2,1)}, u32[]{:S(2)}, u32[]{:S(2)}) collective-permute-start(bf16[512,256]{1,0:T(8,128)(2,1)} %add_convert_fusion), channel_id=1, source_target_pairs={{0,1},{1,2},{2,3},{3,0},{4,5},{5,6},{6,7},{7,4},{8,9},{9,10},{10,1... | collective-permute-start | bytes 786440 | tf_op jit(solution)/shard_map/ppermute | solution.py:999
  453.4 4.1 copy-start.18
  456.9 22.9 %collective-permute-start.44 = (bf16[256,1024]{1,0:T(8,128)(2,1)S(1)}, bf16[256,1024]{1,0:T(8,128)(2,1)S(1)}, u32[]{:S(2)}, u32[]{:S(2)}) collective-permute-start(bf16[256,1024]{1,0:T(8,128)(2,1)S(1)} %copy-done.19), channel_id=1, source_target_pairs={{0,16},{4,20},{8,24},{12,28},{16,0},{20,4},{24,8},{28,12},{1,17},{... | collective-permute-start | bytes 1572872 | tf_op jit(solution)/shard_map/ppermute | solution.py:921
  457.5 24.0 %collective-permute-start.45 = (bf16[256,1024]{1,0:T(8,128)(2,1)S(1)}, bf16[256,1024]{1,0:T(8,128)(2,1)}, u32[]{:S(2)}, u32[]{:S(2)}) collective-permute-start(bf16[256,1024]{1,0:T(8,128)(2,1)S(1)} %copy-done.18), channel_id=1, source_target_pairs={{0,8},{4,12},{8,0},{12,4},{16,24},{20,28},{24,16},{28,20},{1,9},{5... | collective-permute-start | bytes 1572872 | tf_op jit(solution)/shard_map/ppermute | solution.py:921
  473.8 13.2 %collective-permute-start.41 = (bf16[256,768]{1,0:T(8,128)(2,1)}, bf16[256,768]{1,0:T(8,128)(2,1)S(1)}, u32[]{:S(2)}, u32[]{:S(2)}) collective-permute-start(bf16[256,768]{1,0:T(8,128)(2,1)} %get-tuple-element.475), channel_id=1, source_target_pairs={{0,16},{4,20},{8,24},{12,28},{16,0},{20,4},{24,8},{28,12},{1,17},{... | collective-permute-start | bytes 1179656 | tf_op jit(solution)/shard_map/ppermute | solution.py:921
  474.3 13.8 %collective-permute-start.42 = (bf16[256,768]{1,0:T(8,128)(2,1)}, bf16[256,768]{1,0:T(8,128)(2,1)S(1)}, u32[]{:S(2)}, u32[]{:S(2)}) collective-permute-start(bf16[256,768]{1,0:T(8,128)(2,1)} %get-tuple-element.477), channel_id=1, source_target_pairs={{0,8},{4,12},{8,0},{12,4},{16,24},{20,28},{24,16},{28,20},{1,9},{5... | collective-permute-start | bytes 1179656 | tf_op jit(solution)/shard_map/ppermute | solution.py:921
  (20 other events, 31.9 us)
Sparse Core Ops, SparseCore 0:
  10.2 83.5 all-gather.9
  95.9 31.1 all-gather.11
  129.2 31.6 all-gather.13
  163.7 30.1 reduce-scatter.3
  196.1 29.9 reduce-scatter.5
  271.3 102.2 all-reduce.1
  375.8 56.6 reduce-scatter.7
  436.8 60.6 all-gather.7

commit v5 on v3

--- a/solution.py
+++ b/solution.py
@@ -19,7 +19,7 @@
 LOW = jnp.bfloat16
 F32 = jnp.float32
 MIB = 1024 * 1024
-PER_MICROSECOND = 8.0e+09
+PER_MICROSECOND = 1.0e+11
 
 NT = (((1,), (1,)), ((), ()))
 TN = (((0,), (0,)), ((), ()))
@@ -821,7 +821,7 @@
 
 def wgrad_stage(piece, *arrays):
     rows, columns = arrays[0].shape
-    tile = min(256, columns)
+    tile = columns // 2 if columns % 256 == 0 else columns
     block = lambda size: pl.BlockSpec((size, tile), lambda i: (0, i))
     return pl.pallas_call(
         functools.partial(stage_kernel, piece),
@@ -1225,16 +1225,18 @@
 
     down.away()
     gate.away()
+    Chain.weight = 0.3
     down.keep()
+    Chain.weight = 1.0
     down.send()
+    output()
     own()
-    gate.keep()
     branch()
-    output()
-    down.wait()
     scatter()
     out.away()
+    gate.keep()
     out.keep()
+    down.wait()
     heads()
     out.send()
     attend_step()
@@ -1242,18 +1244,19 @@
     sum_far()
     out.add()
     sum_near()
+    gate.send()
     down.add()
     up.away()
     arrive()
-    gate.send()
     turn()
     up.took()
     out.send()
     qkv.away()
     up.keep()
+    Chain.weight = 0.3
+    up.send()
+    Chain.weight = 1.0
     gate.wait()
-    out.wait()
-    up.send()
     state.out = out.finish()
     gate.add()
     qkv.keep()
@@ -1262,28 +1265,22 @@
     down.send()
     gate.send()
     up.wait()
-    Chain.weight = 0.03
     tokens_step()
-    Chain.weight = 1.0
     state.ring.step()
     qkv.send()
     down.wait()
     up.add()
+    gate.wait()
+    state.ring.step()
+    state.down = down.finish()
     up.send()
-    state.down = down.finish()
-    gate.wait()
-    Chain.weight = 0.03
     state.gate = gate.finish()
-    Chain.weight = 1.0
-    state.ring.step()
     qkv.wait()
     qkv.add()
     qkv.send()
+    state.up = up.finish()
     ring_end()
-    Chain.weight = 100.0
     state.qkv = qkv.finish()
-    Chain.weight = 1.0
-    state.up = up.finish()
     grad_tokens = (
         state.tokens
         .reshape(plan.tensor, plan.groups, plan.share, plan.width)

time: 510 us -> 508 us (level)
  local copies, waits for them, and re-layouts: 16.6 us -> 10.7 us
    ppermute x6, waiting for transfers between devices: 0.02 us -> 12.5 us  [shifted(): return lax.ppermute(array, 'tensor', pairs)]
    ppermute x25, waiting for transfers between devices: 34.1 us -> 26.1 us  [swap(): return lax.ppermute(array, 'dp', xor_pairs(self.plan.dp, 1 << bit))]
    unnamed x71 -> x29, local copies, waits for them, and re-layouts: 9.96 us -> 4.05 us
  transfers between devices with their start and end apart: 54 -> 54, of which waited for: 22 -> 32; matrix products, arithmetic and copies ran while one was open for 1% -> 2% of each run, Pallas kernels for 55% -> 56%
where the time goes in v5:
time: 508 us; the launch traced here: 501 us
  Pallas kernels  282 us (56%)
  waiting for transfers between devices  142 us (28%)
  starting transfers between devices  47.2 us (9%)
  between operations  14.7 us (3%)
  local copies, waits for them, and re-layouts  10.7 us (2%)
  other arithmetic  5.32 us (1%)
    pallas_call x5, Pallas kernels, wgrad_keep(): pl.pallas_call(functools.partial(keep_kernel, len(lhs), count), grid_spec...  46.3 us
    pallas_call x5, Pallas kernels, wgrad_away(): pl.pallas_call(functools.partial(away_kernel, len(lhs)), grid_spec=pltpu....  39.7 us
    all_gather x2, waiting for transfers between devices, body(): lax.all_gather(tie(part, near), 'tensor', axis=0, tiled=False)  39 us
    pallas_call x2, Pallas kernels, feed_forward(): pl.pallas_call(functools.partial(ff_kernel, tile), grid=(1,), in_specs=[w...  35.6 us
    ppermute x15, waiting for transfers between devices, swap(): return lax.ppermute(array, 'dp', xor_pairs(plan.dp, mask))  30.1 us
    ppermute x25, waiting for transfers between devices, swap(): return lax.ppermute(array, 'dp', xor_pairs(self.plan.dp, 1 << bit))  26.1 us
    ppermute x25, starting transfers between devices, swap(): return lax.ppermute(array, 'dp', xor_pairs(self.plan.dp, 1 << bit))  23.7 us
    pallas_call x1, Pallas kernels, attend_back(): pl.pallas_call(functools.partial(attend_back_kernel, plan), grid_spec=plt...  23 us
  transfers between devices with their start and end apart: 54, of which 32 were waited for; matrix products, arithmetic and copies ran while one was open for 2% of the time, Pallas kernels for 56%

profile of v5, /device:TPU:0, one launch (start us, length us, event | category | flops | bytes accessed | tf_op | source)
XLA Modules:
  0.0 500.9 jit_solution(13058314574520457910)
XLA Ops:
  7.2 2.3 constant_dynamic-slice_fusion
  10.2 11.8 %project_qkv.1 = (bf16[640,2048]{1,0:T(8,128)(2,1)}, bf16[3,640,128]{2,1,0:T(8,128)(2,1)}, bf16[3,640,128]{2,1,0:T(8,128)(2,1)}, bf16[3,640,128]{2,1,0:T(8,128)(2,1)}, bf16[3,640,128]{2,1,0:T(8,128)(2,1)}) custom-call(s32[40]{0:T(128)} %parent.7, s32[6]{0:T(128)} %stack.39.place, bf16[640,2048]{1,0:T(8,128)(2,1)} %refs_1_.1, bf16[2048,512]{1,0:T(8,128)(2,1)} %wq.3, ...), custom_call_target="tpu_custom_call" | custom-call | bytes 1 | tf_op jit(solution)/shard_map/project_qkv/pallas_call | solution.py:169
  22.0 2.9 collective-permute-start
  26.5 10.5 %grad_hidden.1.seed = f32[640,2048]{1,0:T(8,128)} custom-call(bf16[640,2048]{1,0:T(8,128)(2,1)} %refs_5_.1, bf16[2048,2048]{1,0:T(8,128)(2,1)} %refs_2_.1), custom_call_target="tpu_custom_call" | custom-call | bytes 1 | tf_op jit(solution)/shard_map/grad_hidden/pallas_call | solution.py:518
  37.2 11.2 %collective-permute-done.1.refs_2_ = bf16[3,640,128]{2,1,0:T(8,128)(2,1)S(1)} collective-permute-done((bf16[3,640,128]{2,1,0:T(8,128)(2,1)}, bf16[3,640,128]{2,1,0:T(8,128)(2,1)S(1)}, u32[]{:S(2)}, u32[]{:S(2)}) %collective-permute-start.1) | collective-permute-done | bytes 491552 | tf_op jit(solution)/shard_map/ppermute | solution.py:1086
  49.3 3.0 collective-permute-done.3
  52.4 1.7 pad_maximum_fusion
  54.1 12.3 %attend.1 = (bf16[640,128]{1,0:T(8,128)(2,1)}, bf16[640,128]{1,0:T(8,128)(2,1)}, bf16[640,128]{1,0:T(8,128)(2,1)}, bf16[640,128]{1,0:T(8,128)(2,1)}) custom-call(s32[40]{0:T(128)} %parent.7, s32[6]{0:T(128)} %stack.39.place, bf16[3,640,128]{2,1,0:T(8,128)(2,1)} %get-tuple-element.265.refs_0_, bf16[3,640,128]{2,1,0:T(8,128)(2,1)} %copy-done.1, ...), custom_call_target="tpu_custom_call" | custom-call | bytes 1 | tf_op jit(solution)/shard_map/attend/pallas_call | solution.py:247
  69.9 3.8 collective-permute-done.4.refs_1_
  73.7 2.1 collective-permute-done.5.refs_2_
  78.0 2.8 gather_heads.1
  80.8 12.9 %all-gather.10.cloned.1.call-done = bf16[1024,2048]{1,0:T(8,128)(2,1)} async-done(((bf16[256,2048]{1,0:T(8,128)(2,1)}), bf16[1024,2048]{1,0:T(8,128)(2,1)}) %all-gather.10.cloned.1.call-update) | async-done | bytes 4194320 | tf_op jit(solution)/shard_map/all_gather | solution.py:1093
  94.6 32.4 %all-gather.12.cloned.1.call-done = bf16[1280,512]{1,0:T(8,128)(2,1)} async-done(((bf16[320,512]{1,0:T(8,128)(2,1)}), bf16[1280,512]{1,0:T(8,128)(2,1)}) %all-gather.12.cloned.1.call-update) | async-done | bytes 1310736 | tf_op jit(solution)/shard_map/all_gather | solution.py:1111
  127.1 9.2 %project_out.2 = (f32[320,2048]{1,0:T(8,128)}, bf16[320,2048]{1,0:T(8,128)(2,1)}) custom-call(s32[6]{0:T(128)} %stack.39.place, bf16[640,2048]{1,0:T(8,128)(2,1)} %refs_1_.1, bf16[4,320,512]{2,1,0:T(8,128)(2,1)} %bitcast.37, bf16[4,256,2048]{2,1,0:T(8,128)(2,1)} %bitcast.42, bf16[4,256,2048]{2,1,0:T(8,128)(2,1)} %collective-permute-done.7.far.refs_7_), custom_call_target="tpu_custom_call" | custom-call | flops 699999977472 | bytes 1 | tf_op jit(solution)/shard_map/project_out/pallas_call | solution.py:490
  136.3 17.8 %feed_forward.2 = (bf16[320,2048]{1,0:T(8,128)(2,1)}, bf16[320,2048]{1,0:T(8,128)(2,1)}, bf16[320,2048]{1,0:T(8,128)(2,1)}, bf16[320,2048]{1,0:T(8,128)(2,1)}) custom-call(bf16[320,2048]{1,0:T(8,128)(2,1)} %get-tuple-element.286.normed.refs_0_, f32[640,2048]{1,0:T(8,128)} %grad_hidden.1.seed, bf16[2048,2048]{1,0:T(8,128)(2,1)} %wg.3, bf16[2048,2048]{1,0:T(8,128)(2,1)} %wu.3), custom_call_target="tpu_custom_call" | custom-call | flops 1700000038912 | bytes 1 | tf_op jit(solution)/shard_map/feed_forward/pallas_call | solution.py:589
  154.4 6.5 %all-gather.14.cloned.1.call-done = bf16[1280,512]{1,0:T(8,128)(2,1)} async-done(((bf16[320,512]{1,0:T(8,128)(2,1)}), bf16[1280,512]{1,0:T(8,128)(2,1)}) %all-gather.14.cloned.1.call-update) | async-done | bytes 1310736 | tf_op jit(solution)/shard_map/all_gather | solution.py:1111
  160.9 9.2 %project_out.3 = (f32[320,2048]{1,0:T(8,128)}, bf16[320,2048]{1,0:T(8,128)(2,1)}) custom-call(s32[6]{0:T(128)} %stack.39.place, bf16[640,2048]{1,0:T(8,128)(2,1)} %refs_1_.1, bf16[4,320,512]{2,1,0:T(8,128)(2,1)} %bitcast.39, bf16[4,256,2048]{2,1,0:T(8,128)(2,1)} %bitcast.43, bf16[4,256,2048]{2,1,0:T(8,128)(2,1)} %collective-permute-done.7.far.refs_7_), custom_call_target="tpu_custom_call" | custom-call | flops 699999977472 | bytes 1 | tf_op jit(solution)/shard_map/project_out/pallas_call | solution.py:490
  170.2 17.8 %feed_forward.3 = (bf16[320,2048]{1,0:T(8,128)(2,1)}, bf16[320,2048]{1,0:T(8,128)(2,1)}, bf16[320,2048]{1,0:T(8,128)(2,1)}, bf16[320,2048]{1,0:T(8,128)(2,1)}) custom-call(bf16[320,2048]{1,0:T(8,128)(2,1)} %get-tuple-element.293.normed.refs_1_, f32[640,2048]{1,0:T(8,128)} %grad_hidden.1.seed, bf16[2048,2048]{1,0:T(8,128)(2,1)} %wg.3, bf16[2048,2048]{1,0:T(8,128)(2,1)} %wu.3), custom_call_target="tpu_custom_call" | custom-call | flops 1700000038912 | bytes 1 | tf_op jit(solution)/shard_map/feed_forward/pallas_call | solution.py:589
  188.0 9.1 %wgrad_away.5 = bf16[1024,2048]{1,0:T(8,128)(2,1)} custom-call(s32[6]{0:T(128)} %stack.39.place, bf16[640,2048]{1,0:T(8,128)(2,1)} %refs_5_.1, bf16[320,2048]{1,0:T(8,128)(2,1)} %get-tuple-element.304.refs_1_.refs_0_, bf16[320,2048]{1,0:T(8,128)(2,1)} %get-tuple-element.305.refs_2_.refs_1_), custom_call_target="tpu_custom_call" | custom-call | flops 799999983616 | bytes 1 | tf_op jit(solution)/shard_map/wgrad_away/pallas_call | solution.py:737
  197.2 8.8 %wgrad_away.6 = bf16[1024,2048]{1,0:T(8,128)(2,1)} custom-call(s32[6]{0:T(128)} %stack.39.place, bf16[320,2048]{1,0:T(8,128)(2,1)} %get-tuple-element.286.normed.refs_0_, bf16[320,2048]{1,0:T(8,128)(2,1)} %get-tuple-element.293.normed.refs_1_, bf16[320,2048]{1,0:T(8,128)(2,1)} %get-tuple-element.300.refs_2_, bf16[320,2048]{1,0:T(8,128)(2,1)} %get-tuple-element.301.refs_3_), custom_call_target="tpu_custom_call" | custom-call | flops 799999983616 | bytes 1 | tf_op jit(solution)/shard_map/wgrad_away/pallas_call | solution.py:737
  206.6 10.2 %wgrad_keep.5 = (bf16[512,1024]{1,0:T(8,128)(2,1)}, bf16[512,1024]{1,0:T(8,128)(2,1)}, bf16[512,1024]{1,0:T(8,128)(2,1)}, bf16[512,1024]{1,0:T(8,128)(2,1)}) custom-call(s32[6]{0:T(128)} %stack.39.place, bf16[640,2048]{1,0:T(8,128)(2,1)} %refs_5_.1, bf16[320,2048]{1,0:T(8,128)(2,1)} %get-tuple-element.304.refs_1_.refs_0_, ...), custom_call_target="tpu_custom_call" | custom-call | flops 269999996928 | bytes 1 | tf_op jit(solution)/shard_map/wgrad_keep/pallas_call | solution.py:785
  216.7 9.8 %project_down.1 = bf16[640,2048]{1,0:T(8,128)(2,1)} custom-call(bf16[320,2048]{1,0:T(8,128)(2,1)} %get-tuple-element.304.refs_1_.refs_0_, bf16[320,2048]{1,0:T(8,128)(2,1)} %get-tuple-element.305.refs_2_.refs_1_, bf16[2048,2048]{1,0:T(8,128)(2,1)} %refs_2_.1), custom_call_target="tpu_custom_call" | custom-call | flops 1100000002048 | bytes 1 | tf_op jit(solution)/shard_map/project_down/pallas_call | solution.py:619
  227.9 10.1 %branch_back.1 = (f32[160,2048]{1,0:T(8,128)}, bf16[160,2048]{1,0:T(8,128)(2,1)}, bf16[160,512]{1,0:T(8,128)(2,1)}, bf16[160,512]{1,0:T(8,128)(2,1)}, bf16[160,5...) custom-call(s32[6]{0:T(128)} %stack.39.place, bf16[80,2048]{1,0:T(8,128)(2,1)} %reduce-scatter.4.cloned.1.call-done.refs_0_, ...), custom_call_target="tpu_custom_call" | custom-call | flops 899999989760 | bytes 1 | tf_op jit(solution)/shard_map/branch_back/pallas_call | solution.py:671
  238.1 1.7 collective-permute-start.10
  239.8 2.4 collective-permute-start.11
  248.8 10.0 %collective-permute-done.10.refs_2_ = bf16[160,512]{1,0:T(8,128)(2,1)S(1)} collective-permute-done((bf16[160,512]{1,0:T(8,128)(2,1)}, bf16[160,512]{1,0:T(8,128)(2,1)S(1)}, u32[]{:S(2)}, u32[]{:S(2)}) %collective-permute-start.10) | collective-permute-done | bytes 163872 | tf_op jit(solution)/shard_map/ppermute | solution.py:999
  259.5 2.8 scatter_heads.1
  265.2 5.8 %wgrad_away.7 = bf16[1024,2048]{1,0:T(8,128)(2,1)} custom-call(s32[6]{0:T(128)} %stack.39.place, bf16[160,2048]{1,0:T(8,128)(2,1)} %get-tuple-element.325.refs_0_, bf16[160,2048]{1,0:T(8,128)(2,1)} %copy-done.6), custom_call_target="tpu_custom_call" | custom-call | flops 799999983616 | bytes 1 | tf_op jit(solution)/shard_map/wgrad_away/pallas_call | solution.py:737
  271.0 10.4 %wgrad_keep.6 = (bf16[512,1024]{1,0:T(8,128)(2,1)}, bf16[512,1024]{1,0:T(8,128)(2,1)}, bf16[512,1024]{1,0:T(8,128)(2,1)}, bf16[512,1024]{1,0:T(8,128)(2,1)}) custom-call(s32[6]{0:T(128)} %stack.39.place, bf16[320,2048]{1,0:T(8,128)(2,1)} %get-tuple-element.286.normed.refs_0_, bf16[320,2048]{1,0:T(8,128)(2,1)} %get-tuple-element.293.normed.refs_1_, ...), custom_call_target="tpu_custom_call" | custom-call | flops 899999989760 | bytes 1 | tf_op jit(solution)/shard_map/wgrad_keep/pallas_call | solution.py:785
  282.1 7.0 %wgrad_keep.7 = (bf16[512,1024]{1,0:T(8,128)(2,1)}, bf16[512,1024]{1,0:T(8,128)(2,1)}, bf16[512,1024]{1,0:T(8,128)(2,1)}, bf16[512,1024]{1,0:T(8,128)(2,1)}) custom-call(s32[6]{0:T(128)} %stack.39.place, bf16[160,2048]{1,0:T(8,128)(2,1)} %get-tuple-element.325.refs_0_, bf16[160,2048]{1,0:T(8,128)(2,1)} %copy-done.6, ...), custom_call_target="tpu_custom_call" | custom-call | flops 899999989760 | bytes 1 | tf_op jit(solution)/shard_map/wgrad_keep/pallas_call | solution.py:785
  292.1 23.0 %attend_back.1 = (bf16[640,128]{1,0:T(8,128)(2,1)}, bf16[640,128]{1,0:T(8,128)(2,1)}, bf16[640,128]{1,0:T(8,128)(2,1)}, bf16[640,128]{1,0:T(8,128)(2,1)}, f32[40...) custom-call(s32[40]{0:T(128)} %parent.7, s32[6]{0:T(128)} %stack.39.place, ...), custom_call_target="tpu_custom_call" | custom-call | flops 2300000075776 | bytes 1 | tf_op jit(solution)/shard_map/attend_back/pallas_call | solution.py:305
  315.9 3.3 wgrad_stage.5
  319.3 3.8 combine_back.1
  326.6 3.4 wgrad_stage.6
  330.0 8.9 %wgrad_away.8 = bf16[1024,2048]{1,0:T(8,128)(2,1)} custom-call(s32[6]{0:T(128)} %stack.39.place, bf16[320,2048]{1,0:T(8,128)(2,1)} %get-tuple-element.286.normed.refs_0_, bf16[320,2048]{1,0:T(8,128)(2,1)} %get-tuple-element.293.normed.refs_1_, bf16[320,2048]{1,0:T(8,128)(2,1)} %get-tuple-element.375.refs_2_, bf16[320,2048]{1,0:T(8,128)(2,1)} %get-tuple-element.376.refs_3_), custom_call_target="tpu_custom_call" | custom-call | flops 799999983616 | bytes 1 | tf_op jit(solution)/shard_map/wgrad_away/pallas_call | solution.py:737
  340.9 5.5 %collective-permute-done.23.refs_2_ = bf16[3,640,128]{2,1,0:T(8,128)(2,1)} collective-permute-done((bf16[3,640,128]{2,1,0:T(8,128)(2,1)}, bf16[3,640,128]{2,1,0:T(8,128)(2,1)}, u32[]{:S(2)}, u32[]{:S(2)}) %collective-permute-start.23) | collective-permute-done | bytes 491552 | tf_op jit(solution)/shard_map/ppermute | solution.py:1086
  346.4 2.5 collective-permute-done.24.refs_3_
  348.9 10.9 %turn_back.1 = (bf16[640,2048]{1,0:T(8,128)(2,1)}, bf16[640,1536]{1,0:T(8,128)(2,1)}) custom-call(s32[40]{0:T(128)} %parent.7, s32[6]{0:T(128)} %stack.39.place, f32[1280,128]{1,0:T(8,128)} %constant.39.clone.cosine, f32[1280,128]{1,0:T(8,128)} %constant.40.clone.sine, bf16[2048,512]{1,0:T(8,128)(2,1)} %wq.3, bf16[2048,512]{1,0:T(8,128)(2,1)} %wk.3, ...), custom_call_target="tpu_custom_call" | custom-call | flops 1300000014336 | bytes 1 | tf_op jit(solution)/shard_map/turn_back/pallas_call | solution.py:447
  359.9 7.1 %wgrad_away.9 = bf16[1024,1536]{1,0:T(8,128)(2,1)} custom-call(s32[6]{0:T(128)} %stack.39.place, bf16[640,2048]{1,0:T(8,128)(2,1)} %get-tuple-element.258.refs_0_, bf16[640,1536]{1,0:T(8,128)(2,1)} %get-tuple-element.388.refs_1_), custom_call_target="tpu_custom_call" | custom-call | flops 799999983616 | bytes 1 | tf_op jit(solution)/shard_map/wgrad_away/pallas_call | solution.py:737
  367.6 2.0 collective-permute-start.30
  369.7 10.5 %wgrad_keep.8 = (bf16[512,1024]{1,0:T(8,128)(2,1)}, bf16[512,1024]{1,0:T(8,128)(2,1)}, bf16[512,1024]{1,0:T(8,128)(2,1)}, bf16[512,1024]{1,0:T(8,128)(2,1)}) custom-call(s32[6]{0:T(128)} %stack.39.place, bf16[320,2048]{1,0:T(8,128)(2,1)} %get-tuple-element.286.normed.refs_0_, bf16[320,2048]{1,0:T(8,128)(2,1)} %get-tuple-element.293.normed.refs_1_, ...), custom_call_target="tpu_custom_call" | custom-call | flops 899999989760 | bytes 1 | tf_op jit(solution)/shard_map/wgrad_keep/pallas_call | solution.py:785
  382.3 3.9 wgrad_finish_chunks.1
  386.1 3.3 wgrad_stage.7
  389.4 8.2 %wgrad_keep.9 = (bf16[512,768]{1,0:T(8,128)(2,1)}, bf16[512,768]{1,0:T(8,128)(2,1)}, bf16[512,768]{1,0:T(8,128)(2,1)}, bf16[512,768]{1,0:T(8,128)(2,1)}) custom-call(s32[6]{0:T(128)} %stack.39.place, bf16[640,2048]{1,0:T(8,128)(2,1)} %get-tuple-element.258.refs_0_, bf16[640,1536]{1,0:T(8,128)(2,1)} %get-tuple-element.388.refs_1_, ...), custom_call_target="tpu_custom_call" | custom-call | flops 899999989760 | bytes 1 | tf_op jit(solution)/shard_map/wgrad_keep/pallas_call | solution.py:785
  397.6 5.3 %add_residual.1 = bf16[640,2048]{1,0:T(8,128)(2,1)} custom-call(f32[320,2048]{1,0:T(8,128)} %get-tuple-element.282.refs_2_.refs_0_, f32[320,2048]{1,0:T(8,128)} %get-tuple-element.290.refs_3_.refs_1_, bf16[640,2048]{1,0:T(8,128)(2,1)} %all-reduce.2.cloned.1.call-done.refs_2_), custom_call_target="tpu_custom_call" | custom-call | flops 599999971328 | bytes 1 | tf_op jit(solution)/shard_map/add_residual/pallas_call | solution.py:1053
  402.9 2.5 collective-permute-done.31.a_got
  405.7 15.5 %reduce-scatter.8.cloned.1.call-done.part = bf16[160,2048]{1,0:T(8,128)(2,1)} async-done(((bf16[640,2048]{1,0:T(8,128)(2,1)}), bf16[160,2048]{1,0:T(8,128)(2,1)}) %reduce-scatter.8.cloned.1.call-update) | async-done | bytes 655376 | tf_op jit(solution)/shard_map/reduce_scatter | solution.py:1201
  424.8 4.2 tokens_back.1
  431.2 1.7 add_convert_fusion.1
  433.9 3.1 collective-permute-done.38.a_got
  439.9 3.4 wgrad_stage.8
  443.4 4.8 collective-permute-done.36.a_got
  449.7 1.7 add_convert_fusion
  451.4 2.0 collective-permute-start.43
  453.4 3.5 wgrad_finish.3
  458.9 3.1 wgrad_finish.4
  462.0 4.6 collective-permute-done.34.a_got
  466.6 2.8 wgrad_stage.9
  471.4 4.9 collective-permute-done.44.a_got
  477.8 3.0 wgrad_finish.5
  480.8 1.9 add_last.1
  484.4 2.5 wgrad_finish_split.1
  486.9 3.4 all-gather.8.cloned.1.call-done
  490.3 3.6 copy.23
  (130 shorter events, 53.8 us)
Async XLA Ops:
  7.2 86.5 %all-gather.10.cloned.1.call-start = ((), (), s32[]{:S(2)}) async-start(), calls=%async_computation.8 | async-start | bytes 5242880 | tf_op jit(solution)/shard_map/all_gather | solution.py:1093
  9.6 117.5 %all-gather.12.cloned.1.call-start = ((), (), s32[]{:S(2)}) async-start(), calls=%async_computation.9 | async-start | bytes 1638400 | tf_op jit(solution)/shard_map/all_gather | solution.py:1111
  22.0 15.2 %collective-permute-start = (bf16[3,640,128]{2,1,0:T(8,128)(2,1)}, bf16[3,640,128]{2,1,0:T(8,128)(2,1)S(1)}, u32[]{:S(2)}, u32[]{:S(2)}) collective-permute-start(bf16[3,640,128]{2,1,0:T(8,128)(2,1)} %get-tuple-element.255), channel_id=1, source_target_pairs={{0,8},{4,12},{8,0},{12,4},{16,24},{20,28},{24,16},{28,20},{1,9},{5... | collective-permute-start | bytes 1474568 | tf_op jit(solution)/shard_map/ppermute | solution.py:1086
  25.0 23.4 %collective-permute-start.1 = (bf16[3,640,128]{2,1,0:T(8,128)(2,1)}, bf16[3,640,128]{2,1,0:T(8,128)(2,1)S(1)}, u32[]{:S(2)}, u32[]{:S(2)}) collective-permute-start(bf16[3,640,128]{2,1,0:T(8,128)(2,1)} %get-tuple-element.256), channel_id=1, source_target_pairs={{0,16},{4,20},{8,24},{12,28},{16,0},{20,4},{24,8},{28,12},{1,17},{... | collective-permute-start | bytes 1474568 | tf_op jit(solution)/shard_map/ppermute | solution.py:1086
  26.5 21.9 %collective-permute-start.2 = (bf16[3,640,128]{2,1,0:T(8,128)(2,1)}, bf16[3,640,128]{2,1,0:T(8,128)(2,1)S(1)}, u32[]{:S(2)}, u32[]{:S(2)}) collective-permute-start(bf16[3,640,128]{2,1,0:T(8,128)(2,1)} %get-tuple-element.257), channel_id=1, source_target_pairs={{0,24},{4,28},{8,16},{12,20},{16,8},{20,12},{24,0},{28,4},{1,25},{... | collective-permute-start | bytes 1474568 | tf_op jit(solution)/shard_map/ppermute | solution.py:1086
  26.5 21.9 %copy-start = (bf16[3,640,128]{2,1,0:T(8,128)(2,1)S(1)}, bf16[3,640,128]{2,1,0:T(8,128)(2,1)}, u32[]{:S(2)}) copy-start(bf16[3,640,128]{2,1,0:T(8,128)(2,1)} %get-tuple-element.265.refs_0_) | copy-start | bytes 1474564
  37.2 11.5 %copy-start.1 = (bf16[3,640,128]{2,1,0:T(8,128)(2,1)}, bf16[3,640,128]{2,1,0:T(8,128)(2,1)S(1)}, u32[]{:S(2)}) copy-start(bf16[3,640,128]{2,1,0:T(8,128)(2,1)S(1)} %collective-permute-done.refs_1_) | copy-start | bytes 1474564
  48.4 0.8 copy-start.2
  48.4 0.9 copy-start.3
  49.3 3.0 collective-permute-start.3
  66.4 7.3 %collective-permute-start.4 = (bf16[640,128]{1,0:T(8,128)(2,1)}, bf16[640,128]{1,0:T(8,128)(2,1)S(1)}, u32[]{:S(2)}, u32[]{:S(2)}) collective-permute-start(bf16[640,128]{1,0:T(8,128)(2,1)} %get-tuple-element.270), channel_id=1, source_target_pairs={{0,8},{4,12},{8,0},{12,4},{16,24},{20,28},{24,16},{28,20},{1,9},{5... | collective-permute-start | bytes 491528 | tf_op jit(solution)/shard_map/ppermute | solution.py:1086
  67.5 8.3 %collective-permute-start.5 = (bf16[640,128]{1,0:T(8,128)(2,1)}, bf16[640,128]{1,0:T(8,128)(2,1)S(1)}, u32[]{:S(2)}, u32[]{:S(2)}) collective-permute-start(bf16[640,128]{1,0:T(8,128)(2,1)} %get-tuple-element.271), channel_id=1, source_target_pairs={{0,16},{4,20},{8,24},{12,28},{16,0},{20,4},{24,8},{28,12},{1,17},{... | collective-permute-start | bytes 491528 | tf_op jit(solution)/shard_map/ppermute | solution.py:1086
  68.4 8.9 %collective-permute-start.6 = (bf16[640,128]{1,0:T(8,128)(2,1)}, bf16[640,128]{1,0:T(8,128)(2,1)S(1)}, u32[]{:S(2)}, u32[]{:S(2)}) collective-permute-start(bf16[640,128]{1,0:T(8,128)(2,1)} %get-tuple-element.272), channel_id=1, source_target_pairs={{0,24},{4,28},{8,16},{12,20},{16,8},{20,12},{24,0},{28,4},{1,25},{... | collective-permute-start | bytes 491528 | tf_op jit(solution)/shard_map/ppermute | solution.py:1086
  73.7 3.7 copy-start.10
  75.8 1.5 copy-start.11
  93.7 33.4 %collective-permute-start.7 = (bf16[4,256,2048]{2,1,0:T(8,128)(2,1)}, bf16[4,256,2048]{2,1,0:T(8,128)(2,1)}, u32[]{:S(2)}, u32[]{:S(2)}) collective-permute-start(bf16[4,256,2048]{2,1,0:T(8,128)(2,1)} %bitcast.41), channel_id=1, source_target_pairs={{0,4},{4,0},{8,12},{12,8},{16,20},{20,16},{24,28},{28,24},{1,5},{5... | collective-permute-start | bytes 12582920 | tf_op jit(solution)/shard_map/ppermute | solution.py:1086
  93.7 67.2 %all-gather.14.cloned.1.call-start = ((), (), s32[]{:S(2)}) async-start(), calls=%async_computation.10 | async-start | bytes 1638400 | tf_op jit(solution)/shard_map/all_gather | solution.py:1111
  94.4 132.1 %reduce-scatter.4.cloned.1.call-start = ((), (), s32[]{:S(2)}) async-start(), calls=%async_computation.4 | async-start | bytes 1638400 | tf_op jit(solution)/shard_map/reduce_scatter | solution.py:1125
  154.1 73.8 %reduce-scatter.6.cloned.1.call-start = ((), (), s32[]{:S(2)}) async-start(), calls=%async_computation.5 | async-start | bytes 1638400 | tf_op jit(solution)/shard_map/reduce_scatter | solution.py:1125
  197.1 9.5 %collective-permute-start.8 = (bf16[1024,2048]{1,0:T(8,128)(2,1)}, bf16[1024,2048]{1,0:T(8,128)(2,1)}, u32[]{:S(2)}, u32[]{:S(2)}) collective-permute-start(bf16[1024,2048]{1,0:T(8,128)(2,1)} %wgrad_away.5), channel_id=1, source_target_pairs={{0,4},{4,0},{8,12},{12,8},{16,20},{20,16},{24,28},{28,24},{1,5},{5... | collective-permute-start | bytes 12582920 | tf_op jit(solution)/shard_map/ppermute | solution.py:921
  197.2 200.4 %all-reduce.2.cloned.1.call-start = ((), (), s32[]{:S(2)}) async-start(), calls=%async_computation.3 | async-start | bytes 5242880 | tf_op jit(solution)/shard_map/psum | solution.py:1161
  206.1 64.9 %collective-permute-start.18 = (bf16[1024,2048]{1,0:T(8,128)(2,1)}, bf16[1024,2048]{1,0:T(8,128)(2,1)}, u32[]{:S(2)}, u32[]{:S(2)}) collective-permute-start(bf16[1024,2048]{1,0:T(8,128)(2,1)} %wgrad_away.6), channel_id=1, source_target_pairs={{0,4},{4,0},{8,12},{12,8},{16,20},{20,16},{24,28},{28,24},{1,5},{5... | collective-permute-start | bytes 12582920 | tf_op jit(solution)/shard_map/ppermute | solution.py:921
  238.0 9.3 %collective-permute-start.9 = (bf16[160,512]{1,0:T(8,128)(2,1)}, bf16[160,512]{1,0:T(8,128)(2,1)S(1)}, u32[]{:S(2)}, u32[]{:S(2)}) collective-permute-start(bf16[160,512]{1,0:T(8,128)(2,1)} %get-tuple-element.309), channel_id=1, source_target_pairs={{0,1},{1,2},{2,3},{3,0},{4,5},{5,6},{6,7},{7,4},{8,9},{9,10},{10,1... | collective-permute-start | bytes 491528 | tf_op jit(solution)/shard_map/ppermute | solution.py:999
  238.1 20.7 %collective-permute-start.10 = (bf16[160,512]{1,0:T(8,128)(2,1)}, bf16[160,512]{1,0:T(8,128)(2,1)S(1)}, u32[]{:S(2)}, u32[]{:S(2)}) collective-permute-start(bf16[160,512]{1,0:T(8,128)(2,1)} %get-tuple-element.310), channel_id=1, source_target_pairs={{0,2},{1,3},{2,0},{3,1},{4,6},{5,7},{6,4},{7,5},{8,10},{9,11},{10,... | collective-permute-start | bytes 491528 | tf_op jit(solution)/shard_map/ppermute | solution.py:999
  239.8 19.0 %collective-permute-start.11 = (bf16[160,512]{1,0:T(8,128)(2,1)}, bf16[160,512]{1,0:T(8,128)(2,1)S(1)}, u32[]{:S(2)}, u32[]{:S(2)}) collective-permute-start(bf16[160,512]{1,0:T(8,128)(2,1)} %get-tuple-element.311), channel_id=1, source_target_pairs={{0,3},{1,0},{2,1},{3,2},{4,7},{5,4},{6,5},{7,6},{8,11},{9,8},{10,9... | collective-permute-start | bytes 491528 | tf_op jit(solution)/shard_map/ppermute | solution.py:999
  242.2 46.9 %collective-permute-start.15 = (bf16[512,1024]{1,0:T(8,128)(2,1)}, bf16[512,1024]{1,0:T(8,128)(2,1)}, u32[]{:S(2)}, u32[]{:S(2)}) collective-permute-start(bf16[512,1024]{1,0:T(8,128)(2,1)} %get-tuple-element.323), channel_id=1, source_target_pairs={{0,8},{4,12},{8,0},{12,4},{16,24},{20,28},{24,16},{28,20},{1,9},{5... | collective-permute-start | bytes 3145736 | tf_op jit(solution)/shard_map/ppermute | solution.py:921
  243.7 177.5 %reduce-scatter.8.cloned.1.call-start = ((), (), s32[]{:S(2)}) async-start(), calls=%async_computation.6 | async-start | bytes 3276800 | tf_op jit(solution)/shard_map/reduce_scatter | solution.py:1201
  245.9 19.4 %copy-start.6 = (bf16[160,2048]{1,0:T(8,128)(2,1)}, bf16[160,2048]{1,0:T(8,128)(2,1)S(1)}, u32[]{:S(2)}) copy-start(bf16[160,2048]{1,0:T(8,128)(2,1)S(1)} %constant_dynamic-update-slice_fusion.refs_1_) | copy-start | bytes 1966084
  247.3 11.5 %copy-start.7 = (bf16[160,512]{1,0:T(8,128)(2,1)}, bf16[160,512]{1,0:T(8,128)(2,1)S(1)}, u32[]{:S(2)}) copy-start(bf16[160,512]{1,0:T(8,128)(2,1)S(1)} %collective-permute-done.9.refs_1_) | copy-start | bytes 491524
  247.3 41.8 %collective-permute-start.16 = (bf16[512,1024]{1,0:T(8,128)(2,1)}, bf16[512,1024]{1,0:T(8,128)(2,1)}, u32[]{:S(2)}, u32[]{:S(2)}) collective-permute-start(bf16[512,1024]{1,0:T(8,128)(2,1)} %get-tuple-element.324), channel_id=1, source_target_pairs={{0,16},{4,20},{8,24},{12,28},{16,0},{20,4},{24,8},{28,12},{1,17},{... | collective-permute-start | bytes 3145736 | tf_op jit(solution)/shard_map/ppermute | solution.py:921
  262.3 26.8 %collective-permute-start.12 = (bf16[640,128]{1,0:T(8,128)(2,1)}, bf16[640,128]{1,0:T(8,128)(2,1)}, u32[]{:S(2)}, u32[]{:S(2)}) collective-permute-start(bf16[640,128]{1,0:T(8,128)(2,1)} %get-tuple-element.318), channel_id=1, source_target_pairs={{0,8},{4,12},{8,0},{12,4},{16,24},{20,28},{24,16},{28,20},{1,9},{5... | collective-permute-start | bytes 491528 | tf_op jit(solution)/shard_map/ppermute | solution.py:1086
  263.8 25.3 %collective-permute-start.13 = (bf16[640,128]{1,0:T(8,128)(2,1)}, bf16[640,128]{1,0:T(8,128)(2,1)}, u32[]{:S(2)}, u32[]{:S(2)}) collective-permute-start(bf16[640,128]{1,0:T(8,128)(2,1)} %get-tuple-element.319), channel_id=1, source_target_pairs={{0,16},{4,20},{8,24},{12,28},{16,0},{20,4},{24,8},{28,12},{1,17},{... | collective-permute-start | bytes 491528 | tf_op jit(solution)/shard_map/ppermute | solution.py:1086
  271.0 10.4 %collective-permute-start.17 = (bf16[1024,2048]{1,0:T(8,128)(2,1)}, bf16[1024,2048]{1,0:T(8,128)(2,1)}, u32[]{:S(2)}, u32[]{:S(2)}) collective-permute-start(bf16[1024,2048]{1,0:T(8,128)(2,1)} %wgrad_away.7), channel_id=1, source_target_pairs={{0,4},{4,0},{8,12},{12,8},{16,20},{20,16},{24,28},{28,24},{1,5},{5... | collective-permute-start | bytes 12582920 | tf_op jit(solution)/shard_map/ppermute | solution.py:921
  281.4 7.8 %collective-permute-start.14 = (bf16[640,128]{1,0:T(8,128)(2,1)}, bf16[640,128]{1,0:T(8,128)(2,1)}, u32[]{:S(2)}, u32[]{:S(2)}) collective-permute-start(bf16[640,128]{1,0:T(8,128)(2,1)} %get-tuple-element.320), channel_id=1, source_target_pairs={{0,24},{4,28},{8,16},{12,20},{16,8},{20,12},{24,0},{28,4},{1,25},{... | collective-permute-start | bytes 491528 | tf_op jit(solution)/shard_map/ppermute | solution.py:1086
  289.3 25.9 %collective-permute-start.19 = (bf16[512,1024]{1,0:T(8,128)(2,1)}, bf16[512,1024]{1,0:T(8,128)(2,1)}, u32[]{:S(2)}, u32[]{:S(2)}) collective-permute-start(bf16[512,1024]{1,0:T(8,128)(2,1)} %get-tuple-element.350), channel_id=1, source_target_pairs={{0,8},{4,12},{8,0},{12,4},{16,24},{20,28},{24,16},{28,20},{1,9},{5... | collective-permute-start | bytes 3145736 | tf_op jit(solution)/shard_map/ppermute | solution.py:921
  290.6 25.3 %collective-permute-start.20 = (bf16[512,1024]{1,0:T(8,128)(2,1)}, bf16[512,1024]{1,0:T(8,128)(2,1)}, u32[]{:S(2)}, u32[]{:S(2)}) collective-permute-start(bf16[512,1024]{1,0:T(8,128)(2,1)} %get-tuple-element.351), channel_id=1, source_target_pairs={{0,16},{4,20},{8,24},{12,28},{16,0},{20,4},{24,8},{28,12},{1,17},{... | collective-permute-start | bytes 3145736 | tf_op jit(solution)/shard_map/ppermute | solution.py:921
  315.9 3.4 collective-permute-start.21
  323.1 16.3 %collective-permute-start.22 = (bf16[3,640,128]{2,1,0:T(8,128)(2,1)}, bf16[3,640,128]{2,1,0:T(8,128)(2,1)}, u32[]{:S(2)}, u32[]{:S(2)}) collective-permute-start(bf16[3,640,128]{2,1,0:T(8,128)(2,1)} %get-tuple-element.363), channel_id=1, source_target_pairs={{0,8},{4,12},{8,0},{12,4},{16,24},{20,28},{24,16},{28,20},{1,9},{5... | collective-permute-start | bytes 1474568 | tf_op jit(solution)/shard_map/ppermute | solution.py:1086
  323.7 22.7 %collective-permute-start.23 = (bf16[3,640,128]{2,1,0:T(8,128)(2,1)}, bf16[3,640,128]{2,1,0:T(8,128)(2,1)}, u32[]{:S(2)}, u32[]{:S(2)}) collective-permute-start(bf16[3,640,128]{2,1,0:T(8,128)(2,1)} %get-tuple-element.364), channel_id=1, source_target_pairs={{0,16},{4,20},{8,24},{12,28},{16,0},{20,4},{24,8},{28,12},{1,17},{... | collective-permute-start | bytes 1474568 | tf_op jit(solution)/shard_map/ppermute | solution.py:1086
  325.1 23.8 %collective-permute-start.24 = (bf16[3,640,128]{2,1,0:T(8,128)(2,1)}, bf16[3,640,128]{2,1,0:T(8,128)(2,1)}, u32[]{:S(2)}, u32[]{:S(2)}) collective-permute-start(bf16[3,640,128]{2,1,0:T(8,128)(2,1)} %get-tuple-element.365), channel_id=1, source_target_pairs={{0,24},{4,28},{8,16},{12,20},{16,8},{20,12},{24,0},{28,4},{1,25},{... | collective-permute-start | bytes 1474568 | tf_op jit(solution)/shard_map/ppermute | solution.py:1086
  338.9 21.0 %collective-permute-start.25 = (bf16[1024,2048]{1,0:T(8,128)(2,1)}, bf16[1024,2048]{1,0:T(8,128)(2,1)}, u32[]{:S(2)}, u32[]{:S(2)}) collective-permute-start(bf16[1024,2048]{1,0:T(8,128)(2,1)} %wgrad_away.8), channel_id=1, source_target_pairs={{0,4},{4,0},{8,12},{12,8},{16,20},{20,16},{24,28},{28,24},{1,5},{5... | collective-permute-start | bytes 12582920 | tf_op jit(solution)/shard_map/ppermute | solution.py:921
  338.9 41.3 %collective-permute-start.27 = (bf16[512,1024]{1,0:T(8,128)(2,1)}, bf16[512,1024]{1,0:T(8,128)(2,1)}, u32[]{:S(2)}, u32[]{:S(2)}) collective-permute-start(bf16[512,1024]{1,0:T(8,128)(2,1)} %get-tuple-element.391), channel_id=1, source_target_pairs={{0,8},{4,12},{8,0},{12,4},{16,24},{20,28},{24,16},{28,20},{1,9},{5... | collective-permute-start | bytes 3145736 | tf_op jit(solution)/shard_map/ppermute | solution.py:921
  339.4 40.8 %collective-permute-start.28 = (bf16[512,1024]{1,0:T(8,128)(2,1)}, bf16[512,1024]{1,0:T(8,128)(2,1)}, u32[]{:S(2)}, u32[]{:S(2)}) collective-permute-start(bf16[512,1024]{1,0:T(8,128)(2,1)} %get-tuple-element.392), channel_id=1, source_target_pairs={{0,16},{4,20},{8,24},{12,28},{16,0},{20,4},{24,8},{28,12},{1,17},{... | collective-permute-start | bytes 3145736 | tf_op jit(solution)/shard_map/ppermute | solution.py:921
  359.9 130.5 %all-gather.8.cloned.1.call-start = ((), (), s32[]{:S(2)}) async-start(), calls=%async_computation.7 | async-start | bytes 3276800 | tf_op jit(solution)/shard_map/all_gather | solution.py:1211
  367.1 22.4 %collective-permute-start.26 = (bf16[1024,1536]{1,0:T(8,128)(2,1)}, bf16[1024,1536]{1,0:T(8,128)(2,1)}, u32[]{:S(2)}, u32[]{:S(2)}) collective-permute-start(bf16[1024,1536]{1,0:T(8,128)(2,1)} %wgrad_away.9), channel_id=1, source_target_pairs={{0,4},{4,0},{8,12},{12,8},{16,20},{20,16},{24,28},{28,24},{1,5},{5... | collective-permute-start | bytes 9437192 | tf_op jit(solution)/shard_map/ppermute | solution.py:921
  367.1 15.1 %collective-permute-start.29 = (bf16[256,1024]{1,0:T(8,128)(2,1)}, bf16[256,1024]{1,0:T(8,128)(2,1)}, u32[]{:S(2)}, u32[]{:S(2)}) collective-permute-start(bf16[256,1024]{1,0:T(8,128)(2,1)} %get-tuple-element.400), channel_id=1, source_target_pairs={{0,16},{4,20},{8,24},{12,28},{16,0},{20,4},{24,8},{28,12},{1,17},{... | collective-permute-start | bytes 1572872 | tf_op jit(solution)/shard_map/ppermute | solution.py:921
  367.6 14.6 %collective-permute-start.30 = (bf16[256,1024]{1,0:T(8,128)(2,1)}, bf16[256,1024]{1,0:T(8,128)(2,1)}, u32[]{:S(2)}, u32[]{:S(2)}) collective-permute-start(bf16[256,1024]{1,0:T(8,128)(2,1)} %get-tuple-element.402), channel_id=1, source_target_pairs={{0,8},{4,12},{8,0},{12,4},{16,24},{20,28},{24,16},{28,20},{1,9},{5... | collective-permute-start | bytes 1572872 | tf_op jit(solution)/shard_map/ppermute | solution.py:921
  380.2 25.3 %collective-permute-start.31 = (bf16[512,1024]{1,0:T(8,128)(2,1)}, bf16[512,1024]{1,0:T(8,128)(2,1)}, u32[]{:S(2)}, u32[]{:S(2)}) collective-permute-start(bf16[512,1024]{1,0:T(8,128)(2,1)} %get-tuple-element.418), channel_id=1, source_target_pairs={{0,8},{4,12},{8,0},{12,4},{16,24},{20,28},{24,16},{28,20},{1,9},{5... | collective-permute-start | bytes 3145736 | tf_op jit(solution)/shard_map/ppermute | solution.py:921
  380.3 25.4 %collective-permute-start.32 = (bf16[512,1024]{1,0:T(8,128)(2,1)}, bf16[512,1024]{1,0:T(8,128)(2,1)}, u32[]{:S(2)}, u32[]{:S(2)}) collective-permute-start(bf16[512,1024]{1,0:T(8,128)(2,1)} %get-tuple-element.419), channel_id=1, source_target_pairs={{0,16},{4,20},{8,24},{12,28},{16,0},{20,4},{24,8},{28,12},{1,17},{... | collective-permute-start | bytes 3145736 | tf_op jit(solution)/shard_map/ppermute | solution.py:921
  421.2 10.0 %collective-permute-start.33 = (bf16[512,256]{1,0:T(8,128)(2,1)}, bf16[512,256]{1,0:T(8,128)(2,1)}, u32[]{:S(2)}, u32[]{:S(2)}) collective-permute-start(bf16[512,256]{1,0:T(8,128)(2,1)} %get-tuple-element.427), channel_id=1, source_target_pairs={{0,1},{1,2},{2,3},{3,0},{4,5},{5,6},{6,7},{7,4},{8,9},{9,10},{10,1... | collective-permute-start | bytes 786440 | tf_op jit(solution)/shard_map/ppermute | solution.py:999
  421.8 15.2 %collective-permute-start.38 = (bf16[256,1024]{1,0:T(8,128)(2,1)}, bf16[256,1024]{1,0:T(8,128)(2,1)}, u32[]{:S(2)}, u32[]{:S(2)}) collective-permute-start(bf16[256,1024]{1,0:T(8,128)(2,1)} %get-tuple-element.441), channel_id=1, source_target_pairs={{0,16},{4,20},{8,24},{12,28},{16,0},{20,4},{24,8},{28,12},{1,17},{... | collective-permute-start | bytes 1572872 | tf_op jit(solution)/shard_map/ppermute | solution.py:921
  423.3 15.2 %collective-permute-start.39 = (bf16[256,1024]{1,0:T(8,128)(2,1)}, bf16[256,1024]{1,0:T(8,128)(2,1)}, u32[]{:S(2)}, u32[]{:S(2)}) collective-permute-start(bf16[256,1024]{1,0:T(8,128)(2,1)} %get-tuple-element.442), channel_id=1, source_target_pairs={{0,8},{4,12},{8,0},{12,4},{16,24},{20,28},{24,16},{28,20},{1,9},{5... | collective-permute-start | bytes 1572872 | tf_op jit(solution)/shard_map/ppermute | solution.py:921
  424.8 6.4 %copy-start.5 = (bf16[512,256]{1,0:T(8,128)(2,1)S(1)}, bf16[512,256]{1,0:T(8,128)(2,1)}, u32[]{:S(2)}) copy-start(bf16[512,256]{1,0:T(8,128)(2,1)} %get-tuple-element.430) | copy-start | bytes 786436
  429.0 19.2 %collective-permute-start.36 = (bf16[256,1024]{1,0:T(8,128)(2,1)}, bf16[256,1024]{1,0:T(8,128)(2,1)}, u32[]{:S(2)}, u32[]{:S(2)}) collective-permute-start(bf16[256,1024]{1,0:T(8,128)(2,1)} %get-tuple-element.435), channel_id=1, source_target_pairs={{0,16},{4,20},{8,24},{12,28},{16,0},{20,4},{24,8},{28,12},{1,17},{... | collective-permute-start | bytes 1572872 | tf_op jit(solution)/shard_map/ppermute | solution.py:921
  429.6 20.1 %collective-permute-start.37 = (bf16[256,1024]{1,0:T(8,128)(2,1)}, bf16[256,1024]{1,0:T(8,128)(2,1)}, u32[]{:S(2)}, u32[]{:S(2)}) collective-permute-start(bf16[256,1024]{1,0:T(8,128)(2,1)} %get-tuple-element.436), channel_id=1, source_target_pairs={{0,8},{4,12},{8,0},{12,4},{16,24},{20,28},{24,16},{28,20},{1,9},{5... | collective-permute-start | bytes 1572872 | tf_op jit(solution)/shard_map/ppermute | solution.py:921
  432.9 16.8 %collective-permute-start.40 = (bf16[512,256]{1,0:T(8,128)(2,1)}, bf16[512,256]{1,0:T(8,128)(2,1)}, u32[]{:S(2)}, u32[]{:S(2)}) collective-permute-start(bf16[512,256]{1,0:T(8,128)(2,1)} %add_convert_fusion.1), channel_id=1, source_target_pairs={{0,1},{1,2},{2,3},{3,0},{4,5},{5,6},{6,7},{7,4},{8,9},{9,10},{10,1... | collective-permute-start | bytes 786440 | tf_op jit(solution)/shard_map/ppermute | solution.py:999
  437.0 29.6 %collective-permute-start.34 = (bf16[512,768]{1,0:T(8,128)(2,1)}, bf16[512,768]{1,0:T(8,128)(2,1)}, u32[]{:S(2)}, u32[]{:S(2)}) collective-permute-start(bf16[512,768]{1,0:T(8,128)(2,1)} %get-tuple-element.431), channel_id=1, source_target_pairs={{0,8},{4,12},{8,0},{12,4},{16,24},{20,28},{24,16},{28,20},{1,9},{5... | collective-permute-start | bytes 2359304 | tf_op jit(solution)/shard_map/ppermute | solution.py:921
  438.5 28.1 %collective-permute-start.35 = (bf16[512,768]{1,0:T(8,128)(2,1)}, bf16[512,768]{1,0:T(8,128)(2,1)}, u32[]{:S(2)}, u32[]{:S(2)}) collective-permute-start(bf16[512,768]{1,0:T(8,128)(2,1)} %get-tuple-element.432), channel_id=1, source_target_pairs={{0,16},{4,20},{8,24},{12,28},{16,0},{20,4},{24,8},{28,12},{1,17},{... | collective-permute-start | bytes 2359304 | tf_op jit(solution)/shard_map/ppermute | solution.py:921
  439.9 9.8 %copy-start.4 = (bf16[512,256]{1,0:T(8,128)(2,1)S(1)}, bf16[512,256]{1,0:T(8,128)(2,1)}, u32[]{:S(2)}) copy-start(bf16[512,256]{1,0:T(8,128)(2,1)} %get-tuple-element.456) | copy-start | bytes 786436
  451.4 29.4 %collective-permute-start.43 = (bf16[512,256]{1,0:T(8,128)(2,1)}, bf16[512,256]{1,0:T(8,128)(2,1)}, u32[]{:S(2)}, u32[]{:S(2)}) collective-permute-start(bf16[512,256]{1,0:T(8,128)(2,1)} %add_convert_fusion), channel_id=1, source_target_pairs={{0,1},{1,2},{2,3},{3,0},{4,5},{5,6},{6,7},{7,4},{8,9},{9,10},{10,1... | collective-permute-start | bytes 786440 | tf_op jit(solution)/shard_map/ppermute | solution.py:999
  456.9 19.4 %collective-permute-start.44 = (bf16[256,1024]{1,0:T(8,128)(2,1)}, bf16[256,1024]{1,0:T(8,128)(2,1)}, u32[]{:S(2)}, u32[]{:S(2)}) collective-permute-start(bf16[256,1024]{1,0:T(8,128)(2,1)} %get-tuple-element.481), channel_id=1, source_target_pairs={{0,16},{4,20},{8,24},{12,28},{16,0},{20,4},{24,8},{28,12},{1,17},{... | collective-permute-start | bytes 1572872 | tf_op jit(solution)/shard_map/ppermute | solution.py:921
  457.4 20.3 %collective-permute-start.45 = (bf16[256,1024]{1,0:T(8,128)(2,1)}, bf16[256,1024]{1,0:T(8,128)(2,1)}, u32[]{:S(2)}, u32[]{:S(2)}) collective-permute-start(bf16[256,1024]{1,0:T(8,128)(2,1)} %get-tuple-element.483), channel_id=1, source_target_pairs={{0,8},{4,12},{8,0},{12,4},{16,24},{20,28},{24,16},{28,20},{1,9},{5... | collective-permute-start | bytes 1572872 | tf_op jit(solution)/shard_map/ppermute | solution.py:921
  469.3 13.8 %collective-permute-start.41 = (bf16[256,768]{1,0:T(8,128)(2,1)}, bf16[256,768]{1,0:T(8,128)(2,1)}, u32[]{:S(2)}, u32[]{:S(2)}) collective-permute-start(bf16[256,768]{1,0:T(8,128)(2,1)} %get-tuple-element.475), channel_id=1, source_target_pairs={{0,16},{4,20},{8,24},{12,28},{16,0},{20,4},{24,8},{28,12},{1,17},{... | collective-permute-start | bytes 1179656 | tf_op jit(solution)/shard_map/ppermute | solution.py:921
  469.9 14.5 %collective-permute-start.42 = (bf16[256,768]{1,0:T(8,128)(2,1)}, bf16[256,768]{1,0:T(8,128)(2,1)}, u32[]{:S(2)}, u32[]{:S(2)}) collective-permute-start(bf16[256,768]{1,0:T(8,128)(2,1)} %get-tuple-element.477), channel_id=1, source_target_pairs={{0,8},{4,12},{8,0},{12,4},{16,24},{20,28},{24,16},{28,20},{1,9},{5... | collective-permute-start | bytes 1179656 | tf_op jit(solution)/shard_map/ppermute | solution.py:921
  (3 other events, 2.0 us)
Sparse Core Ops, SparseCore 0:
  10.2 83.4 all-gather.9
  95.8 31.2 all-gather.11
  129.2 31.6 all-gather.13
  163.7 30.1 reduce-scatter.3
  197.3 30.5 reduce-scatter.5
  243.8 107.2 all-reduce.1
  360.0 61.1 reduce-scatter.7
  429.1 61.1 all-gather.7

commit v6 on v5

--- a/solution.py
+++ b/solution.py
@@ -1261,11 +1261,11 @@
     gate.add()
     qkv.keep()
     residual()
-    ring_start()
     down.send()
-    gate.send()
     up.wait()
     tokens_step()
+    ring_start()
+    gate.send()
     state.ring.step()
     qkv.send()
     down.wait()

time: 508 us -> 511 us (level)
  waiting for transfers between devices: 142 us -> 150 us
    ppermute x6, waiting for transfers between devices: 12.5 us -> 23.8 us  [shifted(): return lax.ppermute(array, 'tensor', pairs)]
    ppermute x25, waiting for transfers between devices: 26.1 us -> 19 us  [swap(): return lax.ppermute(array, 'dp', xor_pairs(self.plan.dp, 1 << bit))]
  transfers between devices with their start and end apart: 54 -> 54, of which waited for: 32 -> 32; matrix products, arithmetic and copies ran while one was open for 2% -> 1% of each run, Pallas kernels for 56% -> 56%
where the time goes in v6:
time: 511 us; the launch traced here: 505 us
  Pallas kernels  281 us (55%)
  waiting for transfers between devices  150 us (29%)
  starting transfers between devices  43.5 us (9%)
  between operations  14.7 us (3%)
  local copies, waits for them, and re-layouts  10.7 us (2%)
    pallas_call x5, Pallas kernels, wgrad_keep(): pl.pallas_call(functools.partial(keep_kernel, len(lhs), count), grid_spec...  46.3 us
    pallas_call x5, Pallas kernels, wgrad_away(): pl.pallas_call(functools.partial(away_kernel, len(lhs)), grid_spec=pltpu....  39.7 us
    all_gather x2, waiting for transfers between devices, body(): lax.all_gather(tie(part, near), 'tensor', axis=0, tiled=False)  39 us
    pallas_call x2, Pallas kernels, feed_forward(): pl.pallas_call(functools.partial(ff_kernel, tile), grid=(1,), in_specs=[w...  35.6 us
    ppermute x15, waiting for transfers between devices, swap(): return lax.ppermute(array, 'dp', xor_pairs(plan.dp, mask))  30.2 us
    ppermute x6, waiting for transfers between devices, shifted(): return lax.ppermute(array, 'tensor', pairs)  23.8 us
    pallas_call x1, Pallas kernels, attend_back(): pl.pallas_call(functools.partial(attend_back_kernel, plan), grid_spec=plt...  23 us
    ppermute x25, starting transfers between devices, swap(): return lax.ppermute(array, 'dp', xor_pairs(self.plan.dp, 1 << bit))  20.6 us
  transfers between devices with their start and end apart: 54, of which 32 were waited for; matrix products, arithmetic and copies ran while one was open for 1% of the time, Pallas kernels for 56%

profile of v6, /device:TPU:0, one launch (start us, length us, event | category | flops | bytes accessed | tf_op | source)
XLA Modules:
  0.0 504.6 jit_solution(9111662973247498007)
XLA Ops:
  7.2 2.3 constant_dynamic-slice_fusion
  10.2 11.8 %project_qkv.1 = (bf16[640,2048]{1,0:T(8,128)(2,1)}, bf16[3,640,128]{2,1,0:T(8,128)(2,1)}, bf16[3,640,128]{2,1,0:T(8,128)(2,1)}, bf16[3,640,128]{2,1,0:T(8,128)(2,1)}, bf16[3,640,128]{2,1,0:T(8,128)(2,1)}) custom-call(s32[40]{0:T(128)} %parent.7, s32[6]{0:T(128)} %stack.39.place, bf16[640,2048]{1,0:T(8,128)(2,1)} %refs_1_.1, bf16[2048,512]{1,0:T(8,128)(2,1)} %wq.3, ...), custom_call_target="tpu_custom_call" | custom-call | bytes 1 | tf_op jit(solution)/shard_map/project_qkv/pallas_call | solution.py:169
  22.1 2.9 collective-permute-start
  26.5 10.4 %grad_hidden.1.seed = f32[640,2048]{1,0:T(8,128)} custom-call(bf16[640,2048]{1,0:T(8,128)(2,1)} %refs_5_.1, bf16[2048,2048]{1,0:T(8,128)(2,1)} %refs_2_.1), custom_call_target="tpu_custom_call" | custom-call | bytes 1 | tf_op jit(solution)/shard_map/grad_hidden/pallas_call | solution.py:518
  37.3 11.2 %collective-permute-done.1.refs_2_ = bf16[3,640,128]{2,1,0:T(8,128)(2,1)S(1)} collective-permute-done((bf16[3,640,128]{2,1,0:T(8,128)(2,1)}, bf16[3,640,128]{2,1,0:T(8,128)(2,1)S(1)}, u32[]{:S(2)}, u32[]{:S(2)}) %collective-permute-start.1) | collective-permute-done | bytes 491552 | tf_op jit(solution)/shard_map/ppermute | solution.py:1086
  49.4 3.0 collective-permute-done.3
  52.4 1.7 pad_maximum_fusion
  54.1 12.3 %attend.1 = (bf16[640,128]{1,0:T(8,128)(2,1)}, bf16[640,128]{1,0:T(8,128)(2,1)}, bf16[640,128]{1,0:T(8,128)(2,1)}, bf16[640,128]{1,0:T(8,128)(2,1)}) custom-call(s32[40]{0:T(128)} %parent.7, s32[6]{0:T(128)} %stack.39.place, bf16[3,640,128]{2,1,0:T(8,128)(2,1)} %get-tuple-element.265.refs_0_, bf16[3,640,128]{2,1,0:T(8,128)(2,1)} %copy-done.1, ...), custom_call_target="tpu_custom_call" | custom-call | bytes 1 | tf_op jit(solution)/shard_map/attend/pallas_call | solution.py:247
  69.9 3.8 collective-permute-done.4.refs_1_
  73.7 2.1 collective-permute-done.5.refs_2_
  78.0 2.8 gather_heads.1
  80.8 12.9 %all-gather.10.cloned.1.call-done = bf16[1024,2048]{1,0:T(8,128)(2,1)} async-done(((bf16[256,2048]{1,0:T(8,128)(2,1)}), bf16[1024,2048]{1,0:T(8,128)(2,1)}) %all-gather.10.cloned.1.call-update) | async-done | bytes 4194320 | tf_op jit(solution)/shard_map/all_gather | solution.py:1093
  94.7 32.4 %all-gather.12.cloned.1.call-done = bf16[1280,512]{1,0:T(8,128)(2,1)} async-done(((bf16[320,512]{1,0:T(8,128)(2,1)}), bf16[1280,512]{1,0:T(8,128)(2,1)}) %all-gather.12.cloned.1.call-update) | async-done | bytes 1310736 | tf_op jit(solution)/shard_map/all_gather | solution.py:1111
  127.1 9.2 %project_out.2 = (f32[320,2048]{1,0:T(8,128)}, bf16[320,2048]{1,0:T(8,128)(2,1)}) custom-call(s32[6]{0:T(128)} %stack.39.place, bf16[640,2048]{1,0:T(8,128)(2,1)} %refs_1_.1, bf16[4,320,512]{2,1,0:T(8,128)(2,1)} %bitcast.37, bf16[4,256,2048]{2,1,0:T(8,128)(2,1)} %bitcast.42, bf16[4,256,2048]{2,1,0:T(8,128)(2,1)} %collective-permute-done.7.far.refs_7_), custom_call_target="tpu_custom_call" | custom-call | flops 699999977472 | bytes 1 | tf_op jit(solution)/shard_map/project_out/pallas_call | solution.py:490
  136.3 17.8 %feed_forward.2 = (bf16[320,2048]{1,0:T(8,128)(2,1)}, bf16[320,2048]{1,0:T(8,128)(2,1)}, bf16[320,2048]{1,0:T(8,128)(2,1)}, bf16[320,2048]{1,0:T(8,128)(2,1)}) custom-call(bf16[320,2048]{1,0:T(8,128)(2,1)} %get-tuple-element.286.normed.refs_0_, f32[640,2048]{1,0:T(8,128)} %grad_hidden.1.seed, bf16[2048,2048]{1,0:T(8,128)(2,1)} %wg.3, bf16[2048,2048]{1,0:T(8,128)(2,1)} %wu.3), custom_call_target="tpu_custom_call" | custom-call | flops 1700000038912 | bytes 1 | tf_op jit(solution)/shard_map/feed_forward/pallas_call | solution.py:589
  154.4 6.5 %all-gather.14.cloned.1.call-done = bf16[1280,512]{1,0:T(8,128)(2,1)} async-done(((bf16[320,512]{1,0:T(8,128)(2,1)}), bf16[1280,512]{1,0:T(8,128)(2,1)}) %all-gather.14.cloned.1.call-update) | async-done | bytes 1310736 | tf_op jit(solution)/shard_map/all_gather | solution.py:1111
  160.9 9.2 %project_out.3 = (f32[320,2048]{1,0:T(8,128)}, bf16[320,2048]{1,0:T(8,128)(2,1)}) custom-call(s32[6]{0:T(128)} %stack.39.place, bf16[640,2048]{1,0:T(8,128)(2,1)} %refs_1_.1, bf16[4,320,512]{2,1,0:T(8,128)(2,1)} %bitcast.39, bf16[4,256,2048]{2,1,0:T(8,128)(2,1)} %bitcast.43, bf16[4,256,2048]{2,1,0:T(8,128)(2,1)} %collective-permute-done.7.far.refs_7_), custom_call_target="tpu_custom_call" | custom-call | flops 699999977472 | bytes 1 | tf_op jit(solution)/shard_map/project_out/pallas_call | solution.py:490
  170.2 17.8 %feed_forward.3 = (bf16[320,2048]{1,0:T(8,128)(2,1)}, bf16[320,2048]{1,0:T(8,128)(2,1)}, bf16[320,2048]{1,0:T(8,128)(2,1)}, bf16[320,2048]{1,0:T(8,128)(2,1)}) custom-call(bf16[320,2048]{1,0:T(8,128)(2,1)} %get-tuple-element.293.normed.refs_1_, f32[640,2048]{1,0:T(8,128)} %grad_hidden.1.seed, bf16[2048,2048]{1,0:T(8,128)(2,1)} %wg.3, bf16[2048,2048]{1,0:T(8,128)(2,1)} %wu.3), custom_call_target="tpu_custom_call" | custom-call | flops 1700000038912 | bytes 1 | tf_op jit(solution)/shard_map/feed_forward/pallas_call | solution.py:589
  188.0 9.1 %wgrad_away.5 = bf16[1024,2048]{1,0:T(8,128)(2,1)} custom-call(s32[6]{0:T(128)} %stack.39.place, bf16[640,2048]{1,0:T(8,128)(2,1)} %refs_5_.1, bf16[320,2048]{1,0:T(8,128)(2,1)} %get-tuple-element.304.refs_1_.refs_0_, bf16[320,2048]{1,0:T(8,128)(2,1)} %get-tuple-element.305.refs_2_.refs_1_), custom_call_target="tpu_custom_call" | custom-call | flops 799999983616 | bytes 1 | tf_op jit(solution)/shard_map/wgrad_away/pallas_call | solution.py:737
  197.2 8.8 %wgrad_away.6 = bf16[1024,2048]{1,0:T(8,128)(2,1)} custom-call(s32[6]{0:T(128)} %stack.39.place, bf16[320,2048]{1,0:T(8,128)(2,1)} %get-tuple-element.286.normed.refs_0_, bf16[320,2048]{1,0:T(8,128)(2,1)} %get-tuple-element.293.normed.refs_1_, bf16[320,2048]{1,0:T(8,128)(2,1)} %get-tuple-element.300.refs_2_, bf16[320,2048]{1,0:T(8,128)(2,1)} %get-tuple-element.301.refs_3_), custom_call_target="tpu_custom_call" | custom-call | flops 799999983616 | bytes 1 | tf_op jit(solution)/shard_map/wgrad_away/pallas_call | solution.py:737
  206.6 10.2 %wgrad_keep.5 = (bf16[512,1024]{1,0:T(8,128)(2,1)}, bf16[512,1024]{1,0:T(8,128)(2,1)}, bf16[512,1024]{1,0:T(8,128)(2,1)}, bf16[512,1024]{1,0:T(8,128)(2,1)}) custom-call(s32[6]{0:T(128)} %stack.39.place, bf16[640,2048]{1,0:T(8,128)(2,1)} %refs_5_.1, bf16[320,2048]{1,0:T(8,128)(2,1)} %get-tuple-element.304.refs_1_.refs_0_, ...), custom_call_target="tpu_custom_call" | custom-call | flops 269999996928 | bytes 1 | tf_op jit(solution)/shard_map/wgrad_keep/pallas_call | solution.py:785
  216.8 9.8 %project_down.1 = bf16[640,2048]{1,0:T(8,128)(2,1)} custom-call(bf16[320,2048]{1,0:T(8,128)(2,1)} %get-tuple-element.304.refs_1_.refs_0_, bf16[320,2048]{1,0:T(8,128)(2,1)} %get-tuple-element.305.refs_2_.refs_1_, bf16[2048,2048]{1,0:T(8,128)(2,1)} %refs_2_.1), custom_call_target="tpu_custom_call" | custom-call | flops 1100000002048 | bytes 1 | tf_op jit(solution)/shard_map/project_down/pallas_call | solution.py:619
  227.9 10.1 %branch_back.1 = (f32[160,2048]{1,0:T(8,128)}, bf16[160,2048]{1,0:T(8,128)(2,1)}, bf16[160,512]{1,0:T(8,128)(2,1)}, bf16[160,512]{1,0:T(8,128)(2,1)}, bf16[160,5...) custom-call(s32[6]{0:T(128)} %stack.39.place, bf16[80,2048]{1,0:T(8,128)(2,1)} %reduce-scatter.4.cloned.1.call-done.refs_0_, ...), custom_call_target="tpu_custom_call" | custom-call | flops 899999989760 | bytes 1 | tf_op jit(solution)/shard_map/branch_back/pallas_call | solution.py:671
  238.1 1.7 collective-permute-start.10
  239.8 2.4 collective-permute-start.11
  248.7 10.1 %collective-permute-done.10.refs_2_ = bf16[160,512]{1,0:T(8,128)(2,1)S(1)} collective-permute-done((bf16[160,512]{1,0:T(8,128)(2,1)}, bf16[160,512]{1,0:T(8,128)(2,1)S(1)}, u32[]{:S(2)}, u32[]{:S(2)}) %collective-permute-start.10) | collective-permute-done | bytes 163872 | tf_op jit(solution)/shard_map/ppermute | solution.py:999
  259.5 2.8 scatter_heads.1
  265.3 5.7 %wgrad_away.7 = bf16[1024,2048]{1,0:T(8,128)(2,1)} custom-call(s32[6]{0:T(128)} %stack.39.place, bf16[160,2048]{1,0:T(8,128)(2,1)} %get-tuple-element.325.refs_0_, bf16[160,2048]{1,0:T(8,128)(2,1)} %copy-done.6), custom_call_target="tpu_custom_call" | custom-call | flops 799999983616 | bytes 1 | tf_op jit(solution)/shard_map/wgrad_away/pallas_call | solution.py:737
  271.0 10.4 %wgrad_keep.6 = (bf16[512,1024]{1,0:T(8,128)(2,1)}, bf16[512,1024]{1,0:T(8,128)(2,1)}, bf16[512,1024]{1,0:T(8,128)(2,1)}, bf16[512,1024]{1,0:T(8,128)(2,1)}) custom-call(s32[6]{0:T(128)} %stack.39.place, bf16[320,2048]{1,0:T(8,128)(2,1)} %get-tuple-element.286.normed.refs_0_, bf16[320,2048]{1,0:T(8,128)(2,1)} %get-tuple-element.293.normed.refs_1_, ...), custom_call_target="tpu_custom_call" | custom-call | flops 899999989760 | bytes 1 | tf_op jit(solution)/shard_map/wgrad_keep/pallas_call | solution.py:785
  282.0 7.0 %wgrad_keep.7 = (bf16[512,1024]{1,0:T(8,128)(2,1)}, bf16[512,1024]{1,0:T(8,128)(2,1)}, bf16[512,1024]{1,0:T(8,128)(2,1)}, bf16[512,1024]{1,0:T(8,128)(2,1)}) custom-call(s32[6]{0:T(128)} %stack.39.place, bf16[160,2048]{1,0:T(8,128)(2,1)} %get-tuple-element.325.refs_0_, bf16[160,2048]{1,0:T(8,128)(2,1)} %copy-done.6, ...), custom_call_target="tpu_custom_call" | custom-call | flops 899999989760 | bytes 1 | tf_op jit(solution)/shard_map/wgrad_keep/pallas_call | solution.py:785
  292.1 23.0 %attend_back.1 = (bf16[640,128]{1,0:T(8,128)(2,1)}, bf16[640,128]{1,0:T(8,128)(2,1)}, bf16[640,128]{1,0:T(8,128)(2,1)}, bf16[640,128]{1,0:T(8,128)(2,1)}, f32[40...) custom-call(s32[40]{0:T(128)} %parent.7, s32[6]{0:T(128)} %stack.39.place, ...), custom_call_target="tpu_custom_call" | custom-call | flops 2300000075776 | bytes 1 | tf_op jit(solution)/shard_map/attend_back/pallas_call | solution.py:305
  315.9 3.3 wgrad_stage.5
  319.3 3.8 combine_back.1
  326.6 3.4 wgrad_stage.6
  330.0 8.9 %wgrad_away.8 = bf16[1024,2048]{1,0:T(8,128)(2,1)} custom-call(s32[6]{0:T(128)} %stack.39.place, bf16[320,2048]{1,0:T(8,128)(2,1)} %get-tuple-element.286.normed.refs_0_, bf16[320,2048]{1,0:T(8,128)(2,1)} %get-tuple-element.293.normed.refs_1_, bf16[320,2048]{1,0:T(8,128)(2,1)} %get-tuple-element.375.refs_2_, bf16[320,2048]{1,0:T(8,128)(2,1)} %get-tuple-element.376.refs_3_), custom_call_target="tpu_custom_call" | custom-call | flops 799999983616 | bytes 1 | tf_op jit(solution)/shard_map/wgrad_away/pallas_call | solution.py:737
  340.9 5.6 %collective-permute-done.23.refs_2_ = bf16[3,640,128]{2,1,0:T(8,128)(2,1)} collective-permute-done((bf16[3,640,128]{2,1,0:T(8,128)(2,1)}, bf16[3,640,128]{2,1,0:T(8,128)(2,1)}, u32[]{:S(2)}, u32[]{:S(2)}) %collective-permute-start.23) | collective-permute-done | bytes 491552 | tf_op jit(solution)/shard_map/ppermute | solution.py:1086
  346.5 2.4 collective-permute-done.24.refs_3_
  348.9 10.9 %turn_back.1 = (bf16[640,2048]{1,0:T(8,128)(2,1)}, bf16[640,1536]{1,0:T(8,128)(2,1)}) custom-call(s32[40]{0:T(128)} %parent.7, s32[6]{0:T(128)} %stack.39.place, f32[1280,128]{1,0:T(8,128)} %constant.39.clone.cosine, f32[1280,128]{1,0:T(8,128)} %constant.40.clone.sine, bf16[2048,512]{1,0:T(8,128)(2,1)} %wq.3, bf16[2048,512]{1,0:T(8,128)(2,1)} %wk.3, ...), custom_call_target="tpu_custom_call" | custom-call | flops 1300000014336 | bytes 1 | tf_op jit(solution)/shard_map/turn_back/pallas_call | solution.py:447
  360.0 7.2 %wgrad_away.9 = bf16[1024,1536]{1,0:T(8,128)(2,1)} custom-call(s32[6]{0:T(128)} %stack.39.place, bf16[640,2048]{1,0:T(8,128)(2,1)} %get-tuple-element.258.refs_0_, bf16[640,1536]{1,0:T(8,128)(2,1)} %get-tuple-element.388.refs_1_), custom_call_target="tpu_custom_call" | custom-call | flops 799999983616 | bytes 1 | tf_op jit(solution)/shard_map/wgrad_away/pallas_call | solution.py:737
  367.7 2.0 collective-permute-start.30
  369.7 10.5 %wgrad_keep.8 = (bf16[512,1024]{1,0:T(8,128)(2,1)}, bf16[512,1024]{1,0:T(8,128)(2,1)}, bf16[512,1024]{1,0:T(8,128)(2,1)}, bf16[512,1024]{1,0:T(8,128)(2,1)}) custom-call(s32[6]{0:T(128)} %stack.39.place, bf16[320,2048]{1,0:T(8,128)(2,1)} %get-tuple-element.286.normed.refs_0_, bf16[320,2048]{1,0:T(8,128)(2,1)} %get-tuple-element.293.normed.refs_1_, ...), custom_call_target="tpu_custom_call" | custom-call | flops 899999989760 | bytes 1 | tf_op jit(solution)/shard_map/wgrad_keep/pallas_call | solution.py:785
  382.3 3.9 wgrad_finish_chunks.1
  386.2 3.3 wgrad_stage.7
  389.5 8.2 %wgrad_keep.9 = (bf16[512,768]{1,0:T(8,128)(2,1)}, bf16[512,768]{1,0:T(8,128)(2,1)}, bf16[512,768]{1,0:T(8,128)(2,1)}, bf16[512,768]{1,0:T(8,128)(2,1)}) custom-call(s32[6]{0:T(128)} %stack.39.place, bf16[640,2048]{1,0:T(8,128)(2,1)} %get-tuple-element.258.refs_0_, bf16[640,1536]{1,0:T(8,128)(2,1)} %get-tuple-element.388.refs_1_, ...), custom_call_target="tpu_custom_call" | custom-call | flops 899999989760 | bytes 1 | tf_op jit(solution)/shard_map/wgrad_keep/pallas_call | solution.py:785
  397.7 5.3 %add_residual.1 = bf16[640,2048]{1,0:T(8,128)(2,1)} custom-call(f32[320,2048]{1,0:T(8,128)} %get-tuple-element.282.refs_2_.refs_0_, f32[320,2048]{1,0:T(8,128)} %get-tuple-element.290.refs_3_.refs_1_, bf16[640,2048]{1,0:T(8,128)(2,1)} %all-reduce.2.cloned.1.call-done.refs_2_), custom_call_target="tpu_custom_call" | custom-call | flops 599999971328 | bytes 1 | tf_op jit(solution)/shard_map/add_residual/pallas_call | solution.py:1053
  403.0 2.5 collective-permute-done.31.a_got
  405.8 15.5 %reduce-scatter.8.cloned.1.call-done.part = bf16[160,2048]{1,0:T(8,128)(2,1)} async-done(((bf16[640,2048]{1,0:T(8,128)(2,1)}), bf16[160,2048]{1,0:T(8,128)(2,1)}) %reduce-scatter.8.cloned.1.call-update) | async-done | bytes 655376 | tf_op jit(solution)/shard_map/reduce_scatter | solution.py:1201
  424.1 4.2 tokens_back.1
  430.2 7.3 %collective-permute-done.33 = bf16[512,256]{1,0:T(8,128)(2,1)S(1)} collective-permute-done((bf16[512,256]{1,0:T(8,128)(2,1)S(1)}, bf16[512,256]{1,0:T(8,128)(2,1)S(1)}, u32[]{:S(2)}, u32[]{:S(2)}) %collective-permute-start.33) | collective-permute-done | bytes 262176 | tf_op jit(solution)/shard_map/ppermute | solution.py:999
  439.3 3.4 wgrad_stage.8
  442.8 4.8 collective-permute-done.36.a_got
  449.1 5.0 collective-permute-done.40
  454.1 1.7 add_convert_fusion
  455.8 2.4 collective-permute-start.43
  458.2 3.5 wgrad_finish.3
  461.7 3.1 wgrad_finish.4
  465.9 2.8 wgrad_stage.9
  469.5 2.0 collective-permute-start.42
  471.6 5.3 %collective-permute-done.44.a_got = bf16[256,1024]{1,0:T(8,128)(2,1)} collective-permute-done((bf16[256,1024]{1,0:T(8,128)(2,1)}, bf16[256,1024]{1,0:T(8,128)(2,1)}, u32[]{:S(2)}, u32[]{:S(2)}) %collective-permute-start.44) | collective-permute-done | bytes 524320 | tf_op jit(solution)/shard_map/ppermute | solution.py:921
  477.2 3.1 wgrad_finish.5
  480.2 1.9 add_last.1
  484.0 2.5 wgrad_finish_split.1
  486.5 7.5 %all-gather.8.cloned.1.call-done = bf16[640,2048]{1,0:T(8,128)(2,1)} async-done(((bf16[160,2048]{1,0:T(8,128)(2,1)}), bf16[640,2048]{1,0:T(8,128)(2,1)}) %all-gather.8.cloned.1.call-update) | async-done | bytes 2621456 | tf_op jit(solution)/shard_map/all_gather | solution.py:1211
  494.0 3.6 copy.23
  (132 shorter events, 47.8 us)
Async XLA Ops:
  7.2 86.5 %all-gather.10.cloned.1.call-start = ((), (), s32[]{:S(2)}) async-start(), calls=%async_computation.8 | async-start | bytes 5242880 | tf_op jit(solution)/shard_map/all_gather | solution.py:1093
  9.6 117.5 %all-gather.12.cloned.1.call-start = ((), (), s32[]{:S(2)}) async-start(), calls=%async_computation.9 | async-start | bytes 1638400 | tf_op jit(solution)/shard_map/all_gather | solution.py:1111
  22.1 15.2 %collective-permute-start = (bf16[3,640,128]{2,1,0:T(8,128)(2,1)}, bf16[3,640,128]{2,1,0:T(8,128)(2,1)S(1)}, u32[]{:S(2)}, u32[]{:S(2)}) collective-permute-start(bf16[3,640,128]{2,1,0:T(8,128)(2,1)} %get-tuple-element.255), channel_id=1, source_target_pairs={{0,8},{4,12},{8,0},{12,4},{16,24},{20,28},{24,16},{28,20},{1,9},{5... | collective-permute-start | bytes 1474568 | tf_op jit(solution)/shard_map/ppermute | solution.py:1086
  25.0 23.4 %collective-permute-start.1 = (bf16[3,640,128]{2,1,0:T(8,128)(2,1)}, bf16[3,640,128]{2,1,0:T(8,128)(2,1)S(1)}, u32[]{:S(2)}, u32[]{:S(2)}) collective-permute-start(bf16[3,640,128]{2,1,0:T(8,128)(2,1)} %get-tuple-element.256), channel_id=1, source_target_pairs={{0,16},{4,20},{8,24},{12,28},{16,0},{20,4},{24,8},{28,12},{1,17},{... | collective-permute-start | bytes 1474568 | tf_op jit(solution)/shard_map/ppermute | solution.py:1086
  26.5 21.9 %collective-permute-start.2 = (bf16[3,640,128]{2,1,0:T(8,128)(2,1)}, bf16[3,640,128]{2,1,0:T(8,128)(2,1)S(1)}, u32[]{:S(2)}, u32[]{:S(2)}) collective-permute-start(bf16[3,640,128]{2,1,0:T(8,128)(2,1)} %get-tuple-element.257), channel_id=1, source_target_pairs={{0,24},{4,28},{8,16},{12,20},{16,8},{20,12},{24,0},{28,4},{1,25},{... | collective-permute-start | bytes 1474568 | tf_op jit(solution)/shard_map/ppermute | solution.py:1086
  26.5 21.9 %copy-start = (bf16[3,640,128]{2,1,0:T(8,128)(2,1)S(1)}, bf16[3,640,128]{2,1,0:T(8,128)(2,1)}, u32[]{:S(2)}) copy-start(bf16[3,640,128]{2,1,0:T(8,128)(2,1)} %get-tuple-element.265.refs_0_) | copy-start | bytes 1474564
  37.3 11.5 %copy-start.1 = (bf16[3,640,128]{2,1,0:T(8,128)(2,1)}, bf16[3,640,128]{2,1,0:T(8,128)(2,1)S(1)}, u32[]{:S(2)}) copy-start(bf16[3,640,128]{2,1,0:T(8,128)(2,1)S(1)} %collective-permute-done.refs_1_) | copy-start | bytes 1474564
  48.4 0.9 copy-start.3
  49.4 3.0 collective-permute-start.3
  66.5 7.3 %collective-permute-start.4 = (bf16[640,128]{1,0:T(8,128)(2,1)}, bf16[640,128]{1,0:T(8,128)(2,1)S(1)}, u32[]{:S(2)}, u32[]{:S(2)}) collective-permute-start(bf16[640,128]{1,0:T(8,128)(2,1)} %get-tuple-element.270), channel_id=1, source_target_pairs={{0,8},{4,12},{8,0},{12,4},{16,24},{20,28},{24,16},{28,20},{1,9},{5... | collective-permute-start | bytes 491528 | tf_op jit(solution)/shard_map/ppermute | solution.py:1086
  67.5 8.3 %collective-permute-start.5 = (bf16[640,128]{1,0:T(8,128)(2,1)}, bf16[640,128]{1,0:T(8,128)(2,1)S(1)}, u32[]{:S(2)}, u32[]{:S(2)}) collective-permute-start(bf16[640,128]{1,0:T(8,128)(2,1)} %get-tuple-element.271), channel_id=1, source_target_pairs={{0,16},{4,20},{8,24},{12,28},{16,0},{20,4},{24,8},{28,12},{1,17},{... | collective-permute-start | bytes 491528 | tf_op jit(solution)/shard_map/ppermute | solution.py:1086
  68.5 8.9 %collective-permute-start.6 = (bf16[640,128]{1,0:T(8,128)(2,1)}, bf16[640,128]{1,0:T(8,128)(2,1)S(1)}, u32[]{:S(2)}, u32[]{:S(2)}) collective-permute-start(bf16[640,128]{1,0:T(8,128)(2,1)} %get-tuple-element.272), channel_id=1, source_target_pairs={{0,24},{4,28},{8,16},{12,20},{16,8},{20,12},{24,0},{28,4},{1,25},{... | collective-permute-start | bytes 491528 | tf_op jit(solution)/shard_map/ppermute | solution.py:1086
  73.7 3.7 copy-start.10
  75.8 1.5 copy-start.11
  93.7 33.4 %collective-permute-start.7 = (bf16[4,256,2048]{2,1,0:T(8,128)(2,1)}, bf16[4,256,2048]{2,1,0:T(8,128)(2,1)}, u32[]{:S(2)}, u32[]{:S(2)}) collective-permute-start(bf16[4,256,2048]{2,1,0:T(8,128)(2,1)} %bitcast.41), channel_id=1, source_target_pairs={{0,4},{4,0},{8,12},{12,8},{16,20},{20,16},{24,28},{28,24},{1,5},{5... | collective-permute-start | bytes 12582920 | tf_op jit(solution)/shard_map/ppermute | solution.py:1086
  93.7 67.2 %all-gather.14.cloned.1.call-start = ((), (), s32[]{:S(2)}) async-start(), calls=%async_computation.10 | async-start | bytes 1638400 | tf_op jit(solution)/shard_map/all_gather | solution.py:1111
  94.4 132.1 %reduce-scatter.4.cloned.1.call-start = ((), (), s32[]{:S(2)}) async-start(), calls=%async_computation.4 | async-start | bytes 1638400 | tf_op jit(solution)/shard_map/reduce_scatter | solution.py:1125
  154.1 73.8 %reduce-scatter.6.cloned.1.call-start = ((), (), s32[]{:S(2)}) async-start(), calls=%async_computation.5 | async-start | bytes 1638400 | tf_op jit(solution)/shard_map/reduce_scatter | solution.py:1125
  197.1 9.5 %collective-permute-start.8 = (bf16[1024,2048]{1,0:T(8,128)(2,1)}, bf16[1024,2048]{1,0:T(8,128)(2,1)}, u32[]{:S(2)}, u32[]{:S(2)}) collective-permute-start(bf16[1024,2048]{1,0:T(8,128)(2,1)} %wgrad_away.5), channel_id=1, source_target_pairs={{0,4},{4,0},{8,12},{12,8},{16,20},{20,16},{24,28},{28,24},{1,5},{5... | collective-permute-start | bytes 12582920 | tf_op jit(solution)/shard_map/ppermute | solution.py:921
  197.2 200.5 %all-reduce.2.cloned.1.call-start = ((), (), s32[]{:S(2)}) async-start(), calls=%async_computation.3 | async-start | bytes 5242880 | tf_op jit(solution)/shard_map/psum | solution.py:1161
  206.1 64.9 %collective-permute-start.18 = (bf16[1024,2048]{1,0:T(8,128)(2,1)}, bf16[1024,2048]{1,0:T(8,128)(2,1)}, u32[]{:S(2)}, u32[]{:S(2)}) collective-permute-start(bf16[1024,2048]{1,0:T(8,128)(2,1)} %wgrad_away.6), channel_id=1, source_target_pairs={{0,4},{4,0},{8,12},{12,8},{16,20},{20,16},{24,28},{28,24},{1,5},{5... | collective-permute-start | bytes 12582920 | tf_op jit(solution)/shard_map/ppermute | solution.py:921
  238.0 9.3 %collective-permute-start.9 = (bf16[160,512]{1,0:T(8,128)(2,1)}, bf16[160,512]{1,0:T(8,128)(2,1)S(1)}, u32[]{:S(2)}, u32[]{:S(2)}) collective-permute-start(bf16[160,512]{1,0:T(8,128)(2,1)} %get-tuple-element.309), channel_id=1, source_target_pairs={{0,1},{1,2},{2,3},{3,0},{4,5},{5,6},{6,7},{7,4},{8,9},{9,10},{10,1... | collective-permute-start | bytes 491528 | tf_op jit(solution)/shard_map/ppermute | solution.py:999
  238.1 20.7 %collective-permute-start.10 = (bf16[160,512]{1,0:T(8,128)(2,1)}, bf16[160,512]{1,0:T(8,128)(2,1)S(1)}, u32[]{:S(2)}, u32[]{:S(2)}) collective-permute-start(bf16[160,512]{1,0:T(8,128)(2,1)} %get-tuple-element.310), channel_id=1, source_target_pairs={{0,2},{1,3},{2,0},{3,1},{4,6},{5,7},{6,4},{7,5},{8,10},{9,11},{10,... | collective-permute-start | bytes 491528 | tf_op jit(solution)/shard_map/ppermute | solution.py:999
  239.8 19.0 %collective-permute-start.11 = (bf16[160,512]{1,0:T(8,128)(2,1)}, bf16[160,512]{1,0:T(8,128)(2,1)S(1)}, u32[]{:S(2)}, u32[]{:S(2)}) collective-permute-start(bf16[160,512]{1,0:T(8,128)(2,1)} %get-tuple-element.311), channel_id=1, source_target_pairs={{0,3},{1,0},{2,1},{3,2},{4,7},{5,4},{6,5},{7,6},{8,11},{9,8},{10,9... | collective-permute-start | bytes 491528 | tf_op jit(solution)/shard_map/ppermute | solution.py:999
  242.2 46.9 %collective-permute-start.15 = (bf16[512,1024]{1,0:T(8,128)(2,1)}, bf16[512,1024]{1,0:T(8,128)(2,1)}, u32[]{:S(2)}, u32[]{:S(2)}) collective-permute-start(bf16[512,1024]{1,0:T(8,128)(2,1)} %get-tuple-element.323), channel_id=1, source_target_pairs={{0,8},{4,12},{8,0},{12,4},{16,24},{20,28},{24,16},{28,20},{1,9},{5... | collective-permute-start | bytes 3145736 | tf_op jit(solution)/shard_map/ppermute | solution.py:921
  243.7 177.5 %reduce-scatter.8.cloned.1.call-start = ((), (), s32[]{:S(2)}) async-start(), calls=%async_computation.6 | async-start | bytes 3276800 | tf_op jit(solution)/shard_map/reduce_scatter | solution.py:1201
  245.9 19.4 %copy-start.6 = (bf16[160,2048]{1,0:T(8,128)(2,1)}, bf16[160,2048]{1,0:T(8,128)(2,1)S(1)}, u32[]{:S(2)}) copy-start(bf16[160,2048]{1,0:T(8,128)(2,1)S(1)} %constant_dynamic-update-slice_fusion.refs_1_) | copy-start | bytes 1966084
  247.3 11.5 %copy-start.7 = (bf16[160,512]{1,0:T(8,128)(2,1)}, bf16[160,512]{1,0:T(8,128)(2,1)S(1)}, u32[]{:S(2)}) copy-start(bf16[160,512]{1,0:T(8,128)(2,1)S(1)} %collective-permute-done.9.refs_1_) | copy-start | bytes 491524
  247.3 41.8 %collective-permute-start.16 = (bf16[512,1024]{1,0:T(8,128)(2,1)}, bf16[512,1024]{1,0:T(8,128)(2,1)}, u32[]{:S(2)}, u32[]{:S(2)}) collective-permute-start(bf16[512,1024]{1,0:T(8,128)(2,1)} %get-tuple-element.324), channel_id=1, source_target_pairs={{0,16},{4,20},{8,24},{12,28},{16,0},{20,4},{24,8},{28,12},{1,17},{... | collective-permute-start | bytes 3145736 | tf_op jit(solution)/shard_map/ppermute | solution.py:921
  262.3 26.7 %collective-permute-start.12 = (bf16[640,128]{1,0:T(8,128)(2,1)}, bf16[640,128]{1,0:T(8,128)(2,1)}, u32[]{:S(2)}, u32[]{:S(2)}) collective-permute-start(bf16[640,128]{1,0:T(8,128)(2,1)} %get-tuple-element.318), channel_id=1, source_target_pairs={{0,8},{4,12},{8,0},{12,4},{16,24},{20,28},{24,16},{28,20},{1,9},{5... | collective-permute-start | bytes 491528 | tf_op jit(solution)/shard_map/ppermute | solution.py:1086
  263.8 25.3 %collective-permute-start.13 = (bf16[640,128]{1,0:T(8,128)(2,1)}, bf16[640,128]{1,0:T(8,128)(2,1)}, u32[]{:S(2)}, u32[]{:S(2)}) collective-permute-start(bf16[640,128]{1,0:T(8,128)(2,1)} %get-tuple-element.319), channel_id=1, source_target_pairs={{0,16},{4,20},{8,24},{12,28},{16,0},{20,4},{24,8},{28,12},{1,17},{... | collective-permute-start | bytes 491528 | tf_op jit(solution)/shard_map/ppermute | solution.py:1086
  271.0 10.4 %collective-permute-start.17 = (bf16[1024,2048]{1,0:T(8,128)(2,1)}, bf16[1024,2048]{1,0:T(8,128)(2,1)}, u32[]{:S(2)}, u32[]{:S(2)}) collective-permute-start(bf16[1024,2048]{1,0:T(8,128)(2,1)} %wgrad_away.7), channel_id=1, source_target_pairs={{0,4},{4,0},{8,12},{12,8},{16,20},{20,16},{24,28},{28,24},{1,5},{5... | collective-permute-start | bytes 12582920 | tf_op jit(solution)/shard_map/ppermute | solution.py:921
  281.4 7.9 %collective-permute-start.14 = (bf16[640,128]{1,0:T(8,128)(2,1)}, bf16[640,128]{1,0:T(8,128)(2,1)}, u32[]{:S(2)}, u32[]{:S(2)}) collective-permute-start(bf16[640,128]{1,0:T(8,128)(2,1)} %get-tuple-element.320), channel_id=1, source_target_pairs={{0,24},{4,28},{8,16},{12,20},{16,8},{20,12},{24,0},{28,4},{1,25},{... | collective-permute-start | bytes 491528 | tf_op jit(solution)/shard_map/ppermute | solution.py:1086
  289.3 25.8 %collective-permute-start.19 = (bf16[512,1024]{1,0:T(8,128)(2,1)}, bf16[512,1024]{1,0:T(8,128)(2,1)}, u32[]{:S(2)}, u32[]{:S(2)}) collective-permute-start(bf16[512,1024]{1,0:T(8,128)(2,1)} %get-tuple-element.350), channel_id=1, source_target_pairs={{0,8},{4,12},{8,0},{12,4},{16,24},{20,28},{24,16},{28,20},{1,9},{5... | collective-permute-start | bytes 3145736 | tf_op jit(solution)/shard_map/ppermute | solution.py:921
  290.6 25.3 %collective-permute-start.20 = (bf16[512,1024]{1,0:T(8,128)(2,1)}, bf16[512,1024]{1,0:T(8,128)(2,1)}, u32[]{:S(2)}, u32[]{:S(2)}) collective-permute-start(bf16[512,1024]{1,0:T(8,128)(2,1)} %get-tuple-element.351), channel_id=1, source_target_pairs={{0,16},{4,20},{8,24},{12,28},{16,0},{20,4},{24,8},{28,12},{1,17},{... | collective-permute-start | bytes 3145736 | tf_op jit(solution)/shard_map/ppermute | solution.py:921
  315.9 3.4 collective-permute-start.21
  323.1 16.3 %collective-permute-start.22 = (bf16[3,640,128]{2,1,0:T(8,128)(2,1)}, bf16[3,640,128]{2,1,0:T(8,128)(2,1)}, u32[]{:S(2)}, u32[]{:S(2)}) collective-permute-start(bf16[3,640,128]{2,1,0:T(8,128)(2,1)} %get-tuple-element.363), channel_id=1, source_target_pairs={{0,8},{4,12},{8,0},{12,4},{16,24},{20,28},{24,16},{28,20},{1,9},{5... | collective-permute-start | bytes 1474568 | tf_op jit(solution)/shard_map/ppermute | solution.py:1086
  323.6 22.9 %collective-permute-start.23 = (bf16[3,640,128]{2,1,0:T(8,128)(2,1)}, bf16[3,640,128]{2,1,0:T(8,128)(2,1)}, u32[]{:S(2)}, u32[]{:S(2)}) collective-permute-start(bf16[3,640,128]{2,1,0:T(8,128)(2,1)} %get-tuple-element.364), channel_id=1, source_target_pairs={{0,16},{4,20},{8,24},{12,28},{16,0},{20,4},{24,8},{28,12},{1,17},{... | collective-permute-start | bytes 1474568 | tf_op jit(solution)/shard_map/ppermute | solution.py:1086
  325.2 23.8 %collective-permute-start.24 = (bf16[3,640,128]{2,1,0:T(8,128)(2,1)}, bf16[3,640,128]{2,1,0:T(8,128)(2,1)}, u32[]{:S(2)}, u32[]{:S(2)}) collective-permute-start(bf16[3,640,128]{2,1,0:T(8,128)(2,1)} %get-tuple-element.365), channel_id=1, source_target_pairs={{0,24},{4,28},{8,16},{12,20},{16,8},{20,12},{24,0},{28,4},{1,25},{... | collective-permute-start | bytes 1474568 | tf_op jit(solution)/shard_map/ppermute | solution.py:1086
  338.9 21.1 %collective-permute-start.25 = (bf16[1024,2048]{1,0:T(8,128)(2,1)}, bf16[1024,2048]{1,0:T(8,128)(2,1)}, u32[]{:S(2)}, u32[]{:S(2)}) collective-permute-start(bf16[1024,2048]{1,0:T(8,128)(2,1)} %wgrad_away.8), channel_id=1, source_target_pairs={{0,4},{4,0},{8,12},{12,8},{16,20},{20,16},{24,28},{28,24},{1,5},{5... | collective-permute-start | bytes 12582920 | tf_op jit(solution)/shard_map/ppermute | solution.py:921
  338.9 41.4 %collective-permute-start.27 = (bf16[512,1024]{1,0:T(8,128)(2,1)}, bf16[512,1024]{1,0:T(8,128)(2,1)}, u32[]{:S(2)}, u32[]{:S(2)}) collective-permute-start(bf16[512,1024]{1,0:T(8,128)(2,1)} %get-tuple-element.391), channel_id=1, source_target_pairs={{0,8},{4,12},{8,0},{12,4},{16,24},{20,28},{24,16},{28,20},{1,9},{5... | collective-permute-start | bytes 3145736 | tf_op jit(solution)/shard_map/ppermute | solution.py:921
  339.4 40.8 %collective-permute-start.28 = (bf16[512,1024]{1,0:T(8,128)(2,1)}, bf16[512,1024]{1,0:T(8,128)(2,1)}, u32[]{:S(2)}, u32[]{:S(2)}) collective-permute-start(bf16[512,1024]{1,0:T(8,128)(2,1)} %get-tuple-element.392), channel_id=1, source_target_pairs={{0,16},{4,20},{8,24},{12,28},{16,0},{20,4},{24,8},{28,12},{1,17},{... | collective-permute-start | bytes 3145736 | tf_op jit(solution)/shard_map/ppermute | solution.py:921
  359.9 134.1 %all-gather.8.cloned.1.call-start = ((), (), s32[]{:S(2)}) async-start(), calls=%async_computation.7 | async-start | bytes 3276800 | tf_op jit(solution)/shard_map/all_gather | solution.py:1211
  367.1 22.4 %collective-permute-start.26 = (bf16[1024,1536]{1,0:T(8,128)(2,1)}, bf16[1024,1536]{1,0:T(8,128)(2,1)}, u32[]{:S(2)}, u32[]{:S(2)}) collective-permute-start(bf16[1024,1536]{1,0:T(8,128)(2,1)} %wgrad_away.9), channel_id=1, source_target_pairs={{0,4},{4,0},{8,12},{12,8},{16,20},{20,16},{24,28},{28,24},{1,5},{5... | collective-permute-start | bytes 9437192 | tf_op jit(solution)/shard_map/ppermute | solution.py:921
  367.1 15.0 %collective-permute-start.29 = (bf16[256,1024]{1,0:T(8,128)(2,1)}, bf16[256,1024]{1,0:T(8,128)(2,1)}, u32[]{:S(2)}, u32[]{:S(2)}) collective-permute-start(bf16[256,1024]{1,0:T(8,128)(2,1)} %get-tuple-element.400), channel_id=1, source_target_pairs={{0,16},{4,20},{8,24},{12,28},{16,0},{20,4},{24,8},{28,12},{1,17},{... | collective-permute-start | bytes 1572872 | tf_op jit(solution)/shard_map/ppermute | solution.py:921
  367.7 14.7 %collective-permute-start.30 = (bf16[256,1024]{1,0:T(8,128)(2,1)}, bf16[256,1024]{1,0:T(8,128)(2,1)}, u32[]{:S(2)}, u32[]{:S(2)}) collective-permute-start(bf16[256,1024]{1,0:T(8,128)(2,1)} %get-tuple-element.402), channel_id=1, source_target_pairs={{0,8},{4,12},{8,0},{12,4},{16,24},{20,28},{24,16},{28,20},{1,9},{5... | collective-permute-start | bytes 1572872 | tf_op jit(solution)/shard_map/ppermute | solution.py:921
  380.3 25.3 %collective-permute-start.31 = (bf16[512,1024]{1,0:T(8,128)(2,1)}, bf16[512,1024]{1,0:T(8,128)(2,1)}, u32[]{:S(2)}, u32[]{:S(2)}) collective-permute-start(bf16[512,1024]{1,0:T(8,128)(2,1)} %get-tuple-element.418), channel_id=1, source_target_pairs={{0,8},{4,12},{8,0},{12,4},{16,24},{20,28},{24,16},{28,20},{1,9},{5... | collective-permute-start | bytes 3145736 | tf_op jit(solution)/shard_map/ppermute | solution.py:921
  380.4 25.3 %collective-permute-start.32 = (bf16[512,1024]{1,0:T(8,128)(2,1)}, bf16[512,1024]{1,0:T(8,128)(2,1)}, u32[]{:S(2)}, u32[]{:S(2)}) collective-permute-start(bf16[512,1024]{1,0:T(8,128)(2,1)} %get-tuple-element.419), channel_id=1, source_target_pairs={{0,16},{4,20},{8,24},{12,28},{16,0},{20,4},{24,8},{28,12},{1,17},{... | collective-permute-start | bytes 3145736 | tf_op jit(solution)/shard_map/ppermute | solution.py:921
  421.2 17.0 %collective-permute-start.38 = (bf16[256,1024]{1,0:T(8,128)(2,1)}, bf16[256,1024]{1,0:T(8,128)(2,1)}, u32[]{:S(2)}, u32[]{:S(2)}) collective-permute-start(bf16[256,1024]{1,0:T(8,128)(2,1)} %get-tuple-element.441), channel_id=1, source_target_pairs={{0,16},{4,20},{8,24},{12,28},{16,0},{20,4},{24,8},{28,12},{1,17},{... | collective-permute-start | bytes 1572872 | tf_op jit(solution)/shard_map/ppermute | solution.py:921
  422.7 16.1 %collective-permute-start.39 = (bf16[256,1024]{1,0:T(8,128)(2,1)}, bf16[256,1024]{1,0:T(8,128)(2,1)}, u32[]{:S(2)}, u32[]{:S(2)}) collective-permute-start(bf16[256,1024]{1,0:T(8,128)(2,1)} %get-tuple-element.442), channel_id=1, source_target_pairs={{0,8},{4,12},{8,0},{12,4},{16,24},{20,28},{24,16},{28,20},{1,9},{5... | collective-permute-start | bytes 1572872 | tf_op jit(solution)/shard_map/ppermute | solution.py:921
  424.1 4.2 copy-start.13
  424.1 13.3 %copy-start.5 = (bf16[512,256]{1,0:T(8,128)(2,1)S(1)}, bf16[512,256]{1,0:T(8,128)(2,1)}, u32[]{:S(2)}) copy-start(bf16[512,256]{1,0:T(8,128)(2,1)} %get-tuple-element.430) | copy-start | bytes 786436
  428.3 9.1 %collective-permute-start.33 = (bf16[512,256]{1,0:T(8,128)(2,1)S(1)}, bf16[512,256]{1,0:T(8,128)(2,1)S(1)}, u32[]{:S(2)}, u32[]{:S(2)}) collective-permute-start(bf16[512,256]{1,0:T(8,128)(2,1)S(1)} %copy-done.13), channel_id=1, source_target_pairs={{0,1},{1,2},{2,3},{3,0},{4,5},{5,6},{6,7},{7,4},{8,9},{9,10},{10,1... | collective-permute-start | bytes 786440 | tf_op jit(solution)/shard_map/ppermute | solution.py:999
  429.0 18.6 %collective-permute-start.36 = (bf16[256,1024]{1,0:T(8,128)(2,1)}, bf16[256,1024]{1,0:T(8,128)(2,1)}, u32[]{:S(2)}, u32[]{:S(2)}) collective-permute-start(bf16[256,1024]{1,0:T(8,128)(2,1)} %get-tuple-element.435), channel_id=1, source_target_pairs={{0,16},{4,20},{8,24},{12,28},{16,0},{20,4},{24,8},{28,12},{1,17},{... | collective-permute-start | bytes 1572872 | tf_op jit(solution)/shard_map/ppermute | solution.py:921
  429.6 19.4 %collective-permute-start.37 = (bf16[256,1024]{1,0:T(8,128)(2,1)}, bf16[256,1024]{1,0:T(8,128)(2,1)}, u32[]{:S(2)}, u32[]{:S(2)}) collective-permute-start(bf16[256,1024]{1,0:T(8,128)(2,1)} %get-tuple-element.436), channel_id=1, source_target_pairs={{0,8},{4,12},{8,0},{12,4},{16,24},{20,28},{24,16},{28,20},{1,9},{5... | collective-permute-start | bytes 1572872 | tf_op jit(solution)/shard_map/ppermute | solution.py:921
  438.2 15.9 %collective-permute-start.40 = (bf16[512,256]{1,0:T(8,128)(2,1)}, bf16[512,256]{1,0:T(8,128)(2,1)}, u32[]{:S(2)}, u32[]{:S(2)}) collective-permute-start(bf16[512,256]{1,0:T(8,128)(2,1)} %add_convert_fusion.1), channel_id=1, source_target_pairs={{0,1},{1,2},{2,3},{3,0},{4,5},{5,6},{6,7},{7,4},{8,9},{9,10},{10,1... | collective-permute-start | bytes 786440 | tf_op jit(solution)/shard_map/ppermute | solution.py:999
  438.3 27.7 %collective-permute-start.34 = (bf16[512,768]{1,0:T(8,128)(2,1)}, bf16[512,768]{1,0:T(8,128)(2,1)}, u32[]{:S(2)}, u32[]{:S(2)}) collective-permute-start(bf16[512,768]{1,0:T(8,128)(2,1)} %get-tuple-element.431), channel_id=1, source_target_pairs={{0,8},{4,12},{8,0},{12,4},{16,24},{20,28},{24,16},{28,20},{1,9},{5... | collective-permute-start | bytes 2359304 | tf_op jit(solution)/shard_map/ppermute | solution.py:921
  438.8 27.1 %collective-permute-start.35 = (bf16[512,768]{1,0:T(8,128)(2,1)}, bf16[512,768]{1,0:T(8,128)(2,1)}, u32[]{:S(2)}, u32[]{:S(2)}) collective-permute-start(bf16[512,768]{1,0:T(8,128)(2,1)} %get-tuple-element.432), channel_id=1, source_target_pairs={{0,16},{4,20},{8,24},{12,28},{16,0},{20,4},{24,8},{28,12},{1,17},{... | collective-permute-start | bytes 2359304 | tf_op jit(solution)/shard_map/ppermute | solution.py:921
  439.3 14.8 %copy-start.4 = (bf16[512,256]{1,0:T(8,128)(2,1)S(1)}, bf16[512,256]{1,0:T(8,128)(2,1)}, u32[]{:S(2)}) copy-start(bf16[512,256]{1,0:T(8,128)(2,1)} %get-tuple-element.456) | copy-start | bytes 786436
  455.8 24.4 %collective-permute-start.43 = (bf16[512,256]{1,0:T(8,128)(2,1)}, bf16[512,256]{1,0:T(8,128)(2,1)}, u32[]{:S(2)}, u32[]{:S(2)}) collective-permute-start(bf16[512,256]{1,0:T(8,128)(2,1)} %add_convert_fusion), channel_id=1, source_target_pairs={{0,1},{1,2},{2,3},{3,0},{4,5},{5,6},{6,7},{7,4},{8,9},{9,10},{10,1... | collective-permute-start | bytes 786440 | tf_op jit(solution)/shard_map/ppermute | solution.py:999
  461.7 15.2 %collective-permute-start.44 = (bf16[256,1024]{1,0:T(8,128)(2,1)}, bf16[256,1024]{1,0:T(8,128)(2,1)}, u32[]{:S(2)}, u32[]{:S(2)}) collective-permute-start(bf16[256,1024]{1,0:T(8,128)(2,1)} %get-tuple-element.481), channel_id=1, source_target_pairs={{0,16},{4,20},{8,24},{12,28},{16,0},{20,4},{24,8},{28,12},{1,17},{... | collective-permute-start | bytes 1572872 | tf_op jit(solution)/shard_map/ppermute | solution.py:921
  461.7 15.5 %collective-permute-start.45 = (bf16[256,1024]{1,0:T(8,128)(2,1)}, bf16[256,1024]{1,0:T(8,128)(2,1)}, u32[]{:S(2)}, u32[]{:S(2)}) collective-permute-start(bf16[256,1024]{1,0:T(8,128)(2,1)} %get-tuple-element.483), channel_id=1, source_target_pairs={{0,8},{4,12},{8,0},{12,4},{16,24},{20,28},{24,16},{28,20},{1,9},{5... | collective-permute-start | bytes 1572872 | tf_op jit(solution)/shard_map/ppermute | solution.py:921
  468.7 14.0 %collective-permute-start.41 = (bf16[256,768]{1,0:T(8,128)(2,1)}, bf16[256,768]{1,0:T(8,128)(2,1)}, u32[]{:S(2)}, u32[]{:S(2)}) collective-permute-start(bf16[256,768]{1,0:T(8,128)(2,1)} %get-tuple-element.475), channel_id=1, source_target_pairs={{0,16},{4,20},{8,24},{12,28},{16,0},{20,4},{24,8},{28,12},{1,17},{... | collective-permute-start | bytes 1179656 | tf_op jit(solution)/shard_map/ppermute | solution.py:921
  469.5 14.4 %collective-permute-start.42 = (bf16[256,768]{1,0:T(8,128)(2,1)}, bf16[256,768]{1,0:T(8,128)(2,1)}, u32[]{:S(2)}, u32[]{:S(2)}) collective-permute-start(bf16[256,768]{1,0:T(8,128)(2,1)} %get-tuple-element.477), channel_id=1, source_target_pairs={{0,8},{4,12},{8,0},{12,4},{16,24},{20,28},{24,16},{28,20},{1,9},{5... | collective-permute-start | bytes 1179656 | tf_op jit(solution)/shard_map/ppermute | solution.py:921
  (4 other events, 2.8 us)
Sparse Core Ops, SparseCore 0:
  10.2 83.4 all-gather.9
  95.8 31.2 all-gather.11
  129.2 31.6 all-gather.13
  163.7 30.1 reduce-scatter.3
  197.3 30.5 reduce-scatter.5
  243.8 107.2 all-reduce.1
  360.0 61.1 reduce-scatter.7
  429.1 64.7 all-gather.7
